TPU v7x, 32 devices: a whole 2x2x4 slice. The times are simulated.
32 devices in a mesh: groups: 2 (over y), tp: 4 (over x, core), sub: 4 (over z).
Axes of the slice: x: 2, y: 2, z: 4, core: 2. Of those that a mesh axis runs over, the one named last changes fastest.
Arguments:
- gate_pre: bfloat16 [1536, 32768], P('groups', ('tp', 'sub')), parts along dimension 0, may hold values from -8 to 8
- up_pre: bfloat16 [1536, 32768], P('groups', ('tp', 'sub')), parts along dimension 0, may hold values from -8 to 8
- down_weight: bfloat16 [32768, 16384], P('tp', 'sub'), may hold values from -0.046875 to 0.046875
- residual: bfloat16 [1536, 16384], P('groups', ('sub', 'tp')), parts along dimension 0, may hold values from -20 to 20
- signs: int32 [16384], P('sub'), may hold values from -1 to 1, as said below
- row_slot: int32 [1536], P('groups'), parts along dimension 0, may hold values from 0 to 767, each once
- norm_gain: float32 [16384], P('sub'), may hold values from 0.1 to 1.9
Outputs:
- stream: bfloat16 [1536, 16384], P('groups', ('sub', 'tp')), parts along dimension 0
- normed: bfloat16 [1536, 16384], P('groups', 'sub'), parts along dimension 0
There are 2 independent parts, one for each index of `groups`. A program takes and returns all parts, laid end to end along the dimension named above; an argument that names none is the same for every part. Nothing has to cross between parts.
Inputs may be any that keep to these rules, and one draw needn't show every extreme that they name: `row_slot`: a permutation of the slots. `signs`: every entry is -1 or 1.
All inputs are finite; a program needn't handle non-finite values.
Results may differ from a plain program's by a relative error of at most 0.0056.
Values may be sent and summed in bfloat16 or wider, within the bound.
No kernel may reach another device: no remote copies, remote signals or barrier semaphores. Data moves between devices by JAX's collectives and lax.ppermute only.
A program may use at most 256 MiB of HBM per device.

v0:
```python
import functools

import jax
import jax.numpy as jnp
import numpy as np
from jax import lax
from jax.experimental import pallas as pl
from jax.experimental.pallas import tpu as pltpu
from jax.sharding import PartitionSpec as P

D = 16384
H_SCALE = 0.08838834764831845
VMEM = 48 * 1024 * 1024
TOKEN = (8, 128)


def hadamard_signs():
    index = jnp.arange(128, dtype=jnp.int32)
    common = index[:, None] & index[None, :]
    parity = sum((common >> shift & 1 for shift in range(7)))
    return jnp.where(parity % 2 == 0, 1.0, -1.0).astype(jnp.bfloat16)


def row_units(rows):
    return [rows // 3, rows // 3, rows // 3]


def block_of(width, most):
    size = min(width, most)
    while width % size:
        size //= 2
    return size


def lanes(rows):
    return -(-rows // 128) * 128


def params():
    return pltpu.CompilerParams(vmem_limit_bytes=VMEM)


def anywhere():
    return pl.BlockSpec(memory_space=pl.ANY)


def token_spec():
    return pl.BlockSpec(TOKEN, lambda *_: (0, 0))


TOKEN_SHAPE = jax.ShapeDtypeStruct(TOKEN, jnp.float32)


def hidden_kernel(more, gate, up, *refs):
    out, token = refs[more:]
    value = gate[...].astype(jnp.float32)
    value = value / (1.0 + jnp.exp(-value)) * up[...].astype(jnp.float32)
    out[...] = value.astype(jnp.bfloat16)
    token[...] = jnp.zeros(TOKEN, jnp.float32)


def hidden_rows(gate, up, start, rows, after):
    columns = gate.shape[1]
    place = start // rows
    line = pl.BlockSpec((rows, columns), lambda i: (place, 0))
    return pl.pallas_call(
        functools.partial(hidden_kernel, len(after)),
        grid=(1,),
        in_specs=[line, line] + [token_spec()] * len(after),
        out_specs=[pl.BlockSpec((rows, columns), lambda i: (0, 0)), token_spec()],
        out_shape=[jax.ShapeDtypeStruct((rows, columns), jnp.bfloat16), TOKEN_SHAPE],
        compiler_params=params(),
        cost_estimate=pl.CostEstimate(flops=1, bytes_accessed=1, transcendentals=0),
        name="hidden_rows",
    )(gate, up, *after)


def stage_table(sub, stages):
    found = []
    for place in range(sub):
        entries, source = [], 0
        for d in stages:
            if d == 0:
                entries.append((source, place))
                source += 1
                continue
            if place >= d:
                entries.append((source, place - d))
            if place + d < sub:
                entries.append((source + 1, place + d))
            source += 2
        found.append(entries)
    most = max(len(entries) for entries in found)
    table = np.zeros((sub, 1 + 2 * most), np.int32)
    for place, entries in enumerate(found):
        table[place, 0] = len(entries)
        for p in range(most):
            if entries:
                source, piece = entries[min(p, len(entries) - 1)]
                table[place, 1 + p] = source
                table[place, 1 + most + p] = piece
    return table, most


def matmul_kernel(plan, info, *refs):
    most, per, block, tp, spans, sources, gathered, prior_at, final, skip = plan
    parts = len(spans)
    count = 1 if gathered else sources * parts
    inputs = [refs[s * parts : (s + 1) * parts] for s in range(sources)]
    if gathered:
        size = spans[0][1]
        inputs = [[refs[0].at[s * size : (s + 1) * size]] for s in range(sources)]
    weights = refs[count : count + tp]
    at = count + tp
    prior = refs[at] if prior_at is not None else None
    at += (prior_at is not None) + skip
    number = 1 + tp // 2 if final else 1
    outs = refs[at : at + number]
    token = refs[at + number]
    scratch = refs[at + number + 1 :]
    held, total, sems = scratch[:3]
    step = pl.program_id(0)
    me = info[0]
    pieces = info[1]
    active = step < pieces * per

    @pl.when(step == 0)
    def _():
        for p in range(most):
            for s in range(sources):

                @pl.when((p < pieces) & (info[2 + p] == s))
                def _():
                    for n, (first, size) in enumerate(spans):
                        for q in range(per):
                            pltpu.make_async_copy(
                                inputs[s][n].at[:, q * block : (q + 1) * block],
                                held.at[p * per + q, first : first + size],
                                sems.at[p * per + q, n],
                            ).start()

        if prior is not None:
            pltpu.make_async_copy(
                prior.at[:, prior_at : prior_at + total.shape[1]], scratch[3], scratch[4].at[0]
            ).start()

        @pl.when(pieces == 0)
        def _():
            total[...] = jnp.zeros_like(total)

    @pl.when(active)
    def _():
        for n, (first, size) in enumerate(spans):
            pltpu.make_async_copy(
                inputs[0][n].at[:, 0:block], held.at[step, first : first + size], sems.at[step, n]
            ).wait()
        value = held[step]
        for t in range(tp):
            product = jnp.dot(value, weights[t][...], preferred_element_type=jnp.float32)

            @pl.when(step == 0)
            def _():
                total[t] = product

            @pl.when(step != 0)
            def _():
                total[t] += product

    @pl.when(step == most * per - 1)
    def _():
        if prior is not None:
            pltpu.make_async_copy(
                prior.at[:, prior_at : prior_at + total.shape[1]], scratch[3], scratch[4].at[0]
            ).wait()

        def result(t):
            value = total[t]
            return value if prior is None else value + scratch[3][t]

        if final:
            for k in range(tp // 2):
                outs[0][k] = result(me ^ (2 * k))
                outs[1 + k][...] = result(me ^ (2 * k + 1)).astype(jnp.bfloat16)
        else:
            if prior is not None:
                total[...] += scratch[3][...]
            copy = pltpu.make_async_copy(total, outs[0], scratch[-1].at[0])
            copy.start()
            copy.wait()
        token[...] = jnp.zeros(TOKEN, jnp.float32)


def matmul_stage(place, me, stages, sub, tp, inputs, weight, prior, prior_at, final, after):
    gathered = not isinstance(inputs, list)
    if gathered:
        flat = [inputs]
        sizes = [inputs.shape[0] // sub]
    else:
        flat = [part for source in inputs for part in source]
        sizes = [part.shape[0] for part in inputs[0]]
    rows = sum(sizes)
    spans = [(sum(sizes[:n]), size) for n, size in enumerate(sizes)]
    depth = flat[0].shape[1]
    block = block_of(depth, 512)
    per = depth // block
    columns = weight.shape[1]
    width = columns // tp
    if gathered:
        most = sub
        info = jnp.concatenate([me[None], jnp.asarray([sub, *range(sub), *range(sub)], jnp.int32)])
    else:
        table, most = stage_table(sub, stages)
        info = jnp.concatenate([me[None], jnp.asarray(table)[place]])

    def row_block(j, s):
        last = jnp.maximum(s[1] * per - 1, 0)
        j = jnp.minimum(j, last)
        return s[2 + most + j // per] * per + j % per

    operands = [*flat] + [weight] * tp
    specs = [anywhere()] * len(flat) + [
        pl.BlockSpec((block, width), lambda j, s, t=t: (row_block(j, s), t)) for t in range(tp)
    ]
    scratch = [
        pltpu.VMEM((most * per, rows, block), jnp.bfloat16),
        pltpu.VMEM((tp, rows, width), jnp.float32),
        pltpu.SemaphoreType.DMA((most * per, len(sizes))),
    ]
    if prior is not None:
        operands.append(prior)
        specs.append(anywhere())
        scratch += [pltpu.VMEM((tp, rows, width), jnp.float32), pltpu.SemaphoreType.DMA((1,))]
    if not final:
        scratch.append(pltpu.SemaphoreType.DMA((1,)))
    operands += after
    specs += [token_spec()] * len(after)
    if final:
        out_specs = [pl.BlockSpec((tp // 2, rows, width), lambda j, s: (0, 0, 0))]
        out_specs += [pl.BlockSpec((rows, width), lambda j, s: (0, 0))] * (tp // 2)
        out_shape = [jax.ShapeDtypeStruct((tp // 2, rows, width), jnp.float32)]
        out_shape += [jax.ShapeDtypeStruct((rows, width), jnp.bfloat16)] * (tp // 2)
    else:
        out_specs = [anywhere()]
        out_shape = [jax.ShapeDtypeStruct((tp, rows, width), jnp.float32)]
    out_specs.append(token_spec())
    out_shape.append(TOKEN_SHAPE)
    plan = (
        most,
        per,
        block,
        tp,
        spans,
        sub if gathered else len(inputs),
        gathered,
        None if prior is None else prior_at,
        final,
        len(after),
    )
    return pl.pallas_call(
        functools.partial(matmul_kernel, plan),
        grid_spec=pltpu.PrefetchScalarGridSpec(
            num_scalar_prefetch=1,
            grid=(most * per,),
            in_specs=specs,
            out_specs=out_specs,
            scratch_shapes=scratch,
        ),
        out_shape=out_shape,
        compiler_params=params(),
        cost_estimate=pl.CostEstimate(flops=1, bytes_accessed=1, transcendentals=0),
        name="matmul_stage",
    )(info, *operands)


def gate_kernel(count, *refs):
    refs[-1][...] = jnp.zeros(TOKEN, jnp.float32)


def gate(values, after):
    count = len(values)
    outs = pl.pallas_call(
        functools.partial(gate_kernel, count),
        in_specs=[anywhere()] * count + [pl.BlockSpec(TOKEN, lambda: (0, 0))] * len(after),
        out_specs=[anywhere()] * count + [pl.BlockSpec(TOKEN, lambda: (0, 0))],
        out_shape=[jax.ShapeDtypeStruct(v.shape, v.dtype) for v in values] + [TOKEN_SHAPE],
        input_output_aliases={n: n for n in range(count)},
        compiler_params=params(),
        cost_estimate=pl.CostEstimate(flops=1, bytes_accessed=1, transcendentals=0),
        name="gate",
    )(*values, *after)
    return list(outs[:count]), [outs[count]]


def halve_kernel(cut, more, keep, *refs):
    half = keep.shape[0] // 2
    got = refs[: 2 * half]
    *outs, token = refs[2 * half + more :]
    size = keep.shape[1] // cut
    for k in range(half):
        value = (keep[2 * k + 1] + got[2 * k + 1][...].astype(jnp.float32)).astype(jnp.bfloat16)
        for n in range(cut):
            outs[k * cut + n][...] = value[n * size : (n + 1) * size]
        if half > 1:
            outs[half * cut][k] = keep[2 * k] + got[2 * k][...].astype(jnp.float32)
    token[...] = jnp.zeros(TOKEN, jnp.float32)


def halve(keep, got, cut, after):
    count, rows, width = keep.shape
    half = count // 2
    stack = lambda n: pl.BlockSpec((n, rows, width), lambda i: (0, 0, 0))
    flat = lambda n: pl.BlockSpec((n, width), lambda i: (0, 0))
    size = rows // cut
    out_specs = [flat(size)] * (half * cut)
    out_shape = [jax.ShapeDtypeStruct((size, width), jnp.bfloat16)] * (half * cut)
    if half > 1:
        out_specs.append(stack(half))
        out_shape.append(jax.ShapeDtypeStruct((half, rows, width), jnp.float32))
    outs = pl.pallas_call(
        functools.partial(halve_kernel, cut, len(after)),
        grid=(1,),
        in_specs=[stack(count)] + [flat(rows)] * count + [token_spec()] * len(after),
        out_specs=out_specs + [token_spec()],
        out_shape=out_shape + [TOKEN_SHAPE],
        compiler_params=params(),
        cost_estimate=pl.CostEstimate(flops=1, bytes_accessed=1, transcendentals=0),
        name="halve",
    )(keep, *got, *after)
    return outs[: half * cut], outs[half * cut] if half > 1 else None, outs[-1]


def stream_kernel(cut, more, *refs):
    keep, first, *last = refs[: 2 + cut]
    signs, matrix, residual = refs[2 + cut : 5 + cut]
    stream, chunk, squares = refs[5 + cut + more :]
    last = jnp.concatenate([part[...].astype(jnp.float32) for part in last], axis=0)
    total = keep[...] + first[...].astype(jnp.float32) + last
    total = total * signs[...].astype(jnp.float32)
    rows, width = total.shape
    turn = matrix[...]
    for b in range(width // 128):
        piece = total[:, b * 128 : (b + 1) * 128]
        rotated = jnp.zeros((rows, 128), jnp.float32)
        for _ in range(3):
            part = piece.astype(jnp.bfloat16)
            rotated = rotated + jnp.dot(part, turn, preferred_element_type=jnp.float32)
            piece = piece - part.astype(jnp.float32)
        kept = residual[:, b * 128 : (b + 1) * 128].astype(jnp.float32)
        value = (kept + rotated * H_SCALE).astype(jnp.bfloat16)
        stream[:, b * 128 : (b + 1) * 128] = value
        chunk[:, b * 128 : (b + 1) * 128] = value
    local = chunk[...].astype(jnp.float32)
    squares[...] = jnp.zeros_like(squares)
    squares[:, 0:rows] = lax.dot_general(
        jnp.ones((8, width), jnp.float32),
        local * local,
        (((1,), (1,)), ((), ())),
        precision=lax.Precision.HIGHEST,
        preferred_element_type=jnp.float32,
    )


def stream_rows(terms, signs, matrix, residual, so_far, start, after):
    keep, first, last = terms
    _, rows, width = keep.shape
    cut = len(last)
    place = start // rows
    line = pl.BlockSpec((rows, width), lambda i: (place, 0))
    flat = lambda n: pl.BlockSpec((n, width), lambda i: (0, 0))
    operands = [keep, first, *last, signs, matrix, residual]
    specs = [pl.BlockSpec((None, rows, width), lambda i: (0, 0, 0)), flat(rows)]
    specs += [flat(rows // cut)] * cut
    specs += [
        pl.BlockSpec((1, width), lambda i: (0, 0)),
        pl.BlockSpec((128, 128), lambda i: (0, 0)),
        line,
    ]
    aliases = {}
    if so_far is not None:
        aliases = {len(operands): 0}
        operands.append(so_far)
        specs.append(anywhere())
    operands += after
    specs += [token_spec()] * len(after)
    return pl.pallas_call(
        functools.partial(stream_kernel, cut, len(aliases) + len(after)),
        grid=(1,),
        in_specs=specs,
        out_specs=[
            line,
            pl.BlockSpec((rows, width), lambda i: (0, 0)),
            pl.BlockSpec((8, lanes(rows)), lambda i: (0, 0)),
        ],
        out_shape=[
            jax.ShapeDtypeStruct(residual.shape, jnp.bfloat16),
            jax.ShapeDtypeStruct((rows, width), jnp.bfloat16),
            jax.ShapeDtypeStruct((8, lanes(rows)), jnp.float32),
        ],
        input_output_aliases=aliases,
        compiler_params=params(),
        cost_estimate=pl.CostEstimate(flops=1, bytes_accessed=1, transcendentals=0),
        name="stream_rows",
    )(*operands)


def norm_kernel(places, more, info, *refs):
    tp = len(places)
    pieces = refs[:tp]
    first, second, gain = refs[tp : tp + 3]
    out, token = refs[tp + 3 + more :]
    token[...] = jnp.zeros(TOKEN, jnp.float32)
    inverse = lax.rsqrt((first[...] + second[...]) / D + 1e-05)
    rows, width = pieces[0].shape
    scale = jnp.transpose(inverse)[0:rows, 0:1]
    for e, piece in zip(places, pieces):
        at = pl.ds(pl.multiple_of((info[0] ^ e) * width, width), width)
        value = piece[...].astype(jnp.float32) * scale * gain[:, at]
        out[:, at] = value.astype(jnp.bfloat16)


def norm_rows(me, pieces, squares, column, gain, so_far, start, all_rows, after):
    tp = len(pieces)
    rows, width = pieces[0][1].shape
    place = start // rows
    small = pl.BlockSpec((8, lanes(rows)), lambda i, s: (0, column))
    operands = [piece for _, piece in pieces] + [*squares, gain]
    specs = (
        [pl.BlockSpec((rows, width), lambda i, s: (0, 0))] * tp
        + [small] * 2
        + [pl.BlockSpec((1, tp * width), lambda i, s: (0, 0))]
    )
    aliases = {}
    if so_far is not None:
        aliases = {1 + len(operands): 0}
        operands.append(so_far)
        specs.append(anywhere())
    operands += after
    specs += [token_spec()] * len(after)
    return pl.pallas_call(
        functools.partial(norm_kernel, [e for e, _ in pieces], len(aliases) + len(after)),
        grid_spec=pltpu.PrefetchScalarGridSpec(
            num_scalar_prefetch=1,
            grid=(1,),
            in_specs=specs,
            out_specs=[
                pl.BlockSpec((rows, tp * width), lambda i, s: (place, 0)),
                token_spec(),
            ],
        ),
        out_shape=[jax.ShapeDtypeStruct((all_rows, tp * width), jnp.bfloat16), TOKEN_SHAPE],
        input_output_aliases=aliases,
        compiler_params=params(),
        cost_estimate=pl.CostEstimate(flops=1, bytes_accessed=1, transcendentals=0),
        name="norm_rows",
    )(me[None], *operands)


def shards(sub, tp, gate_pre, up_pre, down_weight, residual, signs, row_slot, norm_gain):
    rows = gate_pre.shape[0]
    width = residual.shape[1]
    place = lax.axis_index("sub").astype(jnp.int32)
    me = lax.axis_index("tp").astype(jnp.int32)
    matrix = hadamard_signs()
    mine = jnp.take(residual, row_slot, axis=0, mode="clip")
    signs_own = lax.dynamic_slice_in_dim(signs, me * width, width, 0).reshape(1, width)
    gain = norm_gain.reshape(1, -1)
    bits = [1 << b for b in range(tp.bit_length() - 1)]

    sizes = row_units(rows)
    starts = [sum(sizes[:u]) for u in range(len(sizes))]

    def swap(value, d):
        return lax.ppermute(value, "tp", [(i, i ^ d) for i in range(tp)])

    def onward(pair, d):
        up = lax.ppermute(pair[0], "sub", [(i, i + 1) for i in range(d - 1, sub - 1)])
        down = lax.ppermute(pair[1], "sub", [(i, i - 1) for i in range(1, sub - d + 1)])
        return [up, down]

    def matmul(stages, inputs, prior, start, final, after):
        return matmul_stage(
            place, me, stages, sub, tp, inputs, down_weight, prior, start, final, after
        )

    terms, held = {}, {}
    streams = [None]
    pieces, squares = {}, {}

    def begin_sums(u, keep, *send):
        terms[u] = [keep, [swap(value, bits[0]) for value in send]]

    def halve_sums(u, after):
        keep, got = terms[u]
        for bit in bits[1:]:
            send, kept, token = halve(keep, got, 1, after)
            after = [token]
            arrived = [swap(value, bit) for value in send]
            if kept is None:
                terms[u] = [keep, got[0], arrived]
            else:
                keep, got = kept, arrived
        return after

    def finish(u, after):
        streams[0], chunk, squares[u] = stream_rows(
            terms[u], signs_own, matrix, mine, streams[0], starts[u], after
        )
        found = [(0, chunk)]
        for bit in reversed(bits):
            found += [(e | bit, swap(value, bit)) for e, value in found]
        pieces[u] = found
        return [squares[u]]

    def exchange(local):
        along = local
        for d in range(1, sub):
            along = along + lax.ppermute(local, "sub", [(i, (i + d) % sub) for i in range(sub)])
        for bit in reversed(bits[1:]):
            along = along + swap(along, bit)
        return [along, swap(along, bits[0])]

    normed = [None]

    def normalise(us, totals, after):
        for n, u in enumerate(us):
            normed[0], token = norm_rows(
                me,
                pieces[u],
                totals,
                n,
                gain,
                normed[0],
                starts[u],
                rows,
                after,
            )
            after = [token]
        return after

    early, middle, late = [0, 1], list(range(2, sub - 1)), [sub - 1]
    own = [None] * 3
    came = {}

    def make(u, after):
        own[u], token = hidden_rows(gate_pre, up_pre, starts[u], sizes[u], after)
        came[1, u] = onward([own[u], own[u]], 1)
        return [token]

    def pass_on(u, first, last):
        for d in range(first, last + 1):
            came[d, u] = onward(came[d - 1, u], d)

    def matmul(us, stages, prior, start, final, after):
        inputs = []
        for d in stages:
            if d == 0:
                inputs.append([own[u] for u in us])
            else:
                inputs += [[came[d, u][side] for u in us] for side in range(2)]
        return matmul_stage(
            place, me, stages, sub, tp, inputs, down_weight, prior, start, final, after
        )

    def hold(keys, after):
        values, token = gate([value for key in keys for value in came[key]], after)
        for n, key in enumerate(keys):
            came[key] = values[2 * n : 2 * n + 2]
        return token

    mid = middle[-1]
    token = make(0, [])
    token = make(1, token)
    token = hold([(1, 0)], token)
    pass_on(0, 2, mid)
    token = make(2, token)
    part, *token = matmul([0], early, None, 0, False, token)
    hold([(1, 1)], token)
    pass_on(1, 2, mid)
    token = hold([(mid, 0), (1, 2)], token)
    pass_on(0, sub - 1, sub - 1)
    parts, *token = matmul([1, 2], early, None, 0, False, token)
    token = hold([(1, 2), (mid, 1)], token)
    pass_on(2, 2, mid)
    *sums, token = matmul([0], middle + late, part, 0, True, token)
    begin_sums(0, *sums)
    token = hold([(mid, 1)], [token])
    pass_on(1, sub - 1, sub - 1)
    parts, *token = matmul([1, 2], middle, parts, 0, False, token)
    hold([(mid, 2)], token)
    pass_on(2, sub - 1, sub - 1)
    token = halve_sums(0, token)
    *sums, token = matmul([1], late, parts, 0, True, token)
    begin_sums(1, *sums)
    token = finish(0, [token])
    token = halve_sums(1, token)
    *sums, token = matmul([2], late, parts, sizes[1], True, token)
    begin_sums(2, *sums)
    token = finish(1, [token])
    token = halve_sums(2, token)
    totals = exchange(jnp.concatenate([squares[0], squares[1]], axis=1))
    token = normalise([0, 1], totals, token)
    finish(2, token)
    normalise([2], exchange(squares[2]), [])
    return (streams[0], normed[0])


def solution(mesh):
    return jax.shard_map(
        functools.partial(shards, mesh.shape["sub"], mesh.shape["tp"]),
        mesh=mesh,
        in_specs=(
            P("groups", ("tp", "sub")),
            P("groups", ("tp", "sub")),
            P("tp", "sub"),
            P("groups", ("sub", "tp")),
            P("sub"),
            P("groups"),
            P("sub"),
        ),
        out_specs=(P("groups", ("sub", "tp")), P("groups", "sub")),
        check_vma=False,
    )
```

profile of v0, /device:TPU:0, one launch (start us, length us, event | category | flops | bytes accessed | tf_op | source)
XLA Modules:
  0.0 326.3 jit_solution(17369617214637287362)
XLA Ops:
  0.7 2.0 copy-done.1
  2.7 1.9 hidden_rows.3
  4.5 5.9 %collective-permute-start = (bf16[256,2048]{1,0:T(8,128)(2,1)S(1)}, bf16[256,2048]{1,0:T(8,128)(2,1)}, u32[]{:S(2)}, u32[]{:S(2)}) collective-permute-start(bf16[256,2048]{1,0:T(8,128)(2,1)S(1)} %get-tuple-element.66.refs_0_), channel_id=1, source_target_pairs={{0,1},{1,2},{2,3},{4,5},{5,6},{6,7},{8,9},{9,10},{10,11},{12,13},{... | collective-permute-start | bytes 3145736 | tf_op jit(solution)/shard_map/ppermute | solution.py:476
  11.8 3.0 hidden_rows.4
  14.8 4.6 %collective-permute-start.6 = (bf16[256,2048]{1,0:T(8,128)(2,1)}, bf16[256,2048]{1,0:T(8,128)(2,1)S(1)}, u32[]{:S(2)}, u32[]{:S(2)}) collective-permute-start(bf16[256,2048]{1,0:T(8,128)(2,1)} %get-tuple-element.77.refs_0_), channel_id=1, source_target_pairs={{0,1},{1,2},{2,3},{4,5},{5,6},{6,7},{8,9},{9,10},{10,11},{12,13},{... | collective-permute-start | bytes 3145736 | tf_op jit(solution)/shard_map/ppermute | solution.py:476
  19.4 1.3 collective-permute-start.7
  20.7 12.4 %collective-permute-done.refs_0_ = bf16[256,2048]{1,0:T(8,128)(2,1)} collective-permute-done((bf16[256,2048]{1,0:T(8,128)(2,1)S(1)}, bf16[256,2048]{1,0:T(8,128)(2,1)}, u32[]{:S(2)}, u32[]{:S(2)}) %collective-permute-start) | collective-permute-done | bytes 1048608 | tf_op jit(solution)/shard_map/ppermute | solution.py:476
  33.0 5.5 %collective-permute-done.1.refs_1_ = bf16[256,2048]{1,0:T(8,128)(2,1)} collective-permute-done((bf16[256,2048]{1,0:T(8,128)(2,1)S(1)}, bf16[256,2048]{1,0:T(8,128)(2,1)}, u32[]{:S(2)}, u32[]{:S(2)}) %collective-permute-start.1) | collective-permute-done | bytes 1048608 | tf_op jit(solution)/shard_map/ppermute | solution.py:477
  38.5 2.9 hidden_rows.5
  41.4 2.6 collective-permute-start.4
  44.0 1.3 collective-permute-start.5
  45.3 1.7 collective-permute-start.2
  46.9 8.7 %collective-permute-done.6.refs_0_ = bf16[256,2048]{1,0:T(8,128)(2,1)S(1)} collective-permute-done((bf16[256,2048]{1,0:T(8,128)(2,1)}, bf16[256,2048]{1,0:T(8,128)(2,1)S(1)}, u32[]{:S(2)}, u32[]{:S(2)}) %collective-permute-start.6) | collective-permute-done | bytes 1048608 | tf_op jit(solution)/shard_map/ppermute | solution.py:476
  60.0 23.4 %matmul_stage.6 = (f32[4,256,1024]{2,1,0:T(8,128)}, f32[8,128]{1,0:T(8,128)S(1)}) custom-call(s32[8]{0:T(128)S(1)} %pad_add_fusion.1.info, bf16[256,2048]{1,0:T(8,128)(2,1)S(1)} %copy-done.12, bf16[256,2048]{1,0:T(8,128)(2,1)} %get-tuple-element.69.refs_1_, bf16[256,2048]{1,0:T(8,128)(2,1)} %get-tuple-element.70.refs_2_, bf16[8192,4096]{1,0:T(8,128)(2,1)} %refs_5_.9, ...), custom_call_target="tpu_custom_call" | custom-call | flops 1 | bytes 1 | tf_op jit(solution)/shard_map/matmul_stage/pallas_call | solution.py:259
  84.7 1.3 collective-permute-start.9
  86.0 19.9 %collective-permute-done.3.refs_1_ = bf16[256,2048]{1,0:T(8,128)(2,1)} collective-permute-done((bf16[256,2048]{1,0:T(8,128)(2,1)}, bf16[256,2048]{1,0:T(8,128)(2,1)}, u32[]{:S(2)}, u32[]{:S(2)}) %collective-permute-start.3) | collective-permute-done | bytes 1048608 | tf_op jit(solution)/shard_map/ppermute | solution.py:477
  106.7 1.3 collective-permute-start.13
  108.0 38.4 %matmul_stage.7 = (f32[4,512,1024]{2,1,0:T(8,128)}, f32[8,128]{1,0:T(8,128)S(1)}) custom-call(s32[8]{0:T(128)S(1)} %pad_add_fusion.1.info, bf16[256,2048]{1,0:T(8,128)(2,1)} %get-tuple-element.77.refs_0_, bf16[256,2048]{1,0:T(8,128)(2,1)} %get-tuple-element.72.refs_1_, bf16[256,2048]{1,0:T(8,128)(2,1)S(1)} %get-tuple-element.78.refs_2_, ...), custom_call_target="tpu_custom_call" | custom-call | flops 1 | bytes 1 | tf_op jit(solution)/shard_map/matmul_stage/pallas_call | solution.py:259
  146.4 1.7 collective-permute-start.10
  148.7 1.5 collective-permute-start.11
  150.3 23.9 %matmul_stage.8 = (f32[2,256,1024]{2,1,0:T(8,128)}, bf16[256,1024]{1,0:T(8,128)(2,1)S(1)}, bf16[256,1024]{1,0:T(8,128)(2,1)S(1)}, f32[8,128]{1,0:T(8,128)S(1)}) custom-call(s32[6]{0:T(128)S(1)} %pad_add_fusion.3.info, bf16[256,2048]{1,0:T(8,128)(2,1)} %get-tuple-element.86.refs_0_, bf16[256,2048]{1,0:T(8,128)(2,1)} %get-tuple-element.87.refs_1_, ...), custom_call_target="tpu_custom_call" | custom-call | flops 1 | bytes 1 | tf_op jit(solution)/shard_map/matmul_stage/pallas_call | solution.py:259
  178.3 14.6 %collective-permute-done.11.refs_3_.refs_1_ = bf16[256,2048]{1,0:T(8,128)(2,1)} collective-permute-done((bf16[256,2048]{1,0:T(8,128)(2,1)}, bf16[256,2048]{1,0:T(8,128)(2,1)}, u32[]{:S(2)}, u32[]{:S(2)}) %collective-permute-start.11) | collective-permute-done | bytes 1048608 | tf_op jit(solution)/shard_map/ppermute | solution.py:477
  192.9 23.1 %matmul_stage.9 = (f32[4,512,1024]{2,1,0:T(8,128)}, f32[8,128]{1,0:T(8,128)S(1)}) custom-call(s32[4]{0:T(128)S(1)} %pad_add_fusion.2.info, bf16[256,2048]{1,0:T(8,128)(2,1)S(1)} %get-tuple-element.91.refs_0_, bf16[256,2048]{1,0:T(8,128)(2,1)} %collective-permute-done.10.refs_1_.refs_0_, bf16[256,2048]{1,0:T(8,128)(2,1)S(1)} %get-tuple-element.92.refs_2_, ...), custom_call_target="tpu_custom_call" | custom-call | flops 1 | bytes 1 | tf_op jit(solution)/shard_map/matmul_stage/pallas_call | solution.py:259
  216.6 1.8 collective-permute-start.14
  218.4 1.5 collective-permute-start.15
  220.8 1.5 collective-permute-start.22
  222.4 13.1 %matmul_stage.10 = (f32[2,256,1024]{2,1,0:T(8,128)S(1)}, bf16[256,1024]{1,0:T(8,128)(2,1)}, bf16[256,1024]{1,0:T(8,128)(2,1)}, f32[8,128]{1,0:T(8,128)S(1)}) custom-call(s32[4]{0:T(128)S(1)} %pad_add_fusion.info, bf16[256,2048]{1,0:T(8,128)(2,1)S(1)} %collective-permute-done.16.refs_0_, bf16[256,2048]{1,0:T(8,128)(2,1)S(1)} %collective-permute-done.17.refs_1_, ...), custom_call_target="tpu_custom_call" | custom-call | flops 1 | bytes 1 | tf_op jit(solution)/shard_map/matmul_stage/pallas_call | solution.py:259
  235.5 1.3 copy-done.5
  238.0 2.8 gather_fusion
  240.9 1.6 copy-done.4
  243.6 3.0 stream_rows.3
  248.4 1.5 collective-permute-start.35
  249.9 13.5 %matmul_stage.11 = (f32[2,256,1024]{2,1,0:T(8,128)S(1)}, bf16[256,1024]{1,0:T(8,128)(2,1)S(1)}, bf16[256,1024]{1,0:T(8,128)(2,1)S(1)}, f32[8,128]{1,0:T(8,128)S(1)}) custom-call(s32[4]{0:T(128)S(1)} %pad_add_fusion.info, bf16[256,2048]{1,0:T(8,128)(2,1)} %collective-permute-done.14.refs_0_, bf16[256,2048]{1,0:T(8,128)(2,1)} %collective-permute-done.15.refs_1_, ...), custom_call_target="tpu_custom_call" | custom-call | flops 1 | bytes 1 | tf_op jit(solution)/shard_map/matmul_stage/pallas_call | solution.py:259
  264.0 2.6 stream_rows.4
  267.1 5.5 %collective-permute-done.30 = f32[8,512]{1,0:T(8,128)S(1)} collective-permute-done((f32[8,512]{1,0:T(8,128)S(1)}, f32[8,512]{1,0:T(8,128)S(1)}, u32[]{:S(2)}, u32[]{:S(2)}) %collective-permute-start.30) | collective-permute-done | bytes 16416 | tf_op jit(solution)/shard_map/ppermute | solution.py:517
  272.7 4.6 %collective-permute-done.31 = f32[8,512]{1,0:T(8,128)S(1)} collective-permute-done((f32[8,512]{1,0:T(8,128)S(1)}, f32[8,512]{1,0:T(8,128)S(1)}, u32[]{:S(2)}, u32[]{:S(2)}) %collective-permute-start.31) | collective-permute-done | bytes 16416 | tf_op jit(solution)/shard_map/ppermute | solution.py:517
  277.3 3.7 %collective-permute-done.32 = f32[8,512]{1,0:T(8,128)S(1)} collective-permute-done((f32[8,512]{1,0:T(8,128)S(1)}, f32[8,512]{1,0:T(8,128)S(1)}, u32[]{:S(2)}, u32[]{:S(2)}) %collective-permute-start.32) | collective-permute-done | bytes 16416 | tf_op jit(solution)/shard_map/ppermute | solution.py:517
  281.1 1.6 collective-permute-start.33
  284.9 1.5 collective-permute-start.26
  287.6 2.1 norm_rows.3
  289.7 2.1 norm_rows.4
  291.8 6.9 %collective-permute-done.26.refs_2_ = bf16[256,1024]{1,0:T(8,128)(2,1)S(1)} collective-permute-done((bf16[256,1024]{1,0:T(8,128)(2,1)S(1)}, bf16[256,1024]{1,0:T(8,128)(2,1)S(1)}, u32[]{:S(2)}, u32[]{:S(2)}) %collective-permute-start.26) | collective-permute-done | bytes 524320 | tf_op jit(solution)/shard_map/ppermute | solution.py:473
  298.7 1.5 stream_rows.5
  301.1 12.2 %collective-permute-done.38.refs_1_ = bf16[256,1024]{1,0:T(8,128)(2,1)S(1)} collective-permute-done((bf16[256,1024]{1,0:T(8,128)(2,1)S(1)}, bf16[256,1024]{1,0:T(8,128)(2,1)S(1)}, u32[]{:S(2)}, u32[]{:S(2)}) %collective-permute-start.38) | collective-permute-done | bytes 524320 | tf_op jit(solution)/shard_map/ppermute | solution.py:473
  314.2 2.9 collective-permute-start.43
  317.1 1.6 collective-permute-done.41
  319.6 3.4 %collective-permute-done.44 = f32[8,256]{1,0:T(8,128)S(1)} collective-permute-done((f32[8,256]{1,0:T(8,128)S(1)}, f32[8,256]{1,0:T(8,128)S(1)}, u32[]{:S(2)}, u32[]{:S(2)}) %collective-permute-start.44) | collective-permute-done | bytes 8224 | tf_op jit(solution)/shard_map/ppermute | solution.py:473
  324.2 2.1 norm_rows.5
  (116 shorter events, 26.7 us)
Async XLA Ops:
  0.6 237.4 %copy-start = (bf16[768,1024]{1,0:T(8,128)(2,1)S(1)}, bf16[768,1024]{1,0:T(8,128)(2,1)}, u32[]{:S(2)}) copy-start(bf16[768,1024]{1,0:T(8,128)(2,1)} %param.16) | copy-start | bytes 4718596
  4.5 28.5 %collective-permute-start = (bf16[256,2048]{1,0:T(8,128)(2,1)S(1)}, bf16[256,2048]{1,0:T(8,128)(2,1)}, u32[]{:S(2)}, u32[]{:S(2)}) collective-permute-start(bf16[256,2048]{1,0:T(8,128)(2,1)S(1)} %get-tuple-element.66.refs_0_), channel_id=1, source_target_pairs={{0,1},{1,2},{2,3},{4,5},{5,6},{6,7},{8,9},{9,10},{10,11},{12,13},{... | collective-permute-start | bytes 3145736 | tf_op jit(solution)/shard_map/ppermute | solution.py:476
  10.5 28.1 %collective-permute-start.1 = (bf16[256,2048]{1,0:T(8,128)(2,1)S(1)}, bf16[256,2048]{1,0:T(8,128)(2,1)}, u32[]{:S(2)}, u32[]{:S(2)}) collective-permute-start(bf16[256,2048]{1,0:T(8,128)(2,1)S(1)} %get-tuple-element.66.refs_0_), channel_id=1, source_target_pairs={{1,0},{2,1},{3,2},{5,4},{6,5},{7,6},{9,8},{10,9},{11,10},{13,12},{... | collective-permute-start | bytes 3145736 | tf_op jit(solution)/shard_map/ppermute | solution.py:477
  11.7 26.8 %copy-start.2 = (bf16[768,2048]{1,0:T(8,128)(2,1)S(1)}, bf16[768,2048]{1,0:T(8,128)(2,1)}, u32[]{:S(2)}) copy-start(bf16[768,2048]{1,0:T(8,128)(2,1)} %gate.12) | copy-start | bytes 9437188
  14.8 40.8 %collective-permute-start.6 = (bf16[256,2048]{1,0:T(8,128)(2,1)}, bf16[256,2048]{1,0:T(8,128)(2,1)S(1)}, u32[]{:S(2)}, u32[]{:S(2)}) collective-permute-start(bf16[256,2048]{1,0:T(8,128)(2,1)} %get-tuple-element.77.refs_0_), channel_id=1, source_target_pairs={{0,1},{1,2},{2,3},{4,5},{5,6},{6,7},{8,9},{9,10},{10,11},{12,13},{... | collective-permute-start | bytes 3145736 | tf_op jit(solution)/shard_map/ppermute | solution.py:476
  19.4 64.0 %collective-permute-start.7 = (bf16[256,2048]{1,0:T(8,128)(2,1)}, bf16[256,2048]{1,0:T(8,128)(2,1)}, u32[]{:S(2)}, u32[]{:S(2)}) collective-permute-start(bf16[256,2048]{1,0:T(8,128)(2,1)} %get-tuple-element.77.refs_0_), channel_id=1, source_target_pairs={{1,0},{2,1},{3,2},{5,4},{6,5},{7,6},{9,8},{10,9},{11,10},{13,12},{... | collective-permute-start | bytes 3145736 | tf_op jit(solution)/shard_map/ppermute | solution.py:477
  41.4 43.3 %collective-permute-start.4 = (bf16[256,2048]{1,0:T(8,128)(2,1)}, bf16[256,2048]{1,0:T(8,128)(2,1)S(1)}, u32[]{:S(2)}, u32[]{:S(2)}) collective-permute-start(bf16[256,2048]{1,0:T(8,128)(2,1)} %get-tuple-element.72.refs_1_), channel_id=1, source_target_pairs={{0,1},{1,2},{2,3},{4,5},{5,6},{6,7},{8,9},{9,10},{10,11},{12,13},{... | collective-permute-start | bytes 3145736 | tf_op jit(solution)/shard_map/ppermute | solution.py:476
  44.0 42.0 %collective-permute-start.5 = (bf16[256,2048]{1,0:T(8,128)(2,1)}, bf16[256,2048]{1,0:T(8,128)(2,1)}, u32[]{:S(2)}, u32[]{:S(2)}) collective-permute-start(bf16[256,2048]{1,0:T(8,128)(2,1)} %get-tuple-element.72.refs_1_), channel_id=1, source_target_pairs={{1,0},{2,1},{3,2},{5,4},{6,5},{7,6},{9,8},{10,9},{11,10},{13,12},{... | collective-permute-start | bytes 3145736 | tf_op jit(solution)/shard_map/ppermute | solution.py:477
  45.3 40.7 %collective-permute-start.2 = (bf16[256,2048]{1,0:T(8,128)(2,1)}, bf16[256,2048]{1,0:T(8,128)(2,1)}, u32[]{:S(2)}, u32[]{:S(2)}) collective-permute-start(bf16[256,2048]{1,0:T(8,128)(2,1)} %get-tuple-element.69.refs_1_), channel_id=1, source_target_pairs={{1,2},{2,3},{5,6},{6,7},{9,10},{10,11},{13,14},{14,15},{17,18},{18... | collective-permute-start | bytes 3145736 | tf_op jit(solution)/shard_map/ppermute | solution.py:476
  56.7 49.3 %collective-permute-start.3 = (bf16[256,2048]{1,0:T(8,128)(2,1)}, bf16[256,2048]{1,0:T(8,128)(2,1)}, u32[]{:S(2)}, u32[]{:S(2)}) collective-permute-start(bf16[256,2048]{1,0:T(8,128)(2,1)} %get-tuple-element.70.refs_2_), channel_id=1, source_target_pairs={{1,0},{2,1},{5,4},{6,5},{9,8},{10,9},{13,12},{14,13},{17,16},{18,1... | collective-permute-start | bytes 3145736 | tf_op jit(solution)/shard_map/ppermute | solution.py:477
  84.0 62.4 %collective-permute-start.8 = (bf16[256,2048]{1,0:T(8,128)(2,1)S(1)}, bf16[256,2048]{1,0:T(8,128)(2,1)S(1)}, u32[]{:S(2)}, u32[]{:S(2)}) collective-permute-start(bf16[256,2048]{1,0:T(8,128)(2,1)S(1)} %get-tuple-element.78.refs_2_), channel_id=1, source_target_pairs={{1,2},{2,3},{5,6},{6,7},{9,10},{10,11},{13,14},{14,15},{17,18},{18... | collective-permute-start | bytes 3145736 | tf_op jit(solution)/shard_map/ppermute | solution.py:476
  84.7 61.7 %collective-permute-start.9 = (bf16[256,2048]{1,0:T(8,128)(2,1)}, bf16[256,2048]{1,0:T(8,128)(2,1)S(1)}, u32[]{:S(2)}, u32[]{:S(2)}) collective-permute-start(bf16[256,2048]{1,0:T(8,128)(2,1)} %get-tuple-element.79.refs_4_), channel_id=1, source_target_pairs={{1,0},{2,1},{5,4},{6,5},{9,8},{10,9},{13,12},{14,13},{17,16},{18,1... | collective-permute-start | bytes 3145736 | tf_op jit(solution)/shard_map/ppermute | solution.py:477
  105.9 44.3 %collective-permute-start.12 = (bf16[256,2048]{1,0:T(8,128)(2,1)}, bf16[256,2048]{1,0:T(8,128)(2,1)S(1)}, u32[]{:S(2)}, u32[]{:S(2)}) collective-permute-start(bf16[256,2048]{1,0:T(8,128)(2,1)} %get-tuple-element.86.refs_0_), channel_id=1, source_target_pairs={{2,3},{6,7},{10,11},{14,15},{18,19},{22,23},{26,27},{30,31}} | collective-permute-start | bytes 3145736 | tf_op jit(solution)/shard_map/ppermute | solution.py:476
  106.7 43.6 %collective-permute-start.13 = (bf16[256,2048]{1,0:T(8,128)(2,1)}, bf16[256,2048]{1,0:T(8,128)(2,1)S(1)}, u32[]{:S(2)}, u32[]{:S(2)}) collective-permute-start(bf16[256,2048]{1,0:T(8,128)(2,1)} %get-tuple-element.87.refs_1_), channel_id=1, source_target_pairs={{1,0},{5,4},{9,8},{13,12},{17,16},{21,20},{25,24},{29,28}} | collective-permute-start | bytes 3145736 | tf_op jit(solution)/shard_map/ppermute | solution.py:477
  146.4 29.9 %collective-permute-start.10 = (bf16[256,2048]{1,0:T(8,128)(2,1)S(1)}, bf16[256,2048]{1,0:T(8,128)(2,1)}, u32[]{:S(2)}, u32[]{:S(2)}) collective-permute-start(bf16[256,2048]{1,0:T(8,128)(2,1)S(1)} %get-tuple-element.82), channel_id=1, source_target_pairs={{1,2},{2,3},{5,6},{6,7},{9,10},{10,11},{13,14},{14,15},{17,18},{18... | collective-permute-start | bytes 3145736 | tf_op jit(solution)/shard_map/ppermute | solution.py:476
  148.7 44.2 %collective-permute-start.11 = (bf16[256,2048]{1,0:T(8,128)(2,1)}, bf16[256,2048]{1,0:T(8,128)(2,1)}, u32[]{:S(2)}, u32[]{:S(2)}) collective-permute-start(bf16[256,2048]{1,0:T(8,128)(2,1)} %get-tuple-element.83), channel_id=1, source_target_pairs={{1,0},{2,1},{5,4},{6,5},{9,8},{10,9},{13,12},{14,13},{17,16},{18,1... | collective-permute-start | bytes 3145736 | tf_op jit(solution)/shard_map/ppermute | solution.py:477
  174.2 48.2 %collective-permute-start.16 = (bf16[256,2048]{1,0:T(8,128)(2,1)S(1)}, bf16[256,2048]{1,0:T(8,128)(2,1)S(1)}, u32[]{:S(2)}, u32[]{:S(2)}) collective-permute-start(bf16[256,2048]{1,0:T(8,128)(2,1)S(1)} %get-tuple-element.91.refs_0_), channel_id=1, source_target_pairs={{2,3},{6,7},{10,11},{14,15},{18,19},{22,23},{26,27},{30,31}} | collective-permute-start | bytes 3145736 | tf_op jit(solution)/shard_map/ppermute | solution.py:476
  174.9 47.4 %collective-permute-start.17 = (bf16[256,2048]{1,0:T(8,128)(2,1)S(1)}, bf16[256,2048]{1,0:T(8,128)(2,1)S(1)}, u32[]{:S(2)}, u32[]{:S(2)}) collective-permute-start(bf16[256,2048]{1,0:T(8,128)(2,1)S(1)} %get-tuple-element.92.refs_2_), channel_id=1, source_target_pairs={{1,0},{5,4},{9,8},{13,12},{17,16},{21,20},{25,24},{29,28}} | collective-permute-start | bytes 3145736 | tf_op jit(solution)/shard_map/ppermute | solution.py:477
  176.2 42.2 %collective-permute-start.18 = (bf16[256,1024]{1,0:T(8,128)(2,1)S(1)}, bf16[256,1024]{1,0:T(8,128)(2,1)S(1)}, u32[]{:S(2)}, u32[]{:S(2)}) collective-permute-start(bf16[256,1024]{1,0:T(8,128)(2,1)S(1)} %get-tuple-element.100), channel_id=1, source_target_pairs={{0,4},{4,0},{8,12},{12,8},{1,5},{5,1},{9,13},{13,9},{2,6},{6,2},{1... | collective-permute-start | bytes 1572872 | tf_op jit(solution)/shard_map/ppermute | solution.py:473
  176.3 43.6 %collective-permute-start.19 = (bf16[256,1024]{1,0:T(8,128)(2,1)S(1)}, bf16[256,1024]{1,0:T(8,128)(2,1)S(1)}, u32[]{:S(2)}, u32[]{:S(2)}) collective-permute-start(bf16[256,1024]{1,0:T(8,128)(2,1)S(1)} %get-tuple-element.101), channel_id=1, source_target_pairs={{0,4},{4,0},{8,12},{12,8},{1,5},{5,1},{9,13},{13,9},{2,6},{6,2},{1... | collective-permute-start | bytes 1572872 | tf_op jit(solution)/shard_map/ppermute | solution.py:473
  216.6 33.3 %collective-permute-start.14 = (bf16[256,2048]{1,0:T(8,128)(2,1)}, bf16[256,2048]{1,0:T(8,128)(2,1)}, u32[]{:S(2)}, u32[]{:S(2)}) collective-permute-start(bf16[256,2048]{1,0:T(8,128)(2,1)} %get-tuple-element.96), channel_id=1, source_target_pairs={{2,3},{6,7},{10,11},{14,15},{18,19},{22,23},{26,27},{30,31}} | collective-permute-start | bytes 3145736 | tf_op jit(solution)/shard_map/ppermute | solution.py:476
  218.4 31.5 %collective-permute-start.15 = (bf16[256,2048]{1,0:T(8,128)(2,1)}, bf16[256,2048]{1,0:T(8,128)(2,1)}, u32[]{:S(2)}, u32[]{:S(2)}) collective-permute-start(bf16[256,2048]{1,0:T(8,128)(2,1)} %get-tuple-element.97), channel_id=1, source_target_pairs={{1,0},{5,4},{9,8},{13,12},{17,16},{21,20},{25,24},{29,28}} | collective-permute-start | bytes 3145736 | tf_op jit(solution)/shard_map/ppermute | solution.py:477
  220.8 20.1 %collective-permute-start.22 = (bf16[256,1024]{1,0:T(8,128)(2,1)}, bf16[256,1024]{1,0:T(8,128)(2,1)}, u32[]{:S(2)}, u32[]{:S(2)}) collective-permute-start(bf16[256,1024]{1,0:T(8,128)(2,1)} %get-tuple-element.106), channel_id=1, source_target_pairs={{0,8},{4,12},{8,0},{12,4},{1,9},{5,13},{9,1},{13,5},{2,10},{6,14},... | collective-permute-start | bytes 1572872 | tf_op jit(solution)/shard_map/ppermute | solution.py:473
  236.8 9.8 %collective-permute-start.20 = (bf16[256,1024]{1,0:T(8,128)(2,1)}, bf16[256,1024]{1,0:T(8,128)(2,1)}, u32[]{:S(2)}, u32[]{:S(2)}) collective-permute-start(bf16[256,1024]{1,0:T(8,128)(2,1)} %get-tuple-element.104), channel_id=1, source_target_pairs={{0,4},{4,0},{8,12},{12,8},{1,5},{5,1},{9,13},{13,9},{2,6},{6,2},{1... | collective-permute-start | bytes 1572872 | tf_op jit(solution)/shard_map/ppermute | solution.py:473
  236.8 9.8 %collective-permute-start.21 = (bf16[256,1024]{1,0:T(8,128)(2,1)}, bf16[256,1024]{1,0:T(8,128)(2,1)}, u32[]{:S(2)}, u32[]{:S(2)}) collective-permute-start(bf16[256,1024]{1,0:T(8,128)(2,1)} %get-tuple-element.105), channel_id=1, source_target_pairs={{0,4},{4,0},{8,12},{12,8},{1,5},{5,1},{9,13},{13,9},{2,6},{6,2},{1... | collective-permute-start | bytes 1572872 | tf_op jit(solution)/shard_map/ppermute | solution.py:473
  247.8 16.2 %collective-permute-start.25 = (bf16[256,1024]{1,0:T(8,128)(2,1)S(1)}, bf16[256,1024]{1,0:T(8,128)(2,1)S(1)}, u32[]{:S(2)}, u32[]{:S(2)}) collective-permute-start(bf16[256,1024]{1,0:T(8,128)(2,1)S(1)} %get-tuple-element.113), channel_id=1, source_target_pairs={{0,8},{4,12},{8,0},{12,4},{1,9},{5,13},{9,1},{13,5},{2,10},{6,14},... | collective-permute-start | bytes 1572872 | tf_op jit(solution)/shard_map/ppermute | solution.py:473
  248.4 32.6 %collective-permute-start.35 = (bf16[256,1024]{1,0:T(8,128)(2,1)S(1)}, bf16[256,1024]{1,0:T(8,128)(2,1)S(1)}, u32[]{:S(2)}, u32[]{:S(2)}) collective-permute-start(bf16[256,1024]{1,0:T(8,128)(2,1)S(1)} %get-tuple-element.120.refs_0_), channel_id=1, source_target_pairs={{0,8},{4,12},{8,0},{12,4},{1,9},{5,13},{9,1},{13,5},{2,10},{6,14},... | collective-permute-start | bytes 1572872 | tf_op jit(solution)/shard_map/ppermute | solution.py:473
  263.4 19.2 %collective-permute-start.23 = (bf16[256,1024]{1,0:T(8,128)(2,1)S(1)}, bf16[256,1024]{1,0:T(8,128)(2,1)S(1)}, u32[]{:S(2)}, u32[]{:S(2)}) collective-permute-start(bf16[256,1024]{1,0:T(8,128)(2,1)S(1)} %get-tuple-element.111), channel_id=1, source_target_pairs={{0,4},{4,0},{8,12},{12,8},{1,5},{5,1},{9,13},{13,9},{2,6},{6,2},{1... | collective-permute-start | bytes 1572872 | tf_op jit(solution)/shard_map/ppermute | solution.py:473
  263.5 19.4 %collective-permute-start.24 = (bf16[256,1024]{1,0:T(8,128)(2,1)S(1)}, bf16[256,1024]{1,0:T(8,128)(2,1)S(1)}, u32[]{:S(2)}, u32[]{:S(2)}) collective-permute-start(bf16[256,1024]{1,0:T(8,128)(2,1)S(1)} %get-tuple-element.112), channel_id=1, source_target_pairs={{0,4},{4,0},{8,12},{12,8},{1,5},{5,1},{9,13},{13,9},{2,6},{6,2},{1... | collective-permute-start | bytes 1572872 | tf_op jit(solution)/shard_map/ppermute | solution.py:473
  266.6 17.7 %collective-permute-start.27 = (bf16[256,1024]{1,0:T(8,128)(2,1)S(1)}, bf16[256,1024]{1,0:T(8,128)(2,1)S(1)}, u32[]{:S(2)}, u32[]{:S(2)}) collective-permute-start(bf16[256,1024]{1,0:T(8,128)(2,1)S(1)} %get-tuple-element.119.refs_0_), channel_id=1, source_target_pairs={{0,8},{4,12},{8,0},{12,4},{1,9},{5,13},{9,1},{13,5},{2,10},{6,14},... | collective-permute-start | bytes 1572872 | tf_op jit(solution)/shard_map/ppermute | solution.py:473
  267.1 5.5 %collective-permute-start.30 = (f32[8,512]{1,0:T(8,128)S(1)}, f32[8,512]{1,0:T(8,128)S(1)}, u32[]{:S(2)}, u32[]{:S(2)}) collective-permute-start(f32[8,512]{1,0:T(8,128)S(1)} %constant_dynamic-update-slice_fusion), channel_id=1, source_target_pairs={{0,1},{1,2},{2,3},{3,0},{4,5},{5,6},{6,7},{7,4},{8,9},{9,10},{10,1... | collective-permute-start | bytes 49160 | tf_op jit(solution)/shard_map/ppermute | solution.py:517
  272.7 4.6 %collective-permute-start.31 = (f32[8,512]{1,0:T(8,128)S(1)}, f32[8,512]{1,0:T(8,128)S(1)}, u32[]{:S(2)}, u32[]{:S(2)}) collective-permute-start(f32[8,512]{1,0:T(8,128)S(1)} %constant_dynamic-update-slice_fusion), channel_id=1, source_target_pairs={{0,2},{1,3},{2,0},{3,1},{4,6},{5,7},{6,4},{7,5},{8,10},{9,11},{10,... | collective-permute-start | bytes 49160 | tf_op jit(solution)/shard_map/ppermute | solution.py:517
  277.3 3.7 %collective-permute-start.32 = (f32[8,512]{1,0:T(8,128)S(1)}, f32[8,512]{1,0:T(8,128)S(1)}, u32[]{:S(2)}, u32[]{:S(2)}) collective-permute-start(f32[8,512]{1,0:T(8,128)S(1)} %constant_dynamic-update-slice_fusion), channel_id=1, source_target_pairs={{0,3},{1,0},{2,1},{3,2},{4,7},{5,4},{6,5},{7,6},{8,11},{9,8},{10,9... | collective-permute-start | bytes 49160 | tf_op jit(solution)/shard_map/ppermute | solution.py:517
  281.0 5.3 %collective-permute-start.36 = (bf16[256,1024]{1,0:T(8,128)(2,1)S(1)}, bf16[256,1024]{1,0:T(8,128)(2,1)S(1)}, u32[]{:S(2)}, u32[]{:S(2)}) collective-permute-start(bf16[256,1024]{1,0:T(8,128)(2,1)S(1)} %get-tuple-element.120.refs_0_), channel_id=1, source_target_pairs={{0,4},{4,0},{8,12},{12,8},{1,5},{5,1},{9,13},{13,9},{2,6},{6,2},{1... | collective-permute-start | bytes 1572872 | tf_op jit(solution)/shard_map/ppermute | solution.py:473
  281.1 3.8 %collective-permute-start.33 = (f32[8,512]{1,0:T(8,128)S(1)}, f32[8,512]{1,0:T(8,128)S(1)}, u32[]{:S(2)}, u32[]{:S(2)}) collective-permute-start(f32[8,512]{1,0:T(8,128)S(1)} %add_add_fusion), channel_id=1, source_target_pairs={{0,8},{4,12},{8,0},{12,4},{1,9},{5,13},{9,1},{13,5},{2,10},{6,14},... | collective-permute-start | bytes 49160 | tf_op jit(solution)/shard_map/ppermute | solution.py:473
  282.6 3.8 %collective-permute-start.37 = (bf16[256,1024]{1,0:T(8,128)(2,1)S(1)}, bf16[256,1024]{1,0:T(8,128)(2,1)S(1)}, u32[]{:S(2)}, u32[]{:S(2)}) collective-permute-start(bf16[256,1024]{1,0:T(8,128)(2,1)S(1)} %collective-permute-done.35.refs_1_), channel_id=1, source_target_pairs={{0,4},{4,0},{8,12},{12,8},{1,5},{5,1},{9,13},{13,9},{2,6},{6,2},{1... | collective-permute-start | bytes 1572872 | tf_op jit(solution)/shard_map/ppermute | solution.py:473
  282.9 6.9 %collective-permute-start.28 = (bf16[256,1024]{1,0:T(8,128)(2,1)S(1)}, bf16[256,1024]{1,0:T(8,128)(2,1)S(1)}, u32[]{:S(2)}, u32[]{:S(2)}) collective-permute-start(bf16[256,1024]{1,0:T(8,128)(2,1)S(1)} %get-tuple-element.119.refs_0_), channel_id=1, source_target_pairs={{0,4},{4,0},{8,12},{12,8},{1,5},{5,1},{9,13},{13,9},{2,6},{6,2},{1... | collective-permute-start | bytes 1572872 | tf_op jit(solution)/shard_map/ppermute | solution.py:473
  284.2 5.5 %collective-permute-start.29 = (bf16[256,1024]{1,0:T(8,128)(2,1)S(1)}, bf16[256,1024]{1,0:T(8,128)(2,1)S(1)}, u32[]{:S(2)}, u32[]{:S(2)}) collective-permute-start(bf16[256,1024]{1,0:T(8,128)(2,1)S(1)} %collective-permute-done.27.refs_1_), channel_id=1, source_target_pairs={{0,4},{4,0},{8,12},{12,8},{1,5},{5,1},{9,13},{13,9},{2,6},{6,2},{1... | collective-permute-start | bytes 1572872 | tf_op jit(solution)/shard_map/ppermute | solution.py:473
  284.9 13.9 %collective-permute-start.26 = (bf16[256,1024]{1,0:T(8,128)(2,1)S(1)}, bf16[256,1024]{1,0:T(8,128)(2,1)S(1)}, u32[]{:S(2)}, u32[]{:S(2)}) collective-permute-start(bf16[256,1024]{1,0:T(8,128)(2,1)S(1)} %get-tuple-element.117), channel_id=1, source_target_pairs={{0,8},{4,12},{8,0},{12,4},{1,9},{5,13},{9,1},{13,5},{2,10},{6,14},... | collective-permute-start | bytes 1572872 | tf_op jit(solution)/shard_map/ppermute | solution.py:473
  286.4 1.2 collective-permute-start.34
  300.2 13.1 %collective-permute-start.38 = (bf16[256,1024]{1,0:T(8,128)(2,1)S(1)}, bf16[256,1024]{1,0:T(8,128)(2,1)S(1)}, u32[]{:S(2)}, u32[]{:S(2)}) collective-permute-start(bf16[256,1024]{1,0:T(8,128)(2,1)S(1)} %get-tuple-element.126.refs_0_), channel_id=1, source_target_pairs={{0,8},{4,12},{8,0},{12,4},{1,9},{5,13},{9,1},{13,5},{2,10},{6,14},... | collective-permute-start | bytes 1572872 | tf_op jit(solution)/shard_map/ppermute | solution.py:473
  301.1 23.1 %collective-permute-start.39 = (bf16[256,1024]{1,0:T(8,128)(2,1)S(1)}, bf16[256,1024]{1,0:T(8,128)(2,1)S(1)}, u32[]{:S(2)}, u32[]{:S(2)}) collective-permute-start(bf16[256,1024]{1,0:T(8,128)(2,1)S(1)} %get-tuple-element.126.refs_0_), channel_id=1, source_target_pairs={{0,4},{4,0},{8,12},{12,8},{1,5},{5,1},{9,13},{13,9},{2,6},{6,2},{1... | collective-permute-start | bytes 1572872 | tf_op jit(solution)/shard_map/ppermute | solution.py:473
  313.3 10.9 %collective-permute-start.40 = (bf16[256,1024]{1,0:T(8,128)(2,1)S(1)}, bf16[256,1024]{1,0:T(8,128)(2,1)S(1)}, u32[]{:S(2)}, u32[]{:S(2)}) collective-permute-start(bf16[256,1024]{1,0:T(8,128)(2,1)S(1)} %collective-permute-done.38.refs_1_), channel_id=1, source_target_pairs={{0,4},{4,0},{8,12},{12,8},{1,5},{5,1},{9,13},{13,9},{2,6},{6,2},{1... | collective-permute-start | bytes 1572872 | tf_op jit(solution)/shard_map/ppermute | solution.py:473
  313.3 5.4 %collective-permute-start.41 = (f32[8,256]{1,0:T(8,128)S(1)}, f32[8,256]{1,0:T(8,128)S(1)}, u32[]{:S(2)}, u32[]{:S(2)}) collective-permute-start(f32[8,256]{1,0:T(8,128)S(1)} %get-tuple-element.127), channel_id=1, source_target_pairs={{0,1},{1,2},{2,3},{3,0},{4,5},{5,6},{6,7},{7,4},{8,9},{9,10},{10,1... | collective-permute-start | bytes 24584 | tf_op jit(solution)/shard_map/ppermute | solution.py:517
  313.3 5.4 %collective-permute-start.42 = (f32[8,256]{1,0:T(8,128)S(1)}, f32[8,256]{1,0:T(8,128)S(1)}, u32[]{:S(2)}, u32[]{:S(2)}) collective-permute-start(f32[8,256]{1,0:T(8,128)S(1)} %get-tuple-element.127), channel_id=1, source_target_pairs={{0,2},{1,3},{2,0},{3,1},{4,6},{5,7},{6,4},{7,5},{8,10},{9,11},{10,... | collective-permute-start | bytes 24584 | tf_op jit(solution)/shard_map/ppermute | solution.py:517
  314.2 5.1 %collective-permute-start.43 = (f32[8,256]{1,0:T(8,128)S(1)}, f32[8,256]{1,0:T(8,128)S(1)}, u32[]{:S(2)}, u32[]{:S(2)}) collective-permute-start(f32[8,256]{1,0:T(8,128)S(1)} %get-tuple-element.127), channel_id=1, source_target_pairs={{0,3},{1,0},{2,1},{3,2},{4,7},{5,4},{6,5},{7,6},{8,11},{9,8},{10,9... | collective-permute-start | bytes 24584 | tf_op jit(solution)/shard_map/ppermute | solution.py:517
  319.3 3.7 %collective-permute-start.44 = (f32[8,256]{1,0:T(8,128)S(1)}, f32[8,256]{1,0:T(8,128)S(1)}, u32[]{:S(2)}, u32[]{:S(2)}) collective-permute-start(f32[8,256]{1,0:T(8,128)S(1)} %add_add_fusion.1), channel_id=1, source_target_pairs={{0,8},{4,12},{8,0},{12,4},{1,9},{5,13},{9,1},{13,5},{2,10},{6,14},... | collective-permute-start | bytes 24584 | tf_op jit(solution)/shard_map/ppermute | solution.py:473
  323.0 1.2 collective-permute-start.45
  (13 other events, 89.4 us)
where the time goes:
time: 327 us; the launch traced here: 326 us
  Pallas kernels  160 us (49%)
  waiting for transfers between devices  104 us (32%)
  starting transfers between devices  46.7 us (14%)
  local copies, waits for them, and re-layouts  14.5 us (4%)
    pallas_call x6, Pallas kernels, matmul_stage(): pl.pallas_call(functools.partial(matmul_kernel, plan), grid_spec=pltpu.Pr...  135 us
    ppermute x9, waiting for transfers between devices, onward(): lax.ppermute(pair[1], 'sub', [(i, i - 1) for i in range(1, sub - d + 1)])  40 us
    ppermute x22, waiting for transfers between devices, swap(): return lax.ppermute(value, 'tp', [(i, i ^ d) for i in range(tp)])  26.5 us
    ppermute x9, waiting for transfers between devices, onward(): lax.ppermute(pair[0], 'sub', [(i, i + 1) for i in range(d - 1, sub - 1)])  21 us
    ppermute x9, starting transfers between devices, onward(): lax.ppermute(pair[0], 'sub', [(i, i + 1) for i in range(d - 1, sub - 1)])  20.3 us
    ppermute x6, waiting for transfers between devices, exchange(): lax.ppermute(local, 'sub', [(i, (i + d) % sub) for i in range(sub)])  16.1 us
    ppermute x9, starting transfers between devices, onward(): lax.ppermute(pair[1], 'sub', [(i, i - 1) for i in range(1, sub - d + 1)])  12 us
    ppermute x22, starting transfers between devices, swap(): return lax.ppermute(value, 'tp', [(i, i ^ d) for i in range(tp)])  10.6 us
  transfers between devices with their start and end apart: 46, of which 17 were waited for; matrix products, arithmetic and copies ran while one was open for 2% of the time, Pallas kernels for 47%

commit v1 on v0

--- a/solution.py
+++ b/solution.py
@@ -23,13 +23,6 @@
 
 def row_units(rows):
     return [rows // 3, rows // 3, rows // 3]
-
-
-def block_of(width, most):
-    size = min(width, most)
-    while width % size:
-        size //= 2
-    return size
 
 
 def lanes(rows):
@@ -103,135 +96,115 @@
 
 
 def matmul_kernel(plan, info, *refs):
-    most, per, block, tp, spans, sources, gathered, prior_at, final, skip = plan
+    most, tp, spans, sources, prior_at, final, skip = plan
     parts = len(spans)
-    count = 1 if gathered else sources * parts
+    count = sources * parts
     inputs = [refs[s * parts : (s + 1) * parts] for s in range(sources)]
-    if gathered:
-        size = spans[0][1]
-        inputs = [[refs[0].at[s * size : (s + 1) * size]] for s in range(sources)]
-    weights = refs[count : count + tp]
-    at = count + tp
+    weight = refs[count]
+    at = count + 1
     prior = refs[at] if prior_at is not None else None
     at += (prior_at is not None) + skip
     number = 1 + tp // 2 if final else 1
     outs = refs[at : at + number]
     token = refs[at + number]
-    scratch = refs[at + number + 1 :]
-    held, total, sems = scratch[:3]
+    held, total, sems, early_sems, late_sems = refs[at + number + 1 :]
+    rows = total.shape[1]
     step = pl.program_id(0)
+    p = step // tp
+    t = step % tp
     me = info[0]
     pieces = info[1]
-    active = step < pieces * per
+
+    def load_prior(t):
+        return pltpu.make_async_copy(
+            prior.at[t, prior_at : prior_at + rows], total.at[t], early_sems.at[t]
+        )
+
+    def store(t):
+        return pltpu.make_async_copy(total.at[t], outs[0].at[t], late_sems.at[t])
 
     @pl.when(step == 0)
     def _():
-        for p in range(most):
+        for q in range(most):
             for s in range(sources):
 
-                @pl.when((p < pieces) & (info[2 + p] == s))
+                @pl.when((q < pieces) & (info[2 + q] == s))
                 def _():
                     for n, (first, size) in enumerate(spans):
-                        for q in range(per):
-                            pltpu.make_async_copy(
-                                inputs[s][n].at[:, q * block : (q + 1) * block],
-                                held.at[p * per + q, first : first + size],
-                                sems.at[p * per + q, n],
-                            ).start()
+                        pltpu.make_async_copy(
+                            inputs[s][n], held.at[q, first : first + size], sems.at[q, n]
+                        ).start()
 
         if prior is not None:
-            pltpu.make_async_copy(
-                prior.at[:, prior_at : prior_at + total.shape[1]], scratch[3], scratch[4].at[0]
-            ).start()
-
-        @pl.when(pieces == 0)
+            for k in range(tp):
+                load_prior(k).start()
+
+    if prior is not None:
+
+        @pl.when(p == 0)
         def _():
-            total[...] = jnp.zeros_like(total)
-
-    @pl.when(active)
+            load_prior(t).wait()
+
+    @pl.when(p < pieces)
     def _():
-        for n, (first, size) in enumerate(spans):
-            pltpu.make_async_copy(
-                inputs[0][n].at[:, 0:block], held.at[step, first : first + size], sems.at[step, n]
-            ).wait()
-        value = held[step]
-        for t in range(tp):
-            product = jnp.dot(value, weights[t][...], preferred_element_type=jnp.float32)
-
-            @pl.when(step == 0)
+        @pl.when(t == 0)
+        def _():
+            for n, (first, size) in enumerate(spans):
+                pltpu.make_async_copy(
+                    inputs[0][n], held.at[p, first : first + size], sems.at[p, n]
+                ).wait()
+
+        product = jnp.dot(held[p], weight[...], preferred_element_type=jnp.float32)
+        if prior is not None:
+            total[t] += product
+        else:
+
+            @pl.when(p == 0)
             def _():
                 total[t] = product
 
-            @pl.when(step != 0)
+            @pl.when(p != 0)
             def _():
                 total[t] += product
 
-    @pl.when(step == most * per - 1)
+        if not final:
+
+            @pl.when(p == pieces - 1)
+            def _():
+                store(t).start()
+
+    @pl.when(step == most * tp - 1)
     def _():
-        if prior is not None:
-            pltpu.make_async_copy(
-                prior.at[:, prior_at : prior_at + total.shape[1]], scratch[3], scratch[4].at[0]
-            ).wait()
-
-        def result(t):
-            value = total[t]
-            return value if prior is None else value + scratch[3][t]
-
         if final:
             for k in range(tp // 2):
-                outs[0][k] = result(me ^ (2 * k))
-                outs[1 + k][...] = result(me ^ (2 * k + 1)).astype(jnp.bfloat16)
+                outs[0][k] = total[me ^ (2 * k)]
+                outs[1 + k][...] = total[me ^ (2 * k + 1)].astype(jnp.bfloat16)
         else:
-            if prior is not None:
-                total[...] += scratch[3][...]
-            copy = pltpu.make_async_copy(total, outs[0], scratch[-1].at[0])
-            copy.start()
-            copy.wait()
+            for k in range(tp):
+                store(k).wait()
         token[...] = jnp.zeros(TOKEN, jnp.float32)
 
 
 def matmul_stage(place, me, stages, sub, tp, inputs, weight, prior, prior_at, final, after):
-    gathered = not isinstance(inputs, list)
-    if gathered:
-        flat = [inputs]
-        sizes = [inputs.shape[0] // sub]
-    else:
-        flat = [part for source in inputs for part in source]
-        sizes = [part.shape[0] for part in inputs[0]]
+    flat = [part for source in inputs for part in source]
+    sizes = [part.shape[0] for part in inputs[0]]
     rows = sum(sizes)
     spans = [(sum(sizes[:n]), size) for n, size in enumerate(sizes)]
     depth = flat[0].shape[1]
-    block = block_of(depth, 512)
-    per = depth // block
     columns = weight.shape[1]
     width = columns // tp
-    if gathered:
-        most = sub
-        info = jnp.concatenate([me[None], jnp.asarray([sub, *range(sub), *range(sub)], jnp.int32)])
-    else:
-        table, most = stage_table(sub, stages)
-        info = jnp.concatenate([me[None], jnp.asarray(table)[place]])
-
-    def row_block(j, s):
-        last = jnp.maximum(s[1] * per - 1, 0)
-        j = jnp.minimum(j, last)
-        return s[2 + most + j // per] * per + j % per
-
-    operands = [*flat] + [weight] * tp
-    specs = [anywhere()] * len(flat) + [
-        pl.BlockSpec((block, width), lambda j, s, t=t: (row_block(j, s), t)) for t in range(tp)
-    ]
-    scratch = [
-        pltpu.VMEM((most * per, rows, block), jnp.bfloat16),
-        pltpu.VMEM((tp, rows, width), jnp.float32),
-        pltpu.SemaphoreType.DMA((most * per, len(sizes))),
-    ]
+    table, most = stage_table(sub, stages)
+    info = jnp.concatenate([me[None], jnp.asarray(table)[place]])
+
+    def weight_block(j, s):
+        j = jnp.minimum(j, jnp.maximum(s[1] * tp - 1, 0))
+        return s[2 + most + j // tp], j % tp
+
+    operands = [*flat, weight]
+    specs = [anywhere()] * len(flat) + [pl.BlockSpec((depth, width), weight_block)]
     if prior is not None:
         operands.append(prior)
         specs.append(anywhere())
-        scratch += [pltpu.VMEM((tp, rows, width), jnp.float32), pltpu.SemaphoreType.DMA((1,))]
-    if not final:
-        scratch.append(pltpu.SemaphoreType.DMA((1,)))
     operands += after
     specs += [token_spec()] * len(after)
     if final:
@@ -242,16 +215,11 @@
     else:
         out_specs = [anywhere()]
         out_shape = [jax.ShapeDtypeStruct((tp, rows, width), jnp.float32)]
-    out_specs.append(token_spec())
-    out_shape.append(TOKEN_SHAPE)
     plan = (
         most,
-        per,
-        block,
         tp,
         spans,
-        sub if gathered else len(inputs),
-        gathered,
+        len(inputs),
         None if prior is None else prior_at,
         final,
         len(after),
@@ -260,12 +228,18 @@
         functools.partial(matmul_kernel, plan),
         grid_spec=pltpu.PrefetchScalarGridSpec(
             num_scalar_prefetch=1,
-            grid=(most * per,),
+            grid=(most * tp,),
             in_specs=specs,
-            out_specs=out_specs,
-            scratch_shapes=scratch,
+            out_specs=out_specs + [token_spec()],
+            scratch_shapes=[
+                pltpu.VMEM((most, rows, depth), jnp.bfloat16),
+                pltpu.VMEM((tp, rows, width), jnp.float32),
+                pltpu.SemaphoreType.DMA((most, len(sizes))),
+                pltpu.SemaphoreType.DMA((tp,)),
+                pltpu.SemaphoreType.DMA((tp,)),
+            ],
         ),
-        out_shape=out_shape,
+        out_shape=out_shape + [TOKEN_SHAPE],
         compiler_params=params(),
         cost_estimate=pl.CostEstimate(flops=1, bytes_accessed=1, transcendentals=0),
         name="matmul_stage",
@@ -280,8 +254,9 @@
     count = len(values)
     outs = pl.pallas_call(
         functools.partial(gate_kernel, count),
-        in_specs=[anywhere()] * count + [pl.BlockSpec(TOKEN, lambda: (0, 0))] * len(after),
-        out_specs=[anywhere()] * count + [pl.BlockSpec(TOKEN, lambda: (0, 0))],
+        grid=(1,),
+        in_specs=[anywhere()] * count + [token_spec()] * len(after),
+        out_specs=[anywhere()] * count + [token_spec()],
         out_shape=[jax.ShapeDtypeStruct(v.shape, v.dtype) for v in values] + [TOKEN_SHAPE],
         input_output_aliases={n: n for n in range(count)},
         compiler_params=params(),
@@ -360,8 +335,7 @@
     )
 
 
-def stream_rows(terms, signs, matrix, residual, so_far, start, after):
-    keep, first, last = terms
+def stream_rows(keep, first, last, signs, matrix, residual, so_far, start, after):
     _, rows, width = keep.shape
     cut = len(last)
     place = start // rows
@@ -501,23 +475,32 @@
                 keep, got = kept, arrived
         return after
 
-    def finish(u, after):
+    def finish(u, after, pause=False):
         streams[0], chunk, squares[u] = stream_rows(
-            terms[u], signs_own, matrix, mine, streams[0], starts[u], after
+            *terms[u], signs_own, matrix, mine, streams[0], starts[u], after
         )
         found = [(0, chunk)]
         for bit in reversed(bits):
+            if pause and bit == bits[0]:
+                along.append(sum_along(jnp.concatenate([squares[b] for b in range(u + 1)], axis=1)))
+                values, _ = gate([value for _, value in found[1:]], along)
+                found[1:] = [(e, value) for (e, _), value in zip(found[1:], values)]
             found += [(e | bit, swap(value, bit)) for e, value in found]
         pieces[u] = found
         return [squares[u]]
 
-    def exchange(local):
-        along = local
+    along = []
+
+    def sum_along(local):
+        total = local
         for d in range(1, sub):
-            along = along + lax.ppermute(local, "sub", [(i, (i + d) % sub) for i in range(sub)])
+            total = total + lax.ppermute(local, "sub", [(i, (i + d) % sub) for i in range(sub)])
+        return total
+
+    def sum_across(total):
         for bit in reversed(bits[1:]):
-            along = along + swap(along, bit)
-        return [along, swap(along, bits[0])]
+            total = total + swap(total, bit)
+        return [total, swap(total, bits[0])]
 
     normed = [None]
 
@@ -597,10 +580,8 @@
     begin_sums(2, *sums)
     token = finish(1, [token])
     token = halve_sums(2, token)
-    totals = exchange(jnp.concatenate([squares[0], squares[1]], axis=1))
-    token = normalise([0, 1], totals, token)
-    finish(2, token)
-    normalise([2], exchange(squares[2]), [])
+    token = finish(2, token, True)
+    normalise([0, 1, 2], sum_across(along[0]), token)
     return (streams[0], normed[0])
 
 

time: 327 us -> 296 us (0.905)
  Pallas kernels: 160 us -> 132 us
  starting transfers between devices: 46.7 us -> 42.7 us
    pallas_call x6, Pallas kernels: 135 us -> 106 us  [matmul_stage(): pl.pallas_call(functools.partial(matmul_kernel, plan), grid_spec=pltpu.Pr...]
    ppermute x6 -> x3, waiting for transfers between devices: 16.1 us -> 4.33 us  [sum_along(): lax.ppermute(local, 'sub', [(i, (i + d) % sub) for i in range(sub)])]
    ppermute x22 -> x20, waiting for transfers between devices: 26.5 us -> 38.1 us  [swap(): return lax.ppermute(value, 'tp', [(i, i ^ d) for i in range(tp)])]
    ppermute x6 -> x3, starting transfers between devices: 3.84 us -> 0.4 us  [sum_along(): lax.ppermute(local, 'sub', [(i, (i + d) % sub) for i in range(sub)])]
    ppermute x22 -> x20, starting transfers between devices: 10.6 us -> 10.2 us  [swap(): return lax.ppermute(value, 'tp', [(i, i ^ d) for i in range(tp)])]
    unnamed x31 -> x32, local copies, waits for them, and re-layouts: 8.29 us -> 8.27 us
  transfers between devices with their start and end apart: 46 -> 41, of which waited for: 17 -> 13; matrix products, arithmetic and copies ran while one was open for 2% -> 2% of each run, Pallas kernels for 47% -> 43%
where the time goes in v1:
time: 296 us; the launch traced here: 295 us
  Pallas kernels  132 us (45%)
  waiting for transfers between devices  105 us (35%)
  starting transfers between devices  42.7 us (14%)
  local copies, waits for them, and re-layouts  14.5 us (5%)
    pallas_call x6, Pallas kernels, matmul_stage(): pl.pallas_call(functools.partial(matmul_kernel, plan), grid_spec=pltpu.Pr...  106 us
    ppermute x9, waiting for transfers between devices, onward(): lax.ppermute(pair[1], 'sub', [(i, i - 1) for i in range(1, sub - d + 1)])  41.3 us
    ppermute x20, waiting for transfers between devices, swap(): return lax.ppermute(value, 'tp', [(i, i ^ d) for i in range(tp)])  38.1 us
    ppermute x9, waiting for transfers between devices, onward(): lax.ppermute(pair[0], 'sub', [(i, i + 1) for i in range(d - 1, sub - 1)])  21 us
    ppermute x9, starting transfers between devices, onward(): lax.ppermute(pair[0], 'sub', [(i, i + 1) for i in range(d - 1, sub - 1)])  20.3 us
    ppermute x9, starting transfers between devices, onward(): lax.ppermute(pair[1], 'sub', [(i, i - 1) for i in range(1, sub - d + 1)])  11.8 us
    ppermute x20, starting transfers between devices, swap(): return lax.ppermute(value, 'tp', [(i, i ^ d) for i in range(tp)])  10.2 us
    unnamed x32, local copies, waits for them, and re-layouts  8.27 us
  transfers between devices with their start and end apart: 41, of which 13 were waited for; matrix products, arithmetic and copies ran while one was open for 2% of the time, Pallas kernels for 43%

profile of v1, /device:TPU:0, one launch (start us, length us, event | category | flops | bytes accessed | tf_op | source)
XLA Modules:
  0.0 295.0 jit_solution(8918839139715025924)
XLA Ops:
  0.7 2.0 copy-done.1
  2.7 1.9 hidden_rows.3
  4.5 5.9 %collective-permute-start = (bf16[256,2048]{1,0:T(8,128)(2,1)S(1)}, bf16[256,2048]{1,0:T(8,128)(2,1)}, u32[]{:S(2)}, u32[]{:S(2)}) collective-permute-start(bf16[256,2048]{1,0:T(8,128)(2,1)S(1)} %get-tuple-element.67.refs_0_), channel_id=1, source_target_pairs={{0,1},{1,2},{2,3},{4,5},{5,6},{6,7},{8,9},{9,10},{10,11},{12,13},{... | collective-permute-start | bytes 3145736 | tf_op jit(solution)/shard_map/ppermute | solution.py:450
  10.5 1.3 collective-permute-start.1
  11.8 3.0 %hidden_rows.4 = (bf16[256,2048]{1,0:T(8,128)(2,1)}, f32[8,128]{1,0:T(8,128)S(1)}) custom-call(bf16[768,2048]{1,0:T(8,128)(2,1)S(1)} %copy-done.1, bf16[768,2048]{1,0:T(8,128)(2,1)} %up.5, f32[8,128]{1,0:T(8,128)S(1)} %get-tuple-element.68.refs_0_), custom_call_target="tpu_custom_call" | custom-call | flops 1 | bytes 1 | tf_op jit(solution)/shard_map/hidden_rows/pallas_call | solution.py:59
  14.8 4.6 %collective-permute-start.6 = (bf16[256,2048]{1,0:T(8,128)(2,1)}, bf16[256,2048]{1,0:T(8,128)(2,1)S(1)}, u32[]{:S(2)}, u32[]{:S(2)}) collective-permute-start(bf16[256,2048]{1,0:T(8,128)(2,1)} %get-tuple-element.78.refs_0_), channel_id=1, source_target_pairs={{0,1},{1,2},{2,3},{4,5},{5,6},{6,7},{8,9},{9,10},{10,11},{12,13},{... | collective-permute-start | bytes 3145736 | tf_op jit(solution)/shard_map/ppermute | solution.py:450
  19.4 1.3 collective-permute-start.7
  20.7 12.3 %collective-permute-done.refs_0_ = bf16[256,2048]{1,0:T(8,128)(2,1)} collective-permute-done((bf16[256,2048]{1,0:T(8,128)(2,1)S(1)}, bf16[256,2048]{1,0:T(8,128)(2,1)}, u32[]{:S(2)}, u32[]{:S(2)}) %collective-permute-start) | collective-permute-done | bytes 1048608 | tf_op jit(solution)/shard_map/ppermute | solution.py:450
  33.0 5.5 %collective-permute-done.1.refs_1_ = bf16[256,2048]{1,0:T(8,128)(2,1)} collective-permute-done((bf16[256,2048]{1,0:T(8,128)(2,1)S(1)}, bf16[256,2048]{1,0:T(8,128)(2,1)}, u32[]{:S(2)}, u32[]{:S(2)}) %collective-permute-start.1) | collective-permute-done | bytes 1048608 | tf_op jit(solution)/shard_map/ppermute | solution.py:451
  38.6 2.9 hidden_rows.5
  41.4 2.6 collective-permute-start.4
  44.0 1.3 collective-permute-start.5
  45.3 1.6 collective-permute-start.2
  46.9 8.7 %collective-permute-done.6.refs_0_ = bf16[256,2048]{1,0:T(8,128)(2,1)S(1)} collective-permute-done((bf16[256,2048]{1,0:T(8,128)(2,1)}, bf16[256,2048]{1,0:T(8,128)(2,1)S(1)}, u32[]{:S(2)}, u32[]{:S(2)}) %collective-permute-start.6) | collective-permute-done | bytes 1048608 | tf_op jit(solution)/shard_map/ppermute | solution.py:450
  56.7 1.3 collective-permute-start.3
  60.0 18.2 %matmul_stage.6 = (f32[4,256,1024]{2,1,0:T(8,128)}, f32[8,128]{1,0:T(8,128)S(1)}) custom-call(s32[8]{0:T(128)S(1)} %pad_add_fusion.1.info, bf16[256,2048]{1,0:T(8,128)(2,1)S(1)} %copy-done.12, bf16[256,2048]{1,0:T(8,128)(2,1)} %get-tuple-element.70.refs_1_, bf16[256,2048]{1,0:T(8,128)(2,1)} %get-tuple-element.71.refs_2_, bf16[8192,4096]{1,0:T(8,128)(2,1)} %refs_2_.3, ...), custom_call_target="tpu_custom_call" | custom-call | flops 1 | bytes 1 | tf_op jit(solution)/shard_map/matmul_stage/pallas_call | solution.py:227
  79.5 1.3 collective-permute-start.9
  80.8 2.7 collective-permute-done.5.refs_3_
  83.5 22.5 %collective-permute-done.3.refs_1_ = bf16[256,2048]{1,0:T(8,128)(2,1)} collective-permute-done((bf16[256,2048]{1,0:T(8,128)(2,1)}, bf16[256,2048]{1,0:T(8,128)(2,1)}, u32[]{:S(2)}, u32[]{:S(2)}) %collective-permute-start.3) | collective-permute-done | bytes 1048608 | tf_op jit(solution)/shard_map/ppermute | solution.py:451
  106.7 1.3 collective-permute-start.13
  108.0 27.0 %matmul_stage.7 = (f32[4,512,1024]{2,1,0:T(8,128)}, f32[8,128]{1,0:T(8,128)S(1)}) custom-call(s32[8]{0:T(128)S(1)} %pad_add_fusion.1.info, bf16[256,2048]{1,0:T(8,128)(2,1)} %get-tuple-element.78.refs_0_, bf16[256,2048]{1,0:T(8,128)(2,1)} %get-tuple-element.73.refs_1_, bf16[256,2048]{1,0:T(8,128)(2,1)S(1)} %get-tuple-element.79.refs_2_, ...), custom_call_target="tpu_custom_call" | custom-call | flops 1 | bytes 1 | tf_op jit(solution)/shard_map/matmul_stage/pallas_call | solution.py:227
  135.0 1.7 collective-permute-start.10
  136.7 1.3 collective-permute-start.11
  138.7 10.6 %collective-permute-done.13.refs_3_ = bf16[256,2048]{1,0:T(8,128)(2,1)S(1)} collective-permute-done((bf16[256,2048]{1,0:T(8,128)(2,1)}, bf16[256,2048]{1,0:T(8,128)(2,1)S(1)}, u32[]{:S(2)}, u32[]{:S(2)}) %collective-permute-start.13) | collective-permute-done | bytes 1048608 | tf_op jit(solution)/shard_map/ppermute | solution.py:451
  149.3 20.0 %matmul_stage.8 = (f32[2,256,1024]{2,1,0:T(8,128)}, bf16[256,1024]{1,0:T(8,128)(2,1)S(1)}, bf16[256,1024]{1,0:T(8,128)(2,1)S(1)}, f32[8,128]{1,0:T(8,128)S(1)}) custom-call(s32[6]{0:T(128)S(1)} %pad_add_fusion.3.info, bf16[256,2048]{1,0:T(8,128)(2,1)} %get-tuple-element.87.refs_0_, bf16[256,2048]{1,0:T(8,128)(2,1)} %get-tuple-element.88.refs_1_, ...), custom_call_target="tpu_custom_call" | custom-call | flops 1 | bytes 1 | tf_op jit(solution)/shard_map/matmul_stage/pallas_call | solution.py:227
  170.1 1.3 collective-permute-start.17
  172.8 16.8 %matmul_stage.9 = (f32[4,512,1024]{2,1,0:T(8,128)}, f32[8,128]{1,0:T(8,128)S(1)}) custom-call(s32[4]{0:T(128)S(1)} %pad_add_fusion.2.info, bf16[256,2048]{1,0:T(8,128)(2,1)S(1)} %get-tuple-element.92.refs_0_, bf16[256,2048]{1,0:T(8,128)(2,1)} %collective-permute-done.10.refs_1_.refs_0_, bf16[256,2048]{1,0:T(8,128)(2,1)S(1)} %get-tuple-element.93.refs_2_, ...), custom_call_target="tpu_custom_call" | custom-call | flops 1 | bytes 1 | tf_op jit(solution)/shard_map/matmul_stage/pallas_call | solution.py:227
  190.2 1.8 collective-permute-start.14
  192.0 1.5 collective-permute-start.15
  195.1 1.5 collective-permute-start.22
  196.6 12.1 %matmul_stage.10 = (f32[2,256,1024]{2,1,0:T(8,128)S(1)}, bf16[256,1024]{1,0:T(8,128)(2,1)}, bf16[256,1024]{1,0:T(8,128)(2,1)}, f32[8,128]{1,0:T(8,128)S(1)}) custom-call(s32[4]{0:T(128)S(1)} %pad_add_fusion.info, bf16[256,2048]{1,0:T(8,128)(2,1)S(1)} %collective-permute-done.16.refs_0_, bf16[256,2048]{1,0:T(8,128)(2,1)S(1)} %collective-permute-done.17.refs_1_, ...), custom_call_target="tpu_custom_call" | custom-call | flops 1 | bytes 1 | tf_op jit(solution)/shard_map/matmul_stage/pallas_call | solution.py:227
  208.8 1.3 copy-done.5
  211.3 2.8 gather_fusion
  214.2 1.6 copy-done.4
  216.9 3.0 %stream_rows.3 = (bf16[768,1024]{1,0:T(8,128)(2,1)}, bf16[256,1024]{1,0:T(8,128)(2,1)S(1)}, f32[8,256]{1,0:T(8,128)S(1)}) custom-call(f32[2,256,1024]{2,1,0:T(8,128)S(1)} %copy-done.4, bf16[256,1024]{1,0:T(8,128)(2,1)S(1)} %copy-done.10, bf16[256,1024]{1,0:T(8,128)(2,1)} %collective-permute-done.22.refs_2_, s32[1,1024]{1,0:T(1,128)S(1)} %bitcast.14, ...), custom_call_target="tpu_custom_call" | custom-call | flops 1 | bytes 1 | tf_op jit(solution)/shard_map/stream_rows/pallas_call | solution.py:359
  219.8 1.3 halve.4
  221.8 12.3 %matmul_stage.11 = (f32[2,256,1024]{2,1,0:T(8,128)S(1)}, bf16[256,1024]{1,0:T(8,128)(2,1)S(1)}, bf16[256,1024]{1,0:T(8,128)(2,1)S(1)}, f32[8,128]{1,0:T(8,128)S(1)}) custom-call(s32[4]{0:T(128)S(1)} %pad_add_fusion.info, bf16[256,2048]{1,0:T(8,128)(2,1)} %collective-permute-done.14.refs_0_, bf16[256,2048]{1,0:T(8,128)(2,1)} %collective-permute-done.15.refs_1_, ...), custom_call_target="tpu_custom_call" | custom-call | flops 1 | bytes 1 | tf_op jit(solution)/shard_map/matmul_stage/pallas_call | solution.py:227
  235.0 2.6 stream_rows.4
  240.9 11.7 %collective-permute-done.26.refs_2_ = bf16[256,1024]{1,0:T(8,128)(2,1)S(1)} collective-permute-done((bf16[256,1024]{1,0:T(8,128)(2,1)S(1)}, bf16[256,1024]{1,0:T(8,128)(2,1)S(1)}, u32[]{:S(2)}, u32[]{:S(2)}) %collective-permute-start.26) | collective-permute-done | bytes 524320 | tf_op jit(solution)/shard_map/ppermute | solution.py:447
  252.7 1.5 stream_rows.5
  255.2 8.7 %collective-permute-done.38.refs_1_ = bf16[256,1024]{1,0:T(8,128)(2,1)S(1)} collective-permute-done((bf16[256,1024]{1,0:T(8,128)(2,1)S(1)}, bf16[256,1024]{1,0:T(8,128)(2,1)S(1)}, u32[]{:S(2)}, u32[]{:S(2)}) %collective-permute-start.38) | collective-permute-done | bytes 524320 | tf_op jit(solution)/shard_map/ppermute | solution.py:447
  264.3 4.3 %collective-permute-done.29 = f32[8,768]{1,0:T(8,128)S(1)} collective-permute-done((f32[8,768]{1,0:T(8,128)S(1)}, f32[8,768]{1,0:T(8,128)S(1)}, u32[]{:S(2)}, u32[]{:S(2)}) %collective-permute-start.29) | collective-permute-done | bytes 24608 | tf_op jit(solution)/shard_map/ppermute | solution.py:497
  269.7 5.4 %collective-permute-done.35.refs_1_ = bf16[256,1024]{1,0:T(8,128)(2,1)S(1)} collective-permute-done((bf16[256,1024]{1,0:T(8,128)(2,1)S(1)}, bf16[256,1024]{1,0:T(8,128)(2,1)S(1)}, u32[]{:S(2)}, u32[]{:S(2)}) %collective-permute-start.35) | collective-permute-done | bytes 524320 | tf_op jit(solution)/shard_map/ppermute | solution.py:447
  275.1 10.2 %collective-permute-done.27.refs_0_ = bf16[256,1024]{1,0:T(8,128)(2,1)S(1)} collective-permute-done((bf16[256,1024]{1,0:T(8,128)(2,1)S(1)}, bf16[256,1024]{1,0:T(8,128)(2,1)S(1)}, u32[]{:S(2)}, u32[]{:S(2)}) %collective-permute-start.27) | collective-permute-done | bytes 524320 | tf_op jit(solution)/shard_map/ppermute | solution.py:447
  287.0 1.7 collective-permute-done.34.refs_5_
  288.8 2.1 norm_rows.3
  290.8 2.1 norm_rows.4
  292.9 2.1 norm_rows.5
  (106 shorter events, 21.8 us)
Async XLA Ops:
  0.6 210.7 %copy-start = (bf16[768,1024]{1,0:T(8,128)(2,1)S(1)}, bf16[768,1024]{1,0:T(8,128)(2,1)}, u32[]{:S(2)}) copy-start(bf16[768,1024]{1,0:T(8,128)(2,1)} %param.16) | copy-start | bytes 4718596
  4.5 10.3 %copy-start.11 = (bf16[256,2048]{1,0:T(8,128)(2,1)}, bf16[256,2048]{1,0:T(8,128)(2,1)S(1)}, u32[]{:S(2)}) copy-start(bf16[256,2048]{1,0:T(8,128)(2,1)S(1)} %get-tuple-element.67.refs_0_) | copy-start | bytes 3145732
  4.5 28.5 %collective-permute-start = (bf16[256,2048]{1,0:T(8,128)(2,1)S(1)}, bf16[256,2048]{1,0:T(8,128)(2,1)}, u32[]{:S(2)}, u32[]{:S(2)}) collective-permute-start(bf16[256,2048]{1,0:T(8,128)(2,1)S(1)} %get-tuple-element.67.refs_0_), channel_id=1, source_target_pairs={{0,1},{1,2},{2,3},{4,5},{5,6},{6,7},{8,9},{9,10},{10,11},{12,13},{... | collective-permute-start | bytes 3145736 | tf_op jit(solution)/shard_map/ppermute | solution.py:450
  10.5 28.1 %collective-permute-start.1 = (bf16[256,2048]{1,0:T(8,128)(2,1)S(1)}, bf16[256,2048]{1,0:T(8,128)(2,1)}, u32[]{:S(2)}, u32[]{:S(2)}) collective-permute-start(bf16[256,2048]{1,0:T(8,128)(2,1)S(1)} %get-tuple-element.67.refs_0_), channel_id=1, source_target_pairs={{1,0},{2,1},{3,2},{5,4},{6,5},{7,6},{9,8},{10,9},{11,10},{13,12},{... | collective-permute-start | bytes 3145736 | tf_op jit(solution)/shard_map/ppermute | solution.py:451
  11.8 26.8 %copy-start.2 = (bf16[768,2048]{1,0:T(8,128)(2,1)S(1)}, bf16[768,2048]{1,0:T(8,128)(2,1)}, u32[]{:S(2)}) copy-start(bf16[768,2048]{1,0:T(8,128)(2,1)} %gate.13) | copy-start | bytes 9437188
  14.8 40.8 %collective-permute-start.6 = (bf16[256,2048]{1,0:T(8,128)(2,1)}, bf16[256,2048]{1,0:T(8,128)(2,1)S(1)}, u32[]{:S(2)}, u32[]{:S(2)}) collective-permute-start(bf16[256,2048]{1,0:T(8,128)(2,1)} %get-tuple-element.78.refs_0_), channel_id=1, source_target_pairs={{0,1},{1,2},{2,3},{4,5},{5,6},{6,7},{8,9},{9,10},{10,11},{12,13},{... | collective-permute-start | bytes 3145736 | tf_op jit(solution)/shard_map/ppermute | solution.py:450
  19.4 58.8 %collective-permute-start.7 = (bf16[256,2048]{1,0:T(8,128)(2,1)}, bf16[256,2048]{1,0:T(8,128)(2,1)}, u32[]{:S(2)}, u32[]{:S(2)}) collective-permute-start(bf16[256,2048]{1,0:T(8,128)(2,1)} %get-tuple-element.78.refs_0_), channel_id=1, source_target_pairs={{1,0},{2,1},{3,2},{5,4},{6,5},{7,6},{9,8},{10,9},{11,10},{13,12},{... | collective-permute-start | bytes 3145736 | tf_op jit(solution)/shard_map/ppermute | solution.py:451
  41.4 38.1 %collective-permute-start.4 = (bf16[256,2048]{1,0:T(8,128)(2,1)}, bf16[256,2048]{1,0:T(8,128)(2,1)S(1)}, u32[]{:S(2)}, u32[]{:S(2)}) collective-permute-start(bf16[256,2048]{1,0:T(8,128)(2,1)} %get-tuple-element.73.refs_1_), channel_id=1, source_target_pairs={{0,1},{1,2},{2,3},{4,5},{5,6},{6,7},{8,9},{9,10},{10,11},{12,13},{... | collective-permute-start | bytes 3145736 | tf_op jit(solution)/shard_map/ppermute | solution.py:450
  44.0 39.5 %collective-permute-start.5 = (bf16[256,2048]{1,0:T(8,128)(2,1)}, bf16[256,2048]{1,0:T(8,128)(2,1)}, u32[]{:S(2)}, u32[]{:S(2)}) collective-permute-start(bf16[256,2048]{1,0:T(8,128)(2,1)} %get-tuple-element.73.refs_1_), channel_id=1, source_target_pairs={{1,0},{2,1},{3,2},{5,4},{6,5},{7,6},{9,8},{10,9},{11,10},{13,12},{... | collective-permute-start | bytes 3145736 | tf_op jit(solution)/shard_map/ppermute | solution.py:451
  45.3 38.2 %collective-permute-start.2 = (bf16[256,2048]{1,0:T(8,128)(2,1)}, bf16[256,2048]{1,0:T(8,128)(2,1)}, u32[]{:S(2)}, u32[]{:S(2)}) collective-permute-start(bf16[256,2048]{1,0:T(8,128)(2,1)} %get-tuple-element.70.refs_1_), channel_id=1, source_target_pairs={{1,2},{2,3},{5,6},{6,7},{9,10},{10,11},{13,14},{14,15},{17,18},{18... | collective-permute-start | bytes 3145736 | tf_op jit(solution)/shard_map/ppermute | solution.py:450
  56.7 49.3 %collective-permute-start.3 = (bf16[256,2048]{1,0:T(8,128)(2,1)}, bf16[256,2048]{1,0:T(8,128)(2,1)}, u32[]{:S(2)}, u32[]{:S(2)}) collective-permute-start(bf16[256,2048]{1,0:T(8,128)(2,1)} %get-tuple-element.71.refs_2_), channel_id=1, source_target_pairs={{1,0},{2,1},{5,4},{6,5},{9,8},{10,9},{13,12},{14,13},{17,16},{18,1... | collective-permute-start | bytes 3145736 | tf_op jit(solution)/shard_map/ppermute | solution.py:451
  60.0 18.2 %copy-start.8 = (bf16[256,2048]{1,0:T(8,128)(2,1)S(1)}, bf16[256,2048]{1,0:T(8,128)(2,1)}, u32[]{:S(2)}) copy-start(bf16[256,2048]{1,0:T(8,128)(2,1)} %copy-done.7) | copy-start | bytes 3145732
  78.8 56.2 %collective-permute-start.8 = (bf16[256,2048]{1,0:T(8,128)(2,1)S(1)}, bf16[256,2048]{1,0:T(8,128)(2,1)S(1)}, u32[]{:S(2)}, u32[]{:S(2)}) collective-permute-start(bf16[256,2048]{1,0:T(8,128)(2,1)S(1)} %get-tuple-element.79.refs_2_), channel_id=1, source_target_pairs={{1,2},{2,3},{5,6},{6,7},{9,10},{10,11},{13,14},{14,15},{17,18},{18... | collective-permute-start | bytes 3145736 | tf_op jit(solution)/shard_map/ppermute | solution.py:450
  79.5 55.5 %collective-permute-start.9 = (bf16[256,2048]{1,0:T(8,128)(2,1)}, bf16[256,2048]{1,0:T(8,128)(2,1)S(1)}, u32[]{:S(2)}, u32[]{:S(2)}) collective-permute-start(bf16[256,2048]{1,0:T(8,128)(2,1)} %get-tuple-element.80.refs_4_), channel_id=1, source_target_pairs={{1,0},{2,1},{5,4},{6,5},{9,8},{10,9},{13,12},{14,13},{17,16},{18,1... | collective-permute-start | bytes 3145736 | tf_op jit(solution)/shard_map/ppermute | solution.py:451
  106.0 32.8 %collective-permute-start.12 = (bf16[256,2048]{1,0:T(8,128)(2,1)}, bf16[256,2048]{1,0:T(8,128)(2,1)S(1)}, u32[]{:S(2)}, u32[]{:S(2)}) collective-permute-start(bf16[256,2048]{1,0:T(8,128)(2,1)} %get-tuple-element.87.refs_0_), channel_id=1, source_target_pairs={{2,3},{6,7},{10,11},{14,15},{18,19},{22,23},{26,27},{30,31}} | collective-permute-start | bytes 3145736 | tf_op jit(solution)/shard_map/ppermute | solution.py:450
  106.7 42.6 %collective-permute-start.13 = (bf16[256,2048]{1,0:T(8,128)(2,1)}, bf16[256,2048]{1,0:T(8,128)(2,1)S(1)}, u32[]{:S(2)}, u32[]{:S(2)}) collective-permute-start(bf16[256,2048]{1,0:T(8,128)(2,1)} %get-tuple-element.88.refs_1_), channel_id=1, source_target_pairs={{1,0},{5,4},{9,8},{13,12},{17,16},{21,20},{25,24},{29,28}} | collective-permute-start | bytes 3145736 | tf_op jit(solution)/shard_map/ppermute | solution.py:451
  135.0 37.2 %collective-permute-start.10 = (bf16[256,2048]{1,0:T(8,128)(2,1)S(1)}, bf16[256,2048]{1,0:T(8,128)(2,1)}, u32[]{:S(2)}, u32[]{:S(2)}) collective-permute-start(bf16[256,2048]{1,0:T(8,128)(2,1)S(1)} %get-tuple-element.83), channel_id=1, source_target_pairs={{1,2},{2,3},{5,6},{6,7},{9,10},{10,11},{13,14},{14,15},{17,18},{18... | collective-permute-start | bytes 3145736 | tf_op jit(solution)/shard_map/ppermute | solution.py:450
  136.7 36.1 %collective-permute-start.11 = (bf16[256,2048]{1,0:T(8,128)(2,1)}, bf16[256,2048]{1,0:T(8,128)(2,1)}, u32[]{:S(2)}, u32[]{:S(2)}) collective-permute-start(bf16[256,2048]{1,0:T(8,128)(2,1)} %get-tuple-element.84), channel_id=1, source_target_pairs={{1,0},{2,1},{5,4},{6,5},{9,8},{10,9},{13,12},{14,13},{17,16},{18,1... | collective-permute-start | bytes 3145736 | tf_op jit(solution)/shard_map/ppermute | solution.py:451
  169.3 27.3 %collective-permute-start.16 = (bf16[256,2048]{1,0:T(8,128)(2,1)S(1)}, bf16[256,2048]{1,0:T(8,128)(2,1)S(1)}, u32[]{:S(2)}, u32[]{:S(2)}) collective-permute-start(bf16[256,2048]{1,0:T(8,128)(2,1)S(1)} %get-tuple-element.92.refs_0_), channel_id=1, source_target_pairs={{2,3},{6,7},{10,11},{14,15},{18,19},{22,23},{26,27},{30,31}} | collective-permute-start | bytes 3145736 | tf_op jit(solution)/shard_map/ppermute | solution.py:450
  170.1 26.5 %collective-permute-start.17 = (bf16[256,2048]{1,0:T(8,128)(2,1)S(1)}, bf16[256,2048]{1,0:T(8,128)(2,1)S(1)}, u32[]{:S(2)}, u32[]{:S(2)}) collective-permute-start(bf16[256,2048]{1,0:T(8,128)(2,1)S(1)} %get-tuple-element.93.refs_2_), channel_id=1, source_target_pairs={{1,0},{5,4},{9,8},{13,12},{17,16},{21,20},{25,24},{29,28}} | collective-permute-start | bytes 3145736 | tf_op jit(solution)/shard_map/ppermute | solution.py:451
  171.4 20.6 %collective-permute-start.18 = (bf16[256,1024]{1,0:T(8,128)(2,1)S(1)}, bf16[256,1024]{1,0:T(8,128)(2,1)S(1)}, u32[]{:S(2)}, u32[]{:S(2)}) collective-permute-start(bf16[256,1024]{1,0:T(8,128)(2,1)S(1)} %get-tuple-element.101), channel_id=1, source_target_pairs={{0,4},{4,0},{8,12},{12,8},{1,5},{5,1},{9,13},{13,9},{2,6},{6,2},{1... | collective-permute-start | bytes 1572872 | tf_op jit(solution)/shard_map/ppermute | solution.py:447
  172.2 22.1 %collective-permute-start.19 = (bf16[256,1024]{1,0:T(8,128)(2,1)S(1)}, bf16[256,1024]{1,0:T(8,128)(2,1)S(1)}, u32[]{:S(2)}, u32[]{:S(2)}) collective-permute-start(bf16[256,1024]{1,0:T(8,128)(2,1)S(1)} %get-tuple-element.102), channel_id=1, source_target_pairs={{0,4},{4,0},{8,12},{12,8},{1,5},{5,1},{9,13},{13,9},{2,6},{6,2},{1... | collective-permute-start | bytes 1572872 | tf_op jit(solution)/shard_map/ppermute | solution.py:447
  190.2 31.5 %collective-permute-start.14 = (bf16[256,2048]{1,0:T(8,128)(2,1)}, bf16[256,2048]{1,0:T(8,128)(2,1)}, u32[]{:S(2)}, u32[]{:S(2)}) collective-permute-start(bf16[256,2048]{1,0:T(8,128)(2,1)} %get-tuple-element.97), channel_id=1, source_target_pairs={{2,3},{6,7},{10,11},{14,15},{18,19},{22,23},{26,27},{30,31}} | collective-permute-start | bytes 3145736 | tf_op jit(solution)/shard_map/ppermute | solution.py:450
  192.0 4.6 %copy-start.9 = (bf16[256,1024]{1,0:T(8,128)(2,1)}, bf16[256,1024]{1,0:T(8,128)(2,1)S(1)}, u32[]{:S(2)}) copy-start(bf16[256,1024]{1,0:T(8,128)(2,1)S(1)} %collective-permute-done.18.refs_0_.refs_1_) | copy-start | bytes 1572868
  192.0 29.8 %collective-permute-start.15 = (bf16[256,2048]{1,0:T(8,128)(2,1)}, bf16[256,2048]{1,0:T(8,128)(2,1)}, u32[]{:S(2)}, u32[]{:S(2)}) collective-permute-start(bf16[256,2048]{1,0:T(8,128)(2,1)} %get-tuple-element.98), channel_id=1, source_target_pairs={{1,0},{5,4},{9,8},{13,12},{17,16},{21,20},{25,24},{29,28}} | collective-permute-start | bytes 3145736 | tf_op jit(solution)/shard_map/ppermute | solution.py:451
  195.1 19.1 %collective-permute-start.22 = (bf16[256,1024]{1,0:T(8,128)(2,1)}, bf16[256,1024]{1,0:T(8,128)(2,1)}, u32[]{:S(2)}, u32[]{:S(2)}) collective-permute-start(bf16[256,1024]{1,0:T(8,128)(2,1)} %get-tuple-element.107), channel_id=1, source_target_pairs={{0,8},{4,12},{8,0},{12,4},{1,9},{5,13},{9,1},{13,5},{2,10},{6,14},... | collective-permute-start | bytes 1572872 | tf_op jit(solution)/shard_map/ppermute | solution.py:447
  196.6 14.7 %copy-start.14 = (s32[768]{0:T(1024)S(1)}, s32[768]{0:T(1024)}, u32[]{:S(2)}) copy-start(s32[768]{0:T(1024)} %param.18) | copy-start | bytes 9220
  210.1 9.8 %collective-permute-start.20 = (bf16[256,1024]{1,0:T(8,128)(2,1)}, bf16[256,1024]{1,0:T(8,128)(2,1)}, u32[]{:S(2)}, u32[]{:S(2)}) collective-permute-start(bf16[256,1024]{1,0:T(8,128)(2,1)} %get-tuple-element.105), channel_id=1, source_target_pairs={{0,4},{4,0},{8,12},{12,8},{1,5},{5,1},{9,13},{13,9},{2,6},{6,2},{1... | collective-permute-start | bytes 1572872 | tf_op jit(solution)/shard_map/ppermute | solution.py:447
  210.1 9.8 %collective-permute-start.21 = (bf16[256,1024]{1,0:T(8,128)(2,1)}, bf16[256,1024]{1,0:T(8,128)(2,1)}, u32[]{:S(2)}, u32[]{:S(2)}) collective-permute-start(bf16[256,1024]{1,0:T(8,128)(2,1)} %get-tuple-element.106), channel_id=1, source_target_pairs={{0,4},{4,0},{8,12},{12,8},{1,5},{5,1},{9,13},{13,9},{2,6},{6,2},{1... | collective-permute-start | bytes 1572872 | tf_op jit(solution)/shard_map/ppermute | solution.py:447
  221.1 13.9 %collective-permute-start.25 = (bf16[256,1024]{1,0:T(8,128)(2,1)S(1)}, bf16[256,1024]{1,0:T(8,128)(2,1)S(1)}, u32[]{:S(2)}, u32[]{:S(2)}) collective-permute-start(bf16[256,1024]{1,0:T(8,128)(2,1)S(1)} %get-tuple-element.114), channel_id=1, source_target_pairs={{0,8},{4,12},{8,0},{12,4},{1,9},{5,13},{9,1},{13,5},{2,10},{6,14},... | collective-permute-start | bytes 1572872 | tf_op jit(solution)/shard_map/ppermute | solution.py:447
  234.1 3.5 %collective-permute-start.23 = (bf16[256,1024]{1,0:T(8,128)(2,1)S(1)}, bf16[256,1024]{1,0:T(8,128)(2,1)S(1)}, u32[]{:S(2)}, u32[]{:S(2)}) collective-permute-start(bf16[256,1024]{1,0:T(8,128)(2,1)S(1)} %get-tuple-element.112), channel_id=1, source_target_pairs={{0,4},{4,0},{8,12},{12,8},{1,5},{5,1},{9,13},{13,9},{2,6},{6,2},{1... | collective-permute-start | bytes 1572872 | tf_op jit(solution)/shard_map/ppermute | solution.py:447
  234.1 3.5 %collective-permute-start.24 = (bf16[256,1024]{1,0:T(8,128)(2,1)S(1)}, bf16[256,1024]{1,0:T(8,128)(2,1)S(1)}, u32[]{:S(2)}, u32[]{:S(2)}) collective-permute-start(bf16[256,1024]{1,0:T(8,128)(2,1)S(1)} %get-tuple-element.113), channel_id=1, source_target_pairs={{0,4},{4,0},{8,12},{12,8},{1,5},{5,1},{9,13},{13,9},{2,6},{6,2},{1... | collective-permute-start | bytes 1572872 | tf_op jit(solution)/shard_map/ppermute | solution.py:447
  237.7 14.9 %collective-permute-start.26 = (bf16[256,1024]{1,0:T(8,128)(2,1)S(1)}, bf16[256,1024]{1,0:T(8,128)(2,1)S(1)}, u32[]{:S(2)}, u32[]{:S(2)}) collective-permute-start(bf16[256,1024]{1,0:T(8,128)(2,1)S(1)} %get-tuple-element.118), channel_id=1, source_target_pairs={{0,8},{4,12},{8,0},{12,4},{1,9},{5,13},{9,1},{13,5},{2,10},{6,14},... | collective-permute-start | bytes 1572872 | tf_op jit(solution)/shard_map/ppermute | solution.py:447
  238.9 25.0 %collective-permute-start.38 = (bf16[256,1024]{1,0:T(8,128)(2,1)S(1)}, bf16[256,1024]{1,0:T(8,128)(2,1)S(1)}, u32[]{:S(2)}, u32[]{:S(2)}) collective-permute-start(bf16[256,1024]{1,0:T(8,128)(2,1)S(1)} %get-tuple-element.126.refs_0_), channel_id=1, source_target_pairs={{0,8},{4,12},{8,0},{12,4},{1,9},{5,13},{9,1},{13,5},{2,10},{6,14},... | collective-permute-start | bytes 1572872 | tf_op jit(solution)/shard_map/ppermute | solution.py:447
  239.8 46.1 %collective-permute-start.39 = (bf16[256,1024]{1,0:T(8,128)(2,1)S(1)}, bf16[256,1024]{1,0:T(8,128)(2,1)S(1)}, u32[]{:S(2)}, u32[]{:S(2)}) collective-permute-start(bf16[256,1024]{1,0:T(8,128)(2,1)S(1)} %get-tuple-element.126.refs_0_), channel_id=1, source_target_pairs={{0,4},{4,0},{8,12},{12,8},{1,5},{5,1},{9,13},{13,9},{2,6},{6,2},{1... | collective-permute-start | bytes 1572872 | tf_op jit(solution)/shard_map/ppermute | solution.py:447
  239.8 35.3 %collective-permute-start.35 = (bf16[256,1024]{1,0:T(8,128)(2,1)S(1)}, bf16[256,1024]{1,0:T(8,128)(2,1)S(1)}, u32[]{:S(2)}, u32[]{:S(2)}) collective-permute-start(bf16[256,1024]{1,0:T(8,128)(2,1)S(1)} %get-tuple-element.125.refs_0_), channel_id=1, source_target_pairs={{0,8},{4,12},{8,0},{12,4},{1,9},{5,13},{9,1},{13,5},{2,10},{6,14},... | collective-permute-start | bytes 1572872 | tf_op jit(solution)/shard_map/ppermute | solution.py:447
  252.6 36.1 %copy-start.13 = (f32[4096]{0:T(1024)S(1)}, f32[4096]{0:T(1024)}, u32[]{:S(2)}) copy-start(f32[4096]{0:T(1024)} %param.19) | copy-start | bytes 49156
  254.2 31.1 %collective-permute-start.27 = (bf16[256,1024]{1,0:T(8,128)(2,1)S(1)}, bf16[256,1024]{1,0:T(8,128)(2,1)S(1)}, u32[]{:S(2)}, u32[]{:S(2)}) collective-permute-start(bf16[256,1024]{1,0:T(8,128)(2,1)S(1)} %get-tuple-element.122.refs_0_), channel_id=1, source_target_pairs={{0,8},{4,12},{8,0},{12,4},{1,9},{5,13},{9,1},{13,5},{2,10},{6,14},... | collective-permute-start | bytes 1572872 | tf_op jit(solution)/shard_map/ppermute | solution.py:447
  255.2 8.7 %collective-permute-start.28 = (f32[8,768]{1,0:T(8,128)S(1)}, f32[8,768]{1,0:T(8,128)S(1)}, u32[]{:S(2)}, u32[]{:S(2)}) collective-permute-start(f32[8,768]{1,0:T(8,128)S(1)} %constant_dynamic-update-slice_fusion), channel_id=1, source_target_pairs={{0,1},{1,2},{2,3},{3,0},{4,5},{5,6},{6,7},{7,4},{8,9},{9,10},{10,1... | collective-permute-start | bytes 73736 | tf_op jit(solution)/shard_map/ppermute | solution.py:497
  263.9 4.7 %collective-permute-start.29 = (f32[8,768]{1,0:T(8,128)S(1)}, f32[8,768]{1,0:T(8,128)S(1)}, u32[]{:S(2)}, u32[]{:S(2)}) collective-permute-start(f32[8,768]{1,0:T(8,128)S(1)} %constant_dynamic-update-slice_fusion), channel_id=1, source_target_pairs={{0,2},{1,3},{2,0},{3,1},{4,6},{5,7},{6,4},{7,5},{8,10},{9,11},{10,... | collective-permute-start | bytes 73736 | tf_op jit(solution)/shard_map/ppermute | solution.py:497
  263.9 4.7 %collective-permute-start.30 = (f32[8,768]{1,0:T(8,128)S(1)}, f32[8,768]{1,0:T(8,128)S(1)}, u32[]{:S(2)}, u32[]{:S(2)}) collective-permute-start(f32[8,768]{1,0:T(8,128)S(1)} %constant_dynamic-update-slice_fusion), channel_id=1, source_target_pairs={{0,3},{1,0},{2,1},{3,2},{4,7},{5,4},{6,5},{7,6},{8,11},{9,8},{10,9... | collective-permute-start | bytes 73736 | tf_op jit(solution)/shard_map/ppermute | solution.py:497
  268.6 17.9 %collective-permute-start.40 = (bf16[256,1024]{1,0:T(8,128)(2,1)S(1)}, bf16[256,1024]{1,0:T(8,128)(2,1)S(1)}, u32[]{:S(2)}, u32[]{:S(2)}) collective-permute-start(bf16[256,1024]{1,0:T(8,128)(2,1)S(1)} %collective-permute-done.38.refs_1_), channel_id=1, source_target_pairs={{0,4},{4,0},{8,12},{12,8},{1,5},{5,1},{9,13},{13,9},{2,6},{6,2},{1... | collective-permute-start | bytes 1572872 | tf_op jit(solution)/shard_map/ppermute | solution.py:447
  268.6 17.8 %collective-permute-start.33 = (f32[8,768]{1,0:T(8,128)S(1)}, f32[8,768]{1,0:T(8,128)S(1)}, u32[]{:S(2)}, u32[]{:S(2)}) collective-permute-start(f32[8,768]{1,0:T(8,128)S(1)} %add_add_fusion.refs_1_), channel_id=1, source_target_pairs={{0,8},{4,12},{8,0},{12,4},{1,9},{5,13},{9,1},{13,5},{2,10},{6,14},... | collective-permute-start | bytes 73736 | tf_op jit(solution)/shard_map/ppermute | solution.py:447
  275.1 15.7 %collective-permute-start.36 = (bf16[256,1024]{1,0:T(8,128)(2,1)S(1)}, bf16[256,1024]{1,0:T(8,128)(2,1)S(1)}, u32[]{:S(2)}, u32[]{:S(2)}) collective-permute-start(bf16[256,1024]{1,0:T(8,128)(2,1)S(1)} %get-tuple-element.125.refs_0_), channel_id=1, source_target_pairs={{0,4},{4,0},{8,12},{12,8},{1,5},{5,1},{9,13},{13,9},{2,6},{6,2},{1... | collective-permute-start | bytes 1572872 | tf_op jit(solution)/shard_map/ppermute | solution.py:447
  285.3 5.5 %collective-permute-start.37 = (bf16[256,1024]{1,0:T(8,128)(2,1)S(1)}, bf16[256,1024]{1,0:T(8,128)(2,1)S(1)}, u32[]{:S(2)}, u32[]{:S(2)}) collective-permute-start(bf16[256,1024]{1,0:T(8,128)(2,1)S(1)} %collective-permute-done.35.refs_1_), channel_id=1, source_target_pairs={{0,4},{4,0},{8,12},{12,8},{1,5},{5,1},{9,13},{13,9},{2,6},{6,2},{1... | collective-permute-start | bytes 1572872 | tf_op jit(solution)/shard_map/ppermute | solution.py:447
  285.9 7.0 %collective-permute-start.31 = (bf16[256,1024]{1,0:T(8,128)(2,1)S(1)}, bf16[256,1024]{1,0:T(8,128)(2,1)S(1)}, u32[]{:S(2)}, u32[]{:S(2)}) collective-permute-start(bf16[256,1024]{1,0:T(8,128)(2,1)S(1)} %get-tuple-element.122.refs_0_), channel_id=1, source_target_pairs={{0,4},{4,0},{8,12},{12,8},{1,5},{5,1},{9,13},{13,9},{2,6},{6,2},{1... | collective-permute-start | bytes 1572872 | tf_op jit(solution)/shard_map/ppermute | solution.py:447
  286.4 6.5 %collective-permute-start.32 = (bf16[256,1024]{1,0:T(8,128)(2,1)S(1)}, bf16[256,1024]{1,0:T(8,128)(2,1)S(1)}, u32[]{:S(2)}, u32[]{:S(2)}) collective-permute-start(bf16[256,1024]{1,0:T(8,128)(2,1)S(1)} %get-tuple-element.124.refs_1_), channel_id=1, source_target_pairs={{0,4},{4,0},{8,12},{12,8},{1,5},{5,1},{9,13},{13,9},{2,6},{6,2},{1... | collective-permute-start | bytes 1572872 | tf_op jit(solution)/shard_map/ppermute | solution.py:447
  286.5 2.3 collective-permute-start.34
  (8 other events, 15.9 us)

commit v2 on v1

--- a/solution.py
+++ b/solution.py
@@ -44,24 +44,36 @@
 TOKEN_SHAPE = jax.ShapeDtypeStruct(TOKEN, jnp.float32)
 
 
-def hidden_kernel(more, gate, up, *refs):
-    out, token = refs[more:]
-    value = gate[...].astype(jnp.float32)
-    value = value / (1.0 + jnp.exp(-value)) * up[...].astype(jnp.float32)
+def hidden_kernel(start, more, gate, up, *refs):
+    out, token, held, sems = refs[more:]
+    copies = [
+        pltpu.make_async_copy(
+            source.at[start : start + out.shape[0]], held.at[n], sems.at[n]
+        )
+        for n, source in enumerate((gate, up))
+    ]
+    for copy in copies:
+        copy.start()
+    for copy in copies:
+        copy.wait()
+    value = held[0].astype(jnp.float32)
+    value = value / (1.0 + jnp.exp(-value)) * held[1].astype(jnp.float32)
     out[...] = value.astype(jnp.bfloat16)
     token[...] = jnp.zeros(TOKEN, jnp.float32)
 
 
 def hidden_rows(gate, up, start, rows, after):
     columns = gate.shape[1]
-    place = start // rows
-    line = pl.BlockSpec((rows, columns), lambda i: (place, 0))
     return pl.pallas_call(
-        functools.partial(hidden_kernel, len(after)),
+        functools.partial(hidden_kernel, start, len(after)),
         grid=(1,),
-        in_specs=[line, line] + [token_spec()] * len(after),
+        in_specs=[pl.BlockSpec(memory_space=pltpu.HBM)] * 2 + [token_spec()] * len(after),
         out_specs=[pl.BlockSpec((rows, columns), lambda i: (0, 0)), token_spec()],
         out_shape=[jax.ShapeDtypeStruct((rows, columns), jnp.bfloat16), TOKEN_SHAPE],
+        scratch_shapes=[
+            pltpu.VMEM((2, rows, columns), jnp.bfloat16),
+            pltpu.SemaphoreType.DMA((2,)),
+        ],
         compiler_params=params(),
         cost_estimate=pl.CostEstimate(flops=1, bytes_accessed=1, transcendentals=0),
         name="hidden_rows",
@@ -475,21 +487,20 @@
                 keep, got = kept, arrived
         return after
 
-    def finish(u, after, pause=False):
+    def finish(u, after):
         streams[0], chunk, squares[u] = stream_rows(
             *terms[u], signs_own, matrix, mine, streams[0], starts[u], after
         )
-        found = [(0, chunk)]
-        for bit in reversed(bits):
-            if pause and bit == bits[0]:
-                along.append(sum_along(jnp.concatenate([squares[b] for b in range(u + 1)], axis=1)))
-                values, _ = gate([value for _, value in found[1:]], along)
-                found[1:] = [(e, value) for (e, _), value in zip(found[1:], values)]
-            found += [(e | bit, swap(value, bit)) for e, value in found]
-        pieces[u] = found
+        pieces[u] = [(0, chunk)]
+        for bit in reversed(bits[1:]):
+            pieces[u] += [(e | bit, swap(value, bit)) for e, value in pieces[u]]
         return [squares[u]]
 
-    along = []
+    def spread(u, after):
+        values, token = gate([value for _, value in pieces[u][1:]], after)
+        pieces[u][1:] = [(e, value) for (e, _), value in zip(pieces[u][1:], values)]
+        pieces[u] += [(e | bits[0], swap(value, bits[0])) for e, value in pieces[u]]
+        return token
 
     def sum_along(local):
         total = local
@@ -510,7 +521,7 @@
                 me,
                 pieces[u],
                 totals,
-                n,
+                sum(lanes(sizes[b]) for b in us[:n]) // lanes(sizes[u]),
                 gain,
                 normed[0],
                 starts[u],
@@ -551,9 +562,11 @@
         return token
 
     mid = middle[-1]
-    token = make(0, [])
-    token = make(1, token)
-    token = hold([(1, 0)], token)
+    first = gate_pre[: sizes[0]].astype(jnp.float32), up_pre[: sizes[0]].astype(jnp.float32)
+    own[0] = (jax.nn.silu(first[0]) * first[1]).astype(jnp.bfloat16)
+    came[1, 0] = onward([own[0], own[0]], 1)
+    token = make(1, [own[0]])
+    (*came[1, 0], mine), token = gate([*came[1, 0], mine], token)
     pass_on(0, 2, mid)
     token = make(2, token)
     part, *token = matmul([0], early, None, 0, False, token)
@@ -578,10 +591,14 @@
     token = halve_sums(1, token)
     *sums, token = matmul([2], late, parts, sizes[1], True, token)
     begin_sums(2, *sums)
-    token = finish(1, [token])
+    token = spread(0, [token])
+    token = finish(1, token)
     token = halve_sums(2, token)
-    token = finish(2, token, True)
-    normalise([0, 1, 2], sum_across(along[0]), token)
+    token = finish(2, token)
+    along = sum_along(jnp.concatenate([squares[u] for u in range(3)], axis=1))
+    spread(1, token)
+    spread(2, [along])
+    normalise([0, 1, 2], sum_across(along), token)
     return (streams[0], normed[0])
 
 

time: 296 us -> 290 us (0.980)
  waiting for transfers between devices: 105 us -> 97.5 us
  local copies, waits for them, and re-layouts: 14.5 us -> 11.1 us
  other arithmetic: 0.41 us -> 3.75 us
    ppermute x20, waiting for transfers between devices: 38.1 us -> 30.7 us  [swap(): return lax.ppermute(value, 'tp', [(i, i ^ d) for i in range(tp)])]
    ppermute x9, waiting for transfers between devices: 21 us -> 16.7 us  [onward(): lax.ppermute(pair[0], 'sub', [(i, i + 1) for i in range(d - 1, sub - 1)])]
    ppermute x3, waiting for transfers between devices: 4.33 us -> 8.03 us  [sum_along(): lax.ppermute(local, 'sub', [(i, (i + d) % sub) for i in range(sub)])]
    unnamed x32 -> x26, local copies, waits for them, and re-layouts: 8.27 us -> 4.78 us
    convert_element_type x0 -> x1, other arithmetic: none -> 3.34 us  [shards(): own[0] = (jax.nn.silu(first[0]) * first[1]).astype(jnp.bfloat16)]
    pallas_call x3 -> x2, Pallas kernels: 7.75 us -> 6.57 us  [hidden_rows(): pl.pallas_call(functools.partial(hidden_kernel, start, len(after)), grid=...]
  transfers between devices with their start and end apart: 41 -> 41, of which waited for: 13 -> 13; matrix products, arithmetic and copies ran while one was open for 2% -> 2% of each run, Pallas kernels for 43% -> 44%
where the time goes in v2:
time: 290 us; the launch traced here: 289 us
  Pallas kernels  130 us (45%)
  waiting for transfers between devices  97.5 us (34%)
  starting transfers between devices  45.1 us (16%)
  local copies, waits for them, and re-layouts  11.1 us (4%)
  other arithmetic  3.75 us (1%)
    pallas_call x6, Pallas kernels, matmul_stage(): pl.pallas_call(functools.partial(matmul_kernel, plan), grid_spec=pltpu.Pr...  108 us
    ppermute x9, waiting for transfers between devices, onward(): lax.ppermute(pair[1], 'sub', [(i, i - 1) for i in range(1, sub - d + 1)])  42.1 us
    ppermute x20, waiting for transfers between devices, swap(): return lax.ppermute(value, 'tp', [(i, i ^ d) for i in range(tp)])  30.7 us
    ppermute x9, starting transfers between devices, onward(): lax.ppermute(pair[0], 'sub', [(i, i + 1) for i in range(d - 1, sub - 1)])  21.4 us
    ppermute x9, waiting for transfers between devices, onward(): lax.ppermute(pair[0], 'sub', [(i, i + 1) for i in range(d - 1, sub - 1)])  16.7 us
    ppermute x9, starting transfers between devices, onward(): lax.ppermute(pair[1], 'sub', [(i, i - 1) for i in range(1, sub - d + 1)])  11.7 us
    ppermute x20, starting transfers between devices, swap(): return lax.ppermute(value, 'tp', [(i, i ^ d) for i in range(tp)])  10.5 us
    ppermute x3, waiting for transfers between devices, sum_along(): lax.ppermute(local, 'sub', [(i, (i + d) % sub) for i in range(sub)])  8.03 us
  transfers between devices with their start and end apart: 41, of which 13 were waited for; matrix products, arithmetic and copies ran while one was open for 2% of the time, Pallas kernels for 44%

profile of v2, /device:TPU:0, one launch (start us, length us, event | category | flops | bytes accessed | tf_op | source)
XLA Modules:
  0.0 288.6 jit_solution(4020704605398234958)
XLA Ops:
  0.7 3.3 %fusion.4.refs_0_ = bf16[256,2048]{1,0:T(8,128)(2,1)} fusion(bf16[768,2048]{1,0:T(8,128)(2,1)} %up.3, bf16[768,2048]{1,0:T(8,128)(2,1)} %gate.13), kind=kLoop, calls=%fused_computation.7 | loop fusion | flops 4194304 | bytes 3145728 | tf_op jit(solution)/shard_map/convert_element_type | solution.py:566
  4.0 6.1 %collective-permute-start = (bf16[256,2048]{1,0:T(8,128)(2,1)}, bf16[256,2048]{1,0:T(8,128)(2,1)}, u32[]{:S(2)}, u32[]{:S(2)}) collective-permute-start(bf16[256,2048]{1,0:T(8,128)(2,1)} %fusion.4.refs_0_), channel_id=1, source_target_pairs={{0,1},{1,2},{2,3},{4,5},{5,6},{6,7},{8,9},{9,10},{10,11},{12,13},{... | collective-permute-start | bytes 3145736 | tf_op jit(solution)/shard_map/ppermute | solution.py:462
  10.1 1.3 collective-permute-start.1
  11.4 3.6 %hidden_rows.2 = (bf16[256,2048]{1,0:T(8,128)(2,1)}, f32[8,128]{1,0:T(8,128)S(1)}) custom-call(bf16[768,2048]{1,0:T(8,128)(2,1)S(1)} %copy-done.2, bf16[768,2048]{1,0:T(8,128)(2,1)} %up.3, bf16[256,2048]{1,0:T(8,128)(2,1)} %fusion.4.refs_0_), custom_call_target="tpu_custom_call" | custom-call | flops 1 | bytes 1 | tf_op jit(solution)/shard_map/hidden_rows/pallas_call | solution.py:67
  15.1 5.6 %collective-permute-start.6 = (bf16[256,2048]{1,0:T(8,128)(2,1)}, bf16[256,2048]{1,0:T(8,128)(2,1)}, u32[]{:S(2)}, u32[]{:S(2)}) collective-permute-start(bf16[256,2048]{1,0:T(8,128)(2,1)} %get-tuple-element.78.refs_0_), channel_id=1, source_target_pairs={{0,1},{1,2},{2,3},{4,5},{5,6},{6,7},{8,9},{9,10},{10,11},{12,13},{... | collective-permute-start | bytes 3145736 | tf_op jit(solution)/shard_map/ppermute | solution.py:462
  20.7 1.3 collective-permute-start.7
  22.0 2.8 gather_fusion
  24.8 8.1 %collective-permute-done.refs_0_ = bf16[256,2048]{1,0:T(8,128)(2,1)} collective-permute-done((bf16[256,2048]{1,0:T(8,128)(2,1)}, bf16[256,2048]{1,0:T(8,128)(2,1)}, u32[]{:S(2)}, u32[]{:S(2)}) %collective-permute-start) | collective-permute-done | bytes 1048608 | tf_op jit(solution)/shard_map/ppermute | solution.py:462
  32.9 5.5 %collective-permute-done.1.refs_1_ = bf16[256,2048]{1,0:T(8,128)(2,1)} collective-permute-done((bf16[256,2048]{1,0:T(8,128)(2,1)}, bf16[256,2048]{1,0:T(8,128)(2,1)}, u32[]{:S(2)}, u32[]{:S(2)}) %collective-permute-start.1) | collective-permute-done | bytes 1048608 | tf_op jit(solution)/shard_map/ppermute | solution.py:463
  38.4 2.9 %hidden_rows.3 = (bf16[256,2048]{1,0:T(8,128)(2,1)}, f32[8,128]{1,0:T(8,128)S(1)}) custom-call(bf16[768,2048]{1,0:T(8,128)(2,1)S(1)} %copy-done.3, bf16[768,2048]{1,0:T(8,128)(2,1)} %up.3, f32[8,128]{1,0:T(8,128)S(1)} %get-tuple-element.72.refs_0_), custom_call_target="tpu_custom_call" | custom-call | flops 1 | bytes 1 | tf_op jit(solution)/shard_map/hidden_rows/pallas_call | solution.py:67
  41.3 2.5 collective-permute-start.4
  43.9 1.3 collective-permute-start.5
  45.2 1.7 collective-permute-start.2
  46.8 8.6 %collective-permute-done.6.refs_0_ = bf16[256,2048]{1,0:T(8,128)(2,1)} collective-permute-done((bf16[256,2048]{1,0:T(8,128)(2,1)}, bf16[256,2048]{1,0:T(8,128)(2,1)}, u32[]{:S(2)}, u32[]{:S(2)}) %collective-permute-start.6) | collective-permute-done | bytes 1048608 | tf_op jit(solution)/shard_map/ppermute | solution.py:462
  57.5 19.8 %matmul_stage.6 = (f32[4,256,1024]{2,1,0:T(8,128)}, f32[8,128]{1,0:T(8,128)S(1)}) custom-call(s32[8]{0:T(128)S(1)} %pad_add_fusion.1.info, bf16[256,2048]{1,0:T(8,128)(2,1)} %fusion.4.refs_0_, bf16[256,2048]{1,0:T(8,128)(2,1)} %get-tuple-element.70.refs_1_, bf16[256,2048]{1,0:T(8,128)(2,1)} %get-tuple-element.71.refs_2_, bf16[8192,4096]{1,0:T(8,128)(2,1)} %refs_2_.3, ...), custom_call_target="tpu_custom_call" | custom-call | flops 1 | bytes 1 | tf_op jit(solution)/shard_map/matmul_stage/pallas_call | solution.py:239
  78.6 1.3 collective-permute-start.9
  79.9 3.5 %collective-permute-done.5.refs_3_ = bf16[256,2048]{1,0:T(8,128)(2,1)} collective-permute-done((bf16[256,2048]{1,0:T(8,128)(2,1)}, bf16[256,2048]{1,0:T(8,128)(2,1)}, u32[]{:S(2)}, u32[]{:S(2)}) %collective-permute-start.5) | collective-permute-done | bytes 1048608 | tf_op jit(solution)/shard_map/ppermute | solution.py:463
  83.4 22.5 %collective-permute-done.3.refs_1_ = bf16[256,2048]{1,0:T(8,128)(2,1)} collective-permute-done((bf16[256,2048]{1,0:T(8,128)(2,1)}, bf16[256,2048]{1,0:T(8,128)(2,1)}, u32[]{:S(2)}, u32[]{:S(2)}) %collective-permute-start.3) | collective-permute-done | bytes 1048608 | tf_op jit(solution)/shard_map/ppermute | solution.py:463
  106.5 1.3 collective-permute-start.13
  107.8 26.9 %matmul_stage.7 = (f32[4,512,1024]{2,1,0:T(8,128)}, f32[8,128]{1,0:T(8,128)S(1)}) custom-call(s32[8]{0:T(128)S(1)} %pad_add_fusion.1.info, bf16[256,2048]{1,0:T(8,128)(2,1)} %get-tuple-element.78.refs_0_, bf16[256,2048]{1,0:T(8,128)(2,1)} %get-tuple-element.73.refs_1_, bf16[256,2048]{1,0:T(8,128)(2,1)} %get-tuple-element.79.refs_2_, ...), custom_call_target="tpu_custom_call" | custom-call | flops 1 | bytes 1 | tf_op jit(solution)/shard_map/matmul_stage/pallas_call | solution.py:239
  134.8 1.7 collective-permute-start.10
  138.6 10.6 %collective-permute-done.13.refs_3_ = bf16[256,2048]{1,0:T(8,128)(2,1)S(1)} collective-permute-done((bf16[256,2048]{1,0:T(8,128)(2,1)}, bf16[256,2048]{1,0:T(8,128)(2,1)S(1)}, u32[]{:S(2)}, u32[]{:S(2)}) %collective-permute-start.13) | collective-permute-done | bytes 1048608 | tf_op jit(solution)/shard_map/ppermute | solution.py:463
  149.2 20.0 %matmul_stage.8 = (f32[2,256,1024]{2,1,0:T(8,128)}, bf16[256,1024]{1,0:T(8,128)(2,1)S(1)}, bf16[256,1024]{1,0:T(8,128)(2,1)S(1)}, f32[8,128]{1,0:T(8,128)S(1)}) custom-call(s32[6]{0:T(128)S(1)} %pad_add_fusion.3.info, bf16[256,2048]{1,0:T(8,128)(2,1)} %get-tuple-element.87.refs_0_, bf16[256,2048]{1,0:T(8,128)(2,1)} %get-tuple-element.88.refs_1_, ...), custom_call_target="tpu_custom_call" | custom-call | flops 1 | bytes 1 | tf_op jit(solution)/shard_map/matmul_stage/pallas_call | solution.py:239
  169.9 1.3 collective-permute-start.17
  172.6 16.8 %matmul_stage.9 = (f32[4,512,1024]{2,1,0:T(8,128)}, f32[8,128]{1,0:T(8,128)S(1)}) custom-call(s32[4]{0:T(128)S(1)} %pad_add_fusion.2.info, bf16[256,2048]{1,0:T(8,128)(2,1)S(1)} %get-tuple-element.92.refs_0_, bf16[256,2048]{1,0:T(8,128)(2,1)} %collective-permute-done.10.refs_1_.refs_0_, bf16[256,2048]{1,0:T(8,128)(2,1)S(1)} %get-tuple-element.93.refs_2_, ...), custom_call_target="tpu_custom_call" | custom-call | flops 1 | bytes 1 | tf_op jit(solution)/shard_map/matmul_stage/pallas_call | solution.py:239
  190.0 1.8 collective-permute-start.14
  191.8 1.5 collective-permute-start.15
  194.9 1.5 collective-permute-start.22
  196.4 12.1 %matmul_stage.10 = (f32[2,256,1024]{2,1,0:T(8,128)S(1)}, bf16[256,1024]{1,0:T(8,128)(2,1)}, bf16[256,1024]{1,0:T(8,128)(2,1)}, f32[8,128]{1,0:T(8,128)S(1)}) custom-call(s32[4]{0:T(128)S(1)} %pad_add_fusion.info, bf16[256,2048]{1,0:T(8,128)(2,1)S(1)} %collective-permute-done.16.refs_0_, bf16[256,2048]{1,0:T(8,128)(2,1)S(1)} %collective-permute-done.17.refs_1_, ...), custom_call_target="tpu_custom_call" | custom-call | flops 1 | bytes 1 | tf_op jit(solution)/shard_map/matmul_stage/pallas_call | solution.py:239
  208.5 1.3 copy-done.6
  211.9 1.6 copy-done.5
  214.6 1.8 stream_rows.3
  218.1 1.5 collective-permute-start.25
  219.6 12.3 %matmul_stage.11 = (f32[2,256,1024]{2,1,0:T(8,128)S(1)}, bf16[256,1024]{1,0:T(8,128)(2,1)S(1)}, bf16[256,1024]{1,0:T(8,128)(2,1)S(1)}, f32[8,128]{1,0:T(8,128)S(1)}) custom-call(s32[4]{0:T(128)S(1)} %pad_add_fusion.info, bf16[256,2048]{1,0:T(8,128)(2,1)} %collective-permute-done.14.refs_0_, bf16[256,2048]{1,0:T(8,128)(2,1)} %collective-permute-done.15.refs_1_, ...), custom_call_target="tpu_custom_call" | custom-call | flops 1 | bytes 1 | tf_op jit(solution)/shard_map/matmul_stage/pallas_call | solution.py:239
  232.5 8.9 %collective-permute-done.25.refs_2_ = bf16[256,1024]{1,0:T(8,128)(2,1)S(1)} collective-permute-done((bf16[256,1024]{1,0:T(8,128)(2,1)S(1)}, bf16[256,1024]{1,0:T(8,128)(2,1)S(1)}, u32[]{:S(2)}, u32[]{:S(2)}) %collective-permute-start.25) | collective-permute-done | bytes 524320 | tf_op jit(solution)/shard_map/ppermute | solution.py:459
  241.4 1.5 stream_rows.4
  243.8 1.4 collective-permute-start.36
  245.2 12.8 %collective-permute-done.27.refs_2_ = bf16[256,1024]{1,0:T(8,128)(2,1)S(1)} collective-permute-done((bf16[256,1024]{1,0:T(8,128)(2,1)S(1)}, bf16[256,1024]{1,0:T(8,128)(2,1)S(1)}, u32[]{:S(2)}, u32[]{:S(2)}) %collective-permute-start.27) | collective-permute-done | bytes 524320 | tf_op jit(solution)/shard_map/ppermute | solution.py:459
  258.0 1.5 stream_rows.5
  260.2 1.4 collective-permute-start.29
  261.6 4.2 %collective-permute-done.29 = f32[8,768]{1,0:T(8,128)S(1)} collective-permute-done((f32[8,768]{1,0:T(8,128)S(1)}, f32[8,768]{1,0:T(8,128)S(1)}, u32[]{:S(2)}, u32[]{:S(2)}) %collective-permute-start.29) | collective-permute-done | bytes 24608 | tf_op jit(solution)/shard_map/ppermute | solution.py:508
  266.3 3.3 %collective-permute-done.31 = f32[8,768]{1,0:T(8,128)S(1)} collective-permute-done((f32[8,768]{1,0:T(8,128)S(1)}, f32[8,768]{1,0:T(8,128)S(1)}, u32[]{:S(2)}, u32[]{:S(2)}) %collective-permute-start.31) | collective-permute-done | bytes 24608 | tf_op jit(solution)/shard_map/ppermute | solution.py:508
  269.7 1.5 collective-permute-start.34
  271.7 7.1 %collective-permute-done.28.refs_0_ = bf16[256,1024]{1,0:T(8,128)(2,1)S(1)} collective-permute-done((bf16[256,1024]{1,0:T(8,128)(2,1)S(1)}, bf16[256,1024]{1,0:T(8,128)(2,1)S(1)}, u32[]{:S(2)}, u32[]{:S(2)}) %collective-permute-start.28) | collective-permute-done | bytes 524320 | tf_op jit(solution)/shard_map/ppermute | solution.py:459
  280.6 1.7 collective-permute-done.35.refs_5_
  282.3 2.1 norm_rows.3
  284.4 2.1 norm_rows.4
  286.5 2.1 norm_rows.5
  (102 shorter events, 20.3 us)
Async XLA Ops:
  0.6 21.4 %copy-start = (bf16[768,1024]{1,0:T(8,128)(2,1)S(1)}, bf16[768,1024]{1,0:T(8,128)(2,1)}, u32[]{:S(2)}) copy-start(bf16[768,1024]{1,0:T(8,128)(2,1)} %param.16) | copy-start | bytes 4718596
  0.6 10.8 %copy-start.2 = (bf16[768,2048]{1,0:T(8,128)(2,1)S(1)}, bf16[768,2048]{1,0:T(8,128)(2,1)}, u32[]{:S(2)}) copy-start(bf16[768,2048]{1,0:T(8,128)(2,1)} %gate.13) | copy-start | bytes 9437188
  4.0 18.0 %copy-start.11 = (s32[768]{0:T(1024)S(1)}, s32[768]{0:T(1024)}, u32[]{:S(2)}) copy-start(s32[768]{0:T(1024)} %param.18) | copy-start | bytes 9220
  4.0 28.9 %collective-permute-start = (bf16[256,2048]{1,0:T(8,128)(2,1)}, bf16[256,2048]{1,0:T(8,128)(2,1)}, u32[]{:S(2)}, u32[]{:S(2)}) collective-permute-start(bf16[256,2048]{1,0:T(8,128)(2,1)} %fusion.4.refs_0_), channel_id=1, source_target_pairs={{0,1},{1,2},{2,3},{4,5},{5,6},{6,7},{8,9},{9,10},{10,11},{12,13},{... | collective-permute-start | bytes 3145736 | tf_op jit(solution)/shard_map/ppermute | solution.py:462
  10.1 28.3 %collective-permute-start.1 = (bf16[256,2048]{1,0:T(8,128)(2,1)}, bf16[256,2048]{1,0:T(8,128)(2,1)}, u32[]{:S(2)}, u32[]{:S(2)}) collective-permute-start(bf16[256,2048]{1,0:T(8,128)(2,1)} %fusion.4.refs_0_), channel_id=1, source_target_pairs={{1,0},{2,1},{3,2},{5,4},{6,5},{7,6},{9,8},{10,9},{11,10},{13,12},{... | collective-permute-start | bytes 3145736 | tf_op jit(solution)/shard_map/ppermute | solution.py:463
  15.1 40.3 %collective-permute-start.6 = (bf16[256,2048]{1,0:T(8,128)(2,1)}, bf16[256,2048]{1,0:T(8,128)(2,1)}, u32[]{:S(2)}, u32[]{:S(2)}) collective-permute-start(bf16[256,2048]{1,0:T(8,128)(2,1)} %get-tuple-element.78.refs_0_), channel_id=1, source_target_pairs={{0,1},{1,2},{2,3},{4,5},{5,6},{6,7},{8,9},{9,10},{10,11},{12,13},{... | collective-permute-start | bytes 3145736 | tf_op jit(solution)/shard_map/ppermute | solution.py:462
  20.7 56.6 %collective-permute-start.7 = (bf16[256,2048]{1,0:T(8,128)(2,1)}, bf16[256,2048]{1,0:T(8,128)(2,1)}, u32[]{:S(2)}, u32[]{:S(2)}) collective-permute-start(bf16[256,2048]{1,0:T(8,128)(2,1)} %get-tuple-element.78.refs_0_), channel_id=1, source_target_pairs={{1,0},{2,1},{3,2},{5,4},{6,5},{7,6},{9,8},{10,9},{11,10},{13,12},{... | collective-permute-start | bytes 3145736 | tf_op jit(solution)/shard_map/ppermute | solution.py:463
  24.8 13.6 %copy-start.3 = (bf16[768,2048]{1,0:T(8,128)(2,1)S(1)}, bf16[768,2048]{1,0:T(8,128)(2,1)}, u32[]{:S(2)}) copy-start(bf16[768,2048]{1,0:T(8,128)(2,1)} %gate.13) | copy-start | bytes 9437188
  41.3 37.2 %collective-permute-start.4 = (bf16[256,2048]{1,0:T(8,128)(2,1)}, bf16[256,2048]{1,0:T(8,128)(2,1)S(1)}, u32[]{:S(2)}, u32[]{:S(2)}) collective-permute-start(bf16[256,2048]{1,0:T(8,128)(2,1)} %get-tuple-element.73.refs_1_), channel_id=1, source_target_pairs={{0,1},{1,2},{2,3},{4,5},{5,6},{6,7},{8,9},{9,10},{10,11},{12,13},{... | collective-permute-start | bytes 3145736 | tf_op jit(solution)/shard_map/ppermute | solution.py:462
  43.9 39.5 %collective-permute-start.5 = (bf16[256,2048]{1,0:T(8,128)(2,1)}, bf16[256,2048]{1,0:T(8,128)(2,1)}, u32[]{:S(2)}, u32[]{:S(2)}) collective-permute-start(bf16[256,2048]{1,0:T(8,128)(2,1)} %get-tuple-element.73.refs_1_), channel_id=1, source_target_pairs={{1,0},{2,1},{3,2},{5,4},{6,5},{7,6},{9,8},{10,9},{11,10},{13,12},{... | collective-permute-start | bytes 3145736 | tf_op jit(solution)/shard_map/ppermute | solution.py:463
  45.2 38.2 %collective-permute-start.2 = (bf16[256,2048]{1,0:T(8,128)(2,1)}, bf16[256,2048]{1,0:T(8,128)(2,1)}, u32[]{:S(2)}, u32[]{:S(2)}) collective-permute-start(bf16[256,2048]{1,0:T(8,128)(2,1)} %get-tuple-element.70.refs_1_), channel_id=1, source_target_pairs={{1,2},{2,3},{5,6},{6,7},{9,10},{10,11},{13,14},{14,15},{17,18},{18... | collective-permute-start | bytes 3145736 | tf_op jit(solution)/shard_map/ppermute | solution.py:462
  55.4 50.4 %collective-permute-start.3 = (bf16[256,2048]{1,0:T(8,128)(2,1)}, bf16[256,2048]{1,0:T(8,128)(2,1)}, u32[]{:S(2)}, u32[]{:S(2)}) collective-permute-start(bf16[256,2048]{1,0:T(8,128)(2,1)} %get-tuple-element.71.refs_2_), channel_id=1, source_target_pairs={{1,0},{2,1},{5,4},{6,5},{9,8},{10,9},{13,12},{14,13},{17,16},{18,1... | collective-permute-start | bytes 3145736 | tf_op jit(solution)/shard_map/ppermute | solution.py:463
  77.9 56.9 %collective-permute-start.8 = (bf16[256,2048]{1,0:T(8,128)(2,1)}, bf16[256,2048]{1,0:T(8,128)(2,1)S(1)}, u32[]{:S(2)}, u32[]{:S(2)}) collective-permute-start(bf16[256,2048]{1,0:T(8,128)(2,1)} %get-tuple-element.79.refs_2_), channel_id=1, source_target_pairs={{1,2},{2,3},{5,6},{6,7},{9,10},{10,11},{13,14},{14,15},{17,18},{18... | collective-permute-start | bytes 3145736 | tf_op jit(solution)/shard_map/ppermute | solution.py:462
  78.6 56.2 %collective-permute-start.9 = (bf16[256,2048]{1,0:T(8,128)(2,1)}, bf16[256,2048]{1,0:T(8,128)(2,1)S(1)}, u32[]{:S(2)}, u32[]{:S(2)}) collective-permute-start(bf16[256,2048]{1,0:T(8,128)(2,1)} %get-tuple-element.80.refs_4_), channel_id=1, source_target_pairs={{1,0},{2,1},{5,4},{6,5},{9,8},{10,9},{13,12},{14,13},{17,16},{18,1... | collective-permute-start | bytes 3145736 | tf_op jit(solution)/shard_map/ppermute | solution.py:463
  105.8 32.7 %collective-permute-start.12 = (bf16[256,2048]{1,0:T(8,128)(2,1)}, bf16[256,2048]{1,0:T(8,128)(2,1)S(1)}, u32[]{:S(2)}, u32[]{:S(2)}) collective-permute-start(bf16[256,2048]{1,0:T(8,128)(2,1)} %get-tuple-element.87.refs_0_), channel_id=1, source_target_pairs={{2,3},{6,7},{10,11},{14,15},{18,19},{22,23},{26,27},{30,31}} | collective-permute-start | bytes 3145736 | tf_op jit(solution)/shard_map/ppermute | solution.py:462
  106.5 42.6 %collective-permute-start.13 = (bf16[256,2048]{1,0:T(8,128)(2,1)}, bf16[256,2048]{1,0:T(8,128)(2,1)S(1)}, u32[]{:S(2)}, u32[]{:S(2)}) collective-permute-start(bf16[256,2048]{1,0:T(8,128)(2,1)} %get-tuple-element.88.refs_1_), channel_id=1, source_target_pairs={{1,0},{5,4},{9,8},{13,12},{17,16},{21,20},{25,24},{29,28}} | collective-permute-start | bytes 3145736 | tf_op jit(solution)/shard_map/ppermute | solution.py:463
  134.8 37.2 %collective-permute-start.10 = (bf16[256,2048]{1,0:T(8,128)(2,1)S(1)}, bf16[256,2048]{1,0:T(8,128)(2,1)}, u32[]{:S(2)}, u32[]{:S(2)}) collective-permute-start(bf16[256,2048]{1,0:T(8,128)(2,1)S(1)} %get-tuple-element.83), channel_id=1, source_target_pairs={{1,2},{2,3},{5,6},{6,7},{9,10},{10,11},{13,14},{14,15},{17,18},{18... | collective-permute-start | bytes 3145736 | tf_op jit(solution)/shard_map/ppermute | solution.py:462
  136.5 36.1 %collective-permute-start.11 = (bf16[256,2048]{1,0:T(8,128)(2,1)}, bf16[256,2048]{1,0:T(8,128)(2,1)}, u32[]{:S(2)}, u32[]{:S(2)}) collective-permute-start(bf16[256,2048]{1,0:T(8,128)(2,1)} %get-tuple-element.84), channel_id=1, source_target_pairs={{1,0},{2,1},{5,4},{6,5},{9,8},{10,9},{13,12},{14,13},{17,16},{18,1... | collective-permute-start | bytes 3145736 | tf_op jit(solution)/shard_map/ppermute | solution.py:463
  169.2 27.2 %collective-permute-start.16 = (bf16[256,2048]{1,0:T(8,128)(2,1)S(1)}, bf16[256,2048]{1,0:T(8,128)(2,1)S(1)}, u32[]{:S(2)}, u32[]{:S(2)}) collective-permute-start(bf16[256,2048]{1,0:T(8,128)(2,1)S(1)} %get-tuple-element.92.refs_0_), channel_id=1, source_target_pairs={{2,3},{6,7},{10,11},{14,15},{18,19},{22,23},{26,27},{30,31}} | collective-permute-start | bytes 3145736 | tf_op jit(solution)/shard_map/ppermute | solution.py:462
  169.9 26.5 %collective-permute-start.17 = (bf16[256,2048]{1,0:T(8,128)(2,1)S(1)}, bf16[256,2048]{1,0:T(8,128)(2,1)S(1)}, u32[]{:S(2)}, u32[]{:S(2)}) collective-permute-start(bf16[256,2048]{1,0:T(8,128)(2,1)S(1)} %get-tuple-element.93.refs_2_), channel_id=1, source_target_pairs={{1,0},{5,4},{9,8},{13,12},{17,16},{21,20},{25,24},{29,28}} | collective-permute-start | bytes 3145736 | tf_op jit(solution)/shard_map/ppermute | solution.py:463
  171.2 20.6 %collective-permute-start.18 = (bf16[256,1024]{1,0:T(8,128)(2,1)S(1)}, bf16[256,1024]{1,0:T(8,128)(2,1)S(1)}, u32[]{:S(2)}, u32[]{:S(2)}) collective-permute-start(bf16[256,1024]{1,0:T(8,128)(2,1)S(1)} %get-tuple-element.101), channel_id=1, source_target_pairs={{0,4},{4,0},{8,12},{12,8},{1,5},{5,1},{9,13},{13,9},{2,6},{6,2},{1... | collective-permute-start | bytes 1572872 | tf_op jit(solution)/shard_map/ppermute | solution.py:459
  172.0 22.0 %collective-permute-start.19 = (bf16[256,1024]{1,0:T(8,128)(2,1)S(1)}, bf16[256,1024]{1,0:T(8,128)(2,1)S(1)}, u32[]{:S(2)}, u32[]{:S(2)}) collective-permute-start(bf16[256,1024]{1,0:T(8,128)(2,1)S(1)} %get-tuple-element.102), channel_id=1, source_target_pairs={{0,4},{4,0},{8,12},{12,8},{1,5},{5,1},{9,13},{13,9},{2,6},{6,2},{1... | collective-permute-start | bytes 1572872 | tf_op jit(solution)/shard_map/ppermute | solution.py:459
  189.4 4.6 %copy-start.4 = (f32[2,256,1024]{2,1,0:T(8,128)S(1)}, f32[2,256,1024]{2,1,0:T(8,128)}, u32[]{:S(2)}) copy-start(f32[2,256,1024]{2,1,0:T(8,128)} %get-tuple-element.100.keep.refs_0_) | copy-start | bytes 6291460
  190.0 29.6 %collective-permute-start.14 = (bf16[256,2048]{1,0:T(8,128)(2,1)}, bf16[256,2048]{1,0:T(8,128)(2,1)}, u32[]{:S(2)}, u32[]{:S(2)}) collective-permute-start(bf16[256,2048]{1,0:T(8,128)(2,1)} %get-tuple-element.97), channel_id=1, source_target_pairs={{2,3},{6,7},{10,11},{14,15},{18,19},{22,23},{26,27},{30,31}} | collective-permute-start | bytes 3145736 | tf_op jit(solution)/shard_map/ppermute | solution.py:462
  191.8 27.8 %collective-permute-start.15 = (bf16[256,2048]{1,0:T(8,128)(2,1)}, bf16[256,2048]{1,0:T(8,128)(2,1)}, u32[]{:S(2)}, u32[]{:S(2)}) collective-permute-start(bf16[256,2048]{1,0:T(8,128)(2,1)} %get-tuple-element.98), channel_id=1, source_target_pairs={{1,0},{5,4},{9,8},{13,12},{17,16},{21,20},{25,24},{29,28}} | collective-permute-start | bytes 3145736 | tf_op jit(solution)/shard_map/ppermute | solution.py:463
  194.9 16.2 %collective-permute-start.22 = (bf16[256,1024]{1,0:T(8,128)(2,1)}, bf16[256,1024]{1,0:T(8,128)(2,1)S(1)}, u32[]{:S(2)}, u32[]{:S(2)}) collective-permute-start(bf16[256,1024]{1,0:T(8,128)(2,1)} %get-tuple-element.107), channel_id=1, source_target_pairs={{0,8},{4,12},{8,0},{12,4},{1,9},{5,13},{9,1},{13,5},{2,10},{6,14},... | collective-permute-start | bytes 1572872 | tf_op jit(solution)/shard_map/ppermute | solution.py:459
  209.8 7.1 %collective-permute-start.20 = (bf16[256,1024]{1,0:T(8,128)(2,1)}, bf16[256,1024]{1,0:T(8,128)(2,1)S(1)}, u32[]{:S(2)}, u32[]{:S(2)}) collective-permute-start(bf16[256,1024]{1,0:T(8,128)(2,1)} %get-tuple-element.105), channel_id=1, source_target_pairs={{0,4},{4,0},{8,12},{12,8},{1,5},{5,1},{9,13},{13,9},{2,6},{6,2},{1... | collective-permute-start | bytes 1572872 | tf_op jit(solution)/shard_map/ppermute | solution.py:459
  209.8 7.1 %collective-permute-start.21 = (bf16[256,1024]{1,0:T(8,128)(2,1)}, bf16[256,1024]{1,0:T(8,128)(2,1)}, u32[]{:S(2)}, u32[]{:S(2)}) collective-permute-start(bf16[256,1024]{1,0:T(8,128)(2,1)} %get-tuple-element.106), channel_id=1, source_target_pairs={{0,4},{4,0},{8,12},{12,8},{1,5},{5,1},{9,13},{13,9},{2,6},{6,2},{1... | collective-permute-start | bytes 1572872 | tf_op jit(solution)/shard_map/ppermute | solution.py:459
  214.6 2.4 copy-start.7
  216.4 16.1 %collective-permute-start.26 = (bf16[256,1024]{1,0:T(8,128)(2,1)S(1)}, bf16[256,1024]{1,0:T(8,128)(2,1)S(1)}, u32[]{:S(2)}, u32[]{:S(2)}) collective-permute-start(bf16[256,1024]{1,0:T(8,128)(2,1)S(1)} %get-tuple-element.117.refs_0_), channel_id=1, source_target_pairs={{0,8},{4,12},{8,0},{12,4},{1,9},{5,13},{9,1},{13,5},{2,10},{6,14},... | collective-permute-start | bytes 1572872 | tf_op jit(solution)/shard_map/ppermute | solution.py:459
  218.1 23.3 %collective-permute-start.25 = (bf16[256,1024]{1,0:T(8,128)(2,1)S(1)}, bf16[256,1024]{1,0:T(8,128)(2,1)S(1)}, u32[]{:S(2)}, u32[]{:S(2)}) collective-permute-start(bf16[256,1024]{1,0:T(8,128)(2,1)S(1)} %get-tuple-element.115), channel_id=1, source_target_pairs={{0,8},{4,12},{8,0},{12,4},{1,9},{5,13},{9,1},{13,5},{2,10},{6,14},... | collective-permute-start | bytes 1572872 | tf_op jit(solution)/shard_map/ppermute | solution.py:459
  231.9 11.0 %collective-permute-start.23 = (bf16[256,1024]{1,0:T(8,128)(2,1)S(1)}, bf16[256,1024]{1,0:T(8,128)(2,1)S(1)}, u32[]{:S(2)}, u32[]{:S(2)}) collective-permute-start(bf16[256,1024]{1,0:T(8,128)(2,1)S(1)} %get-tuple-element.113), channel_id=1, source_target_pairs={{0,4},{4,0},{8,12},{12,8},{1,5},{5,1},{9,13},{13,9},{2,6},{6,2},{1... | collective-permute-start | bytes 1572872 | tf_op jit(solution)/shard_map/ppermute | solution.py:459
  232.0 11.0 %collective-permute-start.24 = (bf16[256,1024]{1,0:T(8,128)(2,1)S(1)}, bf16[256,1024]{1,0:T(8,128)(2,1)S(1)}, u32[]{:S(2)}, u32[]{:S(2)}) collective-permute-start(bf16[256,1024]{1,0:T(8,128)(2,1)S(1)} %get-tuple-element.114), channel_id=1, source_target_pairs={{0,4},{4,0},{8,12},{12,8},{1,5},{5,1},{9,13},{13,9},{2,6},{6,2},{1... | collective-permute-start | bytes 1572872 | tf_op jit(solution)/shard_map/ppermute | solution.py:459
  243.1 14.9 %collective-permute-start.27 = (bf16[256,1024]{1,0:T(8,128)(2,1)S(1)}, bf16[256,1024]{1,0:T(8,128)(2,1)S(1)}, u32[]{:S(2)}, u32[]{:S(2)}) collective-permute-start(bf16[256,1024]{1,0:T(8,128)(2,1)S(1)} %get-tuple-element.121), channel_id=1, source_target_pairs={{0,8},{4,12},{8,0},{12,4},{1,9},{5,13},{9,1},{13,5},{2,10},{6,14},... | collective-permute-start | bytes 1572872 | tf_op jit(solution)/shard_map/ppermute | solution.py:459
  243.8 35.7 %collective-permute-start.39 = (bf16[256,1024]{1,0:T(8,128)(2,1)S(1)}, bf16[256,1024]{1,0:T(8,128)(2,1)S(1)}, u32[]{:S(2)}, u32[]{:S(2)}) collective-permute-start(bf16[256,1024]{1,0:T(8,128)(2,1)S(1)} %get-tuple-element.117.refs_0_), channel_id=1, source_target_pairs={{0,4},{4,0},{8,12},{12,8},{1,5},{5,1},{9,13},{13,9},{2,6},{6,2},{1... | collective-permute-start | bytes 1572872 | tf_op jit(solution)/shard_map/ppermute | solution.py:459
  243.8 27.4 %collective-permute-start.36 = (bf16[256,1024]{1,0:T(8,128)(2,1)S(1)}, bf16[256,1024]{1,0:T(8,128)(2,1)S(1)}, u32[]{:S(2)}, u32[]{:S(2)}) collective-permute-start(bf16[256,1024]{1,0:T(8,128)(2,1)S(1)} %get-tuple-element.128.refs_0_), channel_id=1, source_target_pairs={{0,8},{4,12},{8,0},{12,4},{1,9},{5,13},{9,1},{13,5},{2,10},{6,14},... | collective-permute-start | bytes 1572872 | tf_op jit(solution)/shard_map/ppermute | solution.py:459
  258.0 24.3 %copy-start.10 = (f32[4096]{0:T(1024)S(1)}, f32[4096]{0:T(1024)}, u32[]{:S(2)}) copy-start(f32[4096]{0:T(1024)} %param.19) | copy-start | bytes 49156
  259.6 19.3 %collective-permute-start.28 = (bf16[256,1024]{1,0:T(8,128)(2,1)S(1)}, bf16[256,1024]{1,0:T(8,128)(2,1)S(1)}, u32[]{:S(2)}, u32[]{:S(2)}) collective-permute-start(bf16[256,1024]{1,0:T(8,128)(2,1)S(1)} %get-tuple-element.125.refs_0_), channel_id=1, source_target_pairs={{0,8},{4,12},{8,0},{12,4},{1,9},{5,13},{9,1},{13,5},{2,10},{6,14},... | collective-permute-start | bytes 1572872 | tf_op jit(solution)/shard_map/ppermute | solution.py:459
  260.2 5.6 %collective-permute-start.29 = (f32[8,768]{1,0:T(8,128)S(1)}, f32[8,768]{1,0:T(8,128)S(1)}, u32[]{:S(2)}, u32[]{:S(2)}) collective-permute-start(f32[8,768]{1,0:T(8,128)S(1)} %constant_dynamic-update-slice_fusion), channel_id=1, source_target_pairs={{0,1},{1,2},{2,3},{3,0},{4,5},{5,6},{6,7},{7,4},{8,9},{9,10},{10,1... | collective-permute-start | bytes 73736 | tf_op jit(solution)/shard_map/ppermute | solution.py:508
  261.6 4.7 %collective-permute-start.30 = (f32[8,768]{1,0:T(8,128)S(1)}, f32[8,768]{1,0:T(8,128)S(1)}, u32[]{:S(2)}, u32[]{:S(2)}) collective-permute-start(f32[8,768]{1,0:T(8,128)S(1)} %constant_dynamic-update-slice_fusion), channel_id=1, source_target_pairs={{0,2},{1,3},{2,0},{3,1},{4,6},{5,7},{6,4},{7,5},{8,10},{9,11},{10,... | collective-permute-start | bytes 73736 | tf_op jit(solution)/shard_map/ppermute | solution.py:508
  265.8 3.8 %collective-permute-start.31 = (f32[8,768]{1,0:T(8,128)S(1)}, f32[8,768]{1,0:T(8,128)S(1)}, u32[]{:S(2)}, u32[]{:S(2)}) collective-permute-start(f32[8,768]{1,0:T(8,128)S(1)} %constant_dynamic-update-slice_fusion), channel_id=1, source_target_pairs={{0,3},{1,0},{2,1},{3,2},{4,7},{5,4},{6,5},{7,6},{8,11},{9,8},{10,9... | collective-permute-start | bytes 73736 | tf_op jit(solution)/shard_map/ppermute | solution.py:508
  266.3 13.7 %collective-permute-start.40 = (bf16[256,1024]{1,0:T(8,128)(2,1)S(1)}, bf16[256,1024]{1,0:T(8,128)(2,1)S(1)}, u32[]{:S(2)}, u32[]{:S(2)}) collective-permute-start(bf16[256,1024]{1,0:T(8,128)(2,1)S(1)} %get-tuple-element.130.refs_1_), channel_id=1, source_target_pairs={{0,4},{4,0},{8,12},{12,8},{1,5},{5,1},{9,13},{13,9},{2,6},{6,2},{1... | collective-permute-start | bytes 1572872 | tf_op jit(solution)/shard_map/ppermute | solution.py:459
  269.7 10.3 %collective-permute-start.34 = (f32[8,768]{1,0:T(8,128)S(1)}, f32[8,768]{1,0:T(8,128)S(1)}, u32[]{:S(2)}, u32[]{:S(2)}) collective-permute-start(f32[8,768]{1,0:T(8,128)S(1)} %add_add_fusion.refs_1_), channel_id=1, source_target_pairs={{0,8},{4,12},{8,0},{12,4},{1,9},{5,13},{9,1},{13,5},{2,10},{6,14},... | collective-permute-start | bytes 73736 | tf_op jit(solution)/shard_map/ppermute | solution.py:459
  271.1 13.3 %collective-permute-start.37 = (bf16[256,1024]{1,0:T(8,128)(2,1)S(1)}, bf16[256,1024]{1,0:T(8,128)(2,1)S(1)}, u32[]{:S(2)}, u32[]{:S(2)}) collective-permute-start(bf16[256,1024]{1,0:T(8,128)(2,1)S(1)} %get-tuple-element.128.refs_0_), channel_id=1, source_target_pairs={{0,4},{4,0},{8,12},{12,8},{1,5},{5,1},{9,13},{13,9},{2,6},{6,2},{1... | collective-permute-start | bytes 1572872 | tf_op jit(solution)/shard_map/ppermute | solution.py:459
  278.9 5.6 %collective-permute-start.38 = (bf16[256,1024]{1,0:T(8,128)(2,1)S(1)}, bf16[256,1024]{1,0:T(8,128)(2,1)S(1)}, u32[]{:S(2)}, u32[]{:S(2)}) collective-permute-start(bf16[256,1024]{1,0:T(8,128)(2,1)S(1)} %get-tuple-element.129.refs_1_), channel_id=1, source_target_pairs={{0,4},{4,0},{8,12},{12,8},{1,5},{5,1},{9,13},{13,9},{2,6},{6,2},{1... | collective-permute-start | bytes 1572872 | tf_op jit(solution)/shard_map/ppermute | solution.py:459
  279.5 7.0 %collective-permute-start.32 = (bf16[256,1024]{1,0:T(8,128)(2,1)S(1)}, bf16[256,1024]{1,0:T(8,128)(2,1)S(1)}, u32[]{:S(2)}, u32[]{:S(2)}) collective-permute-start(bf16[256,1024]{1,0:T(8,128)(2,1)S(1)} %get-tuple-element.125.refs_0_), channel_id=1, source_target_pairs={{0,4},{4,0},{8,12},{12,8},{1,5},{5,1},{9,13},{13,9},{2,6},{6,2},{1... | collective-permute-start | bytes 1572872 | tf_op jit(solution)/shard_map/ppermute | solution.py:459
  280.0 6.5 %collective-permute-start.33 = (bf16[256,1024]{1,0:T(8,128)(2,1)S(1)}, bf16[256,1024]{1,0:T(8,128)(2,1)S(1)}, u32[]{:S(2)}, u32[]{:S(2)}) collective-permute-start(bf16[256,1024]{1,0:T(8,128)(2,1)S(1)} %get-tuple-element.127.refs_1_), channel_id=1, source_target_pairs={{0,4},{4,0},{8,12},{12,8},{1,5},{5,1},{9,13},{13,9},{2,6},{6,2},{1... | collective-permute-start | bytes 1572872 | tf_op jit(solution)/shard_map/ppermute | solution.py:459
  280.1 2.3 collective-permute-start.35
  (5 other events, 6.8 us)

commit v3 on v2

--- a/solution.py
+++ b/solution.py
@@ -116,7 +116,7 @@
     at = count + 1
     prior = refs[at] if prior_at is not None else None
     at += (prior_at is not None) + skip
-    number = 1 + tp // 2 if final else 1
+    number = tp if final else 1
     outs = refs[at : at + number]
     token = refs[at + number]
     held, total, sems, early_sems, late_sems = refs[at + number + 1 :]
@@ -189,8 +189,8 @@
     def _():
         if final:
             for k in range(tp // 2):
-                outs[0][k] = total[me ^ (2 * k)]
-                outs[1 + k][...] = total[me ^ (2 * k + 1)].astype(jnp.bfloat16)
+                outs[k][...] = total[me ^ (2 * k)]
+                outs[tp // 2 + k][...] = total[me ^ (2 * k + 1)].astype(jnp.bfloat16)
         else:
             for k in range(tp):
                 store(k).wait()
@@ -220,9 +220,8 @@
     operands += after
     specs += [token_spec()] * len(after)
     if final:
-        out_specs = [pl.BlockSpec((tp // 2, rows, width), lambda j, s: (0, 0, 0))]
-        out_specs += [pl.BlockSpec((rows, width), lambda j, s: (0, 0))] * (tp // 2)
-        out_shape = [jax.ShapeDtypeStruct((tp // 2, rows, width), jnp.float32)]
+        out_specs = [pl.BlockSpec((rows, width), lambda j, s: (0, 0))] * tp
+        out_shape = [jax.ShapeDtypeStruct((rows, width), jnp.float32)] * (tp // 2)
         out_shape += [jax.ShapeDtypeStruct((rows, width), jnp.bfloat16)] * (tp // 2)
     else:
         out_specs = [anywhere()]
@@ -278,50 +277,42 @@
     return list(outs[:count]), [outs[count]]
 
 
-def halve_kernel(cut, more, keep, *refs):
-    half = keep.shape[0] // 2
-    got = refs[: 2 * half]
-    *outs, token = refs[2 * half + more :]
-    size = keep.shape[1] // cut
+def halve_kernel(half, more, *refs):
+    keep = refs[: 2 * half] if half > 1 else [None, refs[0]]
+    got = refs[len(keep) : len(keep) + 2 * half] if half > 1 else [None, refs[1]]
+    outs = refs[(4 * half if half > 1 else 2) + more :]
     for k in range(half):
-        value = (keep[2 * k + 1] + got[2 * k + 1][...].astype(jnp.float32)).astype(jnp.bfloat16)
-        for n in range(cut):
-            outs[k * cut + n][...] = value[n * size : (n + 1) * size]
+        value = keep[2 * k + 1][...] + got[2 * k + 1][...].astype(jnp.float32)
+        outs[k][...] = value.astype(jnp.bfloat16)
         if half > 1:
-            outs[half * cut][k] = keep[2 * k] + got[2 * k][...].astype(jnp.float32)
-    token[...] = jnp.zeros(TOKEN, jnp.float32)
-
-
-def halve(keep, got, cut, after):
-    count, rows, width = keep.shape
-    half = count // 2
-    stack = lambda n: pl.BlockSpec((n, rows, width), lambda i: (0, 0, 0))
-    flat = lambda n: pl.BlockSpec((n, width), lambda i: (0, 0))
-    size = rows // cut
-    out_specs = [flat(size)] * (half * cut)
-    out_shape = [jax.ShapeDtypeStruct((size, width), jnp.bfloat16)] * (half * cut)
+            outs[half + k][...] = keep[2 * k][...] + got[2 * k][...].astype(jnp.float32)
+    outs[-1][...] = jnp.zeros(TOKEN, jnp.float32)
+
+
+def halve(keep, got, after):
+    half = len(keep) // 2
+    rows, width = keep[0].shape
+    operands = [*keep, *got] if half > 1 else [keep[1], got[1]]
+    flat = pl.BlockSpec((rows, width), lambda i: (0, 0))
+    out_shape = [jax.ShapeDtypeStruct((rows, width), jnp.bfloat16)] * half
     if half > 1:
-        out_specs.append(stack(half))
-        out_shape.append(jax.ShapeDtypeStruct((half, rows, width), jnp.float32))
+        out_shape += [jax.ShapeDtypeStruct((rows, width), jnp.float32)] * half
     outs = pl.pallas_call(
-        functools.partial(halve_kernel, cut, len(after)),
+        functools.partial(halve_kernel, half, len(after)),
         grid=(1,),
-        in_specs=[stack(count)] + [flat(rows)] * count + [token_spec()] * len(after),
-        out_specs=out_specs + [token_spec()],
+        in_specs=[flat] * len(operands) + [token_spec()] * len(after),
+        out_specs=[flat] * len(out_shape) + [token_spec()],
         out_shape=out_shape + [TOKEN_SHAPE],
         compiler_params=params(),
         cost_estimate=pl.CostEstimate(flops=1, bytes_accessed=1, transcendentals=0),
         name="halve",
-    )(keep, *got, *after)
-    return outs[: half * cut], outs[half * cut] if half > 1 else None, outs[-1]
-
-
-def stream_kernel(cut, more, *refs):
-    keep, first, *last = refs[: 2 + cut]
-    signs, matrix, residual = refs[2 + cut : 5 + cut]
-    stream, chunk, squares = refs[5 + cut + more :]
-    last = jnp.concatenate([part[...].astype(jnp.float32) for part in last], axis=0)
-    total = keep[...] + first[...].astype(jnp.float32) + last
+    )(*operands, *after)
+    return outs[:half], outs[half:-1], outs[-1]
+
+
+def stream_kernel(more, keep, first, last, signs, matrix, residual, *refs):
+    stream, chunk, squares = refs[more:]
+    total = keep[...] + first[...].astype(jnp.float32) + last[...].astype(jnp.float32)
     total = total * signs[...].astype(jnp.float32)
     rows, width = total.shape
     turn = matrix[...]
@@ -348,15 +339,11 @@
 
 
 def stream_rows(keep, first, last, signs, matrix, residual, so_far, start, after):
-    _, rows, width = keep.shape
-    cut = len(last)
+    rows, width = keep.shape
     place = start // rows
     line = pl.BlockSpec((rows, width), lambda i: (place, 0))
-    flat = lambda n: pl.BlockSpec((n, width), lambda i: (0, 0))
-    operands = [keep, first, *last, signs, matrix, residual]
-    specs = [pl.BlockSpec((None, rows, width), lambda i: (0, 0, 0)), flat(rows)]
-    specs += [flat(rows // cut)] * cut
-    specs += [
+    operands = [keep, first, last, signs, matrix, residual]
+    specs = [pl.BlockSpec((rows, width), lambda i: (0, 0))] * 3 + [
         pl.BlockSpec((1, width), lambda i: (0, 0)),
         pl.BlockSpec((128, 128), lambda i: (0, 0)),
         line,
@@ -369,7 +356,7 @@
     operands += after
     specs += [token_spec()] * len(after)
     return pl.pallas_call(
-        functools.partial(stream_kernel, cut, len(aliases) + len(after)),
+        functools.partial(stream_kernel, len(aliases) + len(after)),
         grid=(1,),
         in_specs=specs,
         out_specs=[
@@ -472,19 +459,18 @@
     streams = [None]
     pieces, squares = {}, {}
 
-    def begin_sums(u, keep, *send):
-        terms[u] = [keep, [swap(value, bits[0]) for value in send]]
+    def begin_sums(u, sums):
+        terms[u] = [sums[: tp // 2], [swap(value, bits[0]) for value in sums[tp // 2 :]]]
 
     def halve_sums(u, after):
         keep, got = terms[u]
         for bit in bits[1:]:
-            send, kept, token = halve(keep, got, 1, after)
+            send, kept, token = halve(keep, got, after)
             after = [token]
             arrived = [swap(value, bit) for value in send]
-            if kept is None:
-                terms[u] = [keep, got[0], arrived]
-            else:
+            if kept:
                 keep, got = kept, arrived
+        terms[u] = [keep[0], got[0], arrived[0]]
         return after
 
     def finish(u, after):
@@ -497,8 +483,10 @@
         return [squares[u]]
 
     def spread(u, after):
-        values, token = gate([value for _, value in pieces[u][1:]], after)
-        pieces[u][1:] = [(e, value) for (e, _), value in zip(pieces[u][1:], values)]
+        token = after
+        if after:
+            values, token = gate([value for _, value in pieces[u][1:]], after)
+            pieces[u][1:] = [(e, value) for (e, _), value in zip(pieces[u][1:], values)]
         pieces[u] += [(e | bits[0], swap(value, bits[0])) for e, value in pieces[u]]
         return token
 
@@ -578,7 +566,7 @@
     token = hold([(1, 2), (mid, 1)], token)
     pass_on(2, 2, mid)
     *sums, token = matmul([0], middle + late, part, 0, True, token)
-    begin_sums(0, *sums)
+    begin_sums(0, sums)
     token = hold([(mid, 1)], [token])
     pass_on(1, sub - 1, sub - 1)
     parts, *token = matmul([1, 2], middle, parts, 0, False, token)
@@ -586,19 +574,21 @@
     pass_on(2, sub - 1, sub - 1)
     token = halve_sums(0, token)
     *sums, token = matmul([1], late, parts, 0, True, token)
-    begin_sums(1, *sums)
-    token = finish(0, [token])
-    token = halve_sums(1, token)
+    begin_sums(1, sums)
+    token = halve_sums(1, [token])
+    token = finish(0, token)
     *sums, token = matmul([2], late, parts, sizes[1], True, token)
-    begin_sums(2, *sums)
+    begin_sums(2, sums)
     token = spread(0, [token])
     token = finish(1, token)
     token = halve_sums(2, token)
+    along = sum_along(jnp.concatenate([squares[0], squares[1]], axis=1))
     token = finish(2, token)
-    along = sum_along(jnp.concatenate([squares[u] for u in range(3)], axis=1))
-    spread(1, token)
+    spread(1, [])
+    token = normalise([0, 1], sum_across(along), token)
+    along = sum_along(squares[2])
     spread(2, [along])
-    normalise([0, 1, 2], sum_across(along), token)
+    normalise([2], sum_across(along), token)
     return (streams[0], normed[0])
 
 

time: 290 us -> 307 us (1.059)
  waiting for transfers between devices: 97.5 us -> 111 us
    ppermute x20 -> x22, waiting for transfers between devices: 30.7 us -> 38.8 us  [swap(): return lax.ppermute(value, 'tp', [(i, i ^ d) for i in range(tp)])]
    ppermute x3 -> x6, waiting for transfers between devices: 8.03 us -> 11.6 us  [sum_along(): lax.ppermute(local, 'sub', [(i, (i + d) % sub) for i in range(sub)])]
    unnamed x26 -> x37, local copies, waits for them, and re-layouts: 4.78 us -> 6.83 us
    ppermute x20 -> x22, starting transfers between devices: 10.5 us -> 11.9 us  [swap(): return lax.ppermute(value, 'tp', [(i, i ^ d) for i in range(tp)])]
  transfers between devices with their start and end apart: 41 -> 46, of which waited for: 13 -> 16; matrix products, arithmetic and copies ran while one was open for 2% -> 2% of each run, Pallas kernels for 44% -> 42%
where the time goes in v3:
time: 307 us; the launch traced here: 306 us
  Pallas kernels  130 us (42%)
  waiting for transfers between devices  111 us (36%)
  starting transfers between devices  46.2 us (15%)
  local copies, waits for them, and re-layouts  13.2 us (4%)
  other arithmetic  3.76 us (1%)
    pallas_call x6, Pallas kernels, matmul_stage(): pl.pallas_call(functools.partial(matmul_kernel, plan), grid_spec=pltpu.Pr...  107 us
    ppermute x9, waiting for transfers between devices, onward(): lax.ppermute(pair[1], 'sub', [(i, i - 1) for i in range(1, sub - d + 1)])  44.2 us
    ppermute x22, waiting for transfers between devices, swap(): return lax.ppermute(value, 'tp', [(i, i ^ d) for i in range(tp)])  38.8 us
    ppermute x9, starting transfers between devices, onward(): lax.ppermute(pair[0], 'sub', [(i, i + 1) for i in range(d - 1, sub - 1)])  20.4 us
    ppermute x9, waiting for transfers between devices, onward(): lax.ppermute(pair[0], 'sub', [(i, i + 1) for i in range(d - 1, sub - 1)])  16.8 us
    ppermute x22, starting transfers between devices, swap(): return lax.ppermute(value, 'tp', [(i, i ^ d) for i in range(tp)])  11.9 us
    ppermute x9, starting transfers between devices, onward(): lax.ppermute(pair[1], 'sub', [(i, i - 1) for i in range(1, sub - d + 1)])  11.8 us
    ppermute x6, waiting for transfers between devices, sum_along(): lax.ppermute(local, 'sub', [(i, (i + d) % sub) for i in range(sub)])  11.6 us
  transfers between devices with their start and end apart: 46, of which 16 were waited for; matrix products, arithmetic and copies ran while one was open for 2% of the time, Pallas kernels for 42%

profile of v3, /device:TPU:0, one launch (start us, length us, event | category | flops | bytes accessed | tf_op | source)
XLA Modules:
  0.0 305.6 jit_solution(1169511163139443813)
XLA Ops:
  0.7 3.3 %fusion.4.refs_0_ = bf16[256,2048]{1,0:T(8,128)(2,1)} fusion(bf16[768,2048]{1,0:T(8,128)(2,1)} %up.3, bf16[768,2048]{1,0:T(8,128)(2,1)} %gate.12), kind=kLoop, calls=%fused_computation.7 | loop fusion | flops 4194304 | bytes 3145728 | tf_op jit(solution)/shard_map/convert_element_type | solution.py:554
  4.0 6.1 %collective-permute-start = (bf16[256,2048]{1,0:T(8,128)(2,1)}, bf16[256,2048]{1,0:T(8,128)(2,1)}, u32[]{:S(2)}, u32[]{:S(2)}) collective-permute-start(bf16[256,2048]{1,0:T(8,128)(2,1)} %fusion.4.refs_0_), channel_id=1, source_target_pairs={{0,1},{1,2},{2,3},{4,5},{5,6},{6,7},{8,9},{9,10},{10,11},{12,13},{... | collective-permute-start | bytes 3145736 | tf_op jit(solution)/shard_map/ppermute | solution.py:449
  10.1 1.3 collective-permute-start.1
  11.4 3.6 %hidden_rows.2 = (bf16[256,2048]{1,0:T(8,128)(2,1)}, f32[8,128]{1,0:T(8,128)S(1)}) custom-call(bf16[768,2048]{1,0:T(8,128)(2,1)S(1)} %copy-done.2, bf16[768,2048]{1,0:T(8,128)(2,1)} %up.3, bf16[256,2048]{1,0:T(8,128)(2,1)} %fusion.4.refs_0_), custom_call_target="tpu_custom_call" | custom-call | flops 1 | bytes 1 | tf_op jit(solution)/shard_map/hidden_rows/pallas_call | solution.py:67
  15.0 5.6 %collective-permute-start.6 = (bf16[256,2048]{1,0:T(8,128)(2,1)}, bf16[256,2048]{1,0:T(8,128)(2,1)}, u32[]{:S(2)}, u32[]{:S(2)}) collective-permute-start(bf16[256,2048]{1,0:T(8,128)(2,1)} %get-tuple-element.80.refs_0_), channel_id=1, source_target_pairs={{0,1},{1,2},{2,3},{4,5},{5,6},{6,7},{8,9},{9,10},{10,11},{12,13},{... | collective-permute-start | bytes 3145736 | tf_op jit(solution)/shard_map/ppermute | solution.py:449
  20.6 1.3 collective-permute-start.7
  21.9 2.8 gather_fusion
  24.7 8.2 %collective-permute-done.refs_0_ = bf16[256,2048]{1,0:T(8,128)(2,1)} collective-permute-done((bf16[256,2048]{1,0:T(8,128)(2,1)}, bf16[256,2048]{1,0:T(8,128)(2,1)}, u32[]{:S(2)}, u32[]{:S(2)}) %collective-permute-start) | collective-permute-done | bytes 1048608 | tf_op jit(solution)/shard_map/ppermute | solution.py:449
  32.9 5.5 %collective-permute-done.1.refs_1_ = bf16[256,2048]{1,0:T(8,128)(2,1)} collective-permute-done((bf16[256,2048]{1,0:T(8,128)(2,1)}, bf16[256,2048]{1,0:T(8,128)(2,1)}, u32[]{:S(2)}, u32[]{:S(2)}) %collective-permute-start.1) | collective-permute-done | bytes 1048608 | tf_op jit(solution)/shard_map/ppermute | solution.py:450
  38.4 3.0 hidden_rows.3
  41.4 2.5 collective-permute-start.4
  43.9 1.3 collective-permute-start.5
  45.2 1.6 collective-permute-start.2
  46.8 8.6 %collective-permute-done.6.refs_0_ = bf16[256,2048]{1,0:T(8,128)(2,1)} collective-permute-done((bf16[256,2048]{1,0:T(8,128)(2,1)}, bf16[256,2048]{1,0:T(8,128)(2,1)}, u32[]{:S(2)}, u32[]{:S(2)}) %collective-permute-start.6) | collective-permute-done | bytes 1048608 | tf_op jit(solution)/shard_map/ppermute | solution.py:449
  55.4 1.3 collective-permute-start.3
  57.5 19.8 %matmul_stage.6 = (f32[4,256,1024]{2,1,0:T(8,128)}, f32[8,128]{1,0:T(8,128)S(1)}) custom-call(s32[8]{0:T(128)S(1)} %pad_add_fusion.1.info, bf16[256,2048]{1,0:T(8,128)(2,1)} %fusion.4.refs_0_, bf16[256,2048]{1,0:T(8,128)(2,1)} %get-tuple-element.72.refs_1_, bf16[256,2048]{1,0:T(8,128)(2,1)} %get-tuple-element.73.refs_2_, bf16[8192,4096]{1,0:T(8,128)(2,1)} %refs_2_.3, ...), custom_call_target="tpu_custom_call" | custom-call | flops 1 | bytes 1 | tf_op jit(solution)/shard_map/matmul_stage/pallas_call | solution.py:238
  78.6 1.3 collective-permute-start.9
  79.9 3.4 %collective-permute-done.5.refs_3_ = bf16[256,2048]{1,0:T(8,128)(2,1)} collective-permute-done((bf16[256,2048]{1,0:T(8,128)(2,1)}, bf16[256,2048]{1,0:T(8,128)(2,1)}, u32[]{:S(2)}, u32[]{:S(2)}) %collective-permute-start.5) | collective-permute-done | bytes 1048608 | tf_op jit(solution)/shard_map/ppermute | solution.py:450
  83.3 22.5 %collective-permute-done.3.refs_1_ = bf16[256,2048]{1,0:T(8,128)(2,1)} collective-permute-done((bf16[256,2048]{1,0:T(8,128)(2,1)}, bf16[256,2048]{1,0:T(8,128)(2,1)}, u32[]{:S(2)}, u32[]{:S(2)}) %collective-permute-start.3) | collective-permute-done | bytes 1048608 | tf_op jit(solution)/shard_map/ppermute | solution.py:450
  106.5 1.3 collective-permute-start.13
  107.8 27.0 %matmul_stage.7 = (f32[4,512,1024]{2,1,0:T(8,128)}, f32[8,128]{1,0:T(8,128)S(1)}) custom-call(s32[8]{0:T(128)S(1)} %pad_add_fusion.1.info, bf16[256,2048]{1,0:T(8,128)(2,1)} %get-tuple-element.80.refs_0_, bf16[256,2048]{1,0:T(8,128)(2,1)} %get-tuple-element.75.refs_1_, bf16[256,2048]{1,0:T(8,128)(2,1)} %get-tuple-element.81.refs_2_, ...), custom_call_target="tpu_custom_call" | custom-call | flops 1 | bytes 1 | tf_op jit(solution)/shard_map/matmul_stage/pallas_call | solution.py:238
  134.8 1.6 collective-permute-start.10
  138.5 10.6 %collective-permute-done.13.refs_3_ = bf16[256,2048]{1,0:T(8,128)(2,1)S(1)} collective-permute-done((bf16[256,2048]{1,0:T(8,128)(2,1)}, bf16[256,2048]{1,0:T(8,128)(2,1)S(1)}, u32[]{:S(2)}, u32[]{:S(2)}) %collective-permute-start.13) | collective-permute-done | bytes 1048608 | tf_op jit(solution)/shard_map/ppermute | solution.py:450
  150.1 19.5 %matmul_stage.8 = (f32[256,1024]{1,0:T(8,128)S(1)}, f32[256,1024]{1,0:T(8,128)S(1)}, bf16[256,1024]{1,0:T(8,128)(2,1)}, bf16[256,1024]{1,0:T(8,128)(2,1)S(1)}, f32[8,128]{1,0:T(8,128)S(1)}) custom-call(s32[6]{0:T(128)S(1)} %pad_add_fusion.3.info, bf16[256,2048]{1,0:T(8,128)(2,1)} %get-tuple-element.89.refs_0_, bf16[256,2048]{1,0:T(8,128)(2,1)} %get-tuple-element.90.refs_1_, ...), custom_call_target="tpu_custom_call" | custom-call | flops 1 | bytes 1 | tf_op jit(solution)/shard_map/matmul_stage/pallas_call | solution.py:238
  170.4 1.3 collective-permute-start.20
  172.6 16.8 %matmul_stage.9 = (f32[4,512,1024]{2,1,0:T(8,128)}, f32[8,128]{1,0:T(8,128)S(1)}) custom-call(s32[4]{0:T(128)S(1)} %pad_add_fusion.2.info, bf16[256,2048]{1,0:T(8,128)(2,1)S(1)} %get-tuple-element.94.refs_0_, bf16[256,2048]{1,0:T(8,128)(2,1)} %collective-permute-done.10.refs_1_.refs_0_, bf16[256,2048]{1,0:T(8,128)(2,1)S(1)} %get-tuple-element.95.refs_2_, ...), custom_call_target="tpu_custom_call" | custom-call | flops 1 | bytes 1 | tf_op jit(solution)/shard_map/matmul_stage/pallas_call | solution.py:238
  190.7 1.5 collective-permute-start.15
  193.9 2.1 collective-permute-done.20.refs_1_
  196.0 11.8 %matmul_stage.10 = (f32[256,1024]{1,0:T(8,128)S(1)}, f32[256,1024]{1,0:T(8,128)S(1)}, bf16[256,1024]{1,0:T(8,128)(2,1)S(1)}, bf16[256,1024]{1,0:T(8,128)(2,1)}, f32[8,128]{1,0:T(8,128)S(1)}) custom-call(s32[4]{0:T(128)S(1)} %pad_add_fusion.info, bf16[256,2048]{1,0:T(8,128)(2,1)S(1)} %collective-permute-done.19.refs_0_, ...), custom_call_target="tpu_custom_call" | custom-call | flops 1 | bytes 1 | tf_op jit(solution)/shard_map/matmul_stage/pallas_call | solution.py:238
  211.1 1.5 collective-permute-start.18
  216.7 8.6 %collective-permute-done.18.last = bf16[256,1024]{1,0:T(8,128)(2,1)} collective-permute-done((bf16[256,1024]{1,0:T(8,128)(2,1)}, bf16[256,1024]{1,0:T(8,128)(2,1)}, u32[]{:S(2)}, u32[]{:S(2)}) %collective-permute-start.18) | collective-permute-done | bytes 524320 | tf_op jit(solution)/shard_map/ppermute | solution.py:446
  226.3 2.8 stream_rows.3
  229.1 1.5 collective-permute-start.26
  231.2 12.3 %matmul_stage.11 = (f32[256,1024]{1,0:T(8,128)S(1)}, f32[256,1024]{1,0:T(8,128)S(1)}, bf16[256,1024]{1,0:T(8,128)(2,1)S(1)}, bf16[256,1024]{1,0:T(8,128)(2,1)S(1)}, f32[8,128]{1,0:T(8,128)S(1)}) custom-call(s32[4]{0:T(128)S(1)} %pad_add_fusion.info, bf16[256,2048]{1,0:T(8,128)(2,1)S(1)} %collective-permute-done.14.refs_0_, ...), custom_call_target="tpu_custom_call" | custom-call | flops 1 | bytes 1 | tf_op jit(solution)/shard_map/matmul_stage/pallas_call | solution.py:238
  244.1 9.3 %collective-permute-done.25.last = bf16[256,1024]{1,0:T(8,128)(2,1)S(1)} collective-permute-done((bf16[256,1024]{1,0:T(8,128)(2,1)S(1)}, bf16[256,1024]{1,0:T(8,128)(2,1)S(1)}, u32[]{:S(2)}, u32[]{:S(2)}) %collective-permute-start.25) | collective-permute-done | bytes 524320 | tf_op jit(solution)/shard_map/ppermute | solution.py:446
  253.3 1.5 stream_rows.4
  255.1 1.6 collective-permute-start.27
  257.2 12.8 %collective-permute-done.27.last = bf16[256,1024]{1,0:T(8,128)(2,1)S(1)} collective-permute-done((bf16[256,1024]{1,0:T(8,128)(2,1)S(1)}, bf16[256,1024]{1,0:T(8,128)(2,1)S(1)}, u32[]{:S(2)}, u32[]{:S(2)}) %collective-permute-start.27) | collective-permute-done | bytes 524320 | tf_op jit(solution)/shard_map/ppermute | solution.py:446
  270.0 1.5 stream_rows.5
  271.5 1.5 collective-permute-start.28
  274.1 4.5 %collective-permute-done.39 = f32[8,512]{1,0:T(8,128)S(1)} collective-permute-done((f32[8,512]{1,0:T(8,128)S(1)}, f32[8,512]{1,0:T(8,128)S(1)}, u32[]{:S(2)}, u32[]{:S(2)}) %collective-permute-start.39) | collective-permute-done | bytes 16416 | tf_op jit(solution)/shard_map/ppermute | solution.py:496
  278.6 3.7 %collective-permute-done.41 = f32[8,512]{1,0:T(8,128)S(1)} collective-permute-done((f32[8,512]{1,0:T(8,128)S(1)}, f32[8,512]{1,0:T(8,128)S(1)}, u32[]{:S(2)}, u32[]{:S(2)}) %collective-permute-start.41) | collective-permute-done | bytes 16416 | tf_op jit(solution)/shard_map/ppermute | solution.py:496
  282.9 7.2 %collective-permute-done.42 = f32[8,512]{1,0:T(8,128)S(1)} collective-permute-done((f32[8,512]{1,0:T(8,128)S(1)}, f32[8,512]{1,0:T(8,128)S(1)}, u32[]{:S(2)}, u32[]{:S(2)}) %collective-permute-start.42) | collective-permute-done | bytes 16416 | tf_op jit(solution)/shard_map/ppermute | solution.py:446
  291.1 3.4 %collective-permute-done.30 = f32[8,256]{1,0:T(8,128)S(1)} collective-permute-done((f32[8,256]{1,0:T(8,128)S(1)}, f32[8,256]{1,0:T(8,128)S(1)}, u32[]{:S(2)}, u32[]{:S(2)}) %collective-permute-start.30) | collective-permute-done | bytes 8224 | tf_op jit(solution)/shard_map/ppermute | solution.py:496
  295.1 1.6 collective-permute-start.34
  299.3 2.1 norm_rows.3
  301.4 2.1 norm_rows.4
  303.5 2.1 norm_rows.5
  (124 shorter events, 26.7 us)
Async XLA Ops:
  4.0 28.9 %collective-permute-start = (bf16[256,2048]{1,0:T(8,128)(2,1)}, bf16[256,2048]{1,0:T(8,128)(2,1)}, u32[]{:S(2)}, u32[]{:S(2)}) collective-permute-start(bf16[256,2048]{1,0:T(8,128)(2,1)} %fusion.4.refs_0_), channel_id=1, source_target_pairs={{0,1},{1,2},{2,3},{4,5},{5,6},{6,7},{8,9},{9,10},{10,11},{12,13},{... | collective-permute-start | bytes 3145736 | tf_op jit(solution)/shard_map/ppermute | solution.py:449
  10.1 28.3 %collective-permute-start.1 = (bf16[256,2048]{1,0:T(8,128)(2,1)}, bf16[256,2048]{1,0:T(8,128)(2,1)}, u32[]{:S(2)}, u32[]{:S(2)}) collective-permute-start(bf16[256,2048]{1,0:T(8,128)(2,1)} %fusion.4.refs_0_), channel_id=1, source_target_pairs={{1,0},{2,1},{3,2},{5,4},{6,5},{7,6},{9,8},{10,9},{11,10},{13,12},{... | collective-permute-start | bytes 3145736 | tf_op jit(solution)/shard_map/ppermute | solution.py:450
  15.0 40.4 %collective-permute-start.6 = (bf16[256,2048]{1,0:T(8,128)(2,1)}, bf16[256,2048]{1,0:T(8,128)(2,1)}, u32[]{:S(2)}, u32[]{:S(2)}) collective-permute-start(bf16[256,2048]{1,0:T(8,128)(2,1)} %get-tuple-element.80.refs_0_), channel_id=1, source_target_pairs={{0,1},{1,2},{2,3},{4,5},{5,6},{6,7},{8,9},{9,10},{10,11},{12,13},{... | collective-permute-start | bytes 3145736 | tf_op jit(solution)/shard_map/ppermute | solution.py:449
  20.6 56.7 %collective-permute-start.7 = (bf16[256,2048]{1,0:T(8,128)(2,1)}, bf16[256,2048]{1,0:T(8,128)(2,1)}, u32[]{:S(2)}, u32[]{:S(2)}) collective-permute-start(bf16[256,2048]{1,0:T(8,128)(2,1)} %get-tuple-element.80.refs_0_), channel_id=1, source_target_pairs={{1,0},{2,1},{3,2},{5,4},{6,5},{7,6},{9,8},{10,9},{11,10},{13,12},{... | collective-permute-start | bytes 3145736 | tf_op jit(solution)/shard_map/ppermute | solution.py:450
  41.4 37.2 %collective-permute-start.4 = (bf16[256,2048]{1,0:T(8,128)(2,1)}, bf16[256,2048]{1,0:T(8,128)(2,1)S(1)}, u32[]{:S(2)}, u32[]{:S(2)}) collective-permute-start(bf16[256,2048]{1,0:T(8,128)(2,1)} %get-tuple-element.75.refs_1_), channel_id=1, source_target_pairs={{0,1},{1,2},{2,3},{4,5},{5,6},{6,7},{8,9},{9,10},{10,11},{12,13},{... | collective-permute-start | bytes 3145736 | tf_op jit(solution)/shard_map/ppermute | solution.py:449
  43.9 39.5 %collective-permute-start.5 = (bf16[256,2048]{1,0:T(8,128)(2,1)}, bf16[256,2048]{1,0:T(8,128)(2,1)}, u32[]{:S(2)}, u32[]{:S(2)}) collective-permute-start(bf16[256,2048]{1,0:T(8,128)(2,1)} %get-tuple-element.75.refs_1_), channel_id=1, source_target_pairs={{1,0},{2,1},{3,2},{5,4},{6,5},{7,6},{9,8},{10,9},{11,10},{13,12},{... | collective-permute-start | bytes 3145736 | tf_op jit(solution)/shard_map/ppermute | solution.py:450
  45.2 38.2 %collective-permute-start.2 = (bf16[256,2048]{1,0:T(8,128)(2,1)}, bf16[256,2048]{1,0:T(8,128)(2,1)}, u32[]{:S(2)}, u32[]{:S(2)}) collective-permute-start(bf16[256,2048]{1,0:T(8,128)(2,1)} %get-tuple-element.72.refs_1_), channel_id=1, source_target_pairs={{1,2},{2,3},{5,6},{6,7},{9,10},{10,11},{13,14},{14,15},{17,18},{18... | collective-permute-start | bytes 3145736 | tf_op jit(solution)/shard_map/ppermute | solution.py:449
  55.4 50.4 %collective-permute-start.3 = (bf16[256,2048]{1,0:T(8,128)(2,1)}, bf16[256,2048]{1,0:T(8,128)(2,1)}, u32[]{:S(2)}, u32[]{:S(2)}) collective-permute-start(bf16[256,2048]{1,0:T(8,128)(2,1)} %get-tuple-element.73.refs_2_), channel_id=1, source_target_pairs={{1,0},{2,1},{5,4},{6,5},{9,8},{10,9},{13,12},{14,13},{17,16},{18,1... | collective-permute-start | bytes 3145736 | tf_op jit(solution)/shard_map/ppermute | solution.py:450
  77.9 56.9 %collective-permute-start.8 = (bf16[256,2048]{1,0:T(8,128)(2,1)}, bf16[256,2048]{1,0:T(8,128)(2,1)S(1)}, u32[]{:S(2)}, u32[]{:S(2)}) collective-permute-start(bf16[256,2048]{1,0:T(8,128)(2,1)} %get-tuple-element.81.refs_2_), channel_id=1, source_target_pairs={{1,2},{2,3},{5,6},{6,7},{9,10},{10,11},{13,14},{14,15},{17,18},{18... | collective-permute-start | bytes 3145736 | tf_op jit(solution)/shard_map/ppermute | solution.py:449
  78.6 56.2 %collective-permute-start.9 = (bf16[256,2048]{1,0:T(8,128)(2,1)}, bf16[256,2048]{1,0:T(8,128)(2,1)S(1)}, u32[]{:S(2)}, u32[]{:S(2)}) collective-permute-start(bf16[256,2048]{1,0:T(8,128)(2,1)} %get-tuple-element.82.refs_4_), channel_id=1, source_target_pairs={{1,0},{2,1},{5,4},{6,5},{9,8},{10,9},{13,12},{14,13},{17,16},{18,1... | collective-permute-start | bytes 3145736 | tf_op jit(solution)/shard_map/ppermute | solution.py:450
  105.8 32.7 %collective-permute-start.12 = (bf16[256,2048]{1,0:T(8,128)(2,1)}, bf16[256,2048]{1,0:T(8,128)(2,1)S(1)}, u32[]{:S(2)}, u32[]{:S(2)}) collective-permute-start(bf16[256,2048]{1,0:T(8,128)(2,1)} %get-tuple-element.89.refs_0_), channel_id=1, source_target_pairs={{2,3},{6,7},{10,11},{14,15},{18,19},{22,23},{26,27},{30,31}} | collective-permute-start | bytes 3145736 | tf_op jit(solution)/shard_map/ppermute | solution.py:449
  106.5 42.6 %collective-permute-start.13 = (bf16[256,2048]{1,0:T(8,128)(2,1)}, bf16[256,2048]{1,0:T(8,128)(2,1)S(1)}, u32[]{:S(2)}, u32[]{:S(2)}) collective-permute-start(bf16[256,2048]{1,0:T(8,128)(2,1)} %get-tuple-element.90.refs_1_), channel_id=1, source_target_pairs={{1,0},{5,4},{9,8},{13,12},{17,16},{21,20},{25,24},{29,28}} | collective-permute-start | bytes 3145736 | tf_op jit(solution)/shard_map/ppermute | solution.py:450
  134.8 37.6 %collective-permute-start.10 = (bf16[256,2048]{1,0:T(8,128)(2,1)S(1)}, bf16[256,2048]{1,0:T(8,128)(2,1)}, u32[]{:S(2)}, u32[]{:S(2)}) collective-permute-start(bf16[256,2048]{1,0:T(8,128)(2,1)S(1)} %get-tuple-element.85), channel_id=1, source_target_pairs={{1,2},{2,3},{5,6},{6,7},{9,10},{10,11},{13,14},{14,15},{17,18},{18... | collective-permute-start | bytes 3145736 | tf_op jit(solution)/shard_map/ppermute | solution.py:449
  136.5 36.1 %collective-permute-start.11 = (bf16[256,2048]{1,0:T(8,128)(2,1)}, bf16[256,2048]{1,0:T(8,128)(2,1)}, u32[]{:S(2)}, u32[]{:S(2)}) collective-permute-start(bf16[256,2048]{1,0:T(8,128)(2,1)} %get-tuple-element.86), channel_id=1, source_target_pairs={{1,0},{2,1},{5,4},{6,5},{9,8},{10,9},{13,12},{14,13},{17,16},{18,1... | collective-permute-start | bytes 3145736 | tf_op jit(solution)/shard_map/ppermute | solution.py:450
  169.6 24.3 %collective-permute-start.19 = (bf16[256,2048]{1,0:T(8,128)(2,1)S(1)}, bf16[256,2048]{1,0:T(8,128)(2,1)S(1)}, u32[]{:S(2)}, u32[]{:S(2)}) collective-permute-start(bf16[256,2048]{1,0:T(8,128)(2,1)S(1)} %get-tuple-element.94.refs_0_), channel_id=1, source_target_pairs={{2,3},{6,7},{10,11},{14,15},{18,19},{22,23},{26,27},{30,31}} | collective-permute-start | bytes 3145736 | tf_op jit(solution)/shard_map/ppermute | solution.py:449
  170.4 25.6 %collective-permute-start.20 = (bf16[256,2048]{1,0:T(8,128)(2,1)S(1)}, bf16[256,2048]{1,0:T(8,128)(2,1)S(1)}, u32[]{:S(2)}, u32[]{:S(2)}) collective-permute-start(bf16[256,2048]{1,0:T(8,128)(2,1)S(1)} %get-tuple-element.95.refs_2_), channel_id=1, source_target_pairs={{1,0},{5,4},{9,8},{13,12},{17,16},{21,20},{25,24},{29,28}} | collective-permute-start | bytes 3145736 | tf_op jit(solution)/shard_map/ppermute | solution.py:450
  172.4 20.6 %collective-permute-start.17 = (bf16[256,1024]{1,0:T(8,128)(2,1)S(1)}, bf16[256,1024]{1,0:T(8,128)(2,1)S(1)}, u32[]{:S(2)}, u32[]{:S(2)}) collective-permute-start(bf16[256,1024]{1,0:T(8,128)(2,1)S(1)} %get-tuple-element.105), channel_id=1, source_target_pairs={{0,4},{4,0},{8,12},{12,8},{1,5},{5,1},{9,13},{13,9},{2,6},{6,2},{1... | collective-permute-start | bytes 1572872 | tf_op jit(solution)/shard_map/ppermute | solution.py:446
  190.0 41.2 %collective-permute-start.14 = (bf16[256,2048]{1,0:T(8,128)(2,1)}, bf16[256,2048]{1,0:T(8,128)(2,1)S(1)}, u32[]{:S(2)}, u32[]{:S(2)}) collective-permute-start(bf16[256,2048]{1,0:T(8,128)(2,1)} %get-tuple-element.99), channel_id=1, source_target_pairs={{2,3},{6,7},{10,11},{14,15},{18,19},{22,23},{26,27},{30,31}} | collective-permute-start | bytes 3145736 | tf_op jit(solution)/shard_map/ppermute | solution.py:449
  190.7 40.5 %collective-permute-start.15 = (bf16[256,2048]{1,0:T(8,128)(2,1)}, bf16[256,2048]{1,0:T(8,128)(2,1)}, u32[]{:S(2)}, u32[]{:S(2)}) collective-permute-start(bf16[256,2048]{1,0:T(8,128)(2,1)} %get-tuple-element.100), channel_id=1, source_target_pairs={{1,0},{5,4},{9,8},{13,12},{17,16},{21,20},{25,24},{29,28}} | collective-permute-start | bytes 3145736 | tf_op jit(solution)/shard_map/ppermute | solution.py:450
  210.6 2.9 collective-permute-start.21
  210.6 5.3 %collective-permute-start.16 = (bf16[256,1024]{1,0:T(8,128)(2,1)}, bf16[256,1024]{1,0:T(8,128)(2,1)S(1)}, u32[]{:S(2)}, u32[]{:S(2)}) collective-permute-start(bf16[256,1024]{1,0:T(8,128)(2,1)} %get-tuple-element.103), channel_id=1, source_target_pairs={{0,4},{4,0},{8,12},{12,8},{1,5},{5,1},{9,13},{13,9},{2,6},{6,2},{1... | collective-permute-start | bytes 1572872 | tf_op jit(solution)/shard_map/ppermute | solution.py:446
  211.1 14.1 %collective-permute-start.18 = (bf16[256,1024]{1,0:T(8,128)(2,1)}, bf16[256,1024]{1,0:T(8,128)(2,1)}, u32[]{:S(2)}, u32[]{:S(2)}) collective-permute-start(bf16[256,1024]{1,0:T(8,128)(2,1)} %get-tuple-element.106), channel_id=1, source_target_pairs={{0,8},{4,12},{8,0},{12,4},{1,9},{5,13},{9,1},{13,5},{2,10},{6,14},... | collective-permute-start | bytes 1572872 | tf_op jit(solution)/shard_map/ppermute | solution.py:446
  229.1 14.9 %collective-permute-start.26 = (bf16[256,1024]{1,0:T(8,128)(2,1)S(1)}, bf16[256,1024]{1,0:T(8,128)(2,1)S(1)}, u32[]{:S(2)}, u32[]{:S(2)}) collective-permute-start(bf16[256,1024]{1,0:T(8,128)(2,1)S(1)} %get-tuple-element.122.refs_0_), channel_id=1, source_target_pairs={{0,8},{4,12},{8,0},{12,4},{1,9},{5,13},{9,1},{13,5},{2,10},{6,14},... | collective-permute-start | bytes 1572872 | tf_op jit(solution)/shard_map/ppermute | solution.py:446
  230.6 13.4 %collective-permute-start.24 = (bf16[256,1024]{1,0:T(8,128)(2,1)S(1)}, bf16[256,1024]{1,0:T(8,128)(2,1)S(1)}, u32[]{:S(2)}, u32[]{:S(2)}) collective-permute-start(bf16[256,1024]{1,0:T(8,128)(2,1)S(1)} %copy-done.14), channel_id=1, source_target_pairs={{0,4},{4,0},{8,12},{12,8},{1,5},{5,1},{9,13},{13,9},{2,6},{6,2},{1... | collective-permute-start | bytes 1572872 | tf_op jit(solution)/shard_map/ppermute | solution.py:446
  230.6 22.7 %collective-permute-start.25 = (bf16[256,1024]{1,0:T(8,128)(2,1)S(1)}, bf16[256,1024]{1,0:T(8,128)(2,1)S(1)}, u32[]{:S(2)}, u32[]{:S(2)}) collective-permute-start(bf16[256,1024]{1,0:T(8,128)(2,1)S(1)} %get-tuple-element.120), channel_id=1, source_target_pairs={{0,8},{4,12},{8,0},{12,4},{1,9},{5,13},{9,1},{13,5},{2,10},{6,14},... | collective-permute-start | bytes 1572872 | tf_op jit(solution)/shard_map/ppermute | solution.py:446
  231.2 22.2 %copy-start.7 = (f32[256,1024]{1,0:T(8,128)S(1)}, f32[256,1024]{1,0:T(8,128)}, u32[]{:S(2)}) copy-start(f32[256,1024]{1,0:T(8,128)} %copy-done.6) | copy-start | bytes 3145732
  243.5 11.4 %collective-permute-start.23 = (bf16[256,1024]{1,0:T(8,128)(2,1)S(1)}, bf16[256,1024]{1,0:T(8,128)(2,1)S(1)}, u32[]{:S(2)}, u32[]{:S(2)}) collective-permute-start(bf16[256,1024]{1,0:T(8,128)(2,1)S(1)} %get-tuple-element.117), channel_id=1, source_target_pairs={{0,4},{4,0},{8,12},{12,8},{1,5},{5,1},{9,13},{13,9},{2,6},{6,2},{1... | collective-permute-start | bytes 1572872 | tf_op jit(solution)/shard_map/ppermute | solution.py:446
  243.8 13.4 %collective-permute-start.22 = (bf16[256,1024]{1,0:T(8,128)(2,1)S(1)}, bf16[256,1024]{1,0:T(8,128)(2,1)S(1)}, u32[]{:S(2)}, u32[]{:S(2)}) collective-permute-start(bf16[256,1024]{1,0:T(8,128)(2,1)S(1)} %get-tuple-element.115), channel_id=1, source_target_pairs={{0,4},{4,0},{8,12},{12,8},{1,5},{5,1},{9,13},{13,9},{2,6},{6,2},{1... | collective-permute-start | bytes 1572872 | tf_op jit(solution)/shard_map/ppermute | solution.py:446
  255.1 14.9 %collective-permute-start.27 = (bf16[256,1024]{1,0:T(8,128)(2,1)S(1)}, bf16[256,1024]{1,0:T(8,128)(2,1)S(1)}, u32[]{:S(2)}, u32[]{:S(2)}) collective-permute-start(bf16[256,1024]{1,0:T(8,128)(2,1)S(1)} %get-tuple-element.126), channel_id=1, source_target_pairs={{0,8},{4,12},{8,0},{12,4},{1,9},{5,13},{9,1},{13,5},{2,10},{6,14},... | collective-permute-start | bytes 1572872 | tf_op jit(solution)/shard_map/ppermute | solution.py:446
  256.6 38.5 %collective-permute-start.44 = (bf16[256,1024]{1,0:T(8,128)(2,1)S(1)}, bf16[256,1024]{1,0:T(8,128)(2,1)S(1)}, u32[]{:S(2)}, u32[]{:S(2)}) collective-permute-start(bf16[256,1024]{1,0:T(8,128)(2,1)S(1)} %get-tuple-element.122.refs_0_), channel_id=1, source_target_pairs={{0,4},{4,0},{8,12},{12,8},{1,5},{5,1},{9,13},{13,9},{2,6},{6,2},{1... | collective-permute-start | bytes 1572872 | tf_op jit(solution)/shard_map/ppermute | solution.py:446
  256.6 40.0 %collective-permute-start.36 = (bf16[256,1024]{1,0:T(8,128)(2,1)S(1)}, bf16[256,1024]{1,0:T(8,128)(2,1)S(1)}, u32[]{:S(2)}, u32[]{:S(2)}) collective-permute-start(bf16[256,1024]{1,0:T(8,128)(2,1)S(1)} %get-tuple-element.133.refs_0_), channel_id=1, source_target_pairs={{0,8},{4,12},{8,0},{12,4},{1,9},{5,13},{9,1},{13,5},{2,10},{6,14},... | collective-permute-start | bytes 1572872 | tf_op jit(solution)/shard_map/ppermute | solution.py:446
  270.0 29.3 %copy-start.12 = (f32[4096]{0:T(1024)S(1)}, f32[4096]{0:T(1024)}, u32[]{:S(2)}) copy-start(f32[4096]{0:T(1024)} %param.19) | copy-start | bytes 49156
  271.5 25.1 %collective-permute-start.28 = (bf16[256,1024]{1,0:T(8,128)(2,1)S(1)}, bf16[256,1024]{1,0:T(8,128)(2,1)S(1)}, u32[]{:S(2)}, u32[]{:S(2)}) collective-permute-start(bf16[256,1024]{1,0:T(8,128)(2,1)S(1)} %get-tuple-element.130.refs_0_), channel_id=1, source_target_pairs={{0,8},{4,12},{8,0},{12,4},{1,9},{5,13},{9,1},{13,5},{2,10},{6,14},... | collective-permute-start | bytes 1572872 | tf_op jit(solution)/shard_map/ppermute | solution.py:446
  273.0 5.5 %collective-permute-start.39 = (f32[8,512]{1,0:T(8,128)S(1)}, f32[8,512]{1,0:T(8,128)S(1)}, u32[]{:S(2)}, u32[]{:S(2)}) collective-permute-start(f32[8,512]{1,0:T(8,128)S(1)} %constant_dynamic-update-slice_fusion), channel_id=1, source_target_pairs={{0,1},{1,2},{2,3},{3,0},{4,5},{5,6},{6,7},{7,4},{8,9},{9,10},{10,1... | collective-permute-start | bytes 49160 | tf_op jit(solution)/shard_map/ppermute | solution.py:496
  273.0 5.5 %collective-permute-start.40 = (f32[8,512]{1,0:T(8,128)S(1)}, f32[8,512]{1,0:T(8,128)S(1)}, u32[]{:S(2)}, u32[]{:S(2)}) collective-permute-start(f32[8,512]{1,0:T(8,128)S(1)} %constant_dynamic-update-slice_fusion), channel_id=1, source_target_pairs={{0,2},{1,3},{2,0},{3,1},{4,6},{5,7},{6,4},{7,5},{8,10},{9,11},{10,... | collective-permute-start | bytes 49160 | tf_op jit(solution)/shard_map/ppermute | solution.py:496
  278.6 3.7 %collective-permute-start.41 = (f32[8,512]{1,0:T(8,128)S(1)}, f32[8,512]{1,0:T(8,128)S(1)}, u32[]{:S(2)}, u32[]{:S(2)}) collective-permute-start(f32[8,512]{1,0:T(8,128)S(1)} %constant_dynamic-update-slice_fusion), channel_id=1, source_target_pairs={{0,3},{1,0},{2,1},{3,2},{4,7},{5,4},{6,5},{7,6},{8,11},{9,8},{10,9... | collective-permute-start | bytes 49160 | tf_op jit(solution)/shard_map/ppermute | solution.py:496
  282.3 7.7 %collective-permute-start.42 = (f32[8,512]{1,0:T(8,128)S(1)}, f32[8,512]{1,0:T(8,128)S(1)}, u32[]{:S(2)}, u32[]{:S(2)}) collective-permute-start(f32[8,512]{1,0:T(8,128)S(1)} %add_add_fusion), channel_id=1, source_target_pairs={{0,8},{4,12},{8,0},{12,4},{1,9},{5,13},{9,1},{13,5},{2,10},{6,14},... | collective-permute-start | bytes 49160 | tf_op jit(solution)/shard_map/ppermute | solution.py:446
  282.8 7.2 %collective-permute-start.29 = (f32[8,256]{1,0:T(8,128)S(1)}, f32[8,256]{1,0:T(8,128)S(1)}, u32[]{:S(2)}, u32[]{:S(2)}) collective-permute-start(f32[8,256]{1,0:T(8,128)S(1)} %get-tuple-element.131.refs_7_), channel_id=1, source_target_pairs={{0,1},{1,2},{2,3},{3,0},{4,5},{5,6},{6,7},{7,4},{8,9},{9,10},{10,1... | collective-permute-start | bytes 24584 | tf_op jit(solution)/shard_map/ppermute | solution.py:496
  290.0 4.5 %collective-permute-start.30 = (f32[8,256]{1,0:T(8,128)S(1)}, f32[8,256]{1,0:T(8,128)S(1)}, u32[]{:S(2)}, u32[]{:S(2)}) collective-permute-start(f32[8,256]{1,0:T(8,128)S(1)} %get-tuple-element.131.refs_7_), channel_id=1, source_target_pairs={{0,2},{1,3},{2,0},{3,1},{4,6},{5,7},{6,4},{7,5},{8,10},{9,11},{10,... | collective-permute-start | bytes 24584 | tf_op jit(solution)/shard_map/ppermute | solution.py:496
  290.0 4.5 %collective-permute-start.31 = (f32[8,256]{1,0:T(8,128)S(1)}, f32[8,256]{1,0:T(8,128)S(1)}, u32[]{:S(2)}, u32[]{:S(2)}) collective-permute-start(f32[8,256]{1,0:T(8,128)S(1)} %get-tuple-element.131.refs_7_), channel_id=1, source_target_pairs={{0,3},{1,0},{2,1},{3,2},{4,7},{5,4},{6,5},{7,6},{8,11},{9,8},{10,9... | collective-permute-start | bytes 24584 | tf_op jit(solution)/shard_map/ppermute | solution.py:496
  294.6 4.2 %collective-permute-start.45 = (bf16[256,1024]{1,0:T(8,128)(2,1)S(1)}, bf16[256,1024]{1,0:T(8,128)(2,1)S(1)}, u32[]{:S(2)}, u32[]{:S(2)}) collective-permute-start(bf16[256,1024]{1,0:T(8,128)(2,1)S(1)} %get-tuple-element.134.refs_1_), channel_id=1, source_target_pairs={{0,4},{4,0},{8,12},{12,8},{1,5},{5,1},{9,13},{13,9},{2,6},{6,2},{1... | collective-permute-start | bytes 1572872 | tf_op jit(solution)/shard_map/ppermute | solution.py:446
  294.6 3.2 %collective-permute-start.43 = (f32[8,512]{1,0:T(8,128)S(1)}, f32[8,512]{1,0:T(8,128)S(1)}, u32[]{:S(2)}, u32[]{:S(2)}) collective-permute-start(f32[8,512]{1,0:T(8,128)S(1)} %add.108.refs_4_), channel_id=1, source_target_pairs={{0,4},{4,0},{8,12},{12,8},{1,5},{5,1},{9,13},{13,9},{2,6},{6,2},{1... | collective-permute-start | bytes 49160 | tf_op jit(solution)/shard_map/ppermute | solution.py:446
  295.1 3.7 %collective-permute-start.34 = (f32[8,256]{1,0:T(8,128)S(1)}, f32[8,256]{1,0:T(8,128)S(1)}, u32[]{:S(2)}, u32[]{:S(2)}) collective-permute-start(f32[8,256]{1,0:T(8,128)S(1)} %add_add_fusion.1.refs_1_), channel_id=1, source_target_pairs={{0,8},{4,12},{8,0},{12,4},{1,9},{5,13},{9,1},{13,5},{2,10},{6,14},... | collective-permute-start | bytes 24584 | tf_op jit(solution)/shard_map/ppermute | solution.py:446
  296.6 4.8 %collective-permute-start.37 = (bf16[256,1024]{1,0:T(8,128)(2,1)S(1)}, bf16[256,1024]{1,0:T(8,128)(2,1)S(1)}, u32[]{:S(2)}, u32[]{:S(2)}) collective-permute-start(bf16[256,1024]{1,0:T(8,128)(2,1)S(1)} %get-tuple-element.133.refs_0_), channel_id=1, source_target_pairs={{0,4},{4,0},{8,12},{12,8},{1,5},{5,1},{9,13},{13,9},{2,6},{6,2},{1... | collective-permute-start | bytes 1572872 | tf_op jit(solution)/shard_map/ppermute | solution.py:446
  296.6 4.8 %collective-permute-start.38 = (bf16[256,1024]{1,0:T(8,128)(2,1)S(1)}, bf16[256,1024]{1,0:T(8,128)(2,1)S(1)}, u32[]{:S(2)}, u32[]{:S(2)}) collective-permute-start(bf16[256,1024]{1,0:T(8,128)(2,1)S(1)} %collective-permute-done.36.refs_1_), channel_id=1, source_target_pairs={{0,4},{4,0},{8,12},{12,8},{1,5},{5,1},{9,13},{13,9},{2,6},{6,2},{1... | collective-permute-start | bytes 1572872 | tf_op jit(solution)/shard_map/ppermute | solution.py:446
  297.7 5.8 %collective-permute-start.32 = (bf16[256,1024]{1,0:T(8,128)(2,1)S(1)}, bf16[256,1024]{1,0:T(8,128)(2,1)S(1)}, u32[]{:S(2)}, u32[]{:S(2)}) collective-permute-start(bf16[256,1024]{1,0:T(8,128)(2,1)S(1)} %get-tuple-element.130.refs_0_), channel_id=1, source_target_pairs={{0,4},{4,0},{8,12},{12,8},{1,5},{5,1},{9,13},{13,9},{2,6},{6,2},{1... | collective-permute-start | bytes 1572872 | tf_op jit(solution)/shard_map/ppermute | solution.py:446
  298.8 4.7 %collective-permute-start.33 = (bf16[256,1024]{1,0:T(8,128)(2,1)S(1)}, bf16[256,1024]{1,0:T(8,128)(2,1)S(1)}, u32[]{:S(2)}, u32[]{:S(2)}) collective-permute-start(bf16[256,1024]{1,0:T(8,128)(2,1)S(1)} %get-tuple-element.132.refs_1_), channel_id=1, source_target_pairs={{0,4},{4,0},{8,12},{12,8},{1,5},{5,1},{9,13},{13,9},{2,6},{6,2},{1... | collective-permute-start | bytes 1572872 | tf_op jit(solution)/shard_map/ppermute | solution.py:446
  298.8 4.7 %collective-permute-start.35 = (f32[8,256]{1,0:T(8,128)S(1)}, f32[8,256]{1,0:T(8,128)S(1)}, u32[]{:S(2)}, u32[]{:S(2)}) collective-permute-start(f32[8,256]{1,0:T(8,128)S(1)} %add.104.refs_4_), channel_id=1, source_target_pairs={{0,4},{4,0},{8,12},{12,8},{1,5},{5,1},{9,13},{13,9},{2,6},{6,2},{1... | collective-permute-start | bytes 24584 | tf_op jit(solution)/shard_map/ppermute | solution.py:446
  (16 other events, 114.5 us)

commit v4 on v3

--- a/solution.py
+++ b/solution.py
@@ -569,26 +569,24 @@
     begin_sums(0, sums)
     token = hold([(mid, 1)], [token])
     pass_on(1, sub - 1, sub - 1)
+    token = halve_sums(0, token)
     parts, *token = matmul([1, 2], middle, parts, 0, False, token)
-    hold([(mid, 2)], token)
+    token = hold([(mid, 2)], token)
     pass_on(2, sub - 1, sub - 1)
-    token = halve_sums(0, token)
+    token = finish(0, token)
     *sums, token = matmul([1], late, parts, 0, True, token)
     begin_sums(1, sums)
-    token = halve_sums(1, [token])
-    token = finish(0, token)
+    token = spread(0, [token])
+    token = halve_sums(1, token)
     *sums, token = matmul([2], late, parts, sizes[1], True, token)
     begin_sums(2, sums)
-    token = spread(0, [token])
-    token = finish(1, token)
+    token = finish(1, [token])
     token = halve_sums(2, token)
-    along = sum_along(jnp.concatenate([squares[0], squares[1]], axis=1))
     token = finish(2, token)
-    spread(1, [])
-    token = normalise([0, 1], sum_across(along), token)
-    along = sum_along(squares[2])
+    along = sum_along(jnp.concatenate([squares[u] for u in range(3)], axis=1))
+    spread(1, token)
     spread(2, [along])
-    normalise([2], sum_across(along), token)
+    normalise([0, 1, 2], sum_across(along), token)
     return (streams[0], normed[0])
 
 

time: 307 us -> 286 us (0.932)
  waiting for transfers between devices: 111 us -> 94.8 us
    ppermute x22 -> x20, waiting for transfers between devices: 38.8 us -> 24 us  [swap(): return lax.ppermute(value, 'tp', [(i, i ^ d) for i in range(tp)])]
    unnamed x37 -> x26, local copies, waits for them, and re-layouts: 6.83 us -> 4.06 us
    ppermute x6 -> x3, waiting for transfers between devices: 11.6 us -> 9.48 us  [sum_along(): lax.ppermute(local, 'sub', [(i, (i + d) % sub) for i in range(sub)])]
    ppermute x22 -> x20, starting transfers between devices: 11.9 us -> 10.6 us  [swap(): return lax.ppermute(value, 'tp', [(i, i ^ d) for i in range(tp)])]
  transfers between devices with their start and end apart: 46 -> 41, of which waited for: 16 -> 14; matrix products, arithmetic and copies ran while one was open for 2% -> 2% of each run, Pallas kernels for 42% -> 45%
where the time goes in v4:
time: 286 us; the launch traced here: 285 us
  Pallas kernels  130 us (45%)
  waiting for transfers between devices  94.8 us (33%)
  starting transfers between devices  44.7 us (16%)
  local copies, waits for them, and re-layouts  10.3 us (4%)
  other arithmetic  3.75 us (1%)
    pallas_call x6, Pallas kernels, matmul_stage(): pl.pallas_call(functools.partial(matmul_kernel, plan), grid_spec=pltpu.Pr...  109 us
    ppermute x9, waiting for transfers between devices, onward(): lax.ppermute(pair[1], 'sub', [(i, i - 1) for i in range(1, sub - d + 1)])  44.5 us
    ppermute x20, waiting for transfers between devices, swap(): return lax.ppermute(value, 'tp', [(i, i ^ d) for i in range(tp)])  24 us
    ppermute x9, starting transfers between devices, onward(): lax.ppermute(pair[0], 'sub', [(i, i + 1) for i in range(d - 1, sub - 1)])  22.3 us
    ppermute x9, waiting for transfers between devices, onward(): lax.ppermute(pair[0], 'sub', [(i, i + 1) for i in range(d - 1, sub - 1)])  16.8 us
    ppermute x9, starting transfers between devices, onward(): lax.ppermute(pair[1], 'sub', [(i, i - 1) for i in range(1, sub - d + 1)])  11.7 us
    ppermute x20, starting transfers between devices, swap(): return lax.ppermute(value, 'tp', [(i, i ^ d) for i in range(tp)])  10.6 us
    ppermute x3, waiting for transfers between devices, sum_along(): lax.ppermute(local, 'sub', [(i, (i + d) % sub) for i in range(sub)])  9.48 us
  transfers between devices with their start and end apart: 41, of which 14 were waited for; matrix products, arithmetic and copies ran while one was open for 2% of the time, Pallas kernels for 45%

profile of v4, /device:TPU:0, one launch (start us, length us, event | category | flops | bytes accessed | tf_op | source)
XLA Modules:
  0.0 285.1 jit_solution(927594479648287064)
XLA Ops:
  0.7 3.3 %fusion.4.refs_0_ = bf16[256,2048]{1,0:T(8,128)(2,1)} fusion(bf16[768,2048]{1,0:T(8,128)(2,1)} %up.3, bf16[768,2048]{1,0:T(8,128)(2,1)} %gate.13), kind=kLoop, calls=%fused_computation.7 | loop fusion | flops 4194304 | bytes 3145728 | tf_op jit(solution)/shard_map/convert_element_type | solution.py:554
  4.0 6.0 %collective-permute-start = (bf16[256,2048]{1,0:T(8,128)(2,1)}, bf16[256,2048]{1,0:T(8,128)(2,1)}, u32[]{:S(2)}, u32[]{:S(2)}) collective-permute-start(bf16[256,2048]{1,0:T(8,128)(2,1)} %fusion.4.refs_0_), channel_id=1, source_target_pairs={{0,1},{1,2},{2,3},{4,5},{5,6},{6,7},{8,9},{9,10},{10,11},{12,13},{... | collective-permute-start | bytes 3145736 | tf_op jit(solution)/shard_map/ppermute | solution.py:449
  10.0 1.3 collective-permute-start.1
  11.3 3.6 %hidden_rows.2 = (bf16[256,2048]{1,0:T(8,128)(2,1)}, f32[8,128]{1,0:T(8,128)S(1)}) custom-call(bf16[768,2048]{1,0:T(8,128)(2,1)S(1)} %copy-done.2, bf16[768,2048]{1,0:T(8,128)(2,1)} %up.3, bf16[256,2048]{1,0:T(8,128)(2,1)} %fusion.4.refs_0_), custom_call_target="tpu_custom_call" | custom-call | flops 1 | bytes 1 | tf_op jit(solution)/shard_map/hidden_rows/pallas_call | solution.py:67
  15.0 5.6 %collective-permute-start.6 = (bf16[256,2048]{1,0:T(8,128)(2,1)}, bf16[256,2048]{1,0:T(8,128)(2,1)}, u32[]{:S(2)}, u32[]{:S(2)}) collective-permute-start(bf16[256,2048]{1,0:T(8,128)(2,1)} %get-tuple-element.82.refs_0_), channel_id=1, source_target_pairs={{0,1},{1,2},{2,3},{4,5},{5,6},{6,7},{8,9},{9,10},{10,11},{12,13},{... | collective-permute-start | bytes 3145736 | tf_op jit(solution)/shard_map/ppermute | solution.py:449
  20.5 1.3 collective-permute-start.7
  21.9 2.8 gather_fusion
  24.7 8.2 %collective-permute-done.refs_0_ = bf16[256,2048]{1,0:T(8,128)(2,1)} collective-permute-done((bf16[256,2048]{1,0:T(8,128)(2,1)}, bf16[256,2048]{1,0:T(8,128)(2,1)}, u32[]{:S(2)}, u32[]{:S(2)}) %collective-permute-start) | collective-permute-done | bytes 1048608 | tf_op jit(solution)/shard_map/ppermute | solution.py:449
  32.9 5.4 %collective-permute-done.1.refs_1_ = bf16[256,2048]{1,0:T(8,128)(2,1)} collective-permute-done((bf16[256,2048]{1,0:T(8,128)(2,1)}, bf16[256,2048]{1,0:T(8,128)(2,1)}, u32[]{:S(2)}, u32[]{:S(2)}) %collective-permute-start.1) | collective-permute-done | bytes 1048608 | tf_op jit(solution)/shard_map/ppermute | solution.py:450
  38.3 3.0 %hidden_rows.3 = (bf16[256,2048]{1,0:T(8,128)(2,1)}, f32[8,128]{1,0:T(8,128)S(1)}) custom-call(bf16[768,2048]{1,0:T(8,128)(2,1)S(1)} %copy-done.3, bf16[768,2048]{1,0:T(8,128)(2,1)} %up.3, f32[8,128]{1,0:T(8,128)S(1)} %get-tuple-element.76.refs_0_), custom_call_target="tpu_custom_call" | custom-call | flops 1 | bytes 1 | tf_op jit(solution)/shard_map/hidden_rows/pallas_call | solution.py:67
  41.3 2.6 collective-permute-start.4
  43.9 1.3 collective-permute-start.5
  45.2 1.7 collective-permute-start.2
  46.8 8.5 %collective-permute-done.6.refs_0_ = bf16[256,2048]{1,0:T(8,128)(2,1)} collective-permute-done((bf16[256,2048]{1,0:T(8,128)(2,1)}, bf16[256,2048]{1,0:T(8,128)(2,1)}, u32[]{:S(2)}, u32[]{:S(2)}) %collective-permute-start.6) | collective-permute-done | bytes 1048608 | tf_op jit(solution)/shard_map/ppermute | solution.py:449
  55.4 1.3 collective-permute-start.3
  57.5 19.8 %matmul_stage.6 = (f32[4,256,1024]{2,1,0:T(8,128)}, f32[8,128]{1,0:T(8,128)S(1)}) custom-call(s32[8]{0:T(128)S(1)} %pad_add_fusion.1.info, bf16[256,2048]{1,0:T(8,128)(2,1)} %fusion.4.refs_0_, bf16[256,2048]{1,0:T(8,128)(2,1)} %get-tuple-element.74.refs_1_, bf16[256,2048]{1,0:T(8,128)(2,1)} %get-tuple-element.75.refs_2_, bf16[8192,4096]{1,0:T(8,128)(2,1)} %refs_2_.3, ...), custom_call_target="tpu_custom_call" | custom-call | flops 1 | bytes 1 | tf_op jit(solution)/shard_map/matmul_stage/pallas_call | solution.py:238
  77.9 1.7 collective-permute-start.8
  79.5 1.3 collective-permute-start.9
  80.8 2.5 collective-permute-done.5.refs_3_
  83.3 22.5 %collective-permute-done.3.refs_1_ = bf16[256,2048]{1,0:T(8,128)(2,1)} collective-permute-done((bf16[256,2048]{1,0:T(8,128)(2,1)}, bf16[256,2048]{1,0:T(8,128)(2,1)}, u32[]{:S(2)}, u32[]{:S(2)}) %collective-permute-start.3) | collective-permute-done | bytes 1048608 | tf_op jit(solution)/shard_map/ppermute | solution.py:450
  106.5 1.3 collective-permute-start.13
  107.8 27.0 %matmul_stage.7 = (f32[4,512,1024]{2,1,0:T(8,128)}, f32[8,128]{1,0:T(8,128)S(1)}) custom-call(s32[8]{0:T(128)S(1)} %pad_add_fusion.1.info, bf16[256,2048]{1,0:T(8,128)(2,1)} %get-tuple-element.82.refs_0_, bf16[256,2048]{1,0:T(8,128)(2,1)} %get-tuple-element.77.refs_1_, bf16[256,2048]{1,0:T(8,128)(2,1)} %get-tuple-element.83.refs_2_, ...), custom_call_target="tpu_custom_call" | custom-call | flops 1 | bytes 1 | tf_op jit(solution)/shard_map/matmul_stage/pallas_call | solution.py:238
  134.8 1.7 collective-permute-start.10
  137.3 1.3 collective-permute-start.11
  138.6 10.5 %collective-permute-done.13.refs_3_ = bf16[256,2048]{1,0:T(8,128)(2,1)S(1)} collective-permute-done((bf16[256,2048]{1,0:T(8,128)(2,1)}, bf16[256,2048]{1,0:T(8,128)(2,1)S(1)}, u32[]{:S(2)}, u32[]{:S(2)}) %collective-permute-start.13) | collective-permute-done | bytes 1048608 | tf_op jit(solution)/shard_map/ppermute | solution.py:450
  150.1 18.7 %matmul_stage.8 = (f32[256,1024]{1,0:T(8,128)S(1)}, f32[256,1024]{1,0:T(8,128)S(1)}, bf16[256,1024]{1,0:T(8,128)(2,1)S(1)}, bf16[256,1024]{1,0:T(8,128)(2,1)S(1)}, f32[8,128]{1,0:T(8,128)S(1)}) custom-call(s32[6]{0:T(128)S(1)} %pad_add_fusion.3.info, bf16[256,2048]{1,0:T(8,128)(2,1)} %get-tuple-element.91.refs_0_, ...), custom_call_target="tpu_custom_call" | custom-call | flops 1 | bytes 1 | tf_op jit(solution)/shard_map/matmul_stage/pallas_call | solution.py:238
  168.9 1.7 collective-permute-start.17
  170.6 1.3 collective-permute-start.18
  174.0 1.5 collective-permute-start.20
  175.5 18.7 %matmul_stage.9 = (f32[4,512,1024]{2,1,0:T(8,128)}, f32[8,128]{1,0:T(8,128)S(1)}) custom-call(s32[4]{0:T(128)S(1)} %pad_add_fusion.2.info, bf16[256,2048]{1,0:T(8,128)(2,1)} %get-tuple-element.96.refs_0_, bf16[256,2048]{1,0:T(8,128)(2,1)} %collective-permute-done.10.refs_1_.refs_0_, bf16[256,2048]{1,0:T(8,128)(2,1)} %get-tuple-element.97.refs_2_, ...), custom_call_target="tpu_custom_call" | custom-call | flops 1 | bytes 1 | tf_op jit(solution)/shard_map/matmul_stage/pallas_call | solution.py:238
  195.8 1.5 collective-permute-start.16
  201.1 2.8 stream_rows.3
  204.5 12.3 %matmul_stage.10 = (f32[256,1024]{1,0:T(8,128)S(1)}, f32[256,1024]{1,0:T(8,128)S(1)}, bf16[256,1024]{1,0:T(8,128)(2,1)S(1)}, bf16[256,1024]{1,0:T(8,128)(2,1)S(1)}, f32[8,128]{1,0:T(8,128)S(1)}) custom-call(s32[4]{0:T(128)S(1)} %pad_add_fusion.info, bf16[256,2048]{1,0:T(8,128)(2,1)} %collective-permute-done.17.refs_0_, ...), custom_call_target="tpu_custom_call" | custom-call | flops 1 | bytes 1 | tf_op jit(solution)/shard_map/matmul_stage/pallas_call | solution.py:238
  218.9 1.6 collective-permute-start.26
  220.5 3.6 %collective-permute-done.16.refs_1_ = bf16[256,2048]{1,0:T(8,128)(2,1)} collective-permute-done((bf16[256,2048]{1,0:T(8,128)(2,1)}, bf16[256,2048]{1,0:T(8,128)(2,1)}, u32[]{:S(2)}, u32[]{:S(2)}) %collective-permute-start.16) | collective-permute-done | bytes 1048608 | tf_op jit(solution)/shard_map/ppermute | solution.py:450
  224.1 12.3 %matmul_stage.11 = (f32[256,1024]{1,0:T(8,128)S(1)}, f32[256,1024]{1,0:T(8,128)S(1)}, bf16[256,1024]{1,0:T(8,128)(2,1)S(1)}, bf16[256,1024]{1,0:T(8,128)(2,1)S(1)}, f32[8,128]{1,0:T(8,128)S(1)}) custom-call(s32[4]{0:T(128)S(1)} %pad_add_fusion.info, bf16[256,2048]{1,0:T(8,128)(2,1)S(1)} %collective-permute-done.15.refs_0_, ...), custom_call_target="tpu_custom_call" | custom-call | flops 1 | bytes 1 | tf_op jit(solution)/shard_map/matmul_stage/pallas_call | solution.py:238
  236.9 1.5 stream_rows.4
  239.2 1.5 collective-permute-start.36
  240.7 12.7 %collective-permute-done.27.last = bf16[256,1024]{1,0:T(8,128)(2,1)S(1)} collective-permute-done((bf16[256,1024]{1,0:T(8,128)(2,1)S(1)}, bf16[256,1024]{1,0:T(8,128)(2,1)S(1)}, u32[]{:S(2)}, u32[]{:S(2)}) %collective-permute-start.27) | collective-permute-done | bytes 524320 | tf_op jit(solution)/shard_map/ppermute | solution.py:446
  253.5 1.5 stream_rows.5
  255.6 5.7 %collective-permute-done.29 = f32[8,768]{1,0:T(8,128)S(1)} collective-permute-done((f32[8,768]{1,0:T(8,128)S(1)}, f32[8,768]{1,0:T(8,128)S(1)}, u32[]{:S(2)}, u32[]{:S(2)}) %collective-permute-start.29) | collective-permute-done | bytes 24608 | tf_op jit(solution)/shard_map/ppermute | solution.py:496
  261.3 3.8 %collective-permute-done.31 = f32[8,768]{1,0:T(8,128)S(1)} collective-permute-done((f32[8,768]{1,0:T(8,128)S(1)}, f32[8,768]{1,0:T(8,128)S(1)}, u32[]{:S(2)}, u32[]{:S(2)}) %collective-permute-start.31) | collective-permute-done | bytes 24608 | tf_op jit(solution)/shard_map/ppermute | solution.py:496
  265.1 1.6 collective-permute-start.34
  267.2 8.1 %collective-permute-done.28.refs_0_ = bf16[256,1024]{1,0:T(8,128)(2,1)S(1)} collective-permute-done((bf16[256,1024]{1,0:T(8,128)(2,1)S(1)}, bf16[256,1024]{1,0:T(8,128)(2,1)S(1)}, u32[]{:S(2)}, u32[]{:S(2)}) %collective-permute-start.28) | collective-permute-done | bytes 524320 | tf_op jit(solution)/shard_map/ppermute | solution.py:446
  277.0 1.7 collective-permute-done.35.refs_5_
  278.8 2.1 norm_rows.3
  280.9 2.1 norm_rows.4
  283.0 2.1 norm_rows.5
  (102 shorter events, 18.3 us)
Async XLA Ops:
  0.6 21.2 %copy-start = (bf16[768,1024]{1,0:T(8,128)(2,1)S(1)}, bf16[768,1024]{1,0:T(8,128)(2,1)}, u32[]{:S(2)}) copy-start(bf16[768,1024]{1,0:T(8,128)(2,1)} %param.16) | copy-start | bytes 4718596
  0.6 10.7 %copy-start.2 = (bf16[768,2048]{1,0:T(8,128)(2,1)S(1)}, bf16[768,2048]{1,0:T(8,128)(2,1)}, u32[]{:S(2)}) copy-start(bf16[768,2048]{1,0:T(8,128)(2,1)} %gate.13) | copy-start | bytes 9437188
  4.0 17.8 %copy-start.11 = (s32[768]{0:T(1024)S(1)}, s32[768]{0:T(1024)}, u32[]{:S(2)}) copy-start(s32[768]{0:T(1024)} %param.18) | copy-start | bytes 9220
  4.0 28.9 %collective-permute-start = (bf16[256,2048]{1,0:T(8,128)(2,1)}, bf16[256,2048]{1,0:T(8,128)(2,1)}, u32[]{:S(2)}, u32[]{:S(2)}) collective-permute-start(bf16[256,2048]{1,0:T(8,128)(2,1)} %fusion.4.refs_0_), channel_id=1, source_target_pairs={{0,1},{1,2},{2,3},{4,5},{5,6},{6,7},{8,9},{9,10},{10,11},{12,13},{... | collective-permute-start | bytes 3145736 | tf_op jit(solution)/shard_map/ppermute | solution.py:449
  10.0 28.3 %collective-permute-start.1 = (bf16[256,2048]{1,0:T(8,128)(2,1)}, bf16[256,2048]{1,0:T(8,128)(2,1)}, u32[]{:S(2)}, u32[]{:S(2)}) collective-permute-start(bf16[256,2048]{1,0:T(8,128)(2,1)} %fusion.4.refs_0_), channel_id=1, source_target_pairs={{1,0},{2,1},{3,2},{5,4},{6,5},{7,6},{9,8},{10,9},{11,10},{13,12},{... | collective-permute-start | bytes 3145736 | tf_op jit(solution)/shard_map/ppermute | solution.py:450
  15.0 40.4 %collective-permute-start.6 = (bf16[256,2048]{1,0:T(8,128)(2,1)}, bf16[256,2048]{1,0:T(8,128)(2,1)}, u32[]{:S(2)}, u32[]{:S(2)}) collective-permute-start(bf16[256,2048]{1,0:T(8,128)(2,1)} %get-tuple-element.82.refs_0_), channel_id=1, source_target_pairs={{0,1},{1,2},{2,3},{4,5},{5,6},{6,7},{8,9},{9,10},{10,11},{12,13},{... | collective-permute-start | bytes 3145736 | tf_op jit(solution)/shard_map/ppermute | solution.py:449
  20.5 56.7 %collective-permute-start.7 = (bf16[256,2048]{1,0:T(8,128)(2,1)}, bf16[256,2048]{1,0:T(8,128)(2,1)}, u32[]{:S(2)}, u32[]{:S(2)}) collective-permute-start(bf16[256,2048]{1,0:T(8,128)(2,1)} %get-tuple-element.82.refs_0_), channel_id=1, source_target_pairs={{1,0},{2,1},{3,2},{5,4},{6,5},{7,6},{9,8},{10,9},{11,10},{13,12},{... | collective-permute-start | bytes 3145736 | tf_op jit(solution)/shard_map/ppermute | solution.py:450
  24.7 13.7 %copy-start.3 = (bf16[768,2048]{1,0:T(8,128)(2,1)S(1)}, bf16[768,2048]{1,0:T(8,128)(2,1)}, u32[]{:S(2)}) copy-start(bf16[768,2048]{1,0:T(8,128)(2,1)} %gate.13) | copy-start | bytes 9437188
  41.3 38.2 %collective-permute-start.4 = (bf16[256,2048]{1,0:T(8,128)(2,1)}, bf16[256,2048]{1,0:T(8,128)(2,1)S(1)}, u32[]{:S(2)}, u32[]{:S(2)}) collective-permute-start(bf16[256,2048]{1,0:T(8,128)(2,1)} %get-tuple-element.77.refs_1_), channel_id=1, source_target_pairs={{0,1},{1,2},{2,3},{4,5},{5,6},{6,7},{8,9},{9,10},{10,11},{12,13},{... | collective-permute-start | bytes 3145736 | tf_op jit(solution)/shard_map/ppermute | solution.py:449
  43.9 39.4 %collective-permute-start.5 = (bf16[256,2048]{1,0:T(8,128)(2,1)}, bf16[256,2048]{1,0:T(8,128)(2,1)}, u32[]{:S(2)}, u32[]{:S(2)}) collective-permute-start(bf16[256,2048]{1,0:T(8,128)(2,1)} %get-tuple-element.77.refs_1_), channel_id=1, source_target_pairs={{1,0},{2,1},{3,2},{5,4},{6,5},{7,6},{9,8},{10,9},{11,10},{13,12},{... | collective-permute-start | bytes 3145736 | tf_op jit(solution)/shard_map/ppermute | solution.py:450
  45.2 38.1 %collective-permute-start.2 = (bf16[256,2048]{1,0:T(8,128)(2,1)}, bf16[256,2048]{1,0:T(8,128)(2,1)}, u32[]{:S(2)}, u32[]{:S(2)}) collective-permute-start(bf16[256,2048]{1,0:T(8,128)(2,1)} %get-tuple-element.74.refs_1_), channel_id=1, source_target_pairs={{1,2},{2,3},{5,6},{6,7},{9,10},{10,11},{13,14},{14,15},{17,18},{18... | collective-permute-start | bytes 3145736 | tf_op jit(solution)/shard_map/ppermute | solution.py:449
  55.4 50.3 %collective-permute-start.3 = (bf16[256,2048]{1,0:T(8,128)(2,1)}, bf16[256,2048]{1,0:T(8,128)(2,1)}, u32[]{:S(2)}, u32[]{:S(2)}) collective-permute-start(bf16[256,2048]{1,0:T(8,128)(2,1)} %get-tuple-element.75.refs_2_), channel_id=1, source_target_pairs={{1,0},{2,1},{5,4},{6,5},{9,8},{10,9},{13,12},{14,13},{17,16},{18,1... | collective-permute-start | bytes 3145736 | tf_op jit(solution)/shard_map/ppermute | solution.py:450
  77.9 57.0 %collective-permute-start.8 = (bf16[256,2048]{1,0:T(8,128)(2,1)}, bf16[256,2048]{1,0:T(8,128)(2,1)}, u32[]{:S(2)}, u32[]{:S(2)}) collective-permute-start(bf16[256,2048]{1,0:T(8,128)(2,1)} %get-tuple-element.83.refs_2_), channel_id=1, source_target_pairs={{1,2},{2,3},{5,6},{6,7},{9,10},{10,11},{13,14},{14,15},{17,18},{18... | collective-permute-start | bytes 3145736 | tf_op jit(solution)/shard_map/ppermute | solution.py:449
  79.5 55.3 %collective-permute-start.9 = (bf16[256,2048]{1,0:T(8,128)(2,1)}, bf16[256,2048]{1,0:T(8,128)(2,1)}, u32[]{:S(2)}, u32[]{:S(2)}) collective-permute-start(bf16[256,2048]{1,0:T(8,128)(2,1)} %get-tuple-element.84.refs_4_), channel_id=1, source_target_pairs={{1,0},{2,1},{5,4},{6,5},{9,8},{10,9},{13,12},{14,13},{17,16},{18,1... | collective-permute-start | bytes 3145736 | tf_op jit(solution)/shard_map/ppermute | solution.py:450
  105.7 32.8 %collective-permute-start.12 = (bf16[256,2048]{1,0:T(8,128)(2,1)}, bf16[256,2048]{1,0:T(8,128)(2,1)S(1)}, u32[]{:S(2)}, u32[]{:S(2)}) collective-permute-start(bf16[256,2048]{1,0:T(8,128)(2,1)} %get-tuple-element.91.refs_0_), channel_id=1, source_target_pairs={{2,3},{6,7},{10,11},{14,15},{18,19},{22,23},{26,27},{30,31}} | collective-permute-start | bytes 3145736 | tf_op jit(solution)/shard_map/ppermute | solution.py:449
  106.5 42.6 %collective-permute-start.13 = (bf16[256,2048]{1,0:T(8,128)(2,1)}, bf16[256,2048]{1,0:T(8,128)(2,1)S(1)}, u32[]{:S(2)}, u32[]{:S(2)}) collective-permute-start(bf16[256,2048]{1,0:T(8,128)(2,1)} %get-tuple-element.92.refs_1_), channel_id=1, source_target_pairs={{1,0},{5,4},{9,8},{13,12},{17,16},{21,20},{25,24},{29,28}} | collective-permute-start | bytes 3145736 | tf_op jit(solution)/shard_map/ppermute | solution.py:450
  134.8 39.1 %collective-permute-start.10 = (bf16[256,2048]{1,0:T(8,128)(2,1)S(1)}, bf16[256,2048]{1,0:T(8,128)(2,1)}, u32[]{:S(2)}, u32[]{:S(2)}) collective-permute-start(bf16[256,2048]{1,0:T(8,128)(2,1)S(1)} %get-tuple-element.87), channel_id=1, source_target_pairs={{1,2},{2,3},{5,6},{6,7},{9,10},{10,11},{13,14},{14,15},{17,18},{18... | collective-permute-start | bytes 3145736 | tf_op jit(solution)/shard_map/ppermute | solution.py:449
  137.3 38.3 %collective-permute-start.11 = (bf16[256,2048]{1,0:T(8,128)(2,1)}, bf16[256,2048]{1,0:T(8,128)(2,1)}, u32[]{:S(2)}, u32[]{:S(2)}) collective-permute-start(bf16[256,2048]{1,0:T(8,128)(2,1)} %get-tuple-element.88), channel_id=1, source_target_pairs={{1,0},{2,1},{5,4},{6,5},{9,8},{10,9},{13,12},{14,13},{17,16},{18,1... | collective-permute-start | bytes 3145736 | tf_op jit(solution)/shard_map/ppermute | solution.py:450
  138.6 10.5 %copy-start.9 = (bf16[256,2048]{1,0:T(8,128)(2,1)}, bf16[256,2048]{1,0:T(8,128)(2,1)S(1)}, u32[]{:S(2)}) copy-start(bf16[256,2048]{1,0:T(8,128)(2,1)S(1)} %collective-permute-done.12.refs_2_) | copy-start | bytes 3145732
  168.8 5.2 %copy-start.4 = (f32[256,1024]{1,0:T(8,128)}, f32[256,1024]{1,0:T(8,128)S(1)}, u32[]{:S(2)}) copy-start(f32[256,1024]{1,0:T(8,128)S(1)} %get-tuple-element.107.keep) | copy-start | bytes 3145732
  168.8 3.1 %collective-permute-start.14 = (bf16[256,1024]{1,0:T(8,128)(2,1)S(1)}, bf16[256,1024]{1,0:T(8,128)(2,1)S(1)}, u32[]{:S(2)}, u32[]{:S(2)}) collective-permute-start(bf16[256,1024]{1,0:T(8,128)(2,1)S(1)} %get-tuple-element.100), channel_id=1, source_target_pairs={{0,4},{4,0},{8,12},{12,8},{1,5},{5,1},{9,13},{13,9},{2,6},{6,2},{1... | collective-permute-start | bytes 1572872 | tf_op jit(solution)/shard_map/ppermute | solution.py:446
  168.9 35.6 %collective-permute-start.17 = (bf16[256,2048]{1,0:T(8,128)(2,1)}, bf16[256,2048]{1,0:T(8,128)(2,1)}, u32[]{:S(2)}, u32[]{:S(2)}) collective-permute-start(bf16[256,2048]{1,0:T(8,128)(2,1)} %get-tuple-element.96.refs_0_), channel_id=1, source_target_pairs={{2,3},{6,7},{10,11},{14,15},{18,19},{22,23},{26,27},{30,31}} | collective-permute-start | bytes 3145736 | tf_op jit(solution)/shard_map/ppermute | solution.py:449
  170.6 33.9 %collective-permute-start.18 = (bf16[256,2048]{1,0:T(8,128)(2,1)}, bf16[256,2048]{1,0:T(8,128)(2,1)}, u32[]{:S(2)}, u32[]{:S(2)}) collective-permute-start(bf16[256,2048]{1,0:T(8,128)(2,1)} %get-tuple-element.97.refs_2_), channel_id=1, source_target_pairs={{1,0},{5,4},{9,8},{13,12},{17,16},{21,20},{25,24},{29,28}} | collective-permute-start | bytes 3145736 | tf_op jit(solution)/shard_map/ppermute | solution.py:450
  171.9 23.2 %collective-permute-start.19 = (bf16[256,1024]{1,0:T(8,128)(2,1)S(1)}, bf16[256,1024]{1,0:T(8,128)(2,1)S(1)}, u32[]{:S(2)}, u32[]{:S(2)}) collective-permute-start(bf16[256,1024]{1,0:T(8,128)(2,1)S(1)} %get-tuple-element.108), channel_id=1, source_target_pairs={{0,4},{4,0},{8,12},{12,8},{1,5},{5,1},{9,13},{13,9},{2,6},{6,2},{1... | collective-permute-start | bytes 1572872 | tf_op jit(solution)/shard_map/ppermute | solution.py:446
  174.0 24.9 %collective-permute-start.20 = (bf16[256,1024]{1,0:T(8,128)(2,1)}, bf16[256,1024]{1,0:T(8,128)(2,1)}, u32[]{:S(2)}, u32[]{:S(2)}) collective-permute-start(bf16[256,1024]{1,0:T(8,128)(2,1)} %get-tuple-element.109), channel_id=1, source_target_pairs={{0,8},{4,12},{8,0},{12,4},{1,9},{5,13},{9,1},{13,5},{2,10},{6,14},... | collective-permute-start | bytes 1572872 | tf_op jit(solution)/shard_map/ppermute | solution.py:446
  194.3 26.2 %collective-permute-start.15 = (bf16[256,2048]{1,0:T(8,128)(2,1)}, bf16[256,2048]{1,0:T(8,128)(2,1)S(1)}, u32[]{:S(2)}, u32[]{:S(2)}) collective-permute-start(bf16[256,2048]{1,0:T(8,128)(2,1)} %get-tuple-element.104), channel_id=1, source_target_pairs={{2,3},{6,7},{10,11},{14,15},{18,19},{22,23},{26,27},{30,31}} | collective-permute-start | bytes 3145736 | tf_op jit(solution)/shard_map/ppermute | solution.py:449
  195.8 28.2 %collective-permute-start.16 = (bf16[256,2048]{1,0:T(8,128)(2,1)}, bf16[256,2048]{1,0:T(8,128)(2,1)}, u32[]{:S(2)}, u32[]{:S(2)}) collective-permute-start(bf16[256,2048]{1,0:T(8,128)(2,1)} %get-tuple-element.105), channel_id=1, source_target_pairs={{1,0},{5,4},{9,8},{13,12},{17,16},{21,20},{25,24},{29,28}} | collective-permute-start | bytes 3145736 | tf_op jit(solution)/shard_map/ppermute | solution.py:450
  204.0 13.6 %collective-permute-start.22 = (bf16[256,1024]{1,0:T(8,128)(2,1)S(1)}, bf16[256,1024]{1,0:T(8,128)(2,1)S(1)}, u32[]{:S(2)}, u32[]{:S(2)}) collective-permute-start(bf16[256,1024]{1,0:T(8,128)(2,1)S(1)} %get-tuple-element.115.refs_0_), channel_id=1, source_target_pairs={{0,8},{4,12},{8,0},{12,4},{1,9},{5,13},{9,1},{13,5},{2,10},{6,14},... | collective-permute-start | bytes 1572872 | tf_op jit(solution)/shard_map/ppermute | solution.py:446
  216.8 2.0 collective-permute-start.21
  216.9 20.1 %collective-permute-start.25 = (bf16[256,1024]{1,0:T(8,128)(2,1)S(1)}, bf16[256,1024]{1,0:T(8,128)(2,1)S(1)}, u32[]{:S(2)}, u32[]{:S(2)}) collective-permute-start(bf16[256,1024]{1,0:T(8,128)(2,1)S(1)} %get-tuple-element.124), channel_id=1, source_target_pairs={{0,4},{4,0},{8,12},{12,8},{1,5},{5,1},{9,13},{13,9},{2,6},{6,2},{1... | collective-permute-start | bytes 1572872 | tf_op jit(solution)/shard_map/ppermute | solution.py:446
  218.9 18.1 %collective-permute-start.26 = (bf16[256,1024]{1,0:T(8,128)(2,1)S(1)}, bf16[256,1024]{1,0:T(8,128)(2,1)S(1)}, u32[]{:S(2)}, u32[]{:S(2)}) collective-permute-start(bf16[256,1024]{1,0:T(8,128)(2,1)S(1)} %get-tuple-element.125), channel_id=1, source_target_pairs={{0,8},{4,12},{8,0},{12,4},{1,9},{5,13},{9,1},{13,5},{2,10},{6,14},... | collective-permute-start | bytes 1572872 | tf_op jit(solution)/shard_map/ppermute | solution.py:446
  236.4 2.1 collective-permute-start.24
  236.4 4.3 %collective-permute-start.23 = (bf16[256,1024]{1,0:T(8,128)(2,1)S(1)}, bf16[256,1024]{1,0:T(8,128)(2,1)S(1)}, u32[]{:S(2)}, u32[]{:S(2)}) collective-permute-start(bf16[256,1024]{1,0:T(8,128)(2,1)S(1)} %get-tuple-element.120), channel_id=1, source_target_pairs={{0,4},{4,0},{8,12},{12,8},{1,5},{5,1},{9,13},{13,9},{2,6},{6,2},{1... | collective-permute-start | bytes 1572872 | tf_op jit(solution)/shard_map/ppermute | solution.py:446
  238.6 14.8 %collective-permute-start.27 = (bf16[256,1024]{1,0:T(8,128)(2,1)S(1)}, bf16[256,1024]{1,0:T(8,128)(2,1)S(1)}, u32[]{:S(2)}, u32[]{:S(2)}) collective-permute-start(bf16[256,1024]{1,0:T(8,128)(2,1)S(1)} %get-tuple-element.129), channel_id=1, source_target_pairs={{0,8},{4,12},{8,0},{12,4},{1,9},{5,13},{9,1},{13,5},{2,10},{6,14},... | collective-permute-start | bytes 1572872 | tf_op jit(solution)/shard_map/ppermute | solution.py:446
  239.2 36.7 %collective-permute-start.39 = (bf16[256,1024]{1,0:T(8,128)(2,1)S(1)}, bf16[256,1024]{1,0:T(8,128)(2,1)S(1)}, u32[]{:S(2)}, u32[]{:S(2)}) collective-permute-start(bf16[256,1024]{1,0:T(8,128)(2,1)S(1)} %get-tuple-element.115.refs_0_), channel_id=1, source_target_pairs={{0,4},{4,0},{8,12},{12,8},{1,5},{5,1},{9,13},{13,9},{2,6},{6,2},{1... | collective-permute-start | bytes 1572872 | tf_op jit(solution)/shard_map/ppermute | solution.py:446
  239.2 27.4 %collective-permute-start.36 = (bf16[256,1024]{1,0:T(8,128)(2,1)S(1)}, bf16[256,1024]{1,0:T(8,128)(2,1)S(1)}, u32[]{:S(2)}, u32[]{:S(2)}) collective-permute-start(bf16[256,1024]{1,0:T(8,128)(2,1)S(1)} %get-tuple-element.136.refs_0_), channel_id=1, source_target_pairs={{0,8},{4,12},{8,0},{12,4},{1,9},{5,13},{9,1},{13,5},{2,10},{6,14},... | collective-permute-start | bytes 1572872 | tf_op jit(solution)/shard_map/ppermute | solution.py:446
  253.5 25.3 %copy-start.8 = (f32[4096]{0:T(1024)S(1)}, f32[4096]{0:T(1024)}, u32[]{:S(2)}) copy-start(f32[4096]{0:T(1024)} %param.19) | copy-start | bytes 49156
  255.0 20.3 %collective-permute-start.28 = (bf16[256,1024]{1,0:T(8,128)(2,1)S(1)}, bf16[256,1024]{1,0:T(8,128)(2,1)S(1)}, u32[]{:S(2)}, u32[]{:S(2)}) collective-permute-start(bf16[256,1024]{1,0:T(8,128)(2,1)S(1)} %get-tuple-element.133.refs_0_), channel_id=1, source_target_pairs={{0,8},{4,12},{8,0},{12,4},{1,9},{5,13},{9,1},{13,5},{2,10},{6,14},... | collective-permute-start | bytes 1572872 | tf_op jit(solution)/shard_map/ppermute | solution.py:446
  255.6 5.7 %collective-permute-start.29 = (f32[8,768]{1,0:T(8,128)S(1)}, f32[8,768]{1,0:T(8,128)S(1)}, u32[]{:S(2)}, u32[]{:S(2)}) collective-permute-start(f32[8,768]{1,0:T(8,128)S(1)} %constant_dynamic-update-slice_fusion), channel_id=1, source_target_pairs={{0,1},{1,2},{2,3},{3,0},{4,5},{5,6},{6,7},{7,4},{8,9},{9,10},{10,1... | collective-permute-start | bytes 73736 | tf_op jit(solution)/shard_map/ppermute | solution.py:496
  255.6 5.7 %collective-permute-start.30 = (f32[8,768]{1,0:T(8,128)S(1)}, f32[8,768]{1,0:T(8,128)S(1)}, u32[]{:S(2)}, u32[]{:S(2)}) collective-permute-start(f32[8,768]{1,0:T(8,128)S(1)} %constant_dynamic-update-slice_fusion), channel_id=1, source_target_pairs={{0,2},{1,3},{2,0},{3,1},{4,6},{5,7},{6,4},{7,5},{8,10},{9,11},{10,... | collective-permute-start | bytes 73736 | tf_op jit(solution)/shard_map/ppermute | solution.py:496
  261.2 3.8 %collective-permute-start.31 = (f32[8,768]{1,0:T(8,128)S(1)}, f32[8,768]{1,0:T(8,128)S(1)}, u32[]{:S(2)}, u32[]{:S(2)}) collective-permute-start(f32[8,768]{1,0:T(8,128)S(1)} %constant_dynamic-update-slice_fusion), channel_id=1, source_target_pairs={{0,3},{1,0},{2,1},{3,2},{4,7},{5,4},{6,5},{7,6},{8,11},{9,8},{10,9... | collective-permute-start | bytes 73736 | tf_op jit(solution)/shard_map/ppermute | solution.py:496
  261.3 15.3 %collective-permute-start.40 = (bf16[256,1024]{1,0:T(8,128)(2,1)S(1)}, bf16[256,1024]{1,0:T(8,128)(2,1)S(1)}, u32[]{:S(2)}, u32[]{:S(2)}) collective-permute-start(bf16[256,1024]{1,0:T(8,128)(2,1)S(1)} %get-tuple-element.138.refs_1_), channel_id=1, source_target_pairs={{0,4},{4,0},{8,12},{12,8},{1,5},{5,1},{9,13},{13,9},{2,6},{6,2},{1... | collective-permute-start | bytes 1572872 | tf_op jit(solution)/shard_map/ppermute | solution.py:446
  265.1 11.3 %collective-permute-start.34 = (f32[8,768]{1,0:T(8,128)S(1)}, f32[8,768]{1,0:T(8,128)S(1)}, u32[]{:S(2)}, u32[]{:S(2)}) collective-permute-start(f32[8,768]{1,0:T(8,128)S(1)} %add_add_fusion.refs_1_), channel_id=1, source_target_pairs={{0,8},{4,12},{8,0},{12,4},{1,9},{5,13},{9,1},{13,5},{2,10},{6,14},... | collective-permute-start | bytes 73736 | tf_op jit(solution)/shard_map/ppermute | solution.py:446
  266.6 14.2 %collective-permute-start.37 = (bf16[256,1024]{1,0:T(8,128)(2,1)S(1)}, bf16[256,1024]{1,0:T(8,128)(2,1)S(1)}, u32[]{:S(2)}, u32[]{:S(2)}) collective-permute-start(bf16[256,1024]{1,0:T(8,128)(2,1)S(1)} %get-tuple-element.136.refs_0_), channel_id=1, source_target_pairs={{0,4},{4,0},{8,12},{12,8},{1,5},{5,1},{9,13},{13,9},{2,6},{6,2},{1... | collective-permute-start | bytes 1572872 | tf_op jit(solution)/shard_map/ppermute | solution.py:446
  275.3 5.5 %collective-permute-start.38 = (bf16[256,1024]{1,0:T(8,128)(2,1)S(1)}, bf16[256,1024]{1,0:T(8,128)(2,1)S(1)}, u32[]{:S(2)}, u32[]{:S(2)}) collective-permute-start(bf16[256,1024]{1,0:T(8,128)(2,1)S(1)} %get-tuple-element.137.refs_1_), channel_id=1, source_target_pairs={{0,4},{4,0},{8,12},{12,8},{1,5},{5,1},{9,13},{13,9},{2,6},{6,2},{1... | collective-permute-start | bytes 1572872 | tf_op jit(solution)/shard_map/ppermute | solution.py:446
  275.9 7.0 %collective-permute-start.32 = (bf16[256,1024]{1,0:T(8,128)(2,1)S(1)}, bf16[256,1024]{1,0:T(8,128)(2,1)S(1)}, u32[]{:S(2)}, u32[]{:S(2)}) collective-permute-start(bf16[256,1024]{1,0:T(8,128)(2,1)S(1)} %get-tuple-element.133.refs_0_), channel_id=1, source_target_pairs={{0,4},{4,0},{8,12},{12,8},{1,5},{5,1},{9,13},{13,9},{2,6},{6,2},{1... | collective-permute-start | bytes 1572872 | tf_op jit(solution)/shard_map/ppermute | solution.py:446
  276.4 6.5 %collective-permute-start.33 = (bf16[256,1024]{1,0:T(8,128)(2,1)S(1)}, bf16[256,1024]{1,0:T(8,128)(2,1)S(1)}, u32[]{:S(2)}, u32[]{:S(2)}) collective-permute-start(bf16[256,1024]{1,0:T(8,128)(2,1)S(1)} %get-tuple-element.135.refs_1_), channel_id=1, source_target_pairs={{0,4},{4,0},{8,12},{12,8},{1,5},{5,1},{9,13},{13,9},{2,6},{6,2},{1... | collective-permute-start | bytes 1572872 | tf_op jit(solution)/shard_map/ppermute | solution.py:446
  276.5 2.3 collective-permute-start.35
  (5 other events, 6.1 us)

commit v5 on v4

--- a/solution.py
+++ b/solution.py
@@ -108,7 +108,7 @@
 
 
 def matmul_kernel(plan, info, *refs):
-    most, tp, spans, sources, prior_at, final, skip = plan
+    base, most, tp, spans, sources, prior_at, final, skip = plan
     parts = len(spans)
     count = sources * parts
     inputs = [refs[s * parts : (s + 1) * parts] for s in range(sources)]
@@ -125,7 +125,7 @@
     p = step // tp
     t = step % tp
     me = info[0]
-    pieces = info[1]
+    pieces = info[base]
 
     def load_prior(t):
         return pltpu.make_async_copy(
@@ -140,7 +140,7 @@
         for q in range(most):
             for s in range(sources):
 
-                @pl.when((q < pieces) & (info[2 + q] == s))
+                @pl.when((q < pieces) & (info[base + 1 + q] == s))
                 def _():
                     for n, (first, size) in enumerate(spans):
                         pltpu.make_async_copy(
@@ -197,7 +197,7 @@
         token[...] = jnp.zeros(TOKEN, jnp.float32)
 
 
-def matmul_stage(place, me, stages, sub, tp, inputs, weight, prior, prior_at, final, after):
+def matmul_stage(info, base, most, tp, inputs, weight, prior, prior_at, final, after):
     flat = [part for source in inputs for part in source]
     sizes = [part.shape[0] for part in inputs[0]]
     rows = sum(sizes)
@@ -205,12 +205,10 @@
     depth = flat[0].shape[1]
     columns = weight.shape[1]
     width = columns // tp
-    table, most = stage_table(sub, stages)
-    info = jnp.concatenate([me[None], jnp.asarray(table)[place]])
 
     def weight_block(j, s):
-        j = jnp.minimum(j, jnp.maximum(s[1] * tp - 1, 0))
-        return s[2 + most + j // tp], j % tp
+        j = jnp.minimum(j, jnp.maximum(s[base] * tp - 1, 0))
+        return s[base + 1 + most + j // tp], j % tp
 
     operands = [*flat, weight]
     specs = [anywhere()] * len(flat) + [pl.BlockSpec((depth, width), weight_block)]
@@ -227,6 +225,7 @@
         out_specs = [anywhere()]
         out_shape = [jax.ShapeDtypeStruct((tp, rows, width), jnp.float32)]
     plan = (
+        base,
         most,
         tp,
         spans,
@@ -380,25 +379,33 @@
     tp = len(places)
     pieces = refs[:tp]
     first, second, gain = refs[tp : tp + 3]
-    out, token = refs[tp + 3 + more :]
-    token[...] = jnp.zeros(TOKEN, jnp.float32)
-    inverse = lax.rsqrt((first[...] + second[...]) / D + 1e-05)
+    out, token, scale = refs[tp + 3 + more :]
+    step = pl.program_id(0)
+
+    @pl.when(step == 0)
+    def _():
+        inverse = lax.rsqrt((first[...] + second[...]) / D + 1e-05)
+        scale[...] = jnp.transpose(inverse)
+        token[...] = jnp.zeros(TOKEN, jnp.float32)
+
     rows, width = pieces[0].shape
-    scale = jnp.transpose(inverse)[0:rows, 0:1]
+    factor = scale[pl.ds(pl.multiple_of(step * rows, rows), rows), 0:1]
     for e, piece in zip(places, pieces):
         at = pl.ds(pl.multiple_of((info[0] ^ e) * width, width), width)
-        value = piece[...].astype(jnp.float32) * scale * gain[:, at]
+        value = piece[...].astype(jnp.float32) * factor * gain[:, at]
         out[:, at] = value.astype(jnp.bfloat16)
 
 
-def norm_rows(me, pieces, squares, column, gain, so_far, start, all_rows, after):
+def norm_rows(info, pieces, squares, column, gain, so_far, start, all_rows, after):
     tp = len(pieces)
     rows, width = pieces[0][1].shape
-    place = start // rows
+    tiles = 4 if rows % 64 == 0 else 1
+    tile = rows // tiles
+    place = start // tile
     small = pl.BlockSpec((8, lanes(rows)), lambda i, s: (0, column))
     operands = [piece for _, piece in pieces] + [*squares, gain]
     specs = (
-        [pl.BlockSpec((rows, width), lambda i, s: (0, 0))] * tp
+        [pl.BlockSpec((tile, width), lambda i, s: (i, 0))] * tp
         + [small] * 2
         + [pl.BlockSpec((1, tp * width), lambda i, s: (0, 0))]
     )
@@ -413,19 +420,20 @@
         functools.partial(norm_kernel, [e for e, _ in pieces], len(aliases) + len(after)),
         grid_spec=pltpu.PrefetchScalarGridSpec(
             num_scalar_prefetch=1,
-            grid=(1,),
+            grid=(tiles,),
             in_specs=specs,
             out_specs=[
-                pl.BlockSpec((rows, tp * width), lambda i, s: (place, 0)),
+                pl.BlockSpec((tile, tp * width), lambda i, s: (place + i, 0)),
                 token_spec(),
             ],
+            scratch_shapes=[pltpu.VMEM((lanes(rows), 8), jnp.float32)],
         ),
         out_shape=[jax.ShapeDtypeStruct((all_rows, tp * width), jnp.bfloat16), TOKEN_SHAPE],
         input_output_aliases=aliases,
         compiler_params=params(),
         cost_estimate=pl.CostEstimate(flops=1, bytes_accessed=1, transcendentals=0),
         name="norm_rows",
-    )(me[None], *operands)
+    )(info, *operands)
 
 
 def shards(sub, tp, gate_pre, up_pre, down_weight, residual, signs, row_slot, norm_gain):
@@ -451,8 +459,9 @@
         return [up, down]
 
     def matmul(stages, inputs, prior, start, final, after):
+        base, most = bases[tuple(stages)]
         return matmul_stage(
-            place, me, stages, sub, tp, inputs, down_weight, prior, start, final, after
+            info, base, most, tp, inputs, down_weight, prior, start, final, after
         )
 
     terms, held = {}, {}
@@ -506,7 +515,7 @@
     def normalise(us, totals, after):
         for n, u in enumerate(us):
             normed[0], token = norm_rows(
-                me,
+                info,
                 pieces[u],
                 totals,
                 sum(lanes(sizes[b]) for b in us[:n]) // lanes(sizes[u]),
@@ -520,6 +529,13 @@
         return after
 
     early, middle, late = [0, 1], list(range(2, sub - 1)), [sub - 1]
+    bases, tables, base = {}, [], 1
+    for stages in (early, middle + late, middle, late):
+        table, most = stage_table(sub, stages)
+        bases[tuple(stages)] = base, most
+        tables.append(table)
+        base += table.shape[1]
+    info = jnp.concatenate([me[None], jnp.asarray(np.concatenate(tables, axis=1))[place]])
     own = [None] * 3
     came = {}
 
@@ -539,8 +555,9 @@
                 inputs.append([own[u] for u in us])
             else:
                 inputs += [[came[d, u][side] for u in us] for side in range(2)]
+        base, most = bases[tuple(stages)]
         return matmul_stage(
-            place, me, stages, sub, tp, inputs, down_weight, prior, start, final, after
+            info, base, most, tp, inputs, down_weight, prior, start, final, after
         )
 
     def hold(keys, after):
@@ -554,7 +571,7 @@
     own[0] = (jax.nn.silu(first[0]) * first[1]).astype(jnp.bfloat16)
     came[1, 0] = onward([own[0], own[0]], 1)
     token = make(1, [own[0]])
-    (*came[1, 0], mine), token = gate([*came[1, 0], mine], token)
+    (*came[1, 0], mine, signs_own), token = gate([*came[1, 0], mine, signs_own], token)
     pass_on(0, 2, mid)
     token = make(2, token)
     part, *token = matmul([0], early, None, 0, False, token)
@@ -570,9 +587,9 @@
     token = hold([(mid, 1)], [token])
     pass_on(1, sub - 1, sub - 1)
     token = halve_sums(0, token)
-    parts, *token = matmul([1, 2], middle, parts, 0, False, token)
     token = hold([(mid, 2)], token)
     pass_on(2, sub - 1, sub - 1)
+    parts, *token = matmul([1, 2], middle, parts, 0, False, token)
     token = finish(0, token)
     *sums, token = matmul([1], late, parts, 0, True, token)
     begin_sums(1, sums)

time: 286 us -> 284 us (level)
  waiting for transfers between devices: 94.8 us -> 103 us
  local copies, waits for them, and re-layouts: 10.3 us -> 5.22 us
  Pallas kernels: 130 us -> 127 us
    ppermute x9, waiting for transfers between devices: 44.5 us -> 53.7 us  [onward(): lax.ppermute(pair[1], 'sub', [(i, i - 1) for i in range(1, sub - d + 1)])]
    pallas_call x6, Pallas kernels: 109 us -> 105 us  [matmul_stage(): pl.pallas_call(functools.partial(matmul_kernel, plan), grid_spec=pltpu.Pr...]
    unnamed x26 -> x22, local copies, waits for them, and re-layouts: 4.06 us -> 1.02 us
  transfers between devices with their start and end apart: 41 -> 41, of which waited for: 14 -> 14; matrix products, arithmetic and copies ran while one was open for 2% -> 2% of each run, Pallas kernels for 45% -> 44%
where the time goes in v5:
time: 284 us; the launch traced here: 283 us
  Pallas kernels  127 us (45%)
  waiting for transfers between devices  103 us (36%)
  starting transfers between devices  42.9 us (15%)
  local copies, waits for them, and re-layouts  5.22 us (2%)
  other arithmetic  3.52 us (1%)
    pallas_call x6, Pallas kernels, matmul_stage(): pl.pallas_call(functools.partial(matmul_kernel, plan), grid_spec=pltpu.Pr...  105 us
    ppermute x9, waiting for transfers between devices, onward(): lax.ppermute(pair[1], 'sub', [(i, i - 1) for i in range(1, sub - d + 1)])  53.7 us
    ppermute x20, waiting for transfers between devices, swap(): return lax.ppermute(value, 'tp', [(i, i ^ d) for i in range(tp)])  24 us
    ppermute x9, starting transfers between devices, onward(): lax.ppermute(pair[0], 'sub', [(i, i + 1) for i in range(d - 1, sub - 1)])  19.5 us
    ppermute x9, waiting for transfers between devices, onward(): lax.ppermute(pair[0], 'sub', [(i, i + 1) for i in range(d - 1, sub - 1)])  16.1 us
    ppermute x9, starting transfers between devices, onward(): lax.ppermute(pair[1], 'sub', [(i, i - 1) for i in range(1, sub - d + 1)])  11.8 us
    ppermute x20, starting transfers between devices, swap(): return lax.ppermute(value, 'tp', [(i, i ^ d) for i in range(tp)])  11 us
    pallas_call x3, Pallas kernels, norm_rows(): pl.pallas_call(functools.partial(norm_kernel, [e for e, _ in pieces], len...  8.89 us
  transfers between devices with their start and end apart: 41, of which 14 were waited for; matrix products, arithmetic and copies ran while one was open for 2% of the time, Pallas kernels for 44%

profile of v5, /device:TPU:0, one launch (start us, length us, event | category | flops | bytes accessed | tf_op | source)
XLA Modules:
  0.0 282.7 jit_solution(2916924643562229038)
XLA Ops:
  0.7 3.3 %fusion.4.refs_0_ = bf16[256,2048]{1,0:T(8,128)(2,1)} fusion(bf16[768,2048]{1,0:T(8,128)(2,1)} %up.3, bf16[768,2048]{1,0:T(8,128)(2,1)} %gate.13), kind=kLoop, calls=%fused_computation.7 | loop fusion | flops 4194304 | bytes 3145728 | tf_op jit(solution)/shard_map/convert_element_type | solution.py:571
  4.0 6.1 %collective-permute-start = (bf16[256,2048]{1,0:T(8,128)(2,1)}, bf16[256,2048]{1,0:T(8,128)(2,1)}, u32[]{:S(2)}, u32[]{:S(2)}) collective-permute-start(bf16[256,2048]{1,0:T(8,128)(2,1)} %fusion.4.refs_0_), channel_id=1, source_target_pairs={{0,1},{1,2},{2,3},{4,5},{5,6},{6,7},{8,9},{9,10},{10,11},{12,13},{... | collective-permute-start | bytes 3145736 | tf_op jit(solution)/shard_map/ppermute | solution.py:457
  10.1 1.3 collective-permute-start.1
  11.4 3.6 %hidden_rows.2 = (bf16[256,2048]{1,0:T(8,128)(2,1)}, f32[8,128]{1,0:T(8,128)S(1)}) custom-call(bf16[768,2048]{1,0:T(8,128)(2,1)S(1)} %copy-done.2, bf16[768,2048]{1,0:T(8,128)(2,1)} %up.3, bf16[256,2048]{1,0:T(8,128)(2,1)} %fusion.4.refs_0_), custom_call_target="tpu_custom_call" | custom-call | flops 1 | bytes 1 | tf_op jit(solution)/shard_map/hidden_rows/pallas_call | solution.py:67
  15.0 5.6 %collective-permute-start.6 = (bf16[256,2048]{1,0:T(8,128)(2,1)}, bf16[256,2048]{1,0:T(8,128)(2,1)}, u32[]{:S(2)}, u32[]{:S(2)}) collective-permute-start(bf16[256,2048]{1,0:T(8,128)(2,1)} %get-tuple-element.83.refs_0_), channel_id=1, source_target_pairs={{0,1},{1,2},{2,3},{4,5},{5,6},{6,7},{8,9},{9,10},{10,11},{12,13},{... | collective-permute-start | bytes 3145736 | tf_op jit(solution)/shard_map/ppermute | solution.py:457
  20.6 1.3 collective-permute-start.7
  22.6 2.8 gather_fusion
  25.4 7.5 %collective-permute-done.refs_0_ = bf16[256,2048]{1,0:T(8,128)(2,1)} collective-permute-done((bf16[256,2048]{1,0:T(8,128)(2,1)}, bf16[256,2048]{1,0:T(8,128)(2,1)}, u32[]{:S(2)}, u32[]{:S(2)}) %collective-permute-start) | collective-permute-done | bytes 1048608 | tf_op jit(solution)/shard_map/ppermute | solution.py:457
  32.9 5.4 %collective-permute-done.1.refs_1_ = bf16[256,2048]{1,0:T(8,128)(2,1)} collective-permute-done((bf16[256,2048]{1,0:T(8,128)(2,1)}, bf16[256,2048]{1,0:T(8,128)(2,1)}, u32[]{:S(2)}, u32[]{:S(2)}) %collective-permute-start.1) | collective-permute-done | bytes 1048608 | tf_op jit(solution)/shard_map/ppermute | solution.py:458
  38.3 3.0 %hidden_rows.3 = (bf16[256,2048]{1,0:T(8,128)(2,1)}, f32[8,128]{1,0:T(8,128)S(1)}) custom-call(bf16[768,2048]{1,0:T(8,128)(2,1)S(1)} %copy-done.3, bf16[768,2048]{1,0:T(8,128)(2,1)} %up.3, f32[8,128]{1,0:T(8,128)S(1)} %get-tuple-element.77.refs_0_), custom_call_target="tpu_custom_call" | custom-call | flops 1 | bytes 1 | tf_op jit(solution)/shard_map/hidden_rows/pallas_call | solution.py:67
  41.3 2.6 collective-permute-start.4
  43.9 1.3 collective-permute-start.5
  45.2 1.7 collective-permute-start.2
  46.8 8.5 %collective-permute-done.6.refs_0_ = bf16[256,2048]{1,0:T(8,128)(2,1)} collective-permute-done((bf16[256,2048]{1,0:T(8,128)(2,1)}, bf16[256,2048]{1,0:T(8,128)(2,1)}, u32[]{:S(2)}, u32[]{:S(2)}) %collective-permute-start.6) | collective-permute-done | bytes 1048608 | tf_op jit(solution)/shard_map/ppermute | solution.py:457
  55.4 1.3 collective-permute-start.3
  57.5 19.8 %matmul_stage.6 = (f32[4,256,1024]{2,1,0:T(8,128)}, f32[8,128]{1,0:T(8,128)S(1)}) custom-call(s32[19]{0:T(128)S(1)} %pad_add_fusion.info, bf16[256,2048]{1,0:T(8,128)(2,1)} %fusion.4.refs_0_, bf16[256,2048]{1,0:T(8,128)(2,1)} %get-tuple-element.75.refs_1_, bf16[256,2048]{1,0:T(8,128)(2,1)} %get-tuple-element.76.refs_2_, bf16[8192,4096]{1,0:T(8,128)(2,1)} %refs_2_.3, ...), custom_call_target="tpu_custom_call" | custom-call | flops 1 | bytes 1 | tf_op jit(solution)/shard_map/matmul_stage/pallas_call | solution.py:237
  78.6 1.3 collective-permute-start.9
  79.9 3.4 %collective-permute-done.5.refs_3_ = bf16[256,2048]{1,0:T(8,128)(2,1)} collective-permute-done((bf16[256,2048]{1,0:T(8,128)(2,1)}, bf16[256,2048]{1,0:T(8,128)(2,1)}, u32[]{:S(2)}, u32[]{:S(2)}) %collective-permute-start.5) | collective-permute-done | bytes 1048608 | tf_op jit(solution)/shard_map/ppermute | solution.py:458
  83.3 22.5 %collective-permute-done.3.refs_1_ = bf16[256,2048]{1,0:T(8,128)(2,1)} collective-permute-done((bf16[256,2048]{1,0:T(8,128)(2,1)}, bf16[256,2048]{1,0:T(8,128)(2,1)}, u32[]{:S(2)}, u32[]{:S(2)}) %collective-permute-start.3) | collective-permute-done | bytes 1048608 | tf_op jit(solution)/shard_map/ppermute | solution.py:458
  106.5 1.3 collective-permute-start.13
  107.8 27.0 %matmul_stage.7 = (f32[4,512,1024]{2,1,0:T(8,128)}, f32[8,128]{1,0:T(8,128)S(1)}) custom-call(s32[19]{0:T(128)S(1)} %pad_add_fusion.info, bf16[256,2048]{1,0:T(8,128)(2,1)} %get-tuple-element.83.refs_0_, bf16[256,2048]{1,0:T(8,128)(2,1)} %get-tuple-element.78.refs_1_, bf16[256,2048]{1,0:T(8,128)(2,1)} %get-tuple-element.84.refs_2_, ...), custom_call_target="tpu_custom_call" | custom-call | flops 1 | bytes 1 | tf_op jit(solution)/shard_map/matmul_stage/pallas_call | solution.py:237
  135.6 1.3 collective-permute-start.11
  136.9 12.2 %collective-permute-done.13.refs_3_ = bf16[256,2048]{1,0:T(8,128)(2,1)S(1)} collective-permute-done((bf16[256,2048]{1,0:T(8,128)(2,1)}, bf16[256,2048]{1,0:T(8,128)(2,1)S(1)}, u32[]{:S(2)}, u32[]{:S(2)}) %collective-permute-start.13) | collective-permute-done | bytes 1048608 | tf_op jit(solution)/shard_map/ppermute | solution.py:458
  149.1 1.0 copy-done.8
  150.1 19.5 %matmul_stage.8 = (f32[256,1024]{1,0:T(8,128)S(1)}, f32[256,1024]{1,0:T(8,128)S(1)}, bf16[256,1024]{1,0:T(8,128)(2,1)}, bf16[256,1024]{1,0:T(8,128)(2,1)S(1)}, f32[8,128]{1,0:T(8,128)S(1)}) custom-call(s32[19]{0:T(128)S(1)} %pad_add_fusion.info, bf16[256,2048]{1,0:T(8,128)(2,1)} %get-tuple-element.90.refs_0_, bf16[256,2048]{1,0:T(8,128)(2,1)} %get-tuple-element.91.refs_1_, ...), custom_call_target="tpu_custom_call" | custom-call | flops 1 | bytes 1 | tf_op jit(solution)/shard_map/matmul_stage/pallas_call | solution.py:237
  170.4 1.3 collective-permute-start.18
  172.4 1.6 collective-permute-start.20
  174.7 1.5 collective-permute-start.16
  176.3 16.4 %matmul_stage.9 = (f32[4,512,1024]{2,1,0:T(8,128)}, f32[8,128]{1,0:T(8,128)S(1)}) custom-call(s32[19]{0:T(128)S(1)} %pad_add_fusion.info, bf16[256,2048]{1,0:T(8,128)(2,1)S(1)} %get-tuple-element.103.refs_0_, bf16[256,2048]{1,0:T(8,128)(2,1)S(1)} %get-tuple-element.101.refs_1_, bf16[256,2048]{1,0:T(8,128)(2,1)S(1)} %get-tuple-element.104.refs_2_, ...), custom_call_target="tpu_custom_call" | custom-call | flops 1 | bytes 1 | tf_op jit(solution)/shard_map/matmul_stage/pallas_call | solution.py:237
  192.7 1.8 stream_rows.3
  195.3 2.9 %collective-permute-done.18.refs_1_ = bf16[256,2048]{1,0:T(8,128)(2,1)S(1)} collective-permute-done((bf16[256,2048]{1,0:T(8,128)(2,1)S(1)}, bf16[256,2048]{1,0:T(8,128)(2,1)S(1)}, u32[]{:S(2)}, u32[]{:S(2)}) %collective-permute-start.18) | collective-permute-done | bytes 1048608 | tf_op jit(solution)/shard_map/ppermute | solution.py:458
  198.3 11.1 %matmul_stage.10 = (f32[256,1024]{1,0:T(8,128)S(1)}, f32[256,1024]{1,0:T(8,128)S(1)}, bf16[256,1024]{1,0:T(8,128)(2,1)S(1)}, bf16[256,1024]{1,0:T(8,128)(2,1)S(1)}, f32[8,128]{1,0:T(8,128)S(1)}) custom-call(s32[19]{0:T(128)S(1)} %pad_add_fusion.info, bf16[256,2048]{1,0:T(8,128)(2,1)S(1)} %collective-permute-done.17.refs_0_, ...), custom_call_target="tpu_custom_call" | custom-call | flops 1 | bytes 1 | tf_op jit(solution)/shard_map/matmul_stage/pallas_call | solution.py:237
  209.9 1.4 collective-permute-done.21.refs_1_
  211.5 1.6 collective-permute-start.26
  213.0 7.3 %collective-permute-done.16.refs_1_ = bf16[256,2048]{1,0:T(8,128)(2,1)S(1)} collective-permute-done((bf16[256,2048]{1,0:T(8,128)(2,1)S(1)}, bf16[256,2048]{1,0:T(8,128)(2,1)S(1)}, u32[]{:S(2)}, u32[]{:S(2)}) %collective-permute-start.16) | collective-permute-done | bytes 1048608 | tf_op jit(solution)/shard_map/ppermute | solution.py:458
  220.3 11.1 %matmul_stage.11 = (f32[256,1024]{1,0:T(8,128)S(1)}, f32[256,1024]{1,0:T(8,128)S(1)}, bf16[256,1024]{1,0:T(8,128)(2,1)S(1)}, bf16[256,1024]{1,0:T(8,128)(2,1)S(1)}, f32[8,128]{1,0:T(8,128)S(1)}) custom-call(s32[19]{0:T(128)S(1)} %pad_add_fusion.info, bf16[256,2048]{1,0:T(8,128)(2,1)S(1)} %collective-permute-done.15.refs_0_, ...), custom_call_target="tpu_custom_call" | custom-call | flops 1 | bytes 1 | tf_op jit(solution)/shard_map/matmul_stage/pallas_call | solution.py:237
  232.0 1.5 stream_rows.4
  233.7 1.6 collective-permute-start.27
  235.8 12.7 %collective-permute-done.27.last = bf16[256,1024]{1,0:T(8,128)(2,1)S(1)} collective-permute-done((bf16[256,1024]{1,0:T(8,128)(2,1)S(1)}, bf16[256,1024]{1,0:T(8,128)(2,1)S(1)}, u32[]{:S(2)}, u32[]{:S(2)}) %collective-permute-start.27) | collective-permute-done | bytes 524320 | tf_op jit(solution)/shard_map/ppermute | solution.py:454
  248.5 1.5 stream_rows.5
  250.0 1.5 collective-permute-start.28
  252.3 5.0 %collective-permute-done.29 = f32[8,768]{1,0:T(8,128)S(1)} collective-permute-done((f32[8,768]{1,0:T(8,128)S(1)}, f32[8,768]{1,0:T(8,128)S(1)}, u32[]{:S(2)}, u32[]{:S(2)}) %collective-permute-start.29) | collective-permute-done | bytes 24608 | tf_op jit(solution)/shard_map/ppermute | solution.py:505
  257.3 3.8 %collective-permute-done.31 = f32[8,768]{1,0:T(8,128)S(1)} collective-permute-done((f32[8,768]{1,0:T(8,128)S(1)}, f32[8,768]{1,0:T(8,128)S(1)}, u32[]{:S(2)}, u32[]{:S(2)}) %collective-permute-start.31) | collective-permute-done | bytes 24608 | tf_op jit(solution)/shard_map/ppermute | solution.py:505
  262.3 8.1 %collective-permute-done.28.refs_0_ = bf16[256,1024]{1,0:T(8,128)(2,1)S(1)} collective-permute-done((bf16[256,1024]{1,0:T(8,128)(2,1)S(1)}, bf16[256,1024]{1,0:T(8,128)(2,1)S(1)}, u32[]{:S(2)}, u32[]{:S(2)}) %collective-permute-start.28) | collective-permute-done | bytes 524320 | tf_op jit(solution)/shard_map/ppermute | solution.py:454
  272.1 1.7 collective-permute-done.35.refs_5_
  273.8 3.0 %norm_rows.3 = (bf16[768,4096]{1,0:T(8,128)(2,1)}, f32[8,128]{1,0:T(8,128)S(1)}) custom-call(s32[19]{0:T(128)S(1)} %pad_add_fusion.info, bf16[256,1024]{1,0:T(8,128)(2,1)S(1)} %get-tuple-element.117.refs_0_, bf16[256,1024]{1,0:T(8,128)(2,1)S(1)} %get-tuple-element.140.refs_1_, bf16[256,1024]{1,0:T(8,128)(2,1)S(1)} %collective-permute-done.39.refs_2_, ...), custom_call_target="tpu_custom_call" | custom-call | flops 1 | bytes 1 | tf_op jit(solution)/shard_map/norm_rows/pallas_call | solution.py:419
  276.8 3.0 %norm_rows.4 = (bf16[768,4096]{1,0:T(8,128)(2,1)}, f32[8,128]{1,0:T(8,128)S(1)}) custom-call(s32[19]{0:T(128)S(1)} %pad_add_fusion.info, bf16[256,1024]{1,0:T(8,128)(2,1)S(1)} %get-tuple-element.138.refs_0_, bf16[256,1024]{1,0:T(8,128)(2,1)S(1)} %get-tuple-element.139.refs_1_, ...), custom_call_target="tpu_custom_call", output_to_operand_aliasing={{0}: (8, {})} | custom-call | flops 1 | bytes 1 | tf_op jit(solution)/shard_map/norm_rows/pallas_call | solution.py:419
  279.8 3.0 %norm_rows.5 = (bf16[768,4096]{1,0:T(8,128)(2,1)}, f32[8,128]{1,0:T(8,128)}) custom-call(s32[19]{0:T(128)S(1)} %pad_add_fusion.info, bf16[256,1024]{1,0:T(8,128)(2,1)S(1)} %get-tuple-element.135.refs_0_, bf16[256,1024]{1,0:T(8,128)(2,1)S(1)} %get-tuple-element.137.refs_1_, ...), custom_call_target="tpu_custom_call", output_to_operand_aliasing={{0}: (8, {})} | custom-call | flops 1 | bytes 1 | tf_op jit(solution)/shard_map/norm_rows/pallas_call | solution.py:419
  (92 shorter events, 13.0 us)
Async XLA Ops:
  0.6 21.9 %copy-start = (bf16[768,1024]{1,0:T(8,128)(2,1)S(1)}, bf16[768,1024]{1,0:T(8,128)(2,1)}, u32[]{:S(2)}) copy-start(bf16[768,1024]{1,0:T(8,128)(2,1)} %param.11) | copy-start | bytes 4718596
  0.6 10.7 %copy-start.2 = (bf16[768,2048]{1,0:T(8,128)(2,1)S(1)}, bf16[768,2048]{1,0:T(8,128)(2,1)}, u32[]{:S(2)}) copy-start(bf16[768,2048]{1,0:T(8,128)(2,1)} %gate.13) | copy-start | bytes 9437188
  4.0 18.6 %copy-start.9 = (s32[768]{0:T(1024)S(1)}, s32[768]{0:T(1024)}, u32[]{:S(2)}) copy-start(s32[768]{0:T(1024)} %param.13) | copy-start | bytes 9220
  4.0 28.9 %collective-permute-start = (bf16[256,2048]{1,0:T(8,128)(2,1)}, bf16[256,2048]{1,0:T(8,128)(2,1)}, u32[]{:S(2)}, u32[]{:S(2)}) collective-permute-start(bf16[256,2048]{1,0:T(8,128)(2,1)} %fusion.4.refs_0_), channel_id=1, source_target_pairs={{0,1},{1,2},{2,3},{4,5},{5,6},{6,7},{8,9},{9,10},{10,11},{12,13},{... | collective-permute-start | bytes 3145736 | tf_op jit(solution)/shard_map/ppermute | solution.py:457
  10.1 28.3 %collective-permute-start.1 = (bf16[256,2048]{1,0:T(8,128)(2,1)}, bf16[256,2048]{1,0:T(8,128)(2,1)}, u32[]{:S(2)}, u32[]{:S(2)}) collective-permute-start(bf16[256,2048]{1,0:T(8,128)(2,1)} %fusion.4.refs_0_), channel_id=1, source_target_pairs={{1,0},{2,1},{3,2},{5,4},{6,5},{7,6},{9,8},{10,9},{11,10},{13,12},{... | collective-permute-start | bytes 3145736 | tf_op jit(solution)/shard_map/ppermute | solution.py:458
  15.0 40.4 %collective-permute-start.6 = (bf16[256,2048]{1,0:T(8,128)(2,1)}, bf16[256,2048]{1,0:T(8,128)(2,1)}, u32[]{:S(2)}, u32[]{:S(2)}) collective-permute-start(bf16[256,2048]{1,0:T(8,128)(2,1)} %get-tuple-element.83.refs_0_), channel_id=1, source_target_pairs={{0,1},{1,2},{2,3},{4,5},{5,6},{6,7},{8,9},{9,10},{10,11},{12,13},{... | collective-permute-start | bytes 3145736 | tf_op jit(solution)/shard_map/ppermute | solution.py:457
  20.6 56.7 %collective-permute-start.7 = (bf16[256,2048]{1,0:T(8,128)(2,1)}, bf16[256,2048]{1,0:T(8,128)(2,1)}, u32[]{:S(2)}, u32[]{:S(2)}) collective-permute-start(bf16[256,2048]{1,0:T(8,128)(2,1)} %get-tuple-element.83.refs_0_), channel_id=1, source_target_pairs={{1,0},{2,1},{3,2},{5,4},{6,5},{7,6},{9,8},{10,9},{11,10},{13,12},{... | collective-permute-start | bytes 3145736 | tf_op jit(solution)/shard_map/ppermute | solution.py:458
  25.4 13.0 %copy-start.3 = (bf16[768,2048]{1,0:T(8,128)(2,1)S(1)}, bf16[768,2048]{1,0:T(8,128)(2,1)}, u32[]{:S(2)}) copy-start(bf16[768,2048]{1,0:T(8,128)(2,1)} %gate.13) | copy-start | bytes 9437188
  41.3 37.3 %collective-permute-start.4 = (bf16[256,2048]{1,0:T(8,128)(2,1)}, bf16[256,2048]{1,0:T(8,128)(2,1)S(1)}, u32[]{:S(2)}, u32[]{:S(2)}) collective-permute-start(bf16[256,2048]{1,0:T(8,128)(2,1)} %get-tuple-element.78.refs_1_), channel_id=1, source_target_pairs={{0,1},{1,2},{2,3},{4,5},{5,6},{6,7},{8,9},{9,10},{10,11},{12,13},{... | collective-permute-start | bytes 3145736 | tf_op jit(solution)/shard_map/ppermute | solution.py:457
  43.9 39.4 %collective-permute-start.5 = (bf16[256,2048]{1,0:T(8,128)(2,1)}, bf16[256,2048]{1,0:T(8,128)(2,1)}, u32[]{:S(2)}, u32[]{:S(2)}) collective-permute-start(bf16[256,2048]{1,0:T(8,128)(2,1)} %get-tuple-element.78.refs_1_), channel_id=1, source_target_pairs={{1,0},{2,1},{3,2},{5,4},{6,5},{7,6},{9,8},{10,9},{11,10},{13,12},{... | collective-permute-start | bytes 3145736 | tf_op jit(solution)/shard_map/ppermute | solution.py:458
  45.2 38.1 %collective-permute-start.2 = (bf16[256,2048]{1,0:T(8,128)(2,1)}, bf16[256,2048]{1,0:T(8,128)(2,1)}, u32[]{:S(2)}, u32[]{:S(2)}) collective-permute-start(bf16[256,2048]{1,0:T(8,128)(2,1)} %get-tuple-element.75.refs_1_), channel_id=1, source_target_pairs={{1,2},{2,3},{5,6},{6,7},{9,10},{10,11},{13,14},{14,15},{17,18},{18... | collective-permute-start | bytes 3145736 | tf_op jit(solution)/shard_map/ppermute | solution.py:457
  55.4 50.4 %collective-permute-start.3 = (bf16[256,2048]{1,0:T(8,128)(2,1)}, bf16[256,2048]{1,0:T(8,128)(2,1)}, u32[]{:S(2)}, u32[]{:S(2)}) collective-permute-start(bf16[256,2048]{1,0:T(8,128)(2,1)} %get-tuple-element.76.refs_2_), channel_id=1, source_target_pairs={{1,0},{2,1},{5,4},{6,5},{9,8},{10,9},{13,12},{14,13},{17,16},{18,1... | collective-permute-start | bytes 3145736 | tf_op jit(solution)/shard_map/ppermute | solution.py:458
  77.9 57.0 %collective-permute-start.8 = (bf16[256,2048]{1,0:T(8,128)(2,1)}, bf16[256,2048]{1,0:T(8,128)(2,1)S(1)}, u32[]{:S(2)}, u32[]{:S(2)}) collective-permute-start(bf16[256,2048]{1,0:T(8,128)(2,1)} %get-tuple-element.84.refs_2_), channel_id=1, source_target_pairs={{1,2},{2,3},{5,6},{6,7},{9,10},{10,11},{13,14},{14,15},{17,18},{18... | collective-permute-start | bytes 3145736 | tf_op jit(solution)/shard_map/ppermute | solution.py:457
  78.6 56.2 %collective-permute-start.9 = (bf16[256,2048]{1,0:T(8,128)(2,1)}, bf16[256,2048]{1,0:T(8,128)(2,1)S(1)}, u32[]{:S(2)}, u32[]{:S(2)}) collective-permute-start(bf16[256,2048]{1,0:T(8,128)(2,1)} %get-tuple-element.85.refs_4_), channel_id=1, source_target_pairs={{1,0},{2,1},{5,4},{6,5},{9,8},{10,9},{13,12},{14,13},{17,16},{18,1... | collective-permute-start | bytes 3145736 | tf_op jit(solution)/shard_map/ppermute | solution.py:458
  105.8 31.1 %collective-permute-start.12 = (bf16[256,2048]{1,0:T(8,128)(2,1)}, bf16[256,2048]{1,0:T(8,128)(2,1)S(1)}, u32[]{:S(2)}, u32[]{:S(2)}) collective-permute-start(bf16[256,2048]{1,0:T(8,128)(2,1)} %get-tuple-element.90.refs_0_), channel_id=1, source_target_pairs={{2,3},{6,7},{10,11},{14,15},{18,19},{22,23},{26,27},{30,31}} | collective-permute-start | bytes 3145736 | tf_op jit(solution)/shard_map/ppermute | solution.py:457
  106.5 42.6 %collective-permute-start.13 = (bf16[256,2048]{1,0:T(8,128)(2,1)}, bf16[256,2048]{1,0:T(8,128)(2,1)S(1)}, u32[]{:S(2)}, u32[]{:S(2)}) collective-permute-start(bf16[256,2048]{1,0:T(8,128)(2,1)} %get-tuple-element.91.refs_1_), channel_id=1, source_target_pairs={{1,0},{5,4},{9,8},{13,12},{17,16},{21,20},{25,24},{29,28}} | collective-permute-start | bytes 3145736 | tf_op jit(solution)/shard_map/ppermute | solution.py:458
  134.9 37.5 %collective-permute-start.10 = (bf16[256,2048]{1,0:T(8,128)(2,1)S(1)}, bf16[256,2048]{1,0:T(8,128)(2,1)S(1)}, u32[]{:S(2)}, u32[]{:S(2)}) collective-permute-start(bf16[256,2048]{1,0:T(8,128)(2,1)S(1)} %get-tuple-element.88), channel_id=1, source_target_pairs={{1,2},{2,3},{5,6},{6,7},{9,10},{10,11},{13,14},{14,15},{17,18},{18... | collective-permute-start | bytes 3145736 | tf_op jit(solution)/shard_map/ppermute | solution.py:457
  135.6 38.3 %collective-permute-start.11 = (bf16[256,2048]{1,0:T(8,128)(2,1)}, bf16[256,2048]{1,0:T(8,128)(2,1)S(1)}, u32[]{:S(2)}, u32[]{:S(2)}) collective-permute-start(bf16[256,2048]{1,0:T(8,128)(2,1)} %get-tuple-element.89), channel_id=1, source_target_pairs={{1,0},{2,1},{5,4},{6,5},{9,8},{10,9},{13,12},{14,13},{17,16},{18,1... | collective-permute-start | bytes 3145736 | tf_op jit(solution)/shard_map/ppermute | solution.py:458
  136.9 12.2 %copy-start.7 = (bf16[256,2048]{1,0:T(8,128)(2,1)}, bf16[256,2048]{1,0:T(8,128)(2,1)S(1)}, u32[]{:S(2)}) copy-start(bf16[256,2048]{1,0:T(8,128)(2,1)S(1)} %collective-permute-done.12.refs_2_) | copy-start | bytes 3145732
  169.6 2.1 collective-permute-start.14
  169.7 25.7 %collective-permute-start.17 = (bf16[256,2048]{1,0:T(8,128)(2,1)S(1)}, bf16[256,2048]{1,0:T(8,128)(2,1)S(1)}, u32[]{:S(2)}, u32[]{:S(2)}) collective-permute-start(bf16[256,2048]{1,0:T(8,128)(2,1)S(1)} %get-tuple-element.103.refs_0_), channel_id=1, source_target_pairs={{2,3},{6,7},{10,11},{14,15},{18,19},{22,23},{26,27},{30,31}} | collective-permute-start | bytes 3145736 | tf_op jit(solution)/shard_map/ppermute | solution.py:457
  170.4 27.9 %collective-permute-start.18 = (bf16[256,2048]{1,0:T(8,128)(2,1)S(1)}, bf16[256,2048]{1,0:T(8,128)(2,1)S(1)}, u32[]{:S(2)}, u32[]{:S(2)}) collective-permute-start(bf16[256,2048]{1,0:T(8,128)(2,1)S(1)} %get-tuple-element.104.refs_2_), channel_id=1, source_target_pairs={{1,0},{5,4},{9,8},{13,12},{17,16},{21,20},{25,24},{29,28}} | collective-permute-start | bytes 3145736 | tf_op jit(solution)/shard_map/ppermute | solution.py:458
  171.7 3.0 %collective-permute-start.19 = (bf16[256,1024]{1,0:T(8,128)(2,1)}, bf16[256,1024]{1,0:T(8,128)(2,1)S(1)}, u32[]{:S(2)}, u32[]{:S(2)}) collective-permute-start(bf16[256,1024]{1,0:T(8,128)(2,1)} %get-tuple-element.109), channel_id=1, source_target_pairs={{0,4},{4,0},{8,12},{12,8},{1,5},{5,1},{9,13},{13,9},{2,6},{6,2},{1... | collective-permute-start | bytes 1572872 | tf_op jit(solution)/shard_map/ppermute | solution.py:454
  172.4 20.3 %collective-permute-start.20 = (bf16[256,1024]{1,0:T(8,128)(2,1)S(1)}, bf16[256,1024]{1,0:T(8,128)(2,1)S(1)}, u32[]{:S(2)}, u32[]{:S(2)}) collective-permute-start(bf16[256,1024]{1,0:T(8,128)(2,1)S(1)} %get-tuple-element.110), channel_id=1, source_target_pairs={{0,8},{4,12},{8,0},{12,4},{1,9},{5,13},{9,1},{13,5},{2,10},{6,14},... | collective-permute-start | bytes 1572872 | tf_op jit(solution)/shard_map/ppermute | solution.py:454
  173.9 39.1 %collective-permute-start.15 = (bf16[256,2048]{1,0:T(8,128)(2,1)S(1)}, bf16[256,2048]{1,0:T(8,128)(2,1)S(1)}, u32[]{:S(2)}, u32[]{:S(2)}) collective-permute-start(bf16[256,2048]{1,0:T(8,128)(2,1)S(1)} %get-tuple-element.101.refs_1_), channel_id=1, source_target_pairs={{2,3},{6,7},{10,11},{14,15},{18,19},{22,23},{26,27},{30,31}} | collective-permute-start | bytes 3145736 | tf_op jit(solution)/shard_map/ppermute | solution.py:457
  174.7 45.6 %collective-permute-start.16 = (bf16[256,2048]{1,0:T(8,128)(2,1)S(1)}, bf16[256,2048]{1,0:T(8,128)(2,1)S(1)}, u32[]{:S(2)}, u32[]{:S(2)}) collective-permute-start(bf16[256,2048]{1,0:T(8,128)(2,1)S(1)} %get-tuple-element.102.refs_3_), channel_id=1, source_target_pairs={{1,0},{5,4},{9,8},{13,12},{17,16},{21,20},{25,24},{29,28}} | collective-permute-start | bytes 3145736 | tf_op jit(solution)/shard_map/ppermute | solution.py:458
  176.3 16.5 %copy-start.5 = (f32[256,1024]{1,0:T(8,128)S(1)}, f32[256,1024]{1,0:T(8,128)}, u32[]{:S(2)}) copy-start(f32[256,1024]{1,0:T(8,128)} %copy-done.4) | copy-start | bytes 3145732
  194.5 15.4 %collective-permute-start.22 = (bf16[256,1024]{1,0:T(8,128)(2,1)S(1)}, bf16[256,1024]{1,0:T(8,128)(2,1)S(1)}, u32[]{:S(2)}, u32[]{:S(2)}) collective-permute-start(bf16[256,1024]{1,0:T(8,128)(2,1)S(1)} %get-tuple-element.117.refs_0_), channel_id=1, source_target_pairs={{0,8},{4,12},{8,0},{12,4},{1,9},{5,13},{9,1},{13,5},{2,10},{6,14},... | collective-permute-start | bytes 1572872 | tf_op jit(solution)/shard_map/ppermute | solution.py:454
  209.4 2.0 collective-permute-start.21
  209.4 22.5 %collective-permute-start.25 = (bf16[256,1024]{1,0:T(8,128)(2,1)S(1)}, bf16[256,1024]{1,0:T(8,128)(2,1)S(1)}, u32[]{:S(2)}, u32[]{:S(2)}) collective-permute-start(bf16[256,1024]{1,0:T(8,128)(2,1)S(1)} %get-tuple-element.126), channel_id=1, source_target_pairs={{0,4},{4,0},{8,12},{12,8},{1,5},{5,1},{9,13},{13,9},{2,6},{6,2},{1... | collective-permute-start | bytes 1572872 | tf_op jit(solution)/shard_map/ppermute | solution.py:454
  211.5 20.5 %collective-permute-start.26 = (bf16[256,1024]{1,0:T(8,128)(2,1)S(1)}, bf16[256,1024]{1,0:T(8,128)(2,1)S(1)}, u32[]{:S(2)}, u32[]{:S(2)}) collective-permute-start(bf16[256,1024]{1,0:T(8,128)(2,1)S(1)} %get-tuple-element.127), channel_id=1, source_target_pairs={{0,8},{4,12},{8,0},{12,4},{1,9},{5,13},{9,1},{13,5},{2,10},{6,14},... | collective-permute-start | bytes 1572872 | tf_op jit(solution)/shard_map/ppermute | solution.py:454
  231.4 2.1 collective-permute-start.24
  231.5 4.3 %collective-permute-start.23 = (bf16[256,1024]{1,0:T(8,128)(2,1)S(1)}, bf16[256,1024]{1,0:T(8,128)(2,1)S(1)}, u32[]{:S(2)}, u32[]{:S(2)}) collective-permute-start(bf16[256,1024]{1,0:T(8,128)(2,1)S(1)} %get-tuple-element.122), channel_id=1, source_target_pairs={{0,4},{4,0},{8,12},{12,8},{1,5},{5,1},{9,13},{13,9},{2,6},{6,2},{1... | collective-permute-start | bytes 1572872 | tf_op jit(solution)/shard_map/ppermute | solution.py:454
  233.7 14.8 %collective-permute-start.27 = (bf16[256,1024]{1,0:T(8,128)(2,1)S(1)}, bf16[256,1024]{1,0:T(8,128)(2,1)S(1)}, u32[]{:S(2)}, u32[]{:S(2)}) collective-permute-start(bf16[256,1024]{1,0:T(8,128)(2,1)S(1)} %get-tuple-element.131), channel_id=1, source_target_pairs={{0,8},{4,12},{8,0},{12,4},{1,9},{5,13},{9,1},{13,5},{2,10},{6,14},... | collective-permute-start | bytes 1572872 | tf_op jit(solution)/shard_map/ppermute | solution.py:454
  235.2 35.8 %collective-permute-start.39 = (bf16[256,1024]{1,0:T(8,128)(2,1)S(1)}, bf16[256,1024]{1,0:T(8,128)(2,1)S(1)}, u32[]{:S(2)}, u32[]{:S(2)}) collective-permute-start(bf16[256,1024]{1,0:T(8,128)(2,1)S(1)} %get-tuple-element.117.refs_0_), channel_id=1, source_target_pairs={{0,4},{4,0},{8,12},{12,8},{1,5},{5,1},{9,13},{13,9},{2,6},{6,2},{1... | collective-permute-start | bytes 1572872 | tf_op jit(solution)/shard_map/ppermute | solution.py:454
  235.2 26.5 %collective-permute-start.36 = (bf16[256,1024]{1,0:T(8,128)(2,1)S(1)}, bf16[256,1024]{1,0:T(8,128)(2,1)S(1)}, u32[]{:S(2)}, u32[]{:S(2)}) collective-permute-start(bf16[256,1024]{1,0:T(8,128)(2,1)S(1)} %get-tuple-element.138.refs_0_), channel_id=1, source_target_pairs={{0,8},{4,12},{8,0},{12,4},{1,9},{5,13},{9,1},{13,5},{2,10},{6,14},... | collective-permute-start | bytes 1572872 | tf_op jit(solution)/shard_map/ppermute | solution.py:454
  248.5 25.3 %copy-start.6 = (f32[4096]{0:T(1024)S(1)}, f32[4096]{0:T(1024)}, u32[]{:S(2)}) copy-start(f32[4096]{0:T(1024)} %param.14) | copy-start | bytes 49156
  250.0 20.3 %collective-permute-start.28 = (bf16[256,1024]{1,0:T(8,128)(2,1)S(1)}, bf16[256,1024]{1,0:T(8,128)(2,1)S(1)}, u32[]{:S(2)}, u32[]{:S(2)}) collective-permute-start(bf16[256,1024]{1,0:T(8,128)(2,1)S(1)} %get-tuple-element.135.refs_0_), channel_id=1, source_target_pairs={{0,8},{4,12},{8,0},{12,4},{1,9},{5,13},{9,1},{13,5},{2,10},{6,14},... | collective-permute-start | bytes 1572872 | tf_op jit(solution)/shard_map/ppermute | solution.py:454
  251.6 5.7 %collective-permute-start.29 = (f32[8,768]{1,0:T(8,128)S(1)}, f32[8,768]{1,0:T(8,128)S(1)}, u32[]{:S(2)}, u32[]{:S(2)}) collective-permute-start(f32[8,768]{1,0:T(8,128)S(1)} %constant_dynamic-update-slice_fusion), channel_id=1, source_target_pairs={{0,1},{1,2},{2,3},{3,0},{4,5},{5,6},{6,7},{7,4},{8,9},{9,10},{10,1... | collective-permute-start | bytes 73736 | tf_op jit(solution)/shard_map/ppermute | solution.py:505
  251.6 5.7 %collective-permute-start.30 = (f32[8,768]{1,0:T(8,128)S(1)}, f32[8,768]{1,0:T(8,128)S(1)}, u32[]{:S(2)}, u32[]{:S(2)}) collective-permute-start(f32[8,768]{1,0:T(8,128)S(1)} %constant_dynamic-update-slice_fusion), channel_id=1, source_target_pairs={{0,2},{1,3},{2,0},{3,1},{4,6},{5,7},{6,4},{7,5},{8,10},{9,11},{10,... | collective-permute-start | bytes 73736 | tf_op jit(solution)/shard_map/ppermute | solution.py:505
  257.2 3.8 %collective-permute-start.31 = (f32[8,768]{1,0:T(8,128)S(1)}, f32[8,768]{1,0:T(8,128)S(1)}, u32[]{:S(2)}, u32[]{:S(2)}) collective-permute-start(f32[8,768]{1,0:T(8,128)S(1)} %constant_dynamic-update-slice_fusion), channel_id=1, source_target_pairs={{0,3},{1,0},{2,1},{3,2},{4,7},{5,4},{6,5},{7,6},{8,11},{9,8},{10,9... | collective-permute-start | bytes 73736 | tf_op jit(solution)/shard_map/ppermute | solution.py:505
  257.2 14.3 %collective-permute-start.40 = (bf16[256,1024]{1,0:T(8,128)(2,1)S(1)}, bf16[256,1024]{1,0:T(8,128)(2,1)S(1)}, u32[]{:S(2)}, u32[]{:S(2)}) collective-permute-start(bf16[256,1024]{1,0:T(8,128)(2,1)S(1)} %get-tuple-element.140.refs_1_), channel_id=1, source_target_pairs={{0,4},{4,0},{8,12},{12,8},{1,5},{5,1},{9,13},{13,9},{2,6},{6,2},{1... | collective-permute-start | bytes 1572872 | tf_op jit(solution)/shard_map/ppermute | solution.py:454
  261.1 10.4 %collective-permute-start.34 = (f32[8,768]{1,0:T(8,128)S(1)}, f32[8,768]{1,0:T(8,128)S(1)}, u32[]{:S(2)}, u32[]{:S(2)}) collective-permute-start(f32[8,768]{1,0:T(8,128)S(1)} %add_add_fusion.refs_1_), channel_id=1, source_target_pairs={{0,8},{4,12},{8,0},{12,4},{1,9},{5,13},{9,1},{13,5},{2,10},{6,14},... | collective-permute-start | bytes 73736 | tf_op jit(solution)/shard_map/ppermute | solution.py:454
  261.7 15.1 %collective-permute-start.37 = (bf16[256,1024]{1,0:T(8,128)(2,1)S(1)}, bf16[256,1024]{1,0:T(8,128)(2,1)S(1)}, u32[]{:S(2)}, u32[]{:S(2)}) collective-permute-start(bf16[256,1024]{1,0:T(8,128)(2,1)S(1)} %get-tuple-element.138.refs_0_), channel_id=1, source_target_pairs={{0,4},{4,0},{8,12},{12,8},{1,5},{5,1},{9,13},{13,9},{2,6},{6,2},{1... | collective-permute-start | bytes 1572872 | tf_op jit(solution)/shard_map/ppermute | solution.py:454
  270.4 6.4 %collective-permute-start.38 = (bf16[256,1024]{1,0:T(8,128)(2,1)S(1)}, bf16[256,1024]{1,0:T(8,128)(2,1)S(1)}, u32[]{:S(2)}, u32[]{:S(2)}) collective-permute-start(bf16[256,1024]{1,0:T(8,128)(2,1)S(1)} %get-tuple-element.139.refs_1_), channel_id=1, source_target_pairs={{0,4},{4,0},{8,12},{12,8},{1,5},{5,1},{9,13},{13,9},{2,6},{6,2},{1... | collective-permute-start | bytes 1572872 | tf_op jit(solution)/shard_map/ppermute | solution.py:454
  271.0 8.8 %collective-permute-start.32 = (bf16[256,1024]{1,0:T(8,128)(2,1)S(1)}, bf16[256,1024]{1,0:T(8,128)(2,1)S(1)}, u32[]{:S(2)}, u32[]{:S(2)}) collective-permute-start(bf16[256,1024]{1,0:T(8,128)(2,1)S(1)} %get-tuple-element.135.refs_0_), channel_id=1, source_target_pairs={{0,4},{4,0},{8,12},{12,8},{1,5},{5,1},{9,13},{13,9},{2,6},{6,2},{1... | collective-permute-start | bytes 1572872 | tf_op jit(solution)/shard_map/ppermute | solution.py:454
  271.5 8.3 %collective-permute-start.33 = (bf16[256,1024]{1,0:T(8,128)(2,1)S(1)}, bf16[256,1024]{1,0:T(8,128)(2,1)S(1)}, u32[]{:S(2)}, u32[]{:S(2)}) collective-permute-start(bf16[256,1024]{1,0:T(8,128)(2,1)S(1)} %get-tuple-element.137.refs_1_), channel_id=1, source_target_pairs={{0,4},{4,0},{8,12},{12,8},{1,5},{5,1},{9,13},{13,9},{2,6},{6,2},{1... | collective-permute-start | bytes 1572872 | tf_op jit(solution)/shard_map/ppermute | solution.py:454
  271.6 2.3 collective-permute-start.35
  (3 other events, 8.3 us)

commit v6 on v5

--- a/solution.py
+++ b/solution.py
@@ -276,42 +276,49 @@
     return list(outs[:count]), [outs[count]]
 
 
-def halve_kernel(half, more, *refs):
+def halve_kernel(half, cut, more, *refs):
     keep = refs[: 2 * half] if half > 1 else [None, refs[0]]
     got = refs[len(keep) : len(keep) + 2 * half] if half > 1 else [None, refs[1]]
     outs = refs[(4 * half if half > 1 else 2) + more :]
     for k in range(half):
         value = keep[2 * k + 1][...] + got[2 * k + 1][...].astype(jnp.float32)
-        outs[k][...] = value.astype(jnp.bfloat16)
+        value = value.astype(jnp.bfloat16)
+        size = value.shape[0] // cut
+        for n in range(cut):
+            outs[k * cut + n][...] = value[n * size : (n + 1) * size]
         if half > 1:
-            outs[half + k][...] = keep[2 * k][...] + got[2 * k][...].astype(jnp.float32)
+            outs[half * cut + k][...] = keep[2 * k][...] + got[2 * k][...].astype(jnp.float32)
     outs[-1][...] = jnp.zeros(TOKEN, jnp.float32)
 
 
-def halve(keep, got, after):
+def halve(keep, got, cut, after):
     half = len(keep) // 2
     rows, width = keep[0].shape
     operands = [*keep, *got] if half > 1 else [keep[1], got[1]]
-    flat = pl.BlockSpec((rows, width), lambda i: (0, 0))
-    out_shape = [jax.ShapeDtypeStruct((rows, width), jnp.bfloat16)] * half
+    flat = lambda n: pl.BlockSpec((n, width), lambda i: (0, 0))
+    out_specs = [flat(rows // cut)] * (half * cut)
+    out_shape = [jax.ShapeDtypeStruct((rows // cut, width), jnp.bfloat16)] * (half * cut)
     if half > 1:
+        out_specs += [flat(rows)] * half
         out_shape += [jax.ShapeDtypeStruct((rows, width), jnp.float32)] * half
     outs = pl.pallas_call(
-        functools.partial(halve_kernel, half, len(after)),
+        functools.partial(halve_kernel, half, cut, len(after)),
         grid=(1,),
-        in_specs=[flat] * len(operands) + [token_spec()] * len(after),
-        out_specs=[flat] * len(out_shape) + [token_spec()],
+        in_specs=[flat(rows)] * len(operands) + [token_spec()] * len(after),
+        out_specs=out_specs + [token_spec()],
         out_shape=out_shape + [TOKEN_SHAPE],
         compiler_params=params(),
         cost_estimate=pl.CostEstimate(flops=1, bytes_accessed=1, transcendentals=0),
         name="halve",
     )(*operands, *after)
-    return outs[:half], outs[half:-1], outs[-1]
-
-
-def stream_kernel(more, keep, first, last, signs, matrix, residual, *refs):
-    stream, chunk, squares = refs[more:]
-    total = keep[...] + first[...].astype(jnp.float32) + last[...].astype(jnp.float32)
+    return outs[: half * cut], outs[half * cut : -1], outs[-1]
+
+
+def stream_kernel(cut, more, keep, first, *refs):
+    last = jnp.concatenate([part[...] for part in refs[:cut]], axis=0)
+    signs, matrix, residual = refs[cut : cut + 3]
+    stream, chunk, squares = refs[cut + 3 + more :]
+    total = keep[...] + first[...].astype(jnp.float32) + last.astype(jnp.float32)
     total = total * signs[...].astype(jnp.float32)
     rows, width = total.shape
     turn = matrix[...]
@@ -341,8 +348,11 @@
     rows, width = keep.shape
     place = start // rows
     line = pl.BlockSpec((rows, width), lambda i: (place, 0))
-    operands = [keep, first, last, signs, matrix, residual]
-    specs = [pl.BlockSpec((rows, width), lambda i: (0, 0))] * 3 + [
+    cut = len(last)
+    flat = lambda n: pl.BlockSpec((n, width), lambda i: (0, 0))
+    operands = [keep, first, *last, signs, matrix, residual]
+    specs = [flat(rows)] * 2 + [flat(rows // cut)] * cut
+    specs += [
         pl.BlockSpec((1, width), lambda i: (0, 0)),
         pl.BlockSpec((128, 128), lambda i: (0, 0)),
         line,
@@ -355,7 +365,7 @@
     operands += after
     specs += [token_spec()] * len(after)
     return pl.pallas_call(
-        functools.partial(stream_kernel, len(aliases) + len(after)),
+        functools.partial(stream_kernel, cut, len(aliases) + len(after)),
         grid=(1,),
         in_specs=specs,
         out_specs=[
@@ -375,38 +385,34 @@
     )(*operands)
 
 
-def norm_kernel(places, more, info, *refs):
+def norm_kernel(places, sums, more, info, *refs):
     tp = len(places)
     pieces = refs[:tp]
-    first, second, gain = refs[tp : tp + 3]
-    out, token, scale = refs[tp + 3 + more :]
-    step = pl.program_id(0)
-
-    @pl.when(step == 0)
-    def _():
-        inverse = lax.rsqrt((first[...] + second[...]) / D + 1e-05)
-        scale[...] = jnp.transpose(inverse)
-        token[...] = jnp.zeros(TOKEN, jnp.float32)
-
+    squares = refs[tp : tp + sums]
+    gain = refs[tp + sums]
+    out, token = refs[tp + sums + 1 + more :]
+    token[...] = jnp.zeros(TOKEN, jnp.float32)
+    total = 0.0
+    for values in squares:
+        for first in range(0, values.shape[0], 8):
+            total = total + values[first : first + 8]
+    inverse = lax.rsqrt(total / D + 1e-05)
     rows, width = pieces[0].shape
-    factor = scale[pl.ds(pl.multiple_of(step * rows, rows), rows), 0:1]
+    scale = jnp.transpose(inverse)[0:rows, 0:1]
     for e, piece in zip(places, pieces):
         at = pl.ds(pl.multiple_of((info[0] ^ e) * width, width), width)
-        value = piece[...].astype(jnp.float32) * factor * gain[:, at]
+        value = piece[...].astype(jnp.float32) * scale * gain[:, at]
         out[:, at] = value.astype(jnp.bfloat16)
 
 
-def norm_rows(info, pieces, squares, column, gain, so_far, start, all_rows, after):
+def norm_rows(info, pieces, squares, gain, so_far, start, all_rows, after):
     tp = len(pieces)
     rows, width = pieces[0][1].shape
-    tiles = 4 if rows % 64 == 0 else 1
-    tile = rows // tiles
-    place = start // tile
-    small = pl.BlockSpec((8, lanes(rows)), lambda i, s: (0, column))
+    place = start // rows
     operands = [piece for _, piece in pieces] + [*squares, gain]
     specs = (
-        [pl.BlockSpec((tile, width), lambda i, s: (i, 0))] * tp
-        + [small] * 2
+        [pl.BlockSpec((rows, width), lambda i, s: (0, 0))] * tp
+        + [pl.BlockSpec(values.shape, lambda i, s: (0, 0)) for values in squares]
         + [pl.BlockSpec((1, tp * width), lambda i, s: (0, 0))]
     )
     aliases = {}
@@ -416,17 +422,17 @@
         specs.append(anywhere())
     operands += after
     specs += [token_spec()] * len(after)
+    more = len(aliases) + len(after)
     return pl.pallas_call(
-        functools.partial(norm_kernel, [e for e, _ in pieces], len(aliases) + len(after)),
+        functools.partial(norm_kernel, [e for e, _ in pieces], len(squares), more),
         grid_spec=pltpu.PrefetchScalarGridSpec(
             num_scalar_prefetch=1,
-            grid=(tiles,),
+            grid=(1,),
             in_specs=specs,
             out_specs=[
-                pl.BlockSpec((tile, tp * width), lambda i, s: (place + i, 0)),
+                pl.BlockSpec((rows, tp * width), lambda i, s: (place, 0)),
                 token_spec(),
             ],
-            scratch_shapes=[pltpu.VMEM((lanes(rows), 8), jnp.float32)],
         ),
         out_shape=[jax.ShapeDtypeStruct((all_rows, tp * width), jnp.bfloat16), TOKEN_SHAPE],
         input_output_aliases=aliases,
@@ -471,15 +477,15 @@
     def begin_sums(u, sums):
         terms[u] = [sums[: tp // 2], [swap(value, bits[0]) for value in sums[tp // 2 :]]]
 
-    def halve_sums(u, after):
+    def halve_sums(u, after, cut=1):
         keep, got = terms[u]
         for bit in bits[1:]:
-            send, kept, token = halve(keep, got, after)
+            send, kept, token = halve(keep, got, cut if bit == bits[-1] else 1, after)
             after = [token]
             arrived = [swap(value, bit) for value in send]
             if kept:
                 keep, got = kept, arrived
-        terms[u] = [keep[0], got[0], arrived[0]]
+        terms[u] = [keep[0], got[0], arrived]
         return after
 
     def finish(u, after):
@@ -512,21 +518,14 @@
 
     normed = [None]
 
-    def normalise(us, totals, after):
-        for n, u in enumerate(us):
-            normed[0], token = norm_rows(
-                info,
-                pieces[u],
-                totals,
-                sum(lanes(sizes[b]) for b in us[:n]) // lanes(sizes[u]),
-                gain,
-                normed[0],
-                starts[u],
-                rows,
-                after,
-            )
-            after = [token]
-        return after
+    def normalise(u, totals, after):
+        normed[0], token = norm_rows(
+            info, pieces[u], totals, gain, normed[0], starts[u], rows, after
+        )
+        return [token]
+
+    def gather_squares(u):
+        return [lax.all_gather(squares[u], ("sub", "tp"), axis=0, tiled=True)]
 
     early, middle, late = [0, 1], list(range(2, sub - 1)), [sub - 1]
     bases, tables, base = {}, [], 1
@@ -591,19 +590,23 @@
     pass_on(2, sub - 1, sub - 1)
     parts, *token = matmul([1, 2], middle, parts, 0, False, token)
     token = finish(0, token)
+    sums_0 = gather_squares(0)
     *sums, token = matmul([1], late, parts, 0, True, token)
     begin_sums(1, sums)
     token = spread(0, [token])
-    token = halve_sums(1, token)
+    token = halve_sums(1, token, 2)
+    token = finish(1, token)
+    sums_1 = gather_squares(1)
     *sums, token = matmul([2], late, parts, sizes[1], True, token)
     begin_sums(2, sums)
-    token = finish(1, [token])
+    token = spread(1, [token])
     token = halve_sums(2, token)
     token = finish(2, token)
-    along = sum_along(jnp.concatenate([squares[u] for u in range(3)], axis=1))
-    spread(1, token)
-    spread(2, [along])
-    normalise([0, 1, 2], sum_across(along), token)
+    along = sum_along(squares[2])
+    token = normalise(0, sums_0, token)
+    token = normalise(1, sums_1, token)
+    spread(2, [along, *token])
+    normalise(2, sum_across(along), token)
     return (streams[0], normed[0])
 
 

time: 284 us -> 321 us (1.13)
  blocking collectives: 0 us -> 43.2 us
  waiting for transfers between devices: 103 us -> 94.2 us
    all_gather x0 -> x2, blocking collectives: none -> 43.2 us  [gather_squares(): return [lax.all_gather(squares[u], ('sub', 'tp'), axis=0, tiled=True)]]
    ppermute x3, waiting for transfers between devices: 8.77 us -> 0.01 us  [sum_along(): lax.ppermute(local, 'sub', [(i, (i + d) % sub) for i in range(sub)])]
    ppermute x20 -> x21, waiting for transfers between devices: 24 us -> 31.4 us  [swap(): return lax.ppermute(value, 'tp', [(i, i ^ d) for i in range(tp)])]
    ppermute x9, waiting for transfers between devices: 53.7 us -> 46.7 us  [onward(): lax.ppermute(pair[1], 'sub', [(i, i - 1) for i in range(1, sub - d + 1)])]
    ppermute x20 -> x21, starting transfers between devices: 11 us -> 10.8 us  [swap(): return lax.ppermute(value, 'tp', [(i, i ^ d) for i in range(tp)])]
  transfers between devices with their start and end apart: 41 -> 42, of which waited for: 14 -> 14; matrix products, arithmetic and copies ran while one was open for 2% -> 1% of each run, Pallas kernels for 44% -> 39%
where the time goes in v6:
time: 321 us; the launch traced here: 319 us
  Pallas kernels  126 us (39%)
  waiting for transfers between devices  94.2 us (29%)
  starting transfers between devices  45.9 us (14%)
  blocking collectives  43.2 us (13%)
  local copies, waits for them, and re-layouts  5.21 us (2%)
  other arithmetic  3.52 us (1%)
    pallas_call x6, Pallas kernels, matmul_stage(): pl.pallas_call(functools.partial(matmul_kernel, plan), grid_spec=pltpu.Pr...  105 us
    ppermute x9, waiting for transfers between devices, onward(): lax.ppermute(pair[1], 'sub', [(i, i - 1) for i in range(1, sub - d + 1)])  46.7 us
    all_gather x2, blocking collectives, gather_squares(): return [lax.all_gather(squares[u], ('sub', 'tp'), axis=0, tiled=True)]  43.2 us
    ppermute x21, waiting for transfers between devices, swap(): return lax.ppermute(value, 'tp', [(i, i ^ d) for i in range(tp)])  31.4 us
    ppermute x9, starting transfers between devices, onward(): lax.ppermute(pair[0], 'sub', [(i, i + 1) for i in range(d - 1, sub - 1)])  19.5 us
    ppermute x9, waiting for transfers between devices, onward(): lax.ppermute(pair[0], 'sub', [(i, i + 1) for i in range(d - 1, sub - 1)])  16.1 us
    ppermute x9, starting transfers between devices, onward(): lax.ppermute(pair[1], 'sub', [(i, i - 1) for i in range(1, sub - d + 1)])  11.8 us
    ppermute x21, starting transfers between devices, swap(): return lax.ppermute(value, 'tp', [(i, i ^ d) for i in range(tp)])  10.8 us
  transfers between devices with their start and end apart: 42, of which 14 were waited for; matrix products, arithmetic and copies ran while one was open for 1% of the time, Pallas kernels for 39%

profile of v6, /device:TPU:0, one launch (start us, length us, event | category | flops | bytes accessed | tf_op | source)
XLA Modules:
  0.0 319.4 jit_solution(6655630760751792055)
XLA Ops:
  0.7 3.3 %fusion.4.refs_0_ = bf16[256,2048]{1,0:T(8,128)(2,1)} fusion(bf16[768,2048]{1,0:T(8,128)(2,1)} %up.3, bf16[768,2048]{1,0:T(8,128)(2,1)} %gate.13), kind=kLoop, calls=%fused_computation.7 | loop fusion | flops 4194304 | bytes 3145728 | tf_op jit(solution)/shard_map/convert_element_type | solution.py:570
  4.0 6.1 %collective-permute-start = (bf16[256,2048]{1,0:T(8,128)(2,1)}, bf16[256,2048]{1,0:T(8,128)(2,1)}, u32[]{:S(2)}, u32[]{:S(2)}) collective-permute-start(bf16[256,2048]{1,0:T(8,128)(2,1)} %fusion.4.refs_0_), channel_id=1, source_target_pairs={{0,1},{1,2},{2,3},{4,5},{5,6},{6,7},{8,9},{9,10},{10,11},{12,13},{... | collective-permute-start | bytes 3145736 | tf_op jit(solution)/shard_map/ppermute | solution.py:463
  10.1 1.3 collective-permute-start.1
  11.4 3.6 %hidden_rows.2 = (bf16[256,2048]{1,0:T(8,128)(2,1)}, f32[8,128]{1,0:T(8,128)S(1)}) custom-call(bf16[768,2048]{1,0:T(8,128)(2,1)S(1)} %copy-done.2, bf16[768,2048]{1,0:T(8,128)(2,1)} %up.3, bf16[256,2048]{1,0:T(8,128)(2,1)} %fusion.4.refs_0_), custom_call_target="tpu_custom_call" | custom-call | flops 1 | bytes 1 | tf_op jit(solution)/shard_map/hidden_rows/pallas_call | solution.py:67
  15.0 5.6 %collective-permute-start.6 = (bf16[256,2048]{1,0:T(8,128)(2,1)}, bf16[256,2048]{1,0:T(8,128)(2,1)}, u32[]{:S(2)}, u32[]{:S(2)}) collective-permute-start(bf16[256,2048]{1,0:T(8,128)(2,1)} %get-tuple-element.85.refs_0_), channel_id=1, source_target_pairs={{0,1},{1,2},{2,3},{4,5},{5,6},{6,7},{8,9},{9,10},{10,11},{12,13},{... | collective-permute-start | bytes 3145736 | tf_op jit(solution)/shard_map/ppermute | solution.py:463
  20.5 1.3 collective-permute-start.7
  22.6 2.8 gather_fusion
  25.4 7.5 %collective-permute-done.refs_0_ = bf16[256,2048]{1,0:T(8,128)(2,1)} collective-permute-done((bf16[256,2048]{1,0:T(8,128)(2,1)}, bf16[256,2048]{1,0:T(8,128)(2,1)}, u32[]{:S(2)}, u32[]{:S(2)}) %collective-permute-start) | collective-permute-done | bytes 1048608 | tf_op jit(solution)/shard_map/ppermute | solution.py:463
  32.9 5.4 %collective-permute-done.1.refs_1_ = bf16[256,2048]{1,0:T(8,128)(2,1)} collective-permute-done((bf16[256,2048]{1,0:T(8,128)(2,1)}, bf16[256,2048]{1,0:T(8,128)(2,1)}, u32[]{:S(2)}, u32[]{:S(2)}) %collective-permute-start.1) | collective-permute-done | bytes 1048608 | tf_op jit(solution)/shard_map/ppermute | solution.py:464
  38.3 3.0 hidden_rows.3
  41.3 2.6 collective-permute-start.4
  43.9 1.3 collective-permute-start.5
  45.2 1.7 collective-permute-start.2
  46.9 8.5 %collective-permute-done.6.refs_0_ = bf16[256,2048]{1,0:T(8,128)(2,1)} collective-permute-done((bf16[256,2048]{1,0:T(8,128)(2,1)}, bf16[256,2048]{1,0:T(8,128)(2,1)}, u32[]{:S(2)}, u32[]{:S(2)}) %collective-permute-start.6) | collective-permute-done | bytes 1048608 | tf_op jit(solution)/shard_map/ppermute | solution.py:463
  55.4 1.3 collective-permute-start.3
  57.5 19.8 %matmul_stage.6 = (f32[4,256,1024]{2,1,0:T(8,128)}, f32[8,128]{1,0:T(8,128)S(1)}) custom-call(s32[19]{0:T(128)S(1)} %pad_add_fusion.info, bf16[256,2048]{1,0:T(8,128)(2,1)} %fusion.4.refs_0_, bf16[256,2048]{1,0:T(8,128)(2,1)} %get-tuple-element.77.refs_1_, bf16[256,2048]{1,0:T(8,128)(2,1)} %get-tuple-element.78.refs_2_, bf16[8192,4096]{1,0:T(8,128)(2,1)} %refs_2_.3, ...), custom_call_target="tpu_custom_call" | custom-call | flops 1 | bytes 1 | tf_op jit(solution)/shard_map/matmul_stage/pallas_call | solution.py:237
  78.6 1.3 collective-permute-start.9
  79.9 3.4 %collective-permute-done.5.refs_3_ = bf16[256,2048]{1,0:T(8,128)(2,1)} collective-permute-done((bf16[256,2048]{1,0:T(8,128)(2,1)}, bf16[256,2048]{1,0:T(8,128)(2,1)}, u32[]{:S(2)}, u32[]{:S(2)}) %collective-permute-start.5) | collective-permute-done | bytes 1048608 | tf_op jit(solution)/shard_map/ppermute | solution.py:464
  83.3 22.5 %collective-permute-done.3.refs_1_ = bf16[256,2048]{1,0:T(8,128)(2,1)} collective-permute-done((bf16[256,2048]{1,0:T(8,128)(2,1)}, bf16[256,2048]{1,0:T(8,128)(2,1)}, u32[]{:S(2)}, u32[]{:S(2)}) %collective-permute-start.3) | collective-permute-done | bytes 1048608 | tf_op jit(solution)/shard_map/ppermute | solution.py:464
  106.5 1.3 collective-permute-start.13
  107.8 27.0 %matmul_stage.7 = (f32[4,512,1024]{2,1,0:T(8,128)}, f32[8,128]{1,0:T(8,128)S(1)}) custom-call(s32[19]{0:T(128)S(1)} %pad_add_fusion.info, bf16[256,2048]{1,0:T(8,128)(2,1)} %get-tuple-element.85.refs_0_, bf16[256,2048]{1,0:T(8,128)(2,1)} %get-tuple-element.80.refs_1_, bf16[256,2048]{1,0:T(8,128)(2,1)} %get-tuple-element.86.refs_2_, ...), custom_call_target="tpu_custom_call" | custom-call | flops 1 | bytes 1 | tf_op jit(solution)/shard_map/matmul_stage/pallas_call | solution.py:237
  135.6 1.3 collective-permute-start.11
  136.9 12.2 %collective-permute-done.13.refs_3_ = bf16[256,2048]{1,0:T(8,128)(2,1)S(1)} collective-permute-done((bf16[256,2048]{1,0:T(8,128)(2,1)}, bf16[256,2048]{1,0:T(8,128)(2,1)S(1)}, u32[]{:S(2)}, u32[]{:S(2)}) %collective-permute-start.13) | collective-permute-done | bytes 1048608 | tf_op jit(solution)/shard_map/ppermute | solution.py:464
  150.1 18.7 %matmul_stage.8 = (f32[256,1024]{1,0:T(8,128)S(1)}, f32[256,1024]{1,0:T(8,128)S(1)}, bf16[256,1024]{1,0:T(8,128)(2,1)S(1)}, bf16[256,1024]{1,0:T(8,128)(2,1)S(1)}, f32[8,128]{1,0:T(8,128)S(1)}) custom-call(s32[19]{0:T(128)S(1)} %pad_add_fusion.info, bf16[256,2048]{1,0:T(8,128)(2,1)} %get-tuple-element.92.refs_0_, ...), custom_call_target="tpu_custom_call" | custom-call | flops 1 | bytes 1 | tf_op jit(solution)/shard_map/matmul_stage/pallas_call | solution.py:237
  169.6 1.3 collective-permute-start.18
  171.6 1.6 collective-permute-start.20
  173.9 1.5 collective-permute-start.16
  175.5 16.4 %matmul_stage.9 = (f32[4,512,1024]{2,1,0:T(8,128)}, f32[8,128]{1,0:T(8,128)S(1)}) custom-call(s32[19]{0:T(128)S(1)} %pad_add_fusion.info, bf16[256,2048]{1,0:T(8,128)(2,1)S(1)} %get-tuple-element.105.refs_0_, bf16[256,2048]{1,0:T(8,128)(2,1)S(1)} %get-tuple-element.103.refs_1_, bf16[256,2048]{1,0:T(8,128)(2,1)S(1)} %get-tuple-element.106.refs_2_, ...), custom_call_target="tpu_custom_call" | custom-call | flops 1 | bytes 1 | tf_op jit(solution)/shard_map/matmul_stage/pallas_call | solution.py:237
  192.0 1.8 stream_rows.3
  194.4 3.2 %collective-permute-done.18.refs_1_ = bf16[256,2048]{1,0:T(8,128)(2,1)} collective-permute-done((bf16[256,2048]{1,0:T(8,128)(2,1)S(1)}, bf16[256,2048]{1,0:T(8,128)(2,1)}, u32[]{:S(2)}, u32[]{:S(2)}) %collective-permute-start.18) | collective-permute-done | bytes 1048608 | tf_op jit(solution)/shard_map/ppermute | solution.py:464
  197.6 12.3 %matmul_stage.10 = (f32[256,1024]{1,0:T(8,128)S(1)}, f32[256,1024]{1,0:T(8,128)S(1)}, bf16[256,1024]{1,0:T(8,128)(2,1)S(1)}, bf16[256,1024]{1,0:T(8,128)(2,1)S(1)}, f32[8,128]{1,0:T(8,128)S(1)}) custom-call(s32[19]{0:T(128)S(1)} %pad_add_fusion.info, bf16[256,2048]{1,0:T(8,128)(2,1)S(1)} %collective-permute-done.17.refs_0_, ...), custom_call_target="tpu_custom_call" | custom-call | flops 1 | bytes 1 | tf_op jit(solution)/shard_map/matmul_stage/pallas_call | solution.py:237
  210.5 1.4 collective-permute-done.22.refs_1_
  211.9 1.6 collective-permute-start.24
  214.0 7.1 %collective-permute-done.24.refs_0_ = bf16[128,1024]{1,0:T(8,128)(2,1)S(1)} collective-permute-done((bf16[128,1024]{1,0:T(8,128)(2,1)S(1)}, bf16[128,1024]{1,0:T(8,128)(2,1)S(1)}, u32[]{:S(2)}, u32[]{:S(2)}) %collective-permute-start.24) | collective-permute-done | bytes 262176 | tf_op jit(solution)/shard_map/ppermute | solution.py:460
  221.2 4.8 %collective-permute-done.25.refs_1_ = bf16[128,1024]{1,0:T(8,128)(2,1)S(1)} collective-permute-done((bf16[128,1024]{1,0:T(8,128)(2,1)S(1)}, bf16[128,1024]{1,0:T(8,128)(2,1)S(1)}, u32[]{:S(2)}, u32[]{:S(2)}) %collective-permute-start.25) | collective-permute-done | bytes 262176 | tf_op jit(solution)/shard_map/ppermute | solution.py:460
  226.0 1.5 stream_rows.4
  227.5 1.5 collective-permute-start.28
  229.1 11.1 %matmul_stage.11 = (f32[256,1024]{1,0:T(8,128)S(1)}, f32[256,1024]{1,0:T(8,128)S(1)}, bf16[256,1024]{1,0:T(8,128)(2,1)S(1)}, bf16[256,1024]{1,0:T(8,128)(2,1)S(1)}, f32[8,128]{1,0:T(8,128)S(1)}) custom-call(s32[19]{0:T(128)S(1)} %pad_add_fusion.info, bf16[256,2048]{1,0:T(8,128)(2,1)S(1)} %collective-permute-done.15.refs_0_, ...), custom_call_target="tpu_custom_call" | custom-call | flops 1 | bytes 1 | tf_op jit(solution)/shard_map/matmul_stage/pallas_call | solution.py:237
  240.7 1.4 collective-permute-done.27.refs_1_
  243.9 12.4 %collective-permute-done.29.refs_0_ = bf16[256,1024]{1,0:T(8,128)(2,1)S(1)} collective-permute-done((bf16[256,1024]{1,0:T(8,128)(2,1)S(1)}, bf16[256,1024]{1,0:T(8,128)(2,1)S(1)}, u32[]{:S(2)}, u32[]{:S(2)}) %collective-permute-start.29) | collective-permute-done | bytes 524320 | tf_op jit(solution)/shard_map/ppermute | solution.py:460
  256.3 1.5 stream_rows.5
  258.4 24.1 %all_gather.7.refs_4_ = f32[128,256]{1,0:T(8,128)S(1)} all-gather(f32[8,256]{1,0:T(8,128)S(1)} %get-tuple-element.116.refs_4_), channel_id=1, replica_groups=mesh['groups'=2,'tp'=4,'sub'=4] {'sub','tp'}, dimensions={0}, use_global_device_ids=true | all-gather | bytes 139264 | tf_op jit(solution)/shard_map/all_gather | solution.py:528
  282.6 3.8 %collective-permute-start.33 = (f32[8,256]{1,0:T(8,128)S(1)}, f32[8,256]{1,0:T(8,128)S(1)}, u32[]{:S(2)}, u32[]{:S(2)}) collective-permute-start(f32[8,256]{1,0:T(8,128)S(1)} %get-tuple-element.141.refs_6_), channel_id=1, source_target_pairs={{0,3},{1,0},{2,1},{3,2},{4,7},{5,4},{6,5},{7,6},{8,11},{9,8},{10,9... | collective-permute-start | bytes 24584 | tf_op jit(solution)/shard_map/ppermute | solution.py:511
  286.4 19.1 %all_gather.6.refs_4_ = f32[128,256]{1,0:T(8,128)S(1)} all-gather(f32[8,256]{1,0:T(8,128)S(1)} %get-tuple-element.128.refs_4_), channel_id=1, replica_groups=mesh['groups'=2,'tp'=4,'sub'=4] {'sub','tp'}, dimensions={0}, use_global_device_ids=true | all-gather | bytes 139264 | tf_op jit(solution)/shard_map/all_gather | solution.py:528
  305.5 2.6 norm_rows.3
  308.5 2.6 norm_rows.4
  312.5 3.1 collective-permute-done.40
  316.8 2.6 norm_rows.5
  (93 shorter events, 15.1 us)
Async XLA Ops:
  0.6 21.9 %copy-start = (bf16[768,1024]{1,0:T(8,128)(2,1)S(1)}, bf16[768,1024]{1,0:T(8,128)(2,1)}, u32[]{:S(2)}) copy-start(bf16[768,1024]{1,0:T(8,128)(2,1)} %param.11) | copy-start | bytes 4718596
  4.0 18.5 %copy-start.9 = (s32[768]{0:T(1024)S(1)}, s32[768]{0:T(1024)}, u32[]{:S(2)}) copy-start(s32[768]{0:T(1024)} %param.13) | copy-start | bytes 9220
  4.0 28.9 %collective-permute-start = (bf16[256,2048]{1,0:T(8,128)(2,1)}, bf16[256,2048]{1,0:T(8,128)(2,1)}, u32[]{:S(2)}, u32[]{:S(2)}) collective-permute-start(bf16[256,2048]{1,0:T(8,128)(2,1)} %fusion.4.refs_0_), channel_id=1, source_target_pairs={{0,1},{1,2},{2,3},{4,5},{5,6},{6,7},{8,9},{9,10},{10,11},{12,13},{... | collective-permute-start | bytes 3145736 | tf_op jit(solution)/shard_map/ppermute | solution.py:463
  10.1 28.3 %collective-permute-start.1 = (bf16[256,2048]{1,0:T(8,128)(2,1)}, bf16[256,2048]{1,0:T(8,128)(2,1)}, u32[]{:S(2)}, u32[]{:S(2)}) collective-permute-start(bf16[256,2048]{1,0:T(8,128)(2,1)} %fusion.4.refs_0_), channel_id=1, source_target_pairs={{1,0},{2,1},{3,2},{5,4},{6,5},{7,6},{9,8},{10,9},{11,10},{13,12},{... | collective-permute-start | bytes 3145736 | tf_op jit(solution)/shard_map/ppermute | solution.py:464
  15.0 40.4 %collective-permute-start.6 = (bf16[256,2048]{1,0:T(8,128)(2,1)}, bf16[256,2048]{1,0:T(8,128)(2,1)}, u32[]{:S(2)}, u32[]{:S(2)}) collective-permute-start(bf16[256,2048]{1,0:T(8,128)(2,1)} %get-tuple-element.85.refs_0_), channel_id=1, source_target_pairs={{0,1},{1,2},{2,3},{4,5},{5,6},{6,7},{8,9},{9,10},{10,11},{12,13},{... | collective-permute-start | bytes 3145736 | tf_op jit(solution)/shard_map/ppermute | solution.py:463
  20.5 56.7 %collective-permute-start.7 = (bf16[256,2048]{1,0:T(8,128)(2,1)}, bf16[256,2048]{1,0:T(8,128)(2,1)}, u32[]{:S(2)}, u32[]{:S(2)}) collective-permute-start(bf16[256,2048]{1,0:T(8,128)(2,1)} %get-tuple-element.85.refs_0_), channel_id=1, source_target_pairs={{1,0},{2,1},{3,2},{5,4},{6,5},{7,6},{9,8},{10,9},{11,10},{13,12},{... | collective-permute-start | bytes 3145736 | tf_op jit(solution)/shard_map/ppermute | solution.py:464
  25.4 13.0 %copy-start.3 = (bf16[768,2048]{1,0:T(8,128)(2,1)S(1)}, bf16[768,2048]{1,0:T(8,128)(2,1)}, u32[]{:S(2)}) copy-start(bf16[768,2048]{1,0:T(8,128)(2,1)} %gate.13) | copy-start | bytes 9437188
  41.3 37.3 %collective-permute-start.4 = (bf16[256,2048]{1,0:T(8,128)(2,1)}, bf16[256,2048]{1,0:T(8,128)(2,1)S(1)}, u32[]{:S(2)}, u32[]{:S(2)}) collective-permute-start(bf16[256,2048]{1,0:T(8,128)(2,1)} %get-tuple-element.80.refs_1_), channel_id=1, source_target_pairs={{0,1},{1,2},{2,3},{4,5},{5,6},{6,7},{8,9},{9,10},{10,11},{12,13},{... | collective-permute-start | bytes 3145736 | tf_op jit(solution)/shard_map/ppermute | solution.py:463
  43.9 39.4 %collective-permute-start.5 = (bf16[256,2048]{1,0:T(8,128)(2,1)}, bf16[256,2048]{1,0:T(8,128)(2,1)}, u32[]{:S(2)}, u32[]{:S(2)}) collective-permute-start(bf16[256,2048]{1,0:T(8,128)(2,1)} %get-tuple-element.80.refs_1_), channel_id=1, source_target_pairs={{1,0},{2,1},{3,2},{5,4},{6,5},{7,6},{9,8},{10,9},{11,10},{13,12},{... | collective-permute-start | bytes 3145736 | tf_op jit(solution)/shard_map/ppermute | solution.py:464
  45.2 38.1 %collective-permute-start.2 = (bf16[256,2048]{1,0:T(8,128)(2,1)}, bf16[256,2048]{1,0:T(8,128)(2,1)}, u32[]{:S(2)}, u32[]{:S(2)}) collective-permute-start(bf16[256,2048]{1,0:T(8,128)(2,1)} %get-tuple-element.77.refs_1_), channel_id=1, source_target_pairs={{1,2},{2,3},{5,6},{6,7},{9,10},{10,11},{13,14},{14,15},{17,18},{18... | collective-permute-start | bytes 3145736 | tf_op jit(solution)/shard_map/ppermute | solution.py:463
  55.4 50.4 %collective-permute-start.3 = (bf16[256,2048]{1,0:T(8,128)(2,1)}, bf16[256,2048]{1,0:T(8,128)(2,1)}, u32[]{:S(2)}, u32[]{:S(2)}) collective-permute-start(bf16[256,2048]{1,0:T(8,128)(2,1)} %get-tuple-element.78.refs_2_), channel_id=1, source_target_pairs={{1,0},{2,1},{5,4},{6,5},{9,8},{10,9},{13,12},{14,13},{17,16},{18,1... | collective-permute-start | bytes 3145736 | tf_op jit(solution)/shard_map/ppermute | solution.py:464
  77.9 57.0 %collective-permute-start.8 = (bf16[256,2048]{1,0:T(8,128)(2,1)}, bf16[256,2048]{1,0:T(8,128)(2,1)S(1)}, u32[]{:S(2)}, u32[]{:S(2)}) collective-permute-start(bf16[256,2048]{1,0:T(8,128)(2,1)} %get-tuple-element.86.refs_2_), channel_id=1, source_target_pairs={{1,2},{2,3},{5,6},{6,7},{9,10},{10,11},{13,14},{14,15},{17,18},{18... | collective-permute-start | bytes 3145736 | tf_op jit(solution)/shard_map/ppermute | solution.py:463
  78.6 56.2 %collective-permute-start.9 = (bf16[256,2048]{1,0:T(8,128)(2,1)}, bf16[256,2048]{1,0:T(8,128)(2,1)S(1)}, u32[]{:S(2)}, u32[]{:S(2)}) collective-permute-start(bf16[256,2048]{1,0:T(8,128)(2,1)} %get-tuple-element.87.refs_4_), channel_id=1, source_target_pairs={{1,0},{2,1},{5,4},{6,5},{9,8},{10,9},{13,12},{14,13},{17,16},{18,1... | collective-permute-start | bytes 3145736 | tf_op jit(solution)/shard_map/ppermute | solution.py:464
  105.8 31.1 %collective-permute-start.12 = (bf16[256,2048]{1,0:T(8,128)(2,1)}, bf16[256,2048]{1,0:T(8,128)(2,1)S(1)}, u32[]{:S(2)}, u32[]{:S(2)}) collective-permute-start(bf16[256,2048]{1,0:T(8,128)(2,1)} %get-tuple-element.92.refs_0_), channel_id=1, source_target_pairs={{2,3},{6,7},{10,11},{14,15},{18,19},{22,23},{26,27},{30,31}} | collective-permute-start | bytes 3145736 | tf_op jit(solution)/shard_map/ppermute | solution.py:463
  106.5 42.6 %collective-permute-start.13 = (bf16[256,2048]{1,0:T(8,128)(2,1)}, bf16[256,2048]{1,0:T(8,128)(2,1)S(1)}, u32[]{:S(2)}, u32[]{:S(2)}) collective-permute-start(bf16[256,2048]{1,0:T(8,128)(2,1)} %get-tuple-element.93.refs_1_), channel_id=1, source_target_pairs={{1,0},{5,4},{9,8},{13,12},{17,16},{21,20},{25,24},{29,28}} | collective-permute-start | bytes 3145736 | tf_op jit(solution)/shard_map/ppermute | solution.py:464
  134.9 36.7 %collective-permute-start.10 = (bf16[256,2048]{1,0:T(8,128)(2,1)S(1)}, bf16[256,2048]{1,0:T(8,128)(2,1)S(1)}, u32[]{:S(2)}, u32[]{:S(2)}) collective-permute-start(bf16[256,2048]{1,0:T(8,128)(2,1)S(1)} %get-tuple-element.90), channel_id=1, source_target_pairs={{1,2},{2,3},{5,6},{6,7},{9,10},{10,11},{13,14},{14,15},{17,18},{18... | collective-permute-start | bytes 3145736 | tf_op jit(solution)/shard_map/ppermute | solution.py:463
  135.6 37.6 %collective-permute-start.11 = (bf16[256,2048]{1,0:T(8,128)(2,1)}, bf16[256,2048]{1,0:T(8,128)(2,1)S(1)}, u32[]{:S(2)}, u32[]{:S(2)}) collective-permute-start(bf16[256,2048]{1,0:T(8,128)(2,1)} %get-tuple-element.91), channel_id=1, source_target_pairs={{1,0},{2,1},{5,4},{6,5},{9,8},{10,9},{13,12},{14,13},{17,16},{18,1... | collective-permute-start | bytes 3145736 | tf_op jit(solution)/shard_map/ppermute | solution.py:464
  136.9 12.2 %copy-start.7 = (bf16[256,2048]{1,0:T(8,128)(2,1)}, bf16[256,2048]{1,0:T(8,128)(2,1)S(1)}, u32[]{:S(2)}) copy-start(bf16[256,2048]{1,0:T(8,128)(2,1)S(1)} %collective-permute-done.12.refs_2_) | copy-start | bytes 3145732
  168.8 2.1 collective-permute-start.14
  168.9 25.5 %collective-permute-start.17 = (bf16[256,2048]{1,0:T(8,128)(2,1)S(1)}, bf16[256,2048]{1,0:T(8,128)(2,1)S(1)}, u32[]{:S(2)}, u32[]{:S(2)}) collective-permute-start(bf16[256,2048]{1,0:T(8,128)(2,1)S(1)} %get-tuple-element.105.refs_0_), channel_id=1, source_target_pairs={{2,3},{6,7},{10,11},{14,15},{18,19},{22,23},{26,27},{30,31}} | collective-permute-start | bytes 3145736 | tf_op jit(solution)/shard_map/ppermute | solution.py:463
  169.6 28.0 %collective-permute-start.18 = (bf16[256,2048]{1,0:T(8,128)(2,1)S(1)}, bf16[256,2048]{1,0:T(8,128)(2,1)}, u32[]{:S(2)}, u32[]{:S(2)}) collective-permute-start(bf16[256,2048]{1,0:T(8,128)(2,1)S(1)} %get-tuple-element.106.refs_2_), channel_id=1, source_target_pairs={{1,0},{5,4},{9,8},{13,12},{17,16},{21,20},{25,24},{29,28}} | collective-permute-start | bytes 3145736 | tf_op jit(solution)/shard_map/ppermute | solution.py:464
  170.9 3.0 collective-permute-start.19
  171.6 20.3 %collective-permute-start.20 = (bf16[256,1024]{1,0:T(8,128)(2,1)S(1)}, bf16[256,1024]{1,0:T(8,128)(2,1)S(1)}, u32[]{:S(2)}, u32[]{:S(2)}) collective-permute-start(bf16[256,1024]{1,0:T(8,128)(2,1)S(1)} %get-tuple-element.112), channel_id=1, source_target_pairs={{0,8},{4,12},{8,0},{12,4},{1,9},{5,13},{9,1},{13,5},{2,10},{6,14},... | collective-permute-start | bytes 1572872 | tf_op jit(solution)/shard_map/ppermute | solution.py:460
  173.2 55.9 %collective-permute-start.15 = (bf16[256,2048]{1,0:T(8,128)(2,1)S(1)}, bf16[256,2048]{1,0:T(8,128)(2,1)S(1)}, u32[]{:S(2)}, u32[]{:S(2)}) collective-permute-start(bf16[256,2048]{1,0:T(8,128)(2,1)S(1)} %get-tuple-element.103.refs_1_), channel_id=1, source_target_pairs={{2,3},{6,7},{10,11},{14,15},{18,19},{22,23},{26,27},{30,31}} | collective-permute-start | bytes 3145736 | tf_op jit(solution)/shard_map/ppermute | solution.py:463
  173.9 55.2 %collective-permute-start.16 = (bf16[256,2048]{1,0:T(8,128)(2,1)S(1)}, bf16[256,2048]{1,0:T(8,128)(2,1)S(1)}, u32[]{:S(2)}, u32[]{:S(2)}) collective-permute-start(bf16[256,2048]{1,0:T(8,128)(2,1)S(1)} %get-tuple-element.104.refs_3_), channel_id=1, source_target_pairs={{1,0},{5,4},{9,8},{13,12},{17,16},{21,20},{25,24},{29,28}} | collective-permute-start | bytes 3145736 | tf_op jit(solution)/shard_map/ppermute | solution.py:464
  175.5 16.5 %copy-start.5 = (f32[256,1024]{1,0:T(8,128)S(1)}, f32[256,1024]{1,0:T(8,128)}, u32[]{:S(2)}) copy-start(f32[256,1024]{1,0:T(8,128)} %copy-done.4) | copy-start | bytes 3145732
  193.8 16.7 %collective-permute-start.23 = (bf16[256,1024]{1,0:T(8,128)(2,1)S(1)}, bf16[256,1024]{1,0:T(8,128)(2,1)S(1)}, u32[]{:S(2)}, u32[]{:S(2)}) collective-permute-start(bf16[256,1024]{1,0:T(8,128)(2,1)S(1)} %get-tuple-element.121.refs_0_), channel_id=1, source_target_pairs={{0,8},{4,12},{8,0},{12,4},{1,9},{5,13},{9,1},{13,5},{2,10},{6,14},... | collective-permute-start | bytes 1572872 | tf_op jit(solution)/shard_map/ppermute | solution.py:460
  209.9 2.0 collective-permute-start.22
  210.0 4.1 %collective-permute-start.21 = (bf16[256,1024]{1,0:T(8,128)(2,1)S(1)}, bf16[256,1024]{1,0:T(8,128)(2,1)S(1)}, u32[]{:S(2)}, u32[]{:S(2)}) collective-permute-start(bf16[256,1024]{1,0:T(8,128)(2,1)S(1)} %get-tuple-element.118), channel_id=1, source_target_pairs={{0,4},{4,0},{8,12},{12,8},{1,5},{5,1},{9,13},{13,9},{2,6},{6,2},{1... | collective-permute-start | bytes 1572872 | tf_op jit(solution)/shard_map/ppermute | solution.py:460
  211.9 9.2 %collective-permute-start.24 = (bf16[128,1024]{1,0:T(8,128)(2,1)S(1)}, bf16[128,1024]{1,0:T(8,128)(2,1)S(1)}, u32[]{:S(2)}, u32[]{:S(2)}) collective-permute-start(bf16[128,1024]{1,0:T(8,128)(2,1)S(1)} %get-tuple-element.124), channel_id=1, source_target_pairs={{0,8},{4,12},{8,0},{12,4},{1,9},{5,13},{9,1},{13,5},{2,10},{6,14},... | collective-permute-start | bytes 786440 | tf_op jit(solution)/shard_map/ppermute | solution.py:460
  213.5 12.4 %collective-permute-start.25 = (bf16[128,1024]{1,0:T(8,128)(2,1)S(1)}, bf16[128,1024]{1,0:T(8,128)(2,1)S(1)}, u32[]{:S(2)}, u32[]{:S(2)}) collective-permute-start(bf16[128,1024]{1,0:T(8,128)(2,1)S(1)} %get-tuple-element.125), channel_id=1, source_target_pairs={{0,8},{4,12},{8,0},{12,4},{1,9},{5,13},{9,1},{13,5},{2,10},{6,14},... | collective-permute-start | bytes 786440 | tf_op jit(solution)/shard_map/ppermute | solution.py:460
  227.5 13.2 %collective-permute-start.28 = (bf16[256,1024]{1,0:T(8,128)(2,1)S(1)}, bf16[256,1024]{1,0:T(8,128)(2,1)S(1)}, u32[]{:S(2)}, u32[]{:S(2)}) collective-permute-start(bf16[256,1024]{1,0:T(8,128)(2,1)S(1)} %get-tuple-element.133.refs_0_), channel_id=1, source_target_pairs={{0,8},{4,12},{8,0},{12,4},{1,9},{5,13},{9,1},{13,5},{2,10},{6,14},... | collective-permute-start | bytes 1572872 | tf_op jit(solution)/shard_map/ppermute | solution.py:460
  240.2 2.0 collective-permute-start.27
  240.2 3.1 collective-permute-start.26
  242.2 14.0 %collective-permute-start.29 = (bf16[256,1024]{1,0:T(8,128)(2,1)S(1)}, bf16[256,1024]{1,0:T(8,128)(2,1)S(1)}, u32[]{:S(2)}, u32[]{:S(2)}) collective-permute-start(bf16[256,1024]{1,0:T(8,128)(2,1)S(1)} %get-tuple-element.136), channel_id=1, source_target_pairs={{0,8},{4,12},{8,0},{12,4},{1,9},{5,13},{9,1},{13,5},{2,10},{6,14},... | collective-permute-start | bytes 1572872 | tf_op jit(solution)/shard_map/ppermute | solution.py:460
  242.8 39.6 %collective-permute-start.36 = (bf16[256,1024]{1,0:T(8,128)(2,1)S(1)}, bf16[256,1024]{1,0:T(8,128)(2,1)S(1)}, u32[]{:S(2)}, u32[]{:S(2)}) collective-permute-start(bf16[256,1024]{1,0:T(8,128)(2,1)S(1)} %get-tuple-element.121.refs_0_), channel_id=1, source_target_pairs={{0,4},{4,0},{8,12},{12,8},{1,5},{5,1},{9,13},{13,9},{2,6},{6,2},{1... | collective-permute-start | bytes 1572872 | tf_op jit(solution)/shard_map/ppermute | solution.py:460
  242.8 39.6 %collective-permute-start.37 = (bf16[256,1024]{1,0:T(8,128)(2,1)S(1)}, bf16[256,1024]{1,0:T(8,128)(2,1)S(1)}, u32[]{:S(2)}, u32[]{:S(2)}) collective-permute-start(bf16[256,1024]{1,0:T(8,128)(2,1)S(1)} %get-tuple-element.143.refs_1_), channel_id=1, source_target_pairs={{0,4},{4,0},{8,12},{12,8},{1,5},{5,1},{9,13},{13,9},{2,6},{6,2},{1... | collective-permute-start | bytes 1572872 | tf_op jit(solution)/shard_map/ppermute | solution.py:460
  243.3 39.2 %collective-permute-start.34 = (bf16[256,1024]{1,0:T(8,128)(2,1)S(1)}, bf16[256,1024]{1,0:T(8,128)(2,1)S(1)}, u32[]{:S(2)}, u32[]{:S(2)}) collective-permute-start(bf16[256,1024]{1,0:T(8,128)(2,1)S(1)} %get-tuple-element.133.refs_0_), channel_id=1, source_target_pairs={{0,4},{4,0},{8,12},{12,8},{1,5},{5,1},{9,13},{13,9},{2,6},{6,2},{1... | collective-permute-start | bytes 1572872 | tf_op jit(solution)/shard_map/ppermute | solution.py:460
  243.3 64.8 %collective-permute-start.35 = (bf16[256,1024]{1,0:T(8,128)(2,1)S(1)}, bf16[256,1024]{1,0:T(8,128)(2,1)S(1)}, u32[]{:S(2)}, u32[]{:S(2)}) collective-permute-start(bf16[256,1024]{1,0:T(8,128)(2,1)S(1)} %get-tuple-element.142.refs_1_), channel_id=1, source_target_pairs={{0,4},{4,0},{8,12},{12,8},{1,5},{5,1},{9,13},{13,9},{2,6},{6,2},{1... | collective-permute-start | bytes 1572872 | tf_op jit(solution)/shard_map/ppermute | solution.py:460
  256.3 49.2 %copy-start.6 = (f32[4096]{0:T(1024)S(1)}, f32[4096]{0:T(1024)}, u32[]{:S(2)}) copy-start(f32[4096]{0:T(1024)} %param.14) | copy-start | bytes 49156
  257.8 53.4 %collective-permute-start.30 = (bf16[256,1024]{1,0:T(8,128)(2,1)S(1)}, bf16[256,1024]{1,0:T(8,128)(2,1)S(1)}, u32[]{:S(2)}, u32[]{:S(2)}) collective-permute-start(bf16[256,1024]{1,0:T(8,128)(2,1)S(1)} %get-tuple-element.140.refs_0_), channel_id=1, source_target_pairs={{0,8},{4,12},{8,0},{12,4},{1,9},{5,13},{9,1},{13,5},{2,10},{6,14},... | collective-permute-start | bytes 1572872 | tf_op jit(solution)/shard_map/ppermute | solution.py:460
  282.5 28.7 %collective-permute-start.31 = (f32[8,256]{1,0:T(8,128)S(1)}, f32[8,256]{1,0:T(8,128)S(1)}, u32[]{:S(2)}, u32[]{:S(2)}) collective-permute-start(f32[8,256]{1,0:T(8,128)S(1)} %get-tuple-element.141.refs_6_), channel_id=1, source_target_pairs={{0,1},{1,2},{2,3},{3,0},{4,5},{5,6},{6,7},{7,4},{8,9},{9,10},{10,1... | collective-permute-start | bytes 24584 | tf_op jit(solution)/shard_map/ppermute | solution.py:511
  282.5 28.7 %collective-permute-start.32 = (f32[8,256]{1,0:T(8,128)S(1)}, f32[8,256]{1,0:T(8,128)S(1)}, u32[]{:S(2)}, u32[]{:S(2)}) collective-permute-start(f32[8,256]{1,0:T(8,128)S(1)} %get-tuple-element.141.refs_6_), channel_id=1, source_target_pairs={{0,2},{1,3},{2,0},{3,1},{4,6},{5,7},{6,4},{7,5},{8,10},{9,11},{10,... | collective-permute-start | bytes 24584 | tf_op jit(solution)/shard_map/ppermute | solution.py:511
  282.6 28.6 %collective-permute-start.33 = (f32[8,256]{1,0:T(8,128)S(1)}, f32[8,256]{1,0:T(8,128)S(1)}, u32[]{:S(2)}, u32[]{:S(2)}) collective-permute-start(f32[8,256]{1,0:T(8,128)S(1)} %get-tuple-element.141.refs_6_), channel_id=1, source_target_pairs={{0,3},{1,0},{2,1},{3,2},{4,7},{5,4},{6,5},{7,6},{8,11},{9,8},{10,9... | collective-permute-start | bytes 24584 | tf_op jit(solution)/shard_map/ppermute | solution.py:511
  308.1 8.6 %collective-permute-start.38 = (bf16[256,1024]{1,0:T(8,128)(2,1)S(1)}, bf16[256,1024]{1,0:T(8,128)(2,1)S(1)}, u32[]{:S(2)}, u32[]{:S(2)}) collective-permute-start(bf16[256,1024]{1,0:T(8,128)(2,1)S(1)} %get-tuple-element.140.refs_0_), channel_id=1, source_target_pairs={{0,4},{4,0},{8,12},{12,8},{1,5},{5,1},{9,13},{13,9},{2,6},{6,2},{1... | collective-permute-start | bytes 1572872 | tf_op jit(solution)/shard_map/ppermute | solution.py:460
  311.8 5.0 %collective-permute-start.39 = (bf16[256,1024]{1,0:T(8,128)(2,1)S(1)}, bf16[256,1024]{1,0:T(8,128)(2,1)S(1)}, u32[]{:S(2)}, u32[]{:S(2)}) collective-permute-start(bf16[256,1024]{1,0:T(8,128)(2,1)S(1)} %get-tuple-element.147.refs_1_), channel_id=1, source_target_pairs={{0,4},{4,0},{8,12},{12,8},{1,5},{5,1},{9,13},{13,9},{2,6},{6,2},{1... | collective-permute-start | bytes 1572872 | tf_op jit(solution)/shard_map/ppermute | solution.py:460
  311.9 3.7 %collective-permute-start.40 = (f32[8,256]{1,0:T(8,128)S(1)}, f32[8,256]{1,0:T(8,128)S(1)}, u32[]{:S(2)}, u32[]{:S(2)}) collective-permute-start(f32[8,256]{1,0:T(8,128)S(1)} %add_add_fusion.refs_1_), channel_id=1, source_target_pairs={{0,8},{4,12},{8,0},{12,4},{1,9},{5,13},{9,1},{13,5},{2,10},{6,14},... | collective-permute-start | bytes 24584 | tf_op jit(solution)/shard_map/ppermute | solution.py:460
  315.6 1.2 collective-permute-start.41
  (4 other events, 18.7 us)

commit v7 on v5

--- a/solution.py
+++ b/solution.py
@@ -379,33 +379,25 @@
     tp = len(places)
     pieces = refs[:tp]
     first, second, gain = refs[tp : tp + 3]
-    out, token, scale = refs[tp + 3 + more :]
-    step = pl.program_id(0)
-
-    @pl.when(step == 0)
-    def _():
-        inverse = lax.rsqrt((first[...] + second[...]) / D + 1e-05)
-        scale[...] = jnp.transpose(inverse)
-        token[...] = jnp.zeros(TOKEN, jnp.float32)
-
+    out, token = refs[tp + 3 + more :]
+    token[...] = jnp.zeros(TOKEN, jnp.float32)
+    inverse = lax.rsqrt((first[...] + second[...]) / D + 1e-05)
     rows, width = pieces[0].shape
-    factor = scale[pl.ds(pl.multiple_of(step * rows, rows), rows), 0:1]
+    scale = jnp.transpose(inverse)[0:rows, 0:1]
     for e, piece in zip(places, pieces):
         at = pl.ds(pl.multiple_of((info[0] ^ e) * width, width), width)
-        value = piece[...].astype(jnp.float32) * factor * gain[:, at]
+        value = piece[...].astype(jnp.float32) * scale * gain[:, at]
         out[:, at] = value.astype(jnp.bfloat16)
 
 
 def norm_rows(info, pieces, squares, column, gain, so_far, start, all_rows, after):
     tp = len(pieces)
     rows, width = pieces[0][1].shape
-    tiles = 4 if rows % 64 == 0 else 1
-    tile = rows // tiles
-    place = start // tile
+    place = start // rows
     small = pl.BlockSpec((8, lanes(rows)), lambda i, s: (0, column))
     operands = [piece for _, piece in pieces] + [*squares, gain]
     specs = (
-        [pl.BlockSpec((tile, width), lambda i, s: (i, 0))] * tp
+        [pl.BlockSpec((rows, width), lambda i, s: (0, 0))] * tp
         + [small] * 2
         + [pl.BlockSpec((1, tp * width), lambda i, s: (0, 0))]
     )
@@ -420,13 +412,12 @@
         functools.partial(norm_kernel, [e for e, _ in pieces], len(aliases) + len(after)),
         grid_spec=pltpu.PrefetchScalarGridSpec(
             num_scalar_prefetch=1,
-            grid=(tiles,),
+            grid=(1,),
             in_specs=specs,
             out_specs=[
-                pl.BlockSpec((tile, tp * width), lambda i, s: (place + i, 0)),
+                pl.BlockSpec((rows, tp * width), lambda i, s: (place, 0)),
                 token_spec(),
             ],
-            scratch_shapes=[pltpu.VMEM((lanes(rows), 8), jnp.float32)],
         ),
         out_shape=[jax.ShapeDtypeStruct((all_rows, tp * width), jnp.bfloat16), TOKEN_SHAPE],
         input_output_aliases=aliases,

time: 284 us -> 283 us (level)
  no operation moved by 1% of the time
where the time goes in v7:
time: 283 us; the launch traced here: 282 us
  Pallas kernels  126 us (45%)
  waiting for transfers between devices  103 us (36%)
  starting transfers between devices  42.9 us (15%)
  local copies, waits for them, and re-layouts  5.22 us (2%)
  other arithmetic  3.52 us (1%)
    pallas_call x6, Pallas kernels, matmul_stage(): pl.pallas_call(functools.partial(matmul_kernel, plan), grid_spec=pltpu.Pr...  105 us
    ppermute x9, waiting for transfers between devices, onward(): lax.ppermute(pair[1], 'sub', [(i, i - 1) for i in range(1, sub - d + 1)])  53.7 us
    ppermute x20, waiting for transfers between devices, swap(): return lax.ppermute(value, 'tp', [(i, i ^ d) for i in range(tp)])  24 us
    ppermute x9, starting transfers between devices, onward(): lax.ppermute(pair[0], 'sub', [(i, i + 1) for i in range(d - 1, sub - 1)])  19.5 us
    ppermute x9, waiting for transfers between devices, onward(): lax.ppermute(pair[0], 'sub', [(i, i + 1) for i in range(d - 1, sub - 1)])  16.1 us
    ppermute x9, starting transfers between devices, onward(): lax.ppermute(pair[1], 'sub', [(i, i - 1) for i in range(1, sub - d + 1)])  11.8 us
    ppermute x20, starting transfers between devices, swap(): return lax.ppermute(value, 'tp', [(i, i ^ d) for i in range(tp)])  11 us
    ppermute x3, waiting for transfers between devices, sum_along(): lax.ppermute(local, 'sub', [(i, (i + d) % sub) for i in range(sub)])  8.77 us
  transfers between devices with their start and end apart: 41, of which 14 were waited for; matrix products, arithmetic and copies ran while one was open for 2% of the time, Pallas kernels for 44%

profile of v7, /device:TPU:0, one launch (start us, length us, event | category | flops | bytes accessed | tf_op | source)
XLA Modules:
  0.0 281.7 jit_solution(318342833442022917)
XLA Ops:
  0.7 3.3 %fusion.4.refs_0_ = bf16[256,2048]{1,0:T(8,128)(2,1)} fusion(bf16[768,2048]{1,0:T(8,128)(2,1)} %up.3, bf16[768,2048]{1,0:T(8,128)(2,1)} %gate.13), kind=kLoop, calls=%fused_computation.7 | loop fusion | flops 4194304 | bytes 3145728 | tf_op jit(solution)/shard_map/convert_element_type | solution.py:562
  4.0 6.1 %collective-permute-start = (bf16[256,2048]{1,0:T(8,128)(2,1)}, bf16[256,2048]{1,0:T(8,128)(2,1)}, u32[]{:S(2)}, u32[]{:S(2)}) collective-permute-start(bf16[256,2048]{1,0:T(8,128)(2,1)} %fusion.4.refs_0_), channel_id=1, source_target_pairs={{0,1},{1,2},{2,3},{4,5},{5,6},{6,7},{8,9},{9,10},{10,11},{12,13},{... | collective-permute-start | bytes 3145736 | tf_op jit(solution)/shard_map/ppermute | solution.py:448
  10.1 1.3 collective-permute-start.1
  11.4 3.6 %hidden_rows.2 = (bf16[256,2048]{1,0:T(8,128)(2,1)}, f32[8,128]{1,0:T(8,128)S(1)}) custom-call(bf16[768,2048]{1,0:T(8,128)(2,1)S(1)} %copy-done.2, bf16[768,2048]{1,0:T(8,128)(2,1)} %up.3, bf16[256,2048]{1,0:T(8,128)(2,1)} %fusion.4.refs_0_), custom_call_target="tpu_custom_call" | custom-call | flops 1 | bytes 1 | tf_op jit(solution)/shard_map/hidden_rows/pallas_call | solution.py:67
  15.0 5.6 %collective-permute-start.6 = (bf16[256,2048]{1,0:T(8,128)(2,1)}, bf16[256,2048]{1,0:T(8,128)(2,1)}, u32[]{:S(2)}, u32[]{:S(2)}) collective-permute-start(bf16[256,2048]{1,0:T(8,128)(2,1)} %get-tuple-element.83.refs_0_), channel_id=1, source_target_pairs={{0,1},{1,2},{2,3},{4,5},{5,6},{6,7},{8,9},{9,10},{10,11},{12,13},{... | collective-permute-start | bytes 3145736 | tf_op jit(solution)/shard_map/ppermute | solution.py:448
  20.6 1.3 collective-permute-start.7
  22.6 2.8 gather_fusion
  25.4 7.5 %collective-permute-done.refs_0_ = bf16[256,2048]{1,0:T(8,128)(2,1)} collective-permute-done((bf16[256,2048]{1,0:T(8,128)(2,1)}, bf16[256,2048]{1,0:T(8,128)(2,1)}, u32[]{:S(2)}, u32[]{:S(2)}) %collective-permute-start) | collective-permute-done | bytes 1048608 | tf_op jit(solution)/shard_map/ppermute | solution.py:448
  32.9 5.4 %collective-permute-done.1.refs_1_ = bf16[256,2048]{1,0:T(8,128)(2,1)} collective-permute-done((bf16[256,2048]{1,0:T(8,128)(2,1)}, bf16[256,2048]{1,0:T(8,128)(2,1)}, u32[]{:S(2)}, u32[]{:S(2)}) %collective-permute-start.1) | collective-permute-done | bytes 1048608 | tf_op jit(solution)/shard_map/ppermute | solution.py:449
  38.3 3.0 %hidden_rows.3 = (bf16[256,2048]{1,0:T(8,128)(2,1)}, f32[8,128]{1,0:T(8,128)S(1)}) custom-call(bf16[768,2048]{1,0:T(8,128)(2,1)S(1)} %copy-done.3, bf16[768,2048]{1,0:T(8,128)(2,1)} %up.3, f32[8,128]{1,0:T(8,128)S(1)} %get-tuple-element.77.refs_0_), custom_call_target="tpu_custom_call" | custom-call | flops 1 | bytes 1 | tf_op jit(solution)/shard_map/hidden_rows/pallas_call | solution.py:67
  41.3 2.6 collective-permute-start.4
  43.9 1.3 collective-permute-start.5
  45.2 1.7 collective-permute-start.2
  46.8 8.5 %collective-permute-done.6.refs_0_ = bf16[256,2048]{1,0:T(8,128)(2,1)} collective-permute-done((bf16[256,2048]{1,0:T(8,128)(2,1)}, bf16[256,2048]{1,0:T(8,128)(2,1)}, u32[]{:S(2)}, u32[]{:S(2)}) %collective-permute-start.6) | collective-permute-done | bytes 1048608 | tf_op jit(solution)/shard_map/ppermute | solution.py:448
  55.4 1.3 collective-permute-start.3
  57.5 19.8 %matmul_stage.6 = (f32[4,256,1024]{2,1,0:T(8,128)}, f32[8,128]{1,0:T(8,128)S(1)}) custom-call(s32[19]{0:T(128)S(1)} %pad_add_fusion.info, bf16[256,2048]{1,0:T(8,128)(2,1)} %fusion.4.refs_0_, bf16[256,2048]{1,0:T(8,128)(2,1)} %get-tuple-element.75.refs_1_, bf16[256,2048]{1,0:T(8,128)(2,1)} %get-tuple-element.76.refs_2_, bf16[8192,4096]{1,0:T(8,128)(2,1)} %refs_2_.3, ...), custom_call_target="tpu_custom_call" | custom-call | flops 1 | bytes 1 | tf_op jit(solution)/shard_map/matmul_stage/pallas_call | solution.py:237
  78.6 1.3 collective-permute-start.9
  79.9 3.4 %collective-permute-done.5.refs_3_ = bf16[256,2048]{1,0:T(8,128)(2,1)} collective-permute-done((bf16[256,2048]{1,0:T(8,128)(2,1)}, bf16[256,2048]{1,0:T(8,128)(2,1)}, u32[]{:S(2)}, u32[]{:S(2)}) %collective-permute-start.5) | collective-permute-done | bytes 1048608 | tf_op jit(solution)/shard_map/ppermute | solution.py:449
  83.3 22.5 %collective-permute-done.3.refs_1_ = bf16[256,2048]{1,0:T(8,128)(2,1)} collective-permute-done((bf16[256,2048]{1,0:T(8,128)(2,1)}, bf16[256,2048]{1,0:T(8,128)(2,1)}, u32[]{:S(2)}, u32[]{:S(2)}) %collective-permute-start.3) | collective-permute-done | bytes 1048608 | tf_op jit(solution)/shard_map/ppermute | solution.py:449
  106.5 1.3 collective-permute-start.13
  107.8 27.0 %matmul_stage.7 = (f32[4,512,1024]{2,1,0:T(8,128)}, f32[8,128]{1,0:T(8,128)S(1)}) custom-call(s32[19]{0:T(128)S(1)} %pad_add_fusion.info, bf16[256,2048]{1,0:T(8,128)(2,1)} %get-tuple-element.83.refs_0_, bf16[256,2048]{1,0:T(8,128)(2,1)} %get-tuple-element.78.refs_1_, bf16[256,2048]{1,0:T(8,128)(2,1)} %get-tuple-element.84.refs_2_, ...), custom_call_target="tpu_custom_call" | custom-call | flops 1 | bytes 1 | tf_op jit(solution)/shard_map/matmul_stage/pallas_call | solution.py:237
  135.6 1.3 collective-permute-start.11
  136.9 12.2 %collective-permute-done.13.refs_3_ = bf16[256,2048]{1,0:T(8,128)(2,1)S(1)} collective-permute-done((bf16[256,2048]{1,0:T(8,128)(2,1)}, bf16[256,2048]{1,0:T(8,128)(2,1)S(1)}, u32[]{:S(2)}, u32[]{:S(2)}) %collective-permute-start.13) | collective-permute-done | bytes 1048608 | tf_op jit(solution)/shard_map/ppermute | solution.py:449
  149.1 1.0 copy-done.8
  150.1 19.5 %matmul_stage.8 = (f32[256,1024]{1,0:T(8,128)S(1)}, f32[256,1024]{1,0:T(8,128)S(1)}, bf16[256,1024]{1,0:T(8,128)(2,1)}, bf16[256,1024]{1,0:T(8,128)(2,1)S(1)}, f32[8,128]{1,0:T(8,128)S(1)}) custom-call(s32[19]{0:T(128)S(1)} %pad_add_fusion.info, bf16[256,2048]{1,0:T(8,128)(2,1)} %get-tuple-element.90.refs_0_, bf16[256,2048]{1,0:T(8,128)(2,1)} %get-tuple-element.91.refs_1_, ...), custom_call_target="tpu_custom_call" | custom-call | flops 1 | bytes 1 | tf_op jit(solution)/shard_map/matmul_stage/pallas_call | solution.py:237
  170.4 1.3 collective-permute-start.18
  172.4 1.6 collective-permute-start.20
  174.7 1.5 collective-permute-start.16
  176.3 16.4 %matmul_stage.9 = (f32[4,512,1024]{2,1,0:T(8,128)}, f32[8,128]{1,0:T(8,128)S(1)}) custom-call(s32[19]{0:T(128)S(1)} %pad_add_fusion.info, bf16[256,2048]{1,0:T(8,128)(2,1)S(1)} %get-tuple-element.103.refs_0_, bf16[256,2048]{1,0:T(8,128)(2,1)S(1)} %get-tuple-element.101.refs_1_, bf16[256,2048]{1,0:T(8,128)(2,1)S(1)} %get-tuple-element.104.refs_2_, ...), custom_call_target="tpu_custom_call" | custom-call | flops 1 | bytes 1 | tf_op jit(solution)/shard_map/matmul_stage/pallas_call | solution.py:237
  192.7 1.8 stream_rows.3
  195.3 2.9 %collective-permute-done.18.refs_1_ = bf16[256,2048]{1,0:T(8,128)(2,1)S(1)} collective-permute-done((bf16[256,2048]{1,0:T(8,128)(2,1)S(1)}, bf16[256,2048]{1,0:T(8,128)(2,1)S(1)}, u32[]{:S(2)}, u32[]{:S(2)}) %collective-permute-start.18) | collective-permute-done | bytes 1048608 | tf_op jit(solution)/shard_map/ppermute | solution.py:449
  198.3 11.1 %matmul_stage.10 = (f32[256,1024]{1,0:T(8,128)S(1)}, f32[256,1024]{1,0:T(8,128)S(1)}, bf16[256,1024]{1,0:T(8,128)(2,1)S(1)}, bf16[256,1024]{1,0:T(8,128)(2,1)S(1)}, f32[8,128]{1,0:T(8,128)S(1)}) custom-call(s32[19]{0:T(128)S(1)} %pad_add_fusion.info, bf16[256,2048]{1,0:T(8,128)(2,1)S(1)} %collective-permute-done.17.refs_0_, ...), custom_call_target="tpu_custom_call" | custom-call | flops 1 | bytes 1 | tf_op jit(solution)/shard_map/matmul_stage/pallas_call | solution.py:237
  209.9 1.4 collective-permute-done.21.refs_1_
  211.5 1.6 collective-permute-start.26
  213.0 7.3 %collective-permute-done.16.refs_1_ = bf16[256,2048]{1,0:T(8,128)(2,1)S(1)} collective-permute-done((bf16[256,2048]{1,0:T(8,128)(2,1)S(1)}, bf16[256,2048]{1,0:T(8,128)(2,1)S(1)}, u32[]{:S(2)}, u32[]{:S(2)}) %collective-permute-start.16) | collective-permute-done | bytes 1048608 | tf_op jit(solution)/shard_map/ppermute | solution.py:449
  220.3 11.1 %matmul_stage.11 = (f32[256,1024]{1,0:T(8,128)S(1)}, f32[256,1024]{1,0:T(8,128)S(1)}, bf16[256,1024]{1,0:T(8,128)(2,1)S(1)}, bf16[256,1024]{1,0:T(8,128)(2,1)S(1)}, f32[8,128]{1,0:T(8,128)S(1)}) custom-call(s32[19]{0:T(128)S(1)} %pad_add_fusion.info, bf16[256,2048]{1,0:T(8,128)(2,1)S(1)} %collective-permute-done.15.refs_0_, ...), custom_call_target="tpu_custom_call" | custom-call | flops 1 | bytes 1 | tf_op jit(solution)/shard_map/matmul_stage/pallas_call | solution.py:237
  232.0 1.5 stream_rows.4
  233.7 1.6 collective-permute-start.27
  235.8 12.7 %collective-permute-done.27.last = bf16[256,1024]{1,0:T(8,128)(2,1)S(1)} collective-permute-done((bf16[256,1024]{1,0:T(8,128)(2,1)S(1)}, bf16[256,1024]{1,0:T(8,128)(2,1)S(1)}, u32[]{:S(2)}, u32[]{:S(2)}) %collective-permute-start.27) | collective-permute-done | bytes 524320 | tf_op jit(solution)/shard_map/ppermute | solution.py:445
  248.5 1.5 stream_rows.5
  250.0 1.5 collective-permute-start.28
  252.3 5.0 %collective-permute-done.29 = f32[8,768]{1,0:T(8,128)S(1)} collective-permute-done((f32[8,768]{1,0:T(8,128)S(1)}, f32[8,768]{1,0:T(8,128)S(1)}, u32[]{:S(2)}, u32[]{:S(2)}) %collective-permute-start.29) | collective-permute-done | bytes 24608 | tf_op jit(solution)/shard_map/ppermute | solution.py:496
  257.3 3.8 %collective-permute-done.31 = f32[8,768]{1,0:T(8,128)S(1)} collective-permute-done((f32[8,768]{1,0:T(8,128)S(1)}, f32[8,768]{1,0:T(8,128)S(1)}, u32[]{:S(2)}, u32[]{:S(2)}) %collective-permute-start.31) | collective-permute-done | bytes 24608 | tf_op jit(solution)/shard_map/ppermute | solution.py:496
  262.3 8.1 %collective-permute-done.28.refs_0_ = bf16[256,1024]{1,0:T(8,128)(2,1)S(1)} collective-permute-done((bf16[256,1024]{1,0:T(8,128)(2,1)S(1)}, bf16[256,1024]{1,0:T(8,128)(2,1)S(1)}, u32[]{:S(2)}, u32[]{:S(2)}) %collective-permute-start.28) | collective-permute-done | bytes 524320 | tf_op jit(solution)/shard_map/ppermute | solution.py:445
  272.1 1.7 collective-permute-done.35.refs_5_
  273.8 2.6 norm_rows.3
  276.5 2.6 norm_rows.4
  279.1 2.6 norm_rows.5
  (92 shorter events, 13.0 us)
Async XLA Ops:
  0.6 21.9 %copy-start = (bf16[768,1024]{1,0:T(8,128)(2,1)S(1)}, bf16[768,1024]{1,0:T(8,128)(2,1)}, u32[]{:S(2)}) copy-start(bf16[768,1024]{1,0:T(8,128)(2,1)} %param.11) | copy-start | bytes 4718596
  0.6 10.7 %copy-start.2 = (bf16[768,2048]{1,0:T(8,128)(2,1)S(1)}, bf16[768,2048]{1,0:T(8,128)(2,1)}, u32[]{:S(2)}) copy-start(bf16[768,2048]{1,0:T(8,128)(2,1)} %gate.13) | copy-start | bytes 9437188
  4.0 18.6 %copy-start.9 = (s32[768]{0:T(1024)S(1)}, s32[768]{0:T(1024)}, u32[]{:S(2)}) copy-start(s32[768]{0:T(1024)} %param.13) | copy-start | bytes 9220
  4.0 28.9 %collective-permute-start = (bf16[256,2048]{1,0:T(8,128)(2,1)}, bf16[256,2048]{1,0:T(8,128)(2,1)}, u32[]{:S(2)}, u32[]{:S(2)}) collective-permute-start(bf16[256,2048]{1,0:T(8,128)(2,1)} %fusion.4.refs_0_), channel_id=1, source_target_pairs={{0,1},{1,2},{2,3},{4,5},{5,6},{6,7},{8,9},{9,10},{10,11},{12,13},{... | collective-permute-start | bytes 3145736 | tf_op jit(solution)/shard_map/ppermute | solution.py:448
  10.1 28.3 %collective-permute-start.1 = (bf16[256,2048]{1,0:T(8,128)(2,1)}, bf16[256,2048]{1,0:T(8,128)(2,1)}, u32[]{:S(2)}, u32[]{:S(2)}) collective-permute-start(bf16[256,2048]{1,0:T(8,128)(2,1)} %fusion.4.refs_0_), channel_id=1, source_target_pairs={{1,0},{2,1},{3,2},{5,4},{6,5},{7,6},{9,8},{10,9},{11,10},{13,12},{... | collective-permute-start | bytes 3145736 | tf_op jit(solution)/shard_map/ppermute | solution.py:449
  15.0 40.4 %collective-permute-start.6 = (bf16[256,2048]{1,0:T(8,128)(2,1)}, bf16[256,2048]{1,0:T(8,128)(2,1)}, u32[]{:S(2)}, u32[]{:S(2)}) collective-permute-start(bf16[256,2048]{1,0:T(8,128)(2,1)} %get-tuple-element.83.refs_0_), channel_id=1, source_target_pairs={{0,1},{1,2},{2,3},{4,5},{5,6},{6,7},{8,9},{9,10},{10,11},{12,13},{... | collective-permute-start | bytes 3145736 | tf_op jit(solution)/shard_map/ppermute | solution.py:448
  20.6 56.7 %collective-permute-start.7 = (bf16[256,2048]{1,0:T(8,128)(2,1)}, bf16[256,2048]{1,0:T(8,128)(2,1)}, u32[]{:S(2)}, u32[]{:S(2)}) collective-permute-start(bf16[256,2048]{1,0:T(8,128)(2,1)} %get-tuple-element.83.refs_0_), channel_id=1, source_target_pairs={{1,0},{2,1},{3,2},{5,4},{6,5},{7,6},{9,8},{10,9},{11,10},{13,12},{... | collective-permute-start | bytes 3145736 | tf_op jit(solution)/shard_map/ppermute | solution.py:449
  25.4 13.0 %copy-start.3 = (bf16[768,2048]{1,0:T(8,128)(2,1)S(1)}, bf16[768,2048]{1,0:T(8,128)(2,1)}, u32[]{:S(2)}) copy-start(bf16[768,2048]{1,0:T(8,128)(2,1)} %gate.13) | copy-start | bytes 9437188
  41.3 37.3 %collective-permute-start.4 = (bf16[256,2048]{1,0:T(8,128)(2,1)}, bf16[256,2048]{1,0:T(8,128)(2,1)S(1)}, u32[]{:S(2)}, u32[]{:S(2)}) collective-permute-start(bf16[256,2048]{1,0:T(8,128)(2,1)} %get-tuple-element.78.refs_1_), channel_id=1, source_target_pairs={{0,1},{1,2},{2,3},{4,5},{5,6},{6,7},{8,9},{9,10},{10,11},{12,13},{... | collective-permute-start | bytes 3145736 | tf_op jit(solution)/shard_map/ppermute | solution.py:448
  43.9 39.4 %collective-permute-start.5 = (bf16[256,2048]{1,0:T(8,128)(2,1)}, bf16[256,2048]{1,0:T(8,128)(2,1)}, u32[]{:S(2)}, u32[]{:S(2)}) collective-permute-start(bf16[256,2048]{1,0:T(8,128)(2,1)} %get-tuple-element.78.refs_1_), channel_id=1, source_target_pairs={{1,0},{2,1},{3,2},{5,4},{6,5},{7,6},{9,8},{10,9},{11,10},{13,12},{... | collective-permute-start | bytes 3145736 | tf_op jit(solution)/shard_map/ppermute | solution.py:449
  45.2 38.1 %collective-permute-start.2 = (bf16[256,2048]{1,0:T(8,128)(2,1)}, bf16[256,2048]{1,0:T(8,128)(2,1)}, u32[]{:S(2)}, u32[]{:S(2)}) collective-permute-start(bf16[256,2048]{1,0:T(8,128)(2,1)} %get-tuple-element.75.refs_1_), channel_id=1, source_target_pairs={{1,2},{2,3},{5,6},{6,7},{9,10},{10,11},{13,14},{14,15},{17,18},{18... | collective-permute-start | bytes 3145736 | tf_op jit(solution)/shard_map/ppermute | solution.py:448
  55.4 50.4 %collective-permute-start.3 = (bf16[256,2048]{1,0:T(8,128)(2,1)}, bf16[256,2048]{1,0:T(8,128)(2,1)}, u32[]{:S(2)}, u32[]{:S(2)}) collective-permute-start(bf16[256,2048]{1,0:T(8,128)(2,1)} %get-tuple-element.76.refs_2_), channel_id=1, source_target_pairs={{1,0},{2,1},{5,4},{6,5},{9,8},{10,9},{13,12},{14,13},{17,16},{18,1... | collective-permute-start | bytes 3145736 | tf_op jit(solution)/shard_map/ppermute | solution.py:449
  77.9 57.0 %collective-permute-start.8 = (bf16[256,2048]{1,0:T(8,128)(2,1)}, bf16[256,2048]{1,0:T(8,128)(2,1)S(1)}, u32[]{:S(2)}, u32[]{:S(2)}) collective-permute-start(bf16[256,2048]{1,0:T(8,128)(2,1)} %get-tuple-element.84.refs_2_), channel_id=1, source_target_pairs={{1,2},{2,3},{5,6},{6,7},{9,10},{10,11},{13,14},{14,15},{17,18},{18... | collective-permute-start | bytes 3145736 | tf_op jit(solution)/shard_map/ppermute | solution.py:448
  78.6 56.2 %collective-permute-start.9 = (bf16[256,2048]{1,0:T(8,128)(2,1)}, bf16[256,2048]{1,0:T(8,128)(2,1)S(1)}, u32[]{:S(2)}, u32[]{:S(2)}) collective-permute-start(bf16[256,2048]{1,0:T(8,128)(2,1)} %get-tuple-element.85.refs_4_), channel_id=1, source_target_pairs={{1,0},{2,1},{5,4},{6,5},{9,8},{10,9},{13,12},{14,13},{17,16},{18,1... | collective-permute-start | bytes 3145736 | tf_op jit(solution)/shard_map/ppermute | solution.py:449
  105.8 31.1 %collective-permute-start.12 = (bf16[256,2048]{1,0:T(8,128)(2,1)}, bf16[256,2048]{1,0:T(8,128)(2,1)S(1)}, u32[]{:S(2)}, u32[]{:S(2)}) collective-permute-start(bf16[256,2048]{1,0:T(8,128)(2,1)} %get-tuple-element.90.refs_0_), channel_id=1, source_target_pairs={{2,3},{6,7},{10,11},{14,15},{18,19},{22,23},{26,27},{30,31}} | collective-permute-start | bytes 3145736 | tf_op jit(solution)/shard_map/ppermute | solution.py:448
  106.5 42.6 %collective-permute-start.13 = (bf16[256,2048]{1,0:T(8,128)(2,1)}, bf16[256,2048]{1,0:T(8,128)(2,1)S(1)}, u32[]{:S(2)}, u32[]{:S(2)}) collective-permute-start(bf16[256,2048]{1,0:T(8,128)(2,1)} %get-tuple-element.91.refs_1_), channel_id=1, source_target_pairs={{1,0},{5,4},{9,8},{13,12},{17,16},{21,20},{25,24},{29,28}} | collective-permute-start | bytes 3145736 | tf_op jit(solution)/shard_map/ppermute | solution.py:449
  134.9 37.5 %collective-permute-start.10 = (bf16[256,2048]{1,0:T(8,128)(2,1)S(1)}, bf16[256,2048]{1,0:T(8,128)(2,1)S(1)}, u32[]{:S(2)}, u32[]{:S(2)}) collective-permute-start(bf16[256,2048]{1,0:T(8,128)(2,1)S(1)} %get-tuple-element.88), channel_id=1, source_target_pairs={{1,2},{2,3},{5,6},{6,7},{9,10},{10,11},{13,14},{14,15},{17,18},{18... | collective-permute-start | bytes 3145736 | tf_op jit(solution)/shard_map/ppermute | solution.py:448
  135.6 38.3 %collective-permute-start.11 = (bf16[256,2048]{1,0:T(8,128)(2,1)}, bf16[256,2048]{1,0:T(8,128)(2,1)S(1)}, u32[]{:S(2)}, u32[]{:S(2)}) collective-permute-start(bf16[256,2048]{1,0:T(8,128)(2,1)} %get-tuple-element.89), channel_id=1, source_target_pairs={{1,0},{2,1},{5,4},{6,5},{9,8},{10,9},{13,12},{14,13},{17,16},{18,1... | collective-permute-start | bytes 3145736 | tf_op jit(solution)/shard_map/ppermute | solution.py:449
  136.9 12.2 %copy-start.7 = (bf16[256,2048]{1,0:T(8,128)(2,1)}, bf16[256,2048]{1,0:T(8,128)(2,1)S(1)}, u32[]{:S(2)}) copy-start(bf16[256,2048]{1,0:T(8,128)(2,1)S(1)} %collective-permute-done.12.refs_2_) | copy-start | bytes 3145732
  169.6 2.1 collective-permute-start.14
  169.7 25.7 %collective-permute-start.17 = (bf16[256,2048]{1,0:T(8,128)(2,1)S(1)}, bf16[256,2048]{1,0:T(8,128)(2,1)S(1)}, u32[]{:S(2)}, u32[]{:S(2)}) collective-permute-start(bf16[256,2048]{1,0:T(8,128)(2,1)S(1)} %get-tuple-element.103.refs_0_), channel_id=1, source_target_pairs={{2,3},{6,7},{10,11},{14,15},{18,19},{22,23},{26,27},{30,31}} | collective-permute-start | bytes 3145736 | tf_op jit(solution)/shard_map/ppermute | solution.py:448
  170.4 27.9 %collective-permute-start.18 = (bf16[256,2048]{1,0:T(8,128)(2,1)S(1)}, bf16[256,2048]{1,0:T(8,128)(2,1)S(1)}, u32[]{:S(2)}, u32[]{:S(2)}) collective-permute-start(bf16[256,2048]{1,0:T(8,128)(2,1)S(1)} %get-tuple-element.104.refs_2_), channel_id=1, source_target_pairs={{1,0},{5,4},{9,8},{13,12},{17,16},{21,20},{25,24},{29,28}} | collective-permute-start | bytes 3145736 | tf_op jit(solution)/shard_map/ppermute | solution.py:449
  171.7 3.0 %collective-permute-start.19 = (bf16[256,1024]{1,0:T(8,128)(2,1)}, bf16[256,1024]{1,0:T(8,128)(2,1)S(1)}, u32[]{:S(2)}, u32[]{:S(2)}) collective-permute-start(bf16[256,1024]{1,0:T(8,128)(2,1)} %get-tuple-element.109), channel_id=1, source_target_pairs={{0,4},{4,0},{8,12},{12,8},{1,5},{5,1},{9,13},{13,9},{2,6},{6,2},{1... | collective-permute-start | bytes 1572872 | tf_op jit(solution)/shard_map/ppermute | solution.py:445
  172.4 20.3 %collective-permute-start.20 = (bf16[256,1024]{1,0:T(8,128)(2,1)S(1)}, bf16[256,1024]{1,0:T(8,128)(2,1)S(1)}, u32[]{:S(2)}, u32[]{:S(2)}) collective-permute-start(bf16[256,1024]{1,0:T(8,128)(2,1)S(1)} %get-tuple-element.110), channel_id=1, source_target_pairs={{0,8},{4,12},{8,0},{12,4},{1,9},{5,13},{9,1},{13,5},{2,10},{6,14},... | collective-permute-start | bytes 1572872 | tf_op jit(solution)/shard_map/ppermute | solution.py:445
  173.9 39.1 %collective-permute-start.15 = (bf16[256,2048]{1,0:T(8,128)(2,1)S(1)}, bf16[256,2048]{1,0:T(8,128)(2,1)S(1)}, u32[]{:S(2)}, u32[]{:S(2)}) collective-permute-start(bf16[256,2048]{1,0:T(8,128)(2,1)S(1)} %get-tuple-element.101.refs_1_), channel_id=1, source_target_pairs={{2,3},{6,7},{10,11},{14,15},{18,19},{22,23},{26,27},{30,31}} | collective-permute-start | bytes 3145736 | tf_op jit(solution)/shard_map/ppermute | solution.py:448
  174.7 45.6 %collective-permute-start.16 = (bf16[256,2048]{1,0:T(8,128)(2,1)S(1)}, bf16[256,2048]{1,0:T(8,128)(2,1)S(1)}, u32[]{:S(2)}, u32[]{:S(2)}) collective-permute-start(bf16[256,2048]{1,0:T(8,128)(2,1)S(1)} %get-tuple-element.102.refs_3_), channel_id=1, source_target_pairs={{1,0},{5,4},{9,8},{13,12},{17,16},{21,20},{25,24},{29,28}} | collective-permute-start | bytes 3145736 | tf_op jit(solution)/shard_map/ppermute | solution.py:449
  176.3 16.5 %copy-start.5 = (f32[256,1024]{1,0:T(8,128)S(1)}, f32[256,1024]{1,0:T(8,128)}, u32[]{:S(2)}) copy-start(f32[256,1024]{1,0:T(8,128)} %copy-done.4) | copy-start | bytes 3145732
  194.5 15.4 %collective-permute-start.22 = (bf16[256,1024]{1,0:T(8,128)(2,1)S(1)}, bf16[256,1024]{1,0:T(8,128)(2,1)S(1)}, u32[]{:S(2)}, u32[]{:S(2)}) collective-permute-start(bf16[256,1024]{1,0:T(8,128)(2,1)S(1)} %get-tuple-element.117.refs_0_), channel_id=1, source_target_pairs={{0,8},{4,12},{8,0},{12,4},{1,9},{5,13},{9,1},{13,5},{2,10},{6,14},... | collective-permute-start | bytes 1572872 | tf_op jit(solution)/shard_map/ppermute | solution.py:445
  209.4 2.0 collective-permute-start.21
  209.4 22.5 %collective-permute-start.25 = (bf16[256,1024]{1,0:T(8,128)(2,1)S(1)}, bf16[256,1024]{1,0:T(8,128)(2,1)S(1)}, u32[]{:S(2)}, u32[]{:S(2)}) collective-permute-start(bf16[256,1024]{1,0:T(8,128)(2,1)S(1)} %get-tuple-element.126), channel_id=1, source_target_pairs={{0,4},{4,0},{8,12},{12,8},{1,5},{5,1},{9,13},{13,9},{2,6},{6,2},{1... | collective-permute-start | bytes 1572872 | tf_op jit(solution)/shard_map/ppermute | solution.py:445
  211.5 20.5 %collective-permute-start.26 = (bf16[256,1024]{1,0:T(8,128)(2,1)S(1)}, bf16[256,1024]{1,0:T(8,128)(2,1)S(1)}, u32[]{:S(2)}, u32[]{:S(2)}) collective-permute-start(bf16[256,1024]{1,0:T(8,128)(2,1)S(1)} %get-tuple-element.127), channel_id=1, source_target_pairs={{0,8},{4,12},{8,0},{12,4},{1,9},{5,13},{9,1},{13,5},{2,10},{6,14},... | collective-permute-start | bytes 1572872 | tf_op jit(solution)/shard_map/ppermute | solution.py:445
  231.4 2.1 collective-permute-start.24
  231.5 4.3 %collective-permute-start.23 = (bf16[256,1024]{1,0:T(8,128)(2,1)S(1)}, bf16[256,1024]{1,0:T(8,128)(2,1)S(1)}, u32[]{:S(2)}, u32[]{:S(2)}) collective-permute-start(bf16[256,1024]{1,0:T(8,128)(2,1)S(1)} %get-tuple-element.122), channel_id=1, source_target_pairs={{0,4},{4,0},{8,12},{12,8},{1,5},{5,1},{9,13},{13,9},{2,6},{6,2},{1... | collective-permute-start | bytes 1572872 | tf_op jit(solution)/shard_map/ppermute | solution.py:445
  233.7 14.8 %collective-permute-start.27 = (bf16[256,1024]{1,0:T(8,128)(2,1)S(1)}, bf16[256,1024]{1,0:T(8,128)(2,1)S(1)}, u32[]{:S(2)}, u32[]{:S(2)}) collective-permute-start(bf16[256,1024]{1,0:T(8,128)(2,1)S(1)} %get-tuple-element.131), channel_id=1, source_target_pairs={{0,8},{4,12},{8,0},{12,4},{1,9},{5,13},{9,1},{13,5},{2,10},{6,14},... | collective-permute-start | bytes 1572872 | tf_op jit(solution)/shard_map/ppermute | solution.py:445
  235.2 35.8 %collective-permute-start.39 = (bf16[256,1024]{1,0:T(8,128)(2,1)S(1)}, bf16[256,1024]{1,0:T(8,128)(2,1)S(1)}, u32[]{:S(2)}, u32[]{:S(2)}) collective-permute-start(bf16[256,1024]{1,0:T(8,128)(2,1)S(1)} %get-tuple-element.117.refs_0_), channel_id=1, source_target_pairs={{0,4},{4,0},{8,12},{12,8},{1,5},{5,1},{9,13},{13,9},{2,6},{6,2},{1... | collective-permute-start | bytes 1572872 | tf_op jit(solution)/shard_map/ppermute | solution.py:445
  235.2 26.5 %collective-permute-start.36 = (bf16[256,1024]{1,0:T(8,128)(2,1)S(1)}, bf16[256,1024]{1,0:T(8,128)(2,1)S(1)}, u32[]{:S(2)}, u32[]{:S(2)}) collective-permute-start(bf16[256,1024]{1,0:T(8,128)(2,1)S(1)} %get-tuple-element.138.refs_0_), channel_id=1, source_target_pairs={{0,8},{4,12},{8,0},{12,4},{1,9},{5,13},{9,1},{13,5},{2,10},{6,14},... | collective-permute-start | bytes 1572872 | tf_op jit(solution)/shard_map/ppermute | solution.py:445
  248.5 25.3 %copy-start.6 = (f32[4096]{0:T(1024)S(1)}, f32[4096]{0:T(1024)}, u32[]{:S(2)}) copy-start(f32[4096]{0:T(1024)} %param.14) | copy-start | bytes 49156
  250.0 20.3 %collective-permute-start.28 = (bf16[256,1024]{1,0:T(8,128)(2,1)S(1)}, bf16[256,1024]{1,0:T(8,128)(2,1)S(1)}, u32[]{:S(2)}, u32[]{:S(2)}) collective-permute-start(bf16[256,1024]{1,0:T(8,128)(2,1)S(1)} %get-tuple-element.135.refs_0_), channel_id=1, source_target_pairs={{0,8},{4,12},{8,0},{12,4},{1,9},{5,13},{9,1},{13,5},{2,10},{6,14},... | collective-permute-start | bytes 1572872 | tf_op jit(solution)/shard_map/ppermute | solution.py:445
  251.6 5.7 %collective-permute-start.29 = (f32[8,768]{1,0:T(8,128)S(1)}, f32[8,768]{1,0:T(8,128)S(1)}, u32[]{:S(2)}, u32[]{:S(2)}) collective-permute-start(f32[8,768]{1,0:T(8,128)S(1)} %constant_dynamic-update-slice_fusion), channel_id=1, source_target_pairs={{0,1},{1,2},{2,3},{3,0},{4,5},{5,6},{6,7},{7,4},{8,9},{9,10},{10,1... | collective-permute-start | bytes 73736 | tf_op jit(solution)/shard_map/ppermute | solution.py:496
  251.6 5.7 %collective-permute-start.30 = (f32[8,768]{1,0:T(8,128)S(1)}, f32[8,768]{1,0:T(8,128)S(1)}, u32[]{:S(2)}, u32[]{:S(2)}) collective-permute-start(f32[8,768]{1,0:T(8,128)S(1)} %constant_dynamic-update-slice_fusion), channel_id=1, source_target_pairs={{0,2},{1,3},{2,0},{3,1},{4,6},{5,7},{6,4},{7,5},{8,10},{9,11},{10,... | collective-permute-start | bytes 73736 | tf_op jit(solution)/shard_map/ppermute | solution.py:496
  257.2 3.8 %collective-permute-start.31 = (f32[8,768]{1,0:T(8,128)S(1)}, f32[8,768]{1,0:T(8,128)S(1)}, u32[]{:S(2)}, u32[]{:S(2)}) collective-permute-start(f32[8,768]{1,0:T(8,128)S(1)} %constant_dynamic-update-slice_fusion), channel_id=1, source_target_pairs={{0,3},{1,0},{2,1},{3,2},{4,7},{5,4},{6,5},{7,6},{8,11},{9,8},{10,9... | collective-permute-start | bytes 73736 | tf_op jit(solution)/shard_map/ppermute | solution.py:496
  257.2 14.3 %collective-permute-start.40 = (bf16[256,1024]{1,0:T(8,128)(2,1)S(1)}, bf16[256,1024]{1,0:T(8,128)(2,1)S(1)}, u32[]{:S(2)}, u32[]{:S(2)}) collective-permute-start(bf16[256,1024]{1,0:T(8,128)(2,1)S(1)} %get-tuple-element.140.refs_1_), channel_id=1, source_target_pairs={{0,4},{4,0},{8,12},{12,8},{1,5},{5,1},{9,13},{13,9},{2,6},{6,2},{1... | collective-permute-start | bytes 1572872 | tf_op jit(solution)/shard_map/ppermute | solution.py:445
  261.1 10.4 %collective-permute-start.34 = (f32[8,768]{1,0:T(8,128)S(1)}, f32[8,768]{1,0:T(8,128)S(1)}, u32[]{:S(2)}, u32[]{:S(2)}) collective-permute-start(f32[8,768]{1,0:T(8,128)S(1)} %add_add_fusion.refs_1_), channel_id=1, source_target_pairs={{0,8},{4,12},{8,0},{12,4},{1,9},{5,13},{9,1},{13,5},{2,10},{6,14},... | collective-permute-start | bytes 73736 | tf_op jit(solution)/shard_map/ppermute | solution.py:445
  261.7 14.8 %collective-permute-start.37 = (bf16[256,1024]{1,0:T(8,128)(2,1)S(1)}, bf16[256,1024]{1,0:T(8,128)(2,1)S(1)}, u32[]{:S(2)}, u32[]{:S(2)}) collective-permute-start(bf16[256,1024]{1,0:T(8,128)(2,1)S(1)} %get-tuple-element.138.refs_0_), channel_id=1, source_target_pairs={{0,4},{4,0},{8,12},{12,8},{1,5},{5,1},{9,13},{13,9},{2,6},{6,2},{1... | collective-permute-start | bytes 1572872 | tf_op jit(solution)/shard_map/ppermute | solution.py:445
  270.4 6.1 %collective-permute-start.38 = (bf16[256,1024]{1,0:T(8,128)(2,1)S(1)}, bf16[256,1024]{1,0:T(8,128)(2,1)S(1)}, u32[]{:S(2)}, u32[]{:S(2)}) collective-permute-start(bf16[256,1024]{1,0:T(8,128)(2,1)S(1)} %get-tuple-element.139.refs_1_), channel_id=1, source_target_pairs={{0,4},{4,0},{8,12},{12,8},{1,5},{5,1},{9,13},{13,9},{2,6},{6,2},{1... | collective-permute-start | bytes 1572872 | tf_op jit(solution)/shard_map/ppermute | solution.py:445
  271.0 8.1 %collective-permute-start.32 = (bf16[256,1024]{1,0:T(8,128)(2,1)S(1)}, bf16[256,1024]{1,0:T(8,128)(2,1)S(1)}, u32[]{:S(2)}, u32[]{:S(2)}) collective-permute-start(bf16[256,1024]{1,0:T(8,128)(2,1)S(1)} %get-tuple-element.135.refs_0_), channel_id=1, source_target_pairs={{0,4},{4,0},{8,12},{12,8},{1,5},{5,1},{9,13},{13,9},{2,6},{6,2},{1... | collective-permute-start | bytes 1572872 | tf_op jit(solution)/shard_map/ppermute | solution.py:445
  271.5 7.6 %collective-permute-start.33 = (bf16[256,1024]{1,0:T(8,128)(2,1)S(1)}, bf16[256,1024]{1,0:T(8,128)(2,1)S(1)}, u32[]{:S(2)}, u32[]{:S(2)}) collective-permute-start(bf16[256,1024]{1,0:T(8,128)(2,1)S(1)} %get-tuple-element.137.refs_1_), channel_id=1, source_target_pairs={{0,4},{4,0},{8,12},{12,8},{1,5},{5,1},{9,13},{13,9},{2,6},{6,2},{1... | collective-permute-start | bytes 1572872 | tf_op jit(solution)/shard_map/ppermute | solution.py:445
  271.6 2.3 collective-permute-start.35
  (3 other events, 8.0 us)
